TPU v7x, 32 devices: a whole 2x2x4 slice. The times are simulated.
32 devices in a mesh: maps: 4 (over y, x), band: 8 (over z, core).
Axes of the slice: x: 2, y: 2, z: 4, core: 2. Of those that a mesh axis runs over, the one named last changes fastest.
Arguments:
- tokens_in: bfloat16 [512, 48, 256], P(('maps', 'band')), may hold values from -6 to 6
- cotangent: bfloat16 [512, 48, 256], P(('maps', 'band')), may hold values from -6 to 6
- map_sizes: int32 [4, 2], P('maps'), may hold values from 34 to 128, as said below
- w_qkv: float32 [256, 768], P(('maps', 'band')), may hold values from -0.375 to 0.375
- w_out: float32 [256, 256], P(('maps', 'band')), may hold values from -1 to 1
- w_up: float32 [256, 768], P(('maps', 'band')), may hold values from -0.375 to 0.375
- w_down: float32 [768, 256], P(('maps', 'band')), may hold values from -0.21875 to 0.21875
- vectors: float32 [11, 256], P(None, ('maps', 'band'))
- pos_table: float32 [8, 49], replicated, may hold values from -4 to 4
- first_qkv: float32 [256, 768], P(('maps', 'band')), may hold values from -112 to 112
- second_qkv: float32 [256, 768], P(('maps', 'band')), may hold values from 12.288 to 196.608
- first_out: float32 [256, 256], P(('maps', 'band')), may hold values from -112 to 112
- second_out: float32 [256, 256], P(('maps', 'band')), may hold values from 12.288 to 196.608
- first_up: float32 [256, 768], P(('maps', 'band')), may hold values from -112 to 112
- second_up: float32 [256, 768], P(('maps', 'band')), may hold values from 12.288 to 196.608
- first_down: float32 [768, 256], P(('maps', 'band')), may hold values from -112 to 112
- second_down: float32 [768, 256], P(('maps', 'band')), may hold values from 12.288 to 196.608
- first_vectors: float32 [11, 256], P(None, ('maps', 'band')), may hold values from -112 to 112
- second_vectors: float32 [11, 256], P(None, ('maps', 'band')), may hold values from 12.288 to 196.608
- first_table: float32 [8, 49], replicated, may hold values from -112 to 112
- second_table: float32 [8, 49], replicated, may hold values from 12.288 to 196.608
Outputs:
- layer_out: bfloat16 [512, 48, 256], P(('maps', 'band'))
- tokens_grad: bfloat16 [512, 48, 256], P(('maps', 'band'))
- next_first_qkv: float32 [256, 768], P(('maps', 'band'))
- next_second_qkv: float32 [256, 768], P(('maps', 'band'))
- next_qkv: float32 [256, 768], P(('maps', 'band'))
- next_first_out: float32 [256, 256], P(('maps', 'band'))
- next_second_out: float32 [256, 256], P(('maps', 'band'))
- next_out: float32 [256, 256], P(('maps', 'band'))
- next_first_up: float32 [256, 768], P(('maps', 'band'))
- next_second_up: float32 [256, 768], P(('maps', 'band'))
- next_up: float32 [256, 768], P(('maps', 'band'))
- next_first_down: float32 [768, 256], P(('maps', 'band'))
- next_second_down: float32 [768, 256], P(('maps', 'band'))
- next_down: float32 [768, 256], P(('maps', 'band'))
- next_first_vectors: float32 [11, 256], P(None, ('maps', 'band'))
- next_second_vectors: float32 [11, 256], P(None, ('maps', 'band'))
- next_vectors: float32 [11, 256], P(None, ('maps', 'band'))
- next_first_table: float32 [8, 49], replicated
- next_second_table: float32 [8, 49], replicated
- next_table: float32 [8, 49], replicated
- weight_norms: float32 [16], replicated
- update_norms: float32 [16], replicated
Inputs may be any that keep to these rules, and one draw needn't show every extreme that they name: `map_sizes`: column 0 is a map's valid height, between 113 and 128; column 1 its valid width, at least seven tenths of 48; at least one map is valid everywhere.
All inputs are finite; a program needn't handle non-finite values.
Results may differ from a plain program's by a relative error of at most 0.012.
The roundings to bfloat16 on the way count: a program that leaves them out, or rounds other values in their place, can miss the bound.
Values may be sent and summed in bfloat16 or wider, within the bound.
No kernel may reach another device: no remote copies, remote signals or barrier semaphores. Data moves between devices by JAX's collectives and lax.ppermute only.
A program may use at most 256 MiB of HBM per device.

v0:
```python
from functools import partial

import jax
import jax.numpy as jnp
from jax import lax
from jax.sharding import PartitionSpec as P

HEADS = 8
WINDOW = 7
DILATION = 4
STEP = 10


NORM_EPS = 1e-05
BETA_FIRST = 0.9
BETA_SECOND = 0.999
ADAM_EPS = 1e-06
DECAY_RATE = 0.01
LEARN_RATE = 0.2
RATIO_EPS = 1e-06
MASKED = -1e30


def padded_2(shard, sides, width):
    for axis, dim in sides:
        size, length = (lax.axis_size(axis), shard.shape[dim])
        up = [(i, (i + 1) % size) for i in range(size - 1)]
        down = [(j, i) for i, j in up]
        last = lax.slice_in_dim(shard, length - width, length, axis=dim)
        leading = lax.slice_in_dim(shard, 0, width, axis=dim)
        before = lax.ppermute(last, axis, up)
        after = lax.ppermute(leading, axis, down)
        shard = jnp.concatenate([before, shard, after], axis=dim)
    return shard


def from_behind(block, axis, distance):
    devices = range(lax.axis_size(axis))
    route = [(i - distance, i) for i in devices if i - distance in devices]
    return lax.ppermute(block, axis, route)


def layer_norm(values, gain, shift):
    mean = jnp.mean(values, axis=-1, keepdims=True)
    centred = values - mean
    spread = jnp.mean(centred * centred, axis=-1, keepdims=True)
    return centred * lax.rsqrt(spread + NORM_EPS) * gain + shift


def inner(left, right):
    return lax.dot_general(
        left, right, (((0,), (0,)), ((), ())), preferred_element_type=jnp.float32
    )


def against(left, right):
    return lax.dot_general(
        left, right, (((1,), (1,)), ((), ())), preferred_element_type=jnp.float32
    )


def column_shift(block, offset):
    if offset >= 0:
        return jnp.pad(block[:, offset:], ((0, 0), (0, offset), (0, 0)))
    return jnp.pad(block[:, :offset], ((0, 0), (-offset, 0), (0, 0)))


def adam_parts(weight, grad, first, second):
    new_first = BETA_FIRST * first + (1.0 - BETA_FIRST) * grad
    new_second = BETA_SECOND * second + (1.0 - BETA_SECOND) * grad * grad
    update = (
        new_first
        / (1.0 - BETA_FIRST**STEP)
        / (jnp.sqrt(new_second / (1.0 - BETA_SECOND**STEP)) + ADAM_EPS)
        + DECAY_RATE * weight
    )
    return (new_first, new_second, update)


def squares_of(matrices, rowwise):
    return jnp.concatenate(
        [
            jnp.stack([jnp.sum(matrix * matrix) for matrix in matrices]),
            jnp.sum(rowwise * rowwise, axis=1),
        ]
    )


def per_device(
    tokens_in,
    cotangent,
    map_sizes,
    w_qkv,
    w_out,
    w_up,
    w_down,
    vectors,
    pos_table,
    first_qkv,
    second_qkv,
    first_out,
    second_out,
    first_up,
    second_up,
    first_down,
    second_down,
    first_vectors,
    second_vectors,
    first_table,
    second_table,
):
    rows, cols, width = tokens_in.shape
    count = rows * cols
    heads = HEADS
    head_dim = width // heads
    scale = head_dim ** (-0.5)
    half = WINDOW // 2
    reach = half * DILATION
    offsets = [
        (row_step, col_step)
        for row_step in range(-half, half + 1)
        for col_step in range(-half, half + 1)
    ]
    local_weight_sq = squares_of((w_qkv, w_out, w_up, w_down), vectors)
    big_qkv, big_out, big_up, big_down, vec_low = (
        lax.all_gather(w_qkv.astype(jnp.bfloat16), ("maps", "band"), axis=0, tiled=True),
        lax.all_gather(w_out.astype(jnp.bfloat16), ("maps", "band"), axis=0, tiled=True),
        lax.all_gather(w_up.astype(jnp.bfloat16), ("maps", "band"), axis=0, tiled=True),
        lax.all_gather(w_down.astype(jnp.bfloat16), ("maps", "band"), axis=0, tiled=True),
        lax.all_gather(vectors.astype(jnp.bfloat16), ("maps", "band"), axis=1, tiled=True),
    )
    vec = vec_low.astype(jnp.float32)
    band_index = lax.axis_index("band")
    height = map_sizes[0, 0]
    wide = map_sizes[0, 1]
    row_ids = band_index * rows + jnp.arange(rows, dtype=jnp.int32)
    col_ids = jnp.arange(cols, dtype=jnp.int32)

    def allowed_of(row_step, col_step):
        if row_step == 0 and col_step == 0:
            return jnp.ones((count,), dtype=bool)
        key_rows = row_ids + DILATION * row_step
        key_cols = col_ids + DILATION * col_step
        okay_rows = (key_rows >= 0) & (key_rows < height)
        okay_cols = (key_cols >= 0) & (key_cols < wide)
        return (okay_rows[:, None] & okay_cols[None, :]).reshape(count)

    x_flat = tokens_in.reshape(count, width).astype(jnp.float32)
    a_one = layer_norm(x_flat, vec[0], vec[1]).astype(jnp.bfloat16)
    qkv_bias = jnp.concatenate([vec[2], jnp.zeros_like(vec[2]), vec[3]])
    qkv = (jnp.dot(a_one, big_qkv, preferred_element_type=jnp.float32) + qkv_bias).astype(
        jnp.bfloat16
    )
    query = qkv[:, :width].reshape(count, heads, head_dim)
    keyval = qkv[:, width:].reshape(rows, cols, 2 * width)
    padded = padded_2(keyval, (("band", 0),), reach)

    def neighbour(row_step, col_step):
        top = reach + DILATION * row_step
        return column_shift(padded[top : top + rows], DILATION * col_step).reshape(
            count, 2, heads, head_dim
        )

    raw_list = []
    allow_list = []
    for row_step, col_step in offsets:
        piece = neighbour(row_step, col_step)
        raw_list.append(
            jnp.einsum("thd,thd->ht", query, piece[:, 0], preferred_element_type=jnp.float32)
        )
        allow_list.append(allowed_of(row_step, col_step))
    scores = scale * jnp.stack(raw_list) + pos_table.T[:, :, None]
    scores = jnp.where(jnp.stack(allow_list)[:, None, :], scores, MASKED)
    probs = jax.nn.softmax(scores, axis=0)
    probs_low = probs.astype(jnp.bfloat16)
    mixed = jnp.zeros((count, heads, head_dim), jnp.float32)
    for index, (row_step, col_step) in enumerate(offsets):
        piece = neighbour(row_step, col_step)
        mixed = mixed + jnp.einsum(
            "ht,thd->thd", probs_low[index], piece[:, 1], preferred_element_type=jnp.float32
        )
    mixed_low = mixed.reshape(count, width).astype(jnp.bfloat16)
    x_one = x_flat + (jnp.dot(mixed_low, big_out, preferred_element_type=jnp.float32) + vec[4])
    a_two = layer_norm(x_one, vec[5], vec[6]).astype(jnp.bfloat16)
    hidden = jnp.dot(a_two, big_up, preferred_element_type=jnp.float32) + vec[8:].reshape(-1)
    act = jax.nn.gelu(hidden, approximate=True).astype(jnp.bfloat16)
    result = x_one + jnp.dot(act, big_down, preferred_element_type=jnp.float32) + vec[7]
    layer_out = result.astype(jnp.bfloat16).reshape(rows, cols, width)
    grad_top = cotangent.reshape(count, width)
    grad_top_f = grad_top.astype(jnp.float32)
    grad_down = inner(act, grad_top)
    down_bias_grad = jnp.sum(grad_top_f, axis=0)
    grad_act = against(grad_top, big_down)
    _, gelu_back = jax.vjp(partial(jax.nn.gelu, approximate=True), hidden)
    grad_hidden = gelu_back(grad_act)[0].astype(jnp.bfloat16)
    grad_up = inner(a_two, grad_hidden)
    up_bias_grad = jnp.sum(grad_hidden.astype(jnp.float32), axis=0)
    _, norm_back_two = jax.vjp(layer_norm, x_one, vec[5], vec[6])
    norm_in_two, gain_two_grad, shift_two_grad = norm_back_two(against(grad_hidden, big_up))
    grad_x_one = grad_top_f + norm_in_two
    grad_attn = grad_x_one.astype(jnp.bfloat16)
    grad_out = inner(mixed_low, grad_attn)
    out_bias_grad = jnp.sum(grad_attn.astype(jnp.float32), axis=0)
    grad_mixed = against(grad_attn, big_out).astype(jnp.bfloat16).reshape(count, heads, head_dim)
    grad_keys = jnp.zeros((rows + 2 * reach, cols, width), jnp.float32)
    grad_vals = jnp.zeros((rows + 2 * reach, cols, width), jnp.float32)
    dprob_list = []
    for index, (row_step, col_step) in enumerate(offsets):
        piece = neighbour(row_step, col_step)
        dprob_list.append(
            jnp.einsum("thd,thd->ht", grad_mixed, piece[:, 1], preferred_element_type=jnp.float32)
        )
        share = jnp.einsum(
            "ht,thd->thd", probs_low[index], grad_mixed, preferred_element_type=jnp.float32
        )
        top = reach + DILATION * row_step
        grad_vals = grad_vals.at[top : top + rows].add(
            column_shift(share.reshape(rows, cols, width), -DILATION * col_step)
        )
    dprobs = jnp.stack(dprob_list)
    dscores = probs * (dprobs - jnp.sum(probs * dprobs, axis=0, keepdims=True))
    grad_table = jnp.sum(dscores, axis=2).T
    dscores_low = dscores.astype(jnp.bfloat16)
    grad_query = jnp.zeros((count, heads, head_dim), jnp.float32)
    for index, (row_step, col_step) in enumerate(offsets):
        piece = neighbour(row_step, col_step)
        grad_query = grad_query + jnp.einsum(
            "ht,thd->thd", dscores_low[index], piece[:, 0], preferred_element_type=jnp.float32
        )
        share = scale * jnp.einsum(
            "ht,thd->thd", dscores_low[index], query, preferred_element_type=jnp.float32
        )
        top = reach + DILATION * row_step
        grad_keys = grad_keys.at[top : top + rows].add(
            column_shift(share.reshape(rows, cols, width), -DILATION * col_step)
        )
    grad_query = scale * grad_query
    rim_top = jnp.concatenate([grad_keys[:reach], grad_vals[:reach]], axis=-1)
    rim_low = jnp.concatenate([grad_keys[rows + reach :], grad_vals[rows + reach :]], axis=-1)
    from_next = from_behind(rim_top.astype(jnp.bfloat16), "band", -1).astype(rim_top.dtype)
    from_prev = from_behind(rim_low.astype(jnp.bfloat16), "band", 1).astype(rim_low.dtype)
    own = jnp.concatenate(
        [grad_keys[reach : reach + rows], grad_vals[reach : reach + rows]], axis=-1
    )
    own = own.at[:reach].add(from_prev)
    own = own.at[rows - reach :].add(from_next)
    grad_keyval = own.astype(jnp.bfloat16).reshape(count, 2 * width)
    grad_query_low = grad_query.reshape(count, width).astype(jnp.bfloat16)
    grad_cols = jnp.concatenate([grad_query_low, grad_keyval], axis=-1)
    grad_qkv = inner(a_one, grad_cols)
    query_bias_grad = jnp.sum(grad_query_low.astype(jnp.float32), axis=0)
    value_bias_grad = jnp.sum(grad_keyval[:, width:].astype(jnp.float32), axis=0)
    _, norm_back_one = jax.vjp(layer_norm, x_flat, vec[0], vec[1])
    norm_in_one, gain_one_grad, shift_one_grad = norm_back_one(against(grad_cols, big_qkv))
    tokens_grad = (grad_x_one + norm_in_one).astype(jnp.bfloat16).reshape(rows, cols, width)
    grad_vec = jnp.concatenate(
        [
            jnp.stack(
                [
                    gain_one_grad,
                    shift_one_grad,
                    query_bias_grad,
                    value_bias_grad,
                    out_bias_grad,
                    gain_two_grad,
                    shift_two_grad,
                    down_bias_grad,
                ]
            ),
            up_bias_grad.reshape(-1, width),
        ],
        axis=0,
    )
    red_qkv, red_out, red_up, red_down, red_vec = (
        lax.psum_scatter(grad_qkv, ("maps", "band"), scatter_dimension=0, tiled=True),
        lax.psum_scatter(grad_out, ("maps", "band"), scatter_dimension=0, tiled=True),
        lax.psum_scatter(grad_up, ("maps", "band"), scatter_dimension=0, tiled=True),
        lax.psum_scatter(grad_down, ("maps", "band"), scatter_dimension=0, tiled=True),
        lax.psum_scatter(grad_vec, ("maps", "band"), scatter_dimension=1, tiled=True),
    )
    table_total = lax.psum(grad_table, ("maps", "band"))
    part_qkv = adam_parts(w_qkv, red_qkv, first_qkv, second_qkv)
    part_out = adam_parts(w_out, red_out, first_out, second_out)
    part_up = adam_parts(w_up, red_up, first_up, second_up)
    part_down = adam_parts(w_down, red_down, first_down, second_down)
    part_vec = adam_parts(vectors, red_vec, first_vectors, second_vectors)
    part_table = adam_parts(pos_table, table_total, first_table, second_table)
    local_update_sq = squares_of((part_qkv[2], part_out[2], part_up[2], part_down[2]), part_vec[2])
    weight_sq, update_sq = lax.psum((local_weight_sq, local_update_sq), ("maps", "band"))
    table_weight = jnp.sqrt(jnp.sum(pos_table * pos_table))
    table_update = jnp.sqrt(jnp.sum(part_table[2] * part_table[2]))
    weight_norms = jnp.concatenate([jnp.sqrt(weight_sq), table_weight[None]])
    update_norms = jnp.concatenate([jnp.sqrt(update_sq), table_update[None]])
    ratios = weight_norms / (update_norms + RATIO_EPS)
    next_qkv = w_qkv - LEARN_RATE * ratios[0] * part_qkv[2]
    next_out = w_out - LEARN_RATE * ratios[1] * part_out[2]
    next_up = w_up - LEARN_RATE * ratios[2] * part_up[2]
    next_down = w_down - LEARN_RATE * ratios[3] * part_down[2]
    vec_rows = vectors.shape[0]
    next_vectors = vectors - LEARN_RATE * ratios[4 : 4 + vec_rows][:, None] * part_vec[2]
    next_table = pos_table - LEARN_RATE * ratios[4 + vec_rows] * part_table[2]
    return (
        layer_out,
        tokens_grad,
        part_qkv[0],
        part_qkv[1],
        next_qkv,
        part_out[0],
        part_out[1],
        next_out,
        part_up[0],
        part_up[1],
        next_up,
        part_down[0],
        part_down[1],
        next_down,
        part_vec[0],
        part_vec[1],
        next_vectors,
        part_table[0],
        part_table[1],
        next_table,
        weight_norms,
        update_norms,
    )


def solution(mesh):
    return jax.shard_map(
        per_device,
        mesh=mesh,
        in_specs=(
            P(("maps", "band"), None, None),
            P(("maps", "band"), None, None),
            P("maps", None),
            P(("maps", "band"), None),
            P(("maps", "band"), None),
            P(("maps", "band"), None),
            P(("maps", "band"), None),
            P(None, ("maps", "band")),
            P(),
            P(("maps", "band"), None),
            P(("maps", "band"), None),
            P(("maps", "band"), None),
            P(("maps", "band"), None),
            P(("maps", "band"), None),
            P(("maps", "band"), None),
            P(("maps", "band"), None),
            P(("maps", "band"), None),
            P(None, ("maps", "band")),
            P(None, ("maps", "band")),
            P(),
            P(),
        ),
        out_specs=(
            P(("maps", "band"), None, None),
            P(("maps", "band"), None, None),
            P(("maps", "band"), None),
            P(("maps", "band"), None),
            P(("maps", "band"), None),
            P(("maps", "band"), None),
            P(("maps", "band"), None),
            P(("maps", "band"), None),
            P(("maps", "band"), None),
            P(("maps", "band"), None),
            P(("maps", "band"), None),
            P(("maps", "band"), None),
            P(("maps", "band"), None),
            P(("maps", "band"), None),
            P(None, ("maps", "band")),
            P(None, ("maps", "band")),
            P(None, ("maps", "band")),
            P(),
            P(),
            P(),
            P(),
            P(),
        ),
        check_vma=False,
    )
```

profile of v0, /device:TPU:0, one launch (start us, length us, event | category | flops | bytes accessed | tf_op | source)
XLA Modules:
  0.0 2590.2 jit_solution(16985482647388825560)
XLA Ops:
  10.6 43.5 %all_gather.15 = bf16[11,256]{0,1:T(8,128)(2,1)S(1)} all-gather(bf16[11,8]{0,1:T(8,128)(2,1)S(1)} %convert_element_type.371), channel_id=1, replica_groups=mesh['maps'=4,'band'=8] {'maps','band'}, dimensions={1}, use_global_device_ids=true | all-gather | bytes 5808 | tf_op jit(solution)/shard_map/all_gather | solution.py:130
  55.3 38.4 %all_gather.16 = bf16[256,768]{1,0:T(8,128)(2,1)S(1)} all-gather(bf16[8,768]{1,0:T(8,128)(2,1)S(1)} %convert_element_type.374), channel_id=1, replica_groups=mesh['maps'=4,'band'=8] {'maps','band'}, dimensions={0}, use_global_device_ids=true | all-gather | bytes 405504 | tf_op jit(solution)/shard_map/all_gather | solution.py:126
  122.1 43.1 %all_gather.17 = bf16[256,256]{1,0:T(8,128)(2,1)} all-gather(bf16[8,256]{1,0:T(8,128)(2,1)S(1)} %convert_element_type.379), channel_id=1, replica_groups=mesh['maps'=4,'band'=8] {'maps','band'}, dimensions={0}, use_global_device_ids=true | all-gather | bytes 135168 | tf_op jit(solution)/shard_map/all_gather | solution.py:127
  165.2 41.5 %all_gather.18 = bf16[256,768]{1,0:T(8,128)(2,1)} all-gather(bf16[8,768]{1,0:T(8,128)(2,1)S(1)} %convert_element_type.381), channel_id=1, replica_groups=mesh['maps'=4,'band'=8] {'maps','band'}, dimensions={0}, use_global_device_ids=true | all-gather | bytes 405504 | tf_op jit(solution)/shard_map/all_gather | solution.py:128
  775.9 10.4 add_convert_fusion.3
  794.8 91.3 %reduce-scatter.12.cloned.1.call-done = f32[24,256]{1,0:T(8,128)} async-done(((f32[768,256]{1,0:T(8,128)}), f32[24,256]{1,0:T(8,128)}) %reduce-scatter.12.cloned.1.call-update) | async-done | bytes 24592 | tf_op jit(solution)/shard_map/reduce_scatter | solution.py:278
  888.1 41.3 %all_gather.19 = bf16[768,256]{1,0:T(8,128)(2,1)S(1)} all-gather(bf16[24,256]{1,0:T(8,128)(2,1)S(1)} %get-tuple-element.1766), channel_id=1, replica_groups=mesh['maps'=4,'band'=8] {'maps','band'}, dimensions={0}, use_global_device_ids=true | all-gather | bytes 405504 | tf_op jit(solution)/shard_map/all_gather | solution.py:129
  949.8 6.1 convert_multiply_fusion.98
  970.6 9.9 convert_reduce_fusion.4
  1064.4 5.7 fusion.16
  1083.5 6.9 pad_add_fusion.55
  1090.4 13.5 scatter-add.345
  1103.9 13.4 scatter-add.346
  1117.3 13.4 scatter-add.349
  1130.8 13.4 scatter-add.350
  1144.2 13.4 scatter-add.351
  1157.7 13.4 scatter-add.354
  1171.1 13.0 scatter-add.355
  1267.1 6.9 pad_add_fusion.46
  1274.0 13.5 scatter-add.369
  1287.5 13.5 scatter-add.370
  1301.0 13.5 scatter-add.371
  1314.5 13.5 scatter-add.374
  1328.0 13.5 scatter-add.375
  1341.4 13.5 scatter-add.376
  1354.9 13.0 scatter-add.379
  1453.9 7.3 pad_add_fusion.37
  1461.2 13.3 scatter-add.391
  1474.5 13.3 scatter-add.394
  1487.7 13.3 scatter-add.395
  1501.0 13.3 scatter-add.396
  1514.3 13.3 scatter-add.399
  1527.6 13.3 scatter-add.400
  1540.8 12.6 scatter-add.401
  1662.6 7.2 pad_add_fusion.23
  1669.8 13.4 scatter-add.426
  1683.2 13.4 scatter-add.429
  1696.6 13.4 scatter-add.430
  1710.0 13.4 scatter-add.431
  1723.4 13.4 scatter-add.434
  1736.8 13.4 scatter-add.435
  1750.2 12.8 scatter-add.436
  1762.9 5.3 copy.1119
  1845.8 6.9 pad_add_fusion.14
  1852.6 13.5 scatter-add.450
  1866.1 13.4 scatter-add.451
  1879.5 13.4 scatter-add.454
  1893.0 13.4 scatter-add.455
  1906.4 13.4 scatter-add.456
  1919.9 13.4 scatter-add.459
  1933.3 13.2 scatter-add.460
  2032.4 7.0 pad_add_fusion.5
  2039.3 13.3 scatter-add.474
  2052.7 13.3 scatter-add.475
  2066.0 13.3 scatter-add.476
  2079.3 13.3 scatter-add.479
  2092.6 13.3 scatter-add.480
  2106.0 13.3 scatter-add.481
  2119.3 12.7 scatter-add.484
  2221.3 106.7 %reduce-scatter.8.cloned.1.call-done = f32[8,256]{1,0:T(8,128)} async-done(((f32[256,256]{1,0:T(8,128)}), f32[8,256]{1,0:T(8,128)}) %reduce-scatter.8.cloned.1.call-update) | async-done | bytes 8208 | tf_op jit(solution)/shard_map/reduce_scatter | solution.py:276
  2339.2 37.1 %all-reduce.128 = f32[11,256]{1,0:T(8,128)} all-reduce(f32[11,256]{1,0:T(8,128)} %concatenate.252), channel_id=6, replica_groups=mesh['maps'=4,'band'=8] {'maps','band'}, use_global_device_ids=true, to_apply=%region_35.36.clone | all-reduce | flops 2816 | bytes 22528
  2383.7 42.4 %reduce-scatter.10.cloned.1.call-done = f32[8,768]{1,0:T(8,128)} async-done(((f32[256,768]{1,0:T(8,128)}), f32[8,768]{1,0:T(8,128)}) %reduce-scatter.10.cloned.1.call-update) | async-done | bytes 24592 | tf_op jit(solution)/shard_map/reduce_scatter | solution.py:277
  2427.5 98.9 %reduce-scatter.6.cloned.1.call-done = f32[8,768]{1,0:T(8,128)} async-done(((f32[256,768]{1,0:T(8,128)}), f32[8,768]{1,0:T(8,128)}) %reduce-scatter.6.cloned.1.call-update) | async-done | bytes 24592 | tf_op jit(solution)/shard_map/reduce_scatter | solution.py:275
  2533.1 40.0 %all-reduce.129 = (f32[8,49]{1,0:T(8,128)S(1)}, f32[15]{0:T(128)S(1)}, f32[15]{0:T(128)S(1)}) all-reduce(f32[8,49]{1,0:T(8,128)S(1)} %bitcast.2256, f32[15]{0:T(128)S(1)} %concatenate.250, f32[15]{0:T(128)S(1)} %concatenate.253), channel_id=1, replica_groups=mesh['maps'=4,'band'=8] {'maps','band'}, use_global_device_ids=true, to_apply=%region_39.40 | all-reduce | flops 422 | bytes 3376 | tf_op jit(solution)/shard_map/psum | solution.py:281
  (1461 shorter events, 1303.1 us)
Async XLA Ops:
  7.2 86.5 %copy-start.29 = (bf16[16,48,256]{2,1,0:T(8,128)(2,1)S(1)}, bf16[16,48,256]{2,1,0:T(8,128)(2,1)}, u32[]{:S(2)}) copy-start(bf16[16,48,256]{2,1,0:T(8,128)(2,1)} %param.221) | copy-start | bytes 1179652
  7.2 48.1 %copy-start.288 = (f32[8,768]{1,0:T(8,128)S(1)}, f32[8,768]{1,0:T(8,128)}, u32[]{:S(2)}) copy-start(f32[8,768]{1,0:T(8,128)} %param.224) | copy-start | bytes 73732
  7.2 878.8 %reduce-scatter.12.cloned.1.call-start = ((), (), s32[]{:S(2)}) async-start(), calls=%async_computation.7 | async-start | bytes 811008 | tf_op jit(solution)/shard_map/reduce_scatter | solution.py:278
  9.9 85.8 %copy-start.364 = (f32[768]{0:T(1024)}, f32[768]{0:T(1024)S(1)}, u32[]{:S(2)}) copy-start(f32[768]{0:T(1024)S(1)} %div.132) | copy-start | bytes 9220
  55.2 41.7 %copy-start.387 = (f32[256]{0:T(256)}, f32[256]{0:T(256)S(1)}, u32[]{:S(2)}) copy-start(f32[256]{0:T(256)S(1)} %get-tuple-element.1400) | copy-start | bytes 3076
  55.3 41.6 %copy-start.376 = (f32[768]{0:T(1024)}, f32[768]{0:T(1024)S(1)}, u32[]{:S(2)}) copy-start(f32[768]{0:T(1024)S(1)} %add.1666) | copy-start | bytes 9220
  55.3 41.6 %copy-start.366 = (f32[768]{0:T(1024)}, f32[768]{0:T(1024)S(1)}, u32[]{:S(2)}) copy-start(f32[768]{0:T(1024)S(1)} %rsqrt.22) | copy-start | bytes 9220
  96.8 109.8 %collective-permute-start = (bf16[12,48,512]{2,1,0:T(8,128)(2,1)}, bf16[12,48,512]{2,1,0:T(8,128)(2,1)S(1)}, u32[]{:S(2)}, u32[]{:S(2)}) collective-permute-start(bf16[12,48,512]{2,1,0:T(8,128)(2,1)} %bitcast.202), channel_id=1, source_target_pairs={{0,1},{1,2},{2,3},{3,4},{4,5},{5,6},{6,7},{8,9},{9,10},{10,11},{11... | collective-permute-start | bytes 1769480 | tf_op jit(solution)/shard_map/ppermute | solution.py:31
  99.1 107.6 %collective-permute-start.1 = (bf16[12,48,512]{2,1,0:T(8,128)(2,1)}, bf16[12,48,512]{2,1,0:T(8,128)(2,1)S(1)}, u32[]{:S(2)}, u32[]{:S(2)}) collective-permute-start(bf16[12,48,512]{2,1,0:T(8,128)(2,1)} %bitcast.345), channel_id=1, source_target_pairs={{1,0},{2,1},{3,2},{4,3},{5,4},{6,5},{7,6},{9,8},{10,9},{11,10},{12... | collective-permute-start | bytes 1769480 | tf_op jit(solution)/shard_map/ppermute | solution.py:32
  100.5 19.1 copy-start.379
  100.5 19.1 copy-start.362
  100.5 19.8 copy-start.286
  623.9 135.6 %copy-start.171 = (bf16[768,2,8,32]{0,3,2,1:T(8,128)(2,1)}, bf16[768,2,8,32]{0,3,2,1:T(8,128)(2,1)S(1)}, u32[]{:S(2)}) copy-start(bf16[768,2,8,32]{0,3,2,1:T(8,128)(2,1)S(1)} %reshape.5120) | copy-start | bytes 2359300
  630.3 129.3 %copy-start.174 = (bf16[768,2,8,32]{0,3,2,1:T(8,128)(2,1)}, bf16[768,2,8,32]{0,3,2,1:T(8,128)(2,1)S(1)}, u32[]{:S(2)}) copy-start(bf16[768,2,8,32]{0,3,2,1:T(8,128)(2,1)S(1)} %reshape.5127) | copy-start | bytes 2359300
  773.8 12.5 copy-start.316
  773.9 12.5 copy-start.318
  773.9 12.5 copy-start.320
  773.9 12.5 copy-start.322
  773.9 12.5 copy-start.324
  773.9 12.5 copy-start.326
  773.9 12.5 copy-start.328
  773.9 12.5 copy-start.330
  773.9 12.5 copy-start.332
  773.9 12.5 copy-start.334
  787.2 148.0 %copy-start.4 = (f32[768,256]{1,0:T(8,128)}, f32[768,256]{1,0:T(8,128)S(1)}, u32[]{:S(2)}) copy-start(f32[768,256]{1,0:T(8,128)S(1)} %get-tuple-element.1823) | copy-start | bytes 2359300
  787.2 147.9 %copy-start.368 = (f32[768]{0:T(1024)}, f32[768]{0:T(1024)S(1)}, u32[]{:S(2)}) copy-start(f32[768]{0:T(1024)S(1)} %broadcast_multiply_fusion.1) | copy-start | bytes 9220
  787.6 147.6 %copy-start.372 = (f32[768]{0:T(1024)}, f32[768]{0:T(1024)S(1)}, u32[]{:S(2)}) copy-start(f32[768]{0:T(1024)S(1)} %fusion.231) | copy-start | bytes 9220
  793.1 1534.9 %reduce-scatter.8.cloned.1.call-start = ((), (), s32[]{:S(2)}) async-start(), calls=%async_computation.5 | async-start | bytes 270336 | tf_op jit(solution)/shard_map/reduce_scatter | solution.py:276
  929.4 14.7 copy-start.166
  929.5 14.7 copy-start.168
  929.5 14.7 copy-start.170
  999.9 64.5 %copy-start = (f32[16,36,256]{1,0,2:T(8,128)}, f32[16,36,256]{1,0,2:T(8,128)S(1)}, u32[]{:S(2)}) copy-start(f32[16,36,256]{1,0,2:T(8,128)S(1)} %slice.4552) | copy-start | bytes 1769476
  2197.1 229.0 %reduce-scatter.10.cloned.1.call-start = ((), (), s32[]{:S(2)}) async-start(), calls=%async_computation.6 | async-start | bytes 811008 | tf_op jit(solution)/shard_map/reduce_scatter | solution.py:277
  2198.0 133.1 %collective-permute-start.3 = (bf16[12,48,512]{2,1,0:T(8,128)(2,1)}, bf16[12,48,512]{2,1,0:T(8,128)(2,1)}, u32[]{:S(2)}, u32[]{:S(2)}) collective-permute-start(bf16[12,48,512]{2,1,0:T(8,128)(2,1)} %pad_maximum_fusion.7), channel_id=1, source_target_pairs={{1,0},{2,1},{3,2},{4,3},{5,4},{6,5},{7,6},{9,8},{10,9},{11,10},{12... | collective-permute-start | bytes 1769480 | tf_op jit(solution)/shard_map/ppermute | solution.py:40
  2204.7 125.2 %collective-permute-start.2 = (bf16[12,48,512]{2,1,0:T(8,128)(2,1)}, bf16[12,48,512]{2,1,0:T(8,128)(2,1)S(1)}, u32[]{:S(2)}, u32[]{:S(2)}) collective-permute-start(bf16[12,48,512]{2,1,0:T(8,128)(2,1)} %pad_maximum_fusion.6), channel_id=1, source_target_pairs={{0,1},{1,2},{2,3},{3,4},{4,5},{5,6},{6,7},{8,9},{9,10},{10,11},{11... | collective-permute-start | bytes 1769480 | tf_op jit(solution)/shard_map/ppermute | solution.py:40
  2217.3 309.1 %reduce-scatter.6.cloned.1.call-start = ((), (), s32[]{:S(2)}) async-start(), calls=%async_computation.4 | async-start | bytes 811008 | tf_op jit(solution)/shard_map/reduce_scatter | solution.py:275
  2219.9 108.1 %copy-start.363 = (f32[8,256]{1,0:T(8,128)S(1)}, f32[8,256]{1,0:T(8,128)}, u32[]{:S(2)}) copy-start(f32[8,256]{1,0:T(8,128)} %param.225) | copy-start | bytes 24580
  2219.9 108.1 %copy-start.398 = (f32[8,256]{1,0:T(8,128)S(1)}, f32[8,256]{1,0:T(8,128)}, u32[]{:S(2)}) copy-start(f32[8,256]{1,0:T(8,128)} %param.232) | copy-start | bytes 24580
  2219.9 108.1 %copy-start.399 = (f32[8,256]{1,0:T(8,128)S(1)}, f32[8,256]{1,0:T(8,128)}, u32[]{:S(2)}) copy-start(f32[8,256]{1,0:T(8,128)} %param.233) | copy-start | bytes 24580
  2333.7 42.5 %copy-start.272 = (bf16[768,256]{1,0:T(8,128)(2,1)S(1)}, bf16[768,256]{1,0:T(8,128)(2,1)}, u32[]{:S(2)}) copy-start(bf16[768,256]{1,0:T(8,128)(2,1)} %copy-done.271) | copy-start | bytes 1179652
  2335.5 45.8 %copy-start.99 = (f32[768,256]{1,0:T(8,128)S(1)}, f32[768,256]{1,0:T(8,128)}, u32[]{:S(2)}) copy-start(f32[768,256]{1,0:T(8,128)} %copy-done.98) | copy-start | bytes 2359300
  2335.5 45.8 %copy-start.193 = (bf16[16,48,256]{2,1,0:T(8,128)(2,1)S(1)}, bf16[16,48,256]{2,1,0:T(8,128)(2,1)}, u32[]{:S(2)}) copy-start(bf16[16,48,256]{2,1,0:T(8,128)(2,1)} %param.222) | copy-start | bytes 1179652
  2378.7 47.4 %copy-start.287 = (f32[8,768]{1,0:T(8,128)S(1)}, f32[8,768]{1,0:T(8,128)}, u32[]{:S(2)}) copy-start(f32[8,768]{1,0:T(8,128)} %param.226) | copy-start | bytes 73732
  2378.7 47.4 %copy-start.383 = (f32[8,768]{1,0:T(8,128)S(1)}, f32[8,768]{1,0:T(8,128)}, u32[]{:S(2)}) copy-start(f32[8,768]{1,0:T(8,128)} %param.234) | copy-start | bytes 73732
  2378.7 47.4 %copy-start.384 = (f32[8,768]{1,0:T(8,128)S(1)}, f32[8,768]{1,0:T(8,128)}, u32[]{:S(2)}) copy-start(f32[8,768]{1,0:T(8,128)} %param.235) | copy-start | bytes 73732
  2378.7 147.7 %copy-start.289 = (f32[8,768]{1,0:T(8,128)S(1)}, f32[8,768]{1,0:T(8,128)}, u32[]{:S(2)}) copy-start(f32[8,768]{1,0:T(8,128)} %param.224) | copy-start | bytes 73732
  2378.7 147.7 %copy-start.385 = (f32[8,768]{1,0:T(8,128)S(1)}, f32[8,768]{1,0:T(8,128)}, u32[]{:S(2)}) copy-start(f32[8,768]{1,0:T(8,128)} %param.231) | copy-start | bytes 73732
  2378.7 147.7 %copy-start.386 = (f32[8,768]{1,0:T(8,128)S(1)}, f32[8,768]{1,0:T(8,128)}, u32[]{:S(2)}) copy-start(f32[8,768]{1,0:T(8,128)} %param.230) | copy-start | bytes 73732
  2378.7 154.3 %copy-start.394 = (f32[49,8]{0,1:T(8,128)S(1)}, f32[49,8]{0,1:T(8,128)}, u32[]{:S(2)}) copy-start(f32[49,8]{0,1:T(8,128)} %copy.228) | copy-start | bytes 4708
  2378.7 194.4 %copy-start.380 = (f32[8,49]{1,0:T(8,128)S(1)}, f32[8,49]{1,0:T(8,128)}, u32[]{:S(2)}) copy-start(f32[8,49]{1,0:T(8,128)} %param.229) | copy-start | bytes 4708
  2378.8 194.4 %copy-start.401 = (f32[8,49]{1,0:T(8,128)S(1)}, f32[8,49]{1,0:T(8,128)}, u32[]{:S(2)}) copy-start(f32[8,49]{1,0:T(8,128)} %param.240) | copy-start | bytes 4708
  2378.8 194.4 %copy-start.402 = (f32[8,49]{1,0:T(8,128)S(1)}, f32[8,49]{1,0:T(8,128)}, u32[]{:S(2)}) copy-start(f32[8,49]{1,0:T(8,128)} %param.241) | copy-start | bytes 4708
  2378.8 201.5 %copy-start.378 = (f32[11,8]{0,1:T(8,128)S(1)}, f32[11,8]{0,1:T(8,128)}, u32[]{:S(2)}) copy-start(f32[11,8]{0,1:T(8,128)} %param.228) | copy-start | bytes 1060
  2378.8 202.1 %copy-start.355 = (f32[24,256]{1,0:T(8,128)S(1)}, f32[24,256]{1,0:T(8,128)}, u32[]{:S(2)}) copy-start(f32[24,256]{1,0:T(8,128)} %param.227) | copy-start | bytes 73732
  2378.8 202.1 %copy-start.356 = (f32[24,256]{1,0:T(8,128)S(1)}, f32[24,256]{1,0:T(8,128)}, u32[]{:S(2)}) copy-start(f32[24,256]{1,0:T(8,128)} %get-tuple-element.1427) | copy-start | bytes 73732
  2378.8 202.1 %copy-start.357 = (f32[24,256]{1,0:T(8,128)S(1)}, f32[24,256]{1,0:T(8,128)}, u32[]{:S(2)}) copy-start(f32[24,256]{1,0:T(8,128)} %get-tuple-element.1428) | copy-start | bytes 73732
  2378.8 203.4 %copy-start.381 = (f32[8,256]{1,0:T(8,128)S(1)}, f32[8,256]{1,0:T(8,128)}, u32[]{:S(2)}) copy-start(f32[8,256]{1,0:T(8,128)} %get-tuple-element.1431) | copy-start | bytes 24580
  2378.8 203.3 %copy-start.382 = (f32[8,256]{1,0:T(8,128)S(1)}, f32[8,256]{1,0:T(8,128)}, u32[]{:S(2)}) copy-start(f32[8,256]{1,0:T(8,128)} %get-tuple-element.1432) | copy-start | bytes 24580
  2381.3 202.2 %copy-start.390 = (f32[11,8]{0,1:T(8,128)}, f32[11,8]{0,1:T(8,128)S(1)}, u32[]{:S(2)}) copy-start(f32[11,8]{0,1:T(8,128)S(1)} %get-tuple-element.1421) | copy-start | bytes 1060
  2381.3 202.2 %copy-start.391 = (f32[11,8]{0,1:T(8,128)}, f32[11,8]{0,1:T(8,128)S(1)}, u32[]{:S(2)}) copy-start(f32[11,8]{0,1:T(8,128)S(1)} %get-tuple-element.1422) | copy-start | bytes 1060
  2427.4 156.0 %copy-start.358 = (f32[8,768]{1,0:T(8,128)}, f32[8,768]{1,0:T(8,128)S(1)}, u32[]{:S(2)}) copy-start(f32[8,768]{1,0:T(8,128)S(1)} %get-tuple-element.1429) | copy-start | bytes 73732
  2427.4 156.0 %copy-start.359 = (f32[8,768]{1,0:T(8,128)}, f32[8,768]{1,0:T(8,128)S(1)}, u32[]{:S(2)}) copy-start(f32[8,768]{1,0:T(8,128)S(1)} %get-tuple-element.1430) | copy-start | bytes 73732
  2527.8 55.7 %copy-start.360 = (f32[8,768]{1,0:T(8,128)}, f32[8,768]{1,0:T(8,128)S(1)}, u32[]{:S(2)}) copy-start(f32[8,768]{1,0:T(8,128)S(1)} %get-tuple-element.1433) | copy-start | bytes 73732
  2527.8 55.7 %copy-start.361 = (f32[8,768]{1,0:T(8,128)}, f32[8,768]{1,0:T(8,128)S(1)}, u32[]{:S(2)}) copy-start(f32[8,768]{1,0:T(8,128)S(1)} %get-tuple-element.1434) | copy-start | bytes 73732
  (354 other events, 1681.9 us)
Sparse Core Ops, SparseCore 0:
  793.2 92.7 reduce-scatter.11
  2197.2 130.6 reduce-scatter.7
  2333.9 92.1 reduce-scatter.9
  2431.8 94.5 reduce-scatter.5
where the time goes:
time: 2620 us; the launch traced here: 2590 us
  local copies, waits for them, and re-layouts  1590 us (61%)
  waiting for transfers between devices  339 us (13%)
  other arithmetic  318 us (12%)
  blocking collectives  285 us (11%)
    scatter-add x22, local copies, waits for them, and re-layouts, per_device(): grad_keys.at[top:top + rows]  283 us
    scatter-add x22, local copies, waits for them, and re-layouts, per_device(): grad_vals.at[top:top + rows]  282 us
    unnamed x966, local copies, waits for them, and re-layouts  224 us
    reshape x84, local copies, waits for them, and re-layouts, per_device(): share.reshape(rows, cols, width)  214 us
    reshape x48, local copies, waits for them, and re-layouts, neighbour(): column_shift(padded[top:top + rows], DILATION * col_step)  205 us
    slice x42, local copies, waits for them, and re-layouts, column_shift(): return jnp.pad(block[:, offset:], ((0, 0), (0, offset), (0, 0)))  132 us
    reduce_scatter x1, waiting for transfers between devices, per_device(): lax.psum_scatter(grad_out, ('maps', 'band'), scatter_dimension=0, tiled=T...  107 us
    reduce_scatter x1, waiting for transfers between devices, per_device(): lax.psum_scatter(grad_qkv, ('maps', 'band'), scatter_dimension=0, tiled=T...  98.9 us
  transfers between devices with their start and end apart: 8, of which 4 were waited for; matrix products, arithmetic and copies ran while one was open for 2% of the time, Pallas kernels for 0%

commit v1 on v0

v1 whole, which is shorter than its diff:
```python
import functools

import jax
import jax.numpy as jnp
import numpy as np
from jax import lax
from jax.experimental import pallas as pl
from jax.experimental.pallas import tpu as pltpu
from jax.sharding import PartitionSpec as P

HEADS = 8
WINDOW = 7
DIL = 4
STEP = 10
NORM_EPS = 1e-05
BETA_FIRST = 0.9
BETA_SECOND = 0.999
ADAM_EPS = 1e-06
DECAY_RATE = 0.01
LEARN_RATE = 0.2
RATIO_EPS = 1e-06
MASKED = -1e30
LOG2E = 1.4426950408889634
AXES = ("maps", "band")

BF = jnp.bfloat16
F32 = jnp.float32

CLS = DIL * DIL
QN = 48
KN = 128
RIM = 40


def dot(a, b):
    return lax.dot_general(a, b, (((1,), (0,)), ((), ())), preferred_element_type=F32)


def dot_nt(a, b):
    return lax.dot_general(a, b, (((1,), (1,)), ((), ())), preferred_element_type=F32)


def dot_tn(a, b):
    return lax.dot_general(a, b, (((0,), (0,)), ((), ())), preferred_element_type=F32)


def order_own():
    sel = np.zeros((4 * QN, 4 * 48), np.float32)
    for o in range(4 * QN):
        cc, rest = divmod(o, QN)
        qr, qc = divmod(rest, 12)
        sel[o, qr * 48 + qc * 4 + cc] = 1
    return sel


def order_keys():
    sel = np.zeros((4 * KN, 480), np.float32)
    for o in range(4 * KN):
        cc, slot = divmod(o, KN)
        j = (slot + 36) % KN
        if j < 120:
            kr, kc = divmod(j, 12)
            sel[o, kr * 48 + kc * 4 + cc] = 1
    return sel


def normed(v):
    mean = jnp.mean(v, axis=-1, keepdims=True)
    cen = v - mean
    var = jnp.mean(cen * cen, axis=-1, keepdims=True)
    rstd = lax.rsqrt(var + NORM_EPS)
    return cen * rstd, rstd


def norm_back(g, xhat, rstd):
    m1 = jnp.mean(g, axis=-1, keepdims=True)
    m2 = jnp.mean(g * xhat, axis=-1, keepdims=True)
    return rstd * (g - m1 - xhat * m2)


def spread_heads(v, lane_head):
    zero = jnp.zeros_like(v)
    return jnp.concatenate([jnp.where(lane_head == h, v, zero) for h in range(HEADS)], axis=0)


def pick_heads(full, lane_head):
    out = jnp.where(lane_head == 0, full[0:QN], 0.0)
    for h in range(1, HEADS):
        out = out + jnp.where(lane_head == h, full[h * QN : (h + 1) * QN], 0.0)
    return out


def split12(v):
    q = (v * 43) >> 9
    return q, v - 12 * q


def table_slots():
    n = lax.broadcasted_iota(jnp.int32, (WINDOW * WINDOW, KN), 0)
    lane = lax.broadcasted_iota(jnp.int32, (WINDOW * WINDOW, KN), 1)
    nr = (n * 37) >> 8
    nc = n - 7 * nr
    return (((12 * (nr - 3) + nc - 3) & (KN - 1)) == lane).astype(F32)


def layer_kernel(
    where_ref,
    x_ref,
    xb_ref,
    xa_ref,
    cot_ref,
    wqkv_ref,
    wo_ref,
    wu_ref,
    wd_ref,
    vec_ref,
    table_ref,
    po_ref,
    pk_ref,
    out_ref,
    act_ref,
    dy_ref,
    dz_ref,
    a2_ref,
    mixed_ref,
    da_ref,
    a1_ref,
    dq_ref,
    dx1_ref,
    own_ref,
    rima_ref,
    rimb_ref,
    tgrad_ref,
    sums_ref,
    zsum_ref,
    xp_ref,
    q_ref,
    k_ref,
    v_ref,
    bias_ref,
    p_ref,
    x1_ref,
    dmix_ref,
    tacc_ref,
):
    row0 = where_ref[0] * 16
    height = where_ref[1]
    wide = where_ref[2]
    scale = 32 ** (-0.5)
    lane_head = lax.broadcasted_iota(jnp.int32, (QN, 256), 1) >> 5

    def vrow(i):
        return vec_ref[i : i + 1, :]

    slots = lax.dot_general(
        table_ref[...],
        table_slots(),
        (((1,), (0,)), ((), ())),
        precision=lax.Precision.HIGHEST,
        preferred_element_type=F32,
    )
    qi = lax.broadcasted_iota(jnp.int32, (QN, KN), 0)
    si = lax.broadcasted_iota(jnp.int32, (QN, KN), 1)
    ji = (si + 36) & (KN - 1)
    kr, kc = split12(ji)
    qr, qc = split12(qi)
    window = (jnp.abs(kc - qc) <= 3) & (jnp.abs(kr - qr - 3) <= 3) & (ji < 120)
    rows = []
    for h in range(HEADS):
        line = jnp.broadcast_to(slots[h : h + 1, :] * LOG2E, (QN, KN))
        line = pltpu.roll(line, 0, 1, stride=1, stride_axis=0)
        rows.append(jnp.where(window, line, MASKED))
    bias_ref[...] = jnp.concatenate(rows, axis=0).T

    def project(rc, _):
        own = jnp.concatenate([x_ref[4 * i + rc] for i in range(4)], axis=0)
        xp = dot(po_ref[...], own)
        at = pl.ds(pl.multiple_of(rc * 192, 192), 192)
        xp_ref[at, :] = xp
        a1 = (normed(xp)[0] * vrow(0) + vrow(1)).astype(BF)
        a1_ref[at, :] = a1
        q_ref[at, :] = (dot(a1, wqkv_ref[:, 0:256]) + vrow(2)).astype(BF)
        around = jnp.concatenate(
            [xb_ref[4 * i + rc] for i in range(3)]
            + [own]
            + [xa_ref[4 * i + rc] for i in range(3)],
            axis=0,
        )
        xk = dot(pk_ref[...], around)
        a1k = (normed(xk)[0] * vrow(0) + vrow(1)).astype(BF)
        at = pl.ds(pl.multiple_of(rc * 512, 512), 512)
        k_ref[at, :] = dot(a1k, wqkv_ref[:, 256:512]).astype(BF)
        v_ref[at, :] = (dot(a1k, wqkv_ref[:, 512:768]) + vrow(3)).astype(BF)
        return 0

    lax.fori_loop(0, 4, project, 0)

    ks = lax.broadcasted_iota(jnp.int32, (KN, 384), 0)
    ql = lax.broadcasted_iota(jnp.int32, (KN, 384), 1)
    kj = (ks + 36) & (KN - 1)
    krow, kcol = split12(kj)
    qin = ql - 48 * ((ql * 171) >> 13)
    same = ks == qin

    def attend(k, _):
        rc = k >> 2
        cc = k & 3
        at_q = pl.ds(pl.multiple_of(k * QN, QN), QN)
        at_k = pl.ds(pl.multiple_of(k * KN, KN), KN)
        qbd = spread_heads(q_ref[at_q, :], lane_head)
        s = dot_nt(k_ref[at_k, :], qbd) * (scale * LOG2E) + bias_ref[...]
        r = krow * 4 + (row0 + rc - 12)
        c = kcol * 4 + cc
        okay = ((r >= 0) & (r < height) & (c < wide)) | same
        s = jnp.where(okay, s, MASKED)
        top = jnp.max(s, axis=0, keepdims=True)
        e = jnp.exp2(s - top)
        p = e * (1.0 / jnp.sum(e, axis=0, keepdims=True))
        p_ref[at_k, :] = p
        full = dot_tn(p.astype(BF), v_ref[at_k, :])
        mixed_ref[at_q, :] = pick_heads(full, lane_head).astype(BF)
        return 0

    lax.fori_loop(0, CLS, attend, 0)

    sums_ref[...] = jnp.zeros_like(sums_ref)
    zsum_ref[...] = jnp.zeros_like(zsum_ref)

    def feed(rc, _):
        at = pl.ds(pl.multiple_of(rc * 192, 192), 192)
        x1 = xp_ref[at, :] + (dot(mixed_ref[at, :], wo_ref[...]) + vrow(4))
        xhat, rstd = normed(x1)
        a2 = (xhat * vrow(5) + vrow(6)).astype(BF)
        a2_ref[at, :] = a2
        bias = jnp.concatenate([vrow(8), vrow(9), vrow(10)], axis=1)
        z = dot(a2, wu_ref[...]) + bias
        c0 = 0.7978845608028654
        c1 = 0.044715
        z2 = z * z
        t = jnp.tanh(c0 * (z + c1 * z2 * z))
        act = (0.5 * z * (1.0 + t)).astype(BF)
        act_ref[at, :] = act
        res = x1 + dot(act, wd_ref[...]) + vrow(7)
        back = dot_tn(po_ref[...], res.astype(BF)).astype(BF)
        for i in range(4):
            out_ref[4 * i + rc] = back[48 * i : 48 * i + 48]
        dyf = dot(po_ref[...], jnp.concatenate([cot_ref[4 * i + rc] for i in range(4)], axis=0))
        dy = dyf.astype(BF)
        dy_ref[at, :] = dy
        slope = 0.5 * (1.0 + t) + 0.5 * z * (1.0 - t * t) * (c0 * (1.0 + 3.0 * c1 * z2))
        dz = (dot_nt(dy, wd_ref[...]) * slope).astype(BF)
        dz_ref[at, :] = dz
        zsum_ref[...] += jnp.sum(dz.astype(F32), axis=0, keepdims=True)
        dn = dot_nt(dz, wu_ref[...])
        dx1 = dyf + norm_back(dn * vrow(5), xhat, rstd)
        dx1_ref[at, :] = dx1
        da = dx1.astype(BF)
        da_ref[at, :] = da
        dmix_ref[at, :] = dot_nt(da, wo_ref[...]).astype(BF)
        sums_ref[4:5, :] += jnp.sum(da.astype(F32), axis=0, keepdims=True)
        sums_ref[5:6, :] += jnp.sum(dn * xhat, axis=0, keepdims=True)
        sums_ref[6:7, :] += jnp.sum(dn, axis=0, keepdims=True)
        sums_ref[7:8, :] += jnp.sum(dyf, axis=0, keepdims=True)
        return 0

    lax.fori_loop(0, 4, feed, 0)

    tacc_ref[...] = jnp.zeros_like(tacc_ref)

    def back_class(k):
        at_q = pl.ds(pl.multiple_of(k * QN, QN), QN)
        at_k = pl.ds(pl.multiple_of(k * KN, KN), KN)
        qbd = spread_heads(q_ref[at_q, :], lane_head)
        dobd = spread_heads(dmix_ref[at_q, :], lane_head)
        p = p_ref[at_k, :]
        dp = dot_nt(v_ref[at_k, :], dobd)
        dv = dot(p.astype(BF), dobd)
        pdp = p * dp
        ds = pdp - p * jnp.sum(pdp, axis=0, keepdims=True)
        tacc_ref[...] += ds
        dsl = ds.astype(BF)
        dk = dot(dsl, qbd) * scale
        dq = pick_heads(dot_tn(dsl, k_ref[at_k, :]), lane_head) * scale
        dq_ref[at_q, :] = dq.astype(BF)
        own_ref[at_q, 0:256] = dk[0:QN]
        own_ref[at_q, 256:512] = dv[0:QN]
        after = jnp.concatenate([dk[QN : QN + RIM], dv[QN : QN + RIM]], axis=1)
        before = jnp.concatenate([dk[KN - RIM :], dv[KN - RIM :]], axis=1)
        return after, before

    def attend_back(pair, _):
        after0, before0 = back_class(pair * 2)
        after1, before1 = back_class(pair * 2 + 1)
        at = pl.ds(pl.multiple_of(pair * 2 * RIM, 2 * RIM), 2 * RIM)
        rima_ref[at, :] = jnp.concatenate([after0, after1], axis=0).astype(BF)
        rimb_ref[at, :] = jnp.concatenate([before0, before1], axis=0).astype(BF)
        return 0

    lax.fori_loop(0, CLS // 2, attend_back, 0)
    sums_ref[2:3, :] = jnp.sum(dq_ref[...].astype(F32), axis=0, keepdims=True)

    flat = tacc_ref[...].T
    lines = []
    for h in range(HEADS):
        part = flat[h * QN : (h + 1) * QN]
        for bit in range(6):
            turned = pltpu.roll(part, KN - (1 << bit), 1)
            part = jnp.where((qi >> bit) & 1 == 1, turned, part)
        lines.append(jnp.sum(part, axis=0, keepdims=True))
    tgrad_ref[...] = jnp.concatenate(lines, axis=0)


def finish_kernel(
    own_ref,
    fa_ref,
    fb_ref,
    dq_ref,
    dx1_ref,
    x_ref,
    wqkv_ref,
    vec_ref,
    po_ref,
    tok_ref,
    dqkv_ref,
    sums_ref,
):
    sums_ref[...] = jnp.zeros_like(sums_ref)

    def block(rc, _):
        own = jnp.concatenate([x_ref[4 * i + rc] for i in range(4)], axis=0)
        xp = dot(po_ref[...], own)
        xhat, rstd = normed(xp)
        at = pl.ds(pl.multiple_of(rc * 192, 192), 192)
        mine = own_ref[at, :]
        got_a = fa_ref[pl.ds(pl.multiple_of(rc * 160, 160), 160), :].astype(F32)
        got_b = fb_ref[pl.ds(pl.multiple_of(rc * 160, 160), 160), :].astype(F32)
        gap = jnp.zeros((QN - RIM, 512), F32)
        parts = []
        for i in range(4):
            a = jnp.concatenate([got_a[i * RIM : (i + 1) * RIM], gap], axis=0)
            b = jnp.concatenate([gap, got_b[i * RIM : (i + 1) * RIM]], axis=0)
            parts.append(mine[i * QN : (i + 1) * QN] + a + b)
        dkv = jnp.concatenate(parts, axis=0).astype(BF)
        dqkv = jnp.concatenate([dq_ref[at, :], dkv], axis=1)
        dqkv_ref[at, :] = dqkv
        dn = dot_nt(dqkv, wqkv_ref[...])
        gain = vec_ref[0:1, :]
        dx = dx1_ref[at, :] + norm_back(dn * gain, xhat, rstd)
        back = dot_tn(po_ref[...], dx.astype(BF)).astype(BF)
        for i in range(4):
            tok_ref[4 * i + rc] = back[48 * i : 48 * i + 48]
        sums_ref[0:1, :] += jnp.sum(dn * xhat, axis=0, keepdims=True)
        sums_ref[1:2, :] += jnp.sum(dn, axis=0, keepdims=True)
        sums_ref[3:4, :] += jnp.sum(dkv[:, 256:512].astype(F32), axis=0, keepdims=True)
        return 0

    lax.fori_loop(0, 4, block, 0)


def call(kernel, out_shape, scratch, *args, smem=0, flops=10**8):
    vm = pl.BlockSpec(memory_space=pltpu.VMEM)
    specs = [pl.BlockSpec(memory_space=pltpu.SMEM)] * smem + [vm] * (len(args) - smem)
    return pl.pallas_call(
        kernel,
        out_shape=out_shape,
        in_specs=specs,
        out_specs=jax.tree.map(lambda _: vm, out_shape),
        scratch_shapes=scratch,
        compiler_params=pltpu.CompilerParams(vmem_limit_bytes=48 * 2**20),
        cost_estimate=pl.CostEstimate(flops=flops, bytes_accessed=10**6, transcendentals=0),
    )(*args)


def sds(shape, dtype=BF):
    return jax.ShapeDtypeStruct(shape, dtype)


def exchange_groups(maps, band):
    zbits = band.bit_length() - 2
    mbits = maps.bit_length() - 1
    cut = lambda lo, n: [(lo + i, min(2, n - i)) for i in range(0, n, 2)]
    return cut(1, zbits) + cut(1 + zbits, mbits) + [(0, 1)]


def swap(block, mask, count):
    return lax.ppermute(block, AXES, [(k, k ^ mask) for k in range(count)])


def frame_masks(groups):
    masks = [0]
    for lo, bits in groups:
        masks = [m ^ (d << lo) for d in range(1 << bits) for m in masks]
    return masks


def gather_all(slab, groups, count):
    block = slab[None]
    for lo, bits in groups:
        block = jnp.concatenate(
            [block] + [swap(block, d << lo, count) for d in range(1, 1 << bits)], axis=0
        )
    return block


def scatter_sum(grads, groups, count):
    for lo, bits in reversed(groups):
        low = grads.astype(BF).reshape((1 << bits, -1) + grads.shape[1:])
        total = grads.reshape(low.shape)[0].astype(F32)
        for d in range(1, 1 << bits):
            total = total + swap(low[d], d << lo, count).astype(F32)
        grads = total
    return grads[0]


def adam_parts(weight, grad, first, second):
    new_first = BETA_FIRST * first + (1.0 - BETA_FIRST) * grad
    new_second = BETA_SECOND * second + (1.0 - BETA_SECOND) * grad * grad
    update = (
        new_first
        / (1.0 - BETA_FIRST**STEP)
        / (jnp.sqrt(new_second / (1.0 - BETA_SECOND**STEP)) + ADAM_EPS)
        + DECAY_RATE * weight
    )
    return (new_first, new_second, update)


def squares_of(matrices, rowwise):
    return jnp.concatenate(
        [
            jnp.stack([jnp.sum(matrix * matrix) for matrix in matrices]),
            jnp.sum(rowwise * rowwise, axis=1),
        ]
    )


def per_device(
    maps,
    band,
    tokens_in,
    cotangent,
    map_sizes,
    w_qkv,
    w_out,
    w_up,
    w_down,
    vectors,
    pos_table,
    first_qkv,
    second_qkv,
    first_out,
    second_out,
    first_up,
    second_up,
    first_down,
    second_down,
    first_vectors,
    second_vectors,
    first_table,
    second_table,
):
    count = maps * band
    rows = w_qkv.shape[0]
    vrows = vectors.shape[0]
    groups = exchange_groups(maps, band)
    masks = np.array(frame_masks(groups))
    inverse = np.argsort(masks)
    me = lax.axis_index(AXES)
    band_index = lax.axis_index("band")
    reach = 3 * DIL

    up = [(i, i + 1) for i in range(band - 1)]
    down = [(i + 1, i) for i in range(band - 1)]
    x_before = lax.ppermute(tokens_in[-reach:], "band", up)
    x_after = lax.ppermute(tokens_in[:reach], "band", down)

    def pack(qkv, out, upw, dnw, vec):
        dn = dnw.reshape(3, rows, 256).transpose(1, 0, 2).reshape(rows, 768)
        vt = jnp.pad(vec.T, ((0, 0), (0, 128 - vrows)))
        return jnp.concatenate([qkv, out, upw, dn, vt], axis=1)

    slab = pack(*(w.astype(BF) for w in (w_qkv, w_out, w_up, w_down, vectors)))
    block = gather_all(slab, groups, count)
    order = jnp.asarray(inverse, jnp.int32)[jnp.arange(count, dtype=jnp.int32) ^ me]
    whole = jnp.take(block, order, axis=0).reshape(256, -1)
    big_qkv = whole[:, 0:768]
    big_out = whole[:, 768:1024]
    big_up = whole[:, 1024:1792]
    big_down = (
        whole[:, 1792:2560].reshape(count, rows, 3, 256).transpose(0, 2, 1, 3).reshape(768, 256)
    )
    vec = whole[:, 2560 : 2560 + vrows].T.astype(F32)

    po = jnp.asarray(order_own(), BF)
    pk = jnp.asarray(order_keys(), BF)
    place = jnp.stack([band_index, map_sizes[0, 0], map_sizes[0, 1]]).astype(jnp.int32)
    (
        layer_out,
        act,
        dy,
        dz,
        a2,
        mixed,
        da,
        a1,
        dq,
        dx1,
        own,
        rim_a,
        rim_b,
        table_grad,
        sums,
        zsum,
    ) = call(
        layer_kernel,
        (
            sds((16, 48, 256)),
            sds((768, 768)),
            sds((768, 256)),
            sds((768, 768)),
            sds((768, 256)),
            sds((768, 256)),
            sds((768, 256)),
            sds((768, 256)),
            sds((768, 256)),
            sds((768, 256), F32),
            sds((768, 512), F32),
            sds((CLS * RIM, 512)),
            sds((CLS * RIM, 512)),
            sds((HEADS, KN), F32),
            sds((8, 256), F32),
            sds((1, 768), F32),
        ),
        [
            pltpu.VMEM((768, 256), F32),
            pltpu.VMEM((768, 256), BF),
            pltpu.VMEM((CLS * KN, 256), BF),
            pltpu.VMEM((CLS * KN, 256), BF),
            pltpu.VMEM((KN, 384), F32),
            pltpu.VMEM((CLS * KN, 384), F32),
            pltpu.VMEM((768, 256), F32),
            pltpu.VMEM((768, 256), BF),
            pltpu.VMEM((KN, 384), F32),
        ],
        place,
        tokens_in,
        x_before,
        x_after,
        cotangent,
        big_qkv,
        big_out,
        big_up,
        big_down,
        vec,
        pos_table,
        po,
        pk,
        smem=1,
        flops=6 * 10**9,
    )
    from_prev = lax.ppermute(rim_a, "band", up)
    from_next = lax.ppermute(rim_b, "band", down)
    grad_down = dot_tn(act, dy)
    grad_up = dot_tn(a2, dz)
    grad_out = dot_tn(mixed, da)
    tokens_grad, dqkv, sums2 = call(
        finish_kernel,
        (sds((16, 48, 256)), sds((768, 768)), sds((8, 256), F32)),
        [],
        own,
        from_prev,
        from_next,
        dq,
        dx1,
        tokens_in,
        big_qkv,
        vec,
        po,
    )
    grad_qkv = dot_tn(a1, dqkv)
    grad_vec = jnp.concatenate([sums + sums2, zsum.reshape(3, 256)], axis=0)

    packed = jnp.concatenate(
        [
            grad_qkv.reshape(count, rows, 768),
            grad_out.reshape(count, rows, 256),
            grad_up.reshape(count, rows, 768),
            grad_down.reshape(count, 3, rows, 256).transpose(0, 2, 1, 3).reshape(count, rows, 768),
            jnp.pad(grad_vec.T, ((0, 0), (0, 128 - vrows))).reshape(count, rows, 128),
        ],
        axis=2,
    )
    packed = jnp.take(packed, jnp.asarray(masks, jnp.int32) ^ me, axis=0)
    red = scatter_sum(packed, groups, count)
    red_qkv = red[:, 0:768]
    red_out = red[:, 768:1024]
    red_up = red[:, 1024:1792]
    red_down = red[:, 1792:2560].reshape(rows, 3, 256).transpose(1, 0, 2).reshape(3 * rows, 256)
    red_vec = red[:, 2560 : 2560 + vrows].T

    steps = np.arange(-3, 4)
    lanes = ((12 * steps[:, None] + steps[None, :]) % KN).reshape(-1)
    table_total = lax.psum(table_grad, AXES)[:, lanes]

    part_qkv = adam_parts(w_qkv, red_qkv, first_qkv, second_qkv)
    part_out = adam_parts(w_out, red_out, first_out, second_out)
    part_up = adam_parts(w_up, red_up, first_up, second_up)
    part_down = adam_parts(w_down, red_down, first_down, second_down)
    part_vec = adam_parts(vectors, red_vec, first_vectors, second_vectors)
    part_table = adam_parts(pos_table, table_total, first_table, second_table)
    local_weight_sq = squares_of((w_qkv, w_out, w_up, w_down), vectors)
    local_update_sq = squares_of((part_qkv[2], part_out[2], part_up[2], part_down[2]), part_vec[2])
    weight_sq, update_sq = lax.psum((local_weight_sq, local_update_sq), AXES)
    table_weight = jnp.sqrt(jnp.sum(pos_table * pos_table))
    table_update = jnp.sqrt(jnp.sum(part_table[2] * part_table[2]))
    weight_norms = jnp.concatenate([jnp.sqrt(weight_sq), table_weight[None]])
    update_norms = jnp.concatenate([jnp.sqrt(update_sq), table_update[None]])
    ratios = weight_norms / (update_norms + RATIO_EPS)
    next_qkv = w_qkv - LEARN_RATE * ratios[0] * part_qkv[2]
    next_out = w_out - LEARN_RATE * ratios[1] * part_out[2]
    next_up = w_up - LEARN_RATE * ratios[2] * part_up[2]
    next_down = w_down - LEARN_RATE * ratios[3] * part_down[2]
    next_vectors = vectors - LEARN_RATE * ratios[4 : 4 + vrows][:, None] * part_vec[2]
    next_table = pos_table - LEARN_RATE * ratios[4 + vrows] * part_table[2]
    return (
        layer_out,
        tokens_grad,
        part_qkv[0],
        part_qkv[1],
        next_qkv,
        part_out[0],
        part_out[1],
        next_out,
        part_up[0],
        part_up[1],
        next_up,
        part_down[0],
        part_down[1],
        next_down,
        part_vec[0],
        part_vec[1],
        next_vectors,
        part_table[0],
        part_table[1],
        next_table,
        weight_norms,
        update_norms,
    )


def solution(mesh):
    both = P(AXES, None)
    side = P(None, AXES)
    tall = P(AXES, None, None)
    copied = P()
    return jax.shard_map(
        functools.partial(per_device, mesh.shape["maps"], mesh.shape["band"]),
        mesh=mesh,
        in_specs=(tall, tall, P("maps", None))
        + (both,) * 4
        + (side, copied)
        + (both,) * 8
        + (side, side, copied, copied),
        out_specs=(tall, tall) + (both,) * 12 + (side,) * 3 + (copied,) * 5,
        check_vma=False,
    )
```

time: 2620 us -> 193 us (0.07); the launches traced: 2590 us -> 191 us
  local copies, waits for them, and re-layouts: 1590 us -> 39.2 us
  waiting for transfers between devices: 339 us -> 20.2 us
  other arithmetic: 318 us -> 15.9 us
  blocking collectives: 285 us -> 37.2 us
  Pallas kernels: 0 us -> 33.9 us
    scatter-add x44 -> x0, local copies, waits for them, and re-layouts: 565 us -> none  [the longest x22 283 us: per_device(): grad_keys.at[top:top + rows]]
    reshape x133 -> x2, local copies, waits for them, and re-layouts: 420 us -> 0.76 us  [the longest x1 0.6 us: per_device(): grad_vec = jnp.concatenate([sums + sums2, zsum.reshape(3, 256)], axis=0)]
    reduce_scatter x4 -> x0, waiting for transfers between devices: 339 us -> none  [the longest x1 107 us: per_device(): lax.psum_scatter(grad_out, ('maps', 'band'), scatter_dimension=0, tiled=T...]
    unnamed x966 -> x137, local copies, waits for them, and re-layouts: 224 us -> 16.4 us
    all_gather x5 -> x0, blocking collectives: 208 us -> none  [the longest x1 43.5 us: per_device(): lax.all_gather(vectors.astype(jnp.bfloat16), ('maps', 'band'), axis=1, ti...]
    slice x69 -> x13, local copies, waits for them, and re-layouts: 181 us -> 6.98 us  [the longest x1 1.9 us: per_device(): x_after = lax.ppermute(tokens_in[:reach], 'band', down)]
    scatter-add x55 -> x0, other arithmetic: 149 us -> none  [the longest x27 75.2 us: per_device(): grad_keys.at[top:top + rows]]
    pad x44 -> x0, local copies, waits for them, and re-layouts: 148 us -> none  [the longest x21 77.3 us: column_shift(): return jnp.pad(block[:, :offset], ((0, 0), (-offset, 0), (0, 0)))]
  transfers between devices with their start and end apart: 8 -> 18, of which waited for: 4 -> 8; matrix products, arithmetic and copies ran while one was open for 2% -> 13% of each run, Pallas kernels for 0% -> 0%
where the time goes in v1:
time: 193 us; the launch traced here: 191 us
  local copies, waits for them, and re-layouts  39.2 us (20%)
  blocking collectives  37.2 us (19%)
  Pallas kernels  33.9 us (18%)
  starting transfers between devices  33.7 us (17%)
  waiting for transfers between devices  20.2 us (10%)
  other arithmetic  15.9 us (8%)
  between operations  6.12 us (3%)
  matrix products  5.28 us (3%)
    psum x1, blocking collectives, per_device(): table_total = lax.psum(table_grad, AXES)[:, lanes]  37.2 us
    pallas_call x2, Pallas kernels, call(): pl.pallas_call(kernel, out_shape=out_shape, in_specs=specs, out_specs=jax...  33.9 us
    ppermute x14, starting transfers between devices, swap(): return lax.ppermute(block, AXES, [(k, k ^ mask) for k in range(count)])  25.8 us
    ppermute x14, waiting for transfers between devices, swap(): return lax.ppermute(block, AXES, [(k, k ^ mask) for k in range(count)])  20.2 us
    unnamed x137, local copies, waits for them, and re-layouts  16.4 us
    concatenate x2, local copies, waits for them, and re-layouts, squares_of(): jnp.concatenate([jnp.stack([jnp.sum(matrix * matrix) for matrix in matric...  5.35 us
    dot_general x4, matrix products, dot_tn(): lax.dot_general(a, b, (((0,), (0,)), ((), ())), preferred_element_type=F32)  5.28 us
    ppermute x1, starting transfers between devices, per_device(): from_prev = lax.ppermute(rim_a, 'band', up)  3.93 us
  transfers between devices with their start and end apart: 18, of which 8 were waited for; matrix products, arithmetic and copies ran while one was open for 13% of the time, Pallas kernels for 0%

profile of v1, /device:TPU:0, one launch (start us, length us, event | category | flops | bytes accessed | tf_op | source)
XLA Modules:
  0.0 191.4 jit_solution(2703804605001435481)
XLA Ops:
  0.7 0.8 constant_dynamic-update-slice_fusion.4
  1.4 0.7 convert_element_type.57
  2.2 0.7 convert_bitcast_fusion.1
  2.9 0.7 constant_dynamic-update-slice_fusion.3
  3.6 0.7 constant_dynamic-update-slice_fusion.2
  4.3 3.1 %collective-permute-start.2 = (bf16[1,8,2688]{2,1,0:T(8,128)(2,1)S(1)}, bf16[1,8,2688]{2,1,0:T(8,128)(2,1)S(1)}, u32[]{:S(2)}, u32[]{:S(2)}) collective-permute-start(bf16[1,8,2688]{2,1,0:T(8,128)(2,1)S(1)} %bitcast.96), channel_id=1, source_target_pairs={{0,2},{1,3},{2,0},{3,1},{4,6},{5,7},{6,4},{7,5},{8,10},{9,11},{10,... | collective-permute-start | bytes 129032 | tf_op jit(solution)/shard_map/ppermute | solution.py:386
  7.4 2.6 %collective-permute-start.3 = (bf16[1,8,2688]{2,1,0:T(8,128)(2,1)S(1)}, bf16[1,8,2688]{2,1,0:T(8,128)(2,1)S(1)}, u32[]{:S(2)}, u32[]{:S(2)}) collective-permute-start(bf16[1,8,2688]{2,1,0:T(8,128)(2,1)S(1)} %bitcast.97), channel_id=1, source_target_pairs={{0,4},{1,5},{2,6},{3,7},{4,0},{5,1},{6,2},{7,3},{8,12},{9,13},{10,... | collective-permute-start | bytes 129032 | tf_op jit(solution)/shard_map/ppermute | solution.py:386
  10.0 1.9 fusion.30
  11.9 1.3 collective-permute-start
  13.2 1.3 collective-permute-start.1
  14.5 0.6 constant_dynamic-update-slice_fusion.11
  16.3 0.7 gather_fusion
  17.0 1.8 collective-permute-start.5
  18.8 1.5 collective-permute-start.6
  21.2 0.6 constant_dynamic-update-slice_fusion.9
  21.8 0.6 constant_dynamic-update-slice_fusion.8
  23.0 0.8 constant_dynamic-update-slice_fusion.7
  23.8 4.2 %collective-permute-done.6 = bf16[4,8,2688]{2,1,0:T(8,128)(2,1)S(1)} collective-permute-done((bf16[4,8,2688]{2,1,0:T(8,128)(2,1)S(1)}, bf16[4,8,2688]{2,1,0:T(8,128)(2,1)S(1)}, u32[]{:S(2)}, u32[]{:S(2)}) %collective-permute-start.6) | collective-permute-done | bytes 172064 | tf_op jit(solution)/shard_map/ppermute | solution.py:386
  28.0 0.8 constant_dynamic-update-slice_fusion.6
  28.8 0.8 constant_dynamic-update-slice_fusion.5
  29.5 1.5 collective-permute-start.8
  31.8 1.4 pad_add_fusion.where_ref
  33.2 0.9 constant_dynamic-update-slice_fusion.12
  34.1 2.1 %gather_fusion.1 = bf16[32,8,2688]{2,1,0:T(8,128)(2,1)S(1)} fusion(bf16[32,8,2688]{2,1,0:T(8,128)(2,1)} %constant_dynamic-update-slice_fusion.12, s32[1024]{0:T(1024)S(1)} %pad_clamp_fusion.2), kind=kCustom, calls=%fused_computation.1 | custom fusion | bytes 2752640 | tf_op jit(solution)/shard_map/jit(_take)/gather | solution.py:484
  36.2 1.6 copy.86
  37.8 1.5 broadcast_select_fusion.1
  39.3 1.1 fusion.28
  41.1 1.3 copy.89.wqkv_ref
  42.4 1.2 copy.91.wu_ref
  43.7 0.7 convert_bitcast_fusion.vec_ref
  44.4 29.6 %shard_map.426 = (bf16[16,48,256]{2,1,0:T(8,128)(2,1)}, bf16[768,768]{1,0:T(8,128)(2,1)}, bf16[768,256]{1,0:T(8,128)(2,1)S(1)}, bf16[768,768]{1,0:T(8,128)(2,1)}...) custom-call(s32[3]{0:T(128)S(1)} %pad_add_fusion.where_ref, ...), custom_call_target="tpu_custom_call" | custom-call | flops 6000000000 | bytes 1000000 | tf_op jit(solution)/shard_map/pallas_call | solution.py:363
  74.0 0.8 copy-done.5
  74.8 0.8 copy-done.7
  75.6 0.7 copy-done.8
  76.3 0.8 copy-done.10
  77.1 0.8 copy-done.12
  79.0 0.7 copy-done.24
  79.8 1.4 collective-permute-start.10
  81.2 3.9 %collective-permute-start.9 = (bf16[640,512]{1,0:T(8,128)(2,1)}, bf16[640,512]{1,0:T(8,128)(2,1)}, u32[]{:S(2)}, u32[]{:S(2)}) collective-permute-start(bf16[640,512]{1,0:T(8,128)(2,1)} %get-tuple-element.43), channel_id=1, source_target_pairs={{0,1},{1,2},{2,3},{3,4},{4,5},{5,6},{6,7},{8,9},{9,10},{10,11},{11... | collective-permute-start | bytes 1966088 | tf_op jit(solution)/shard_map/ppermute | solution.py:560
  85.7 2.8 %fusion.34 = f32[768,256]{1,0:T(8,128)} fusion(bf16[768,768]{1,0:T(8,128)(2,1)} %get-tuple-element.54, bf16[768,256]{1,0:T(8,128)(2,1)} %copy-done.24), kind=kOutput, calls=%fused_computation.117 | convolution fusion | flops 301989888 | bytes 2359296 | tf_op jit(solution)/shard_map/dot_general | solution.py:44
  88.6 0.8 copy-done.3
  89.4 1.1 copy-done.4
  90.5 1.0 copy-done.9
  91.5 0.9 copy-done.15
  92.4 4.3 %shard_map.427 = (bf16[16,48,256]{2,1,0:T(8,128)(2,1)}, bf16[768,768]{1,0:T(8,128)(2,1)S(1)}, f32[8,256]{1,0:T(8,128)S(1)}) custom-call(f32[768,512]{1,0:T(8,128)S(1)} %copy-done.1, bf16[640,512]{1,0:T(8,128)(2,1)} %collective-permute-done.9.fa_ref, bf16[640,512]{1,0:T(8,128)(2,1)S(1)} %copy-done.4, bf16[768,256]{1,0:T(8,128)(2,1)S(1)} %copy-done.9, ...), custom_call_target="tpu_custom_call" | custom-call | flops 100000000 | bytes 1000000 | tf_op jit(solution)/shard_map/pallas_call | solution.py:363
  96.9 1.6 fusion.1
  100.1 1.5 copy-done.27
  101.6 2.6 %gather_fusion.2 = f32[32,8,2688]{2,1,0:T(8,128)S(1)} fusion(f32[32,8,2688]{2,1,0:T(8,128)} %copy-done.27, s32[1024]{0:T(1024)} %get-tuple-element.177), kind=kCustom, calls=%fused_computation.2 | custom fusion | bytes 5505152 | tf_op jit(solution)/shard_map/jit(_take)/gather | solution.py:592
  104.5 5.1 %collective-permute-start.11 = (bf16[16,8,2688]{2,1,0:T(8,128)(2,1)S(1)}, bf16[16,8,2688]{2,1,0:T(8,128)(2,1)S(1)}, u32[]{:S(2)}, u32[]{:S(2)}) collective-permute-start(bf16[16,8,2688]{2,1,0:T(8,128)(2,1)S(1)} %slice.185), channel_id=1, source_target_pairs={{0,1},{1,0},{2,3},{3,2},{4,5},{5,4},{6,7},{7,6},{8,9},{9,8},{10,11... | collective-permute-start | bytes 2064392 | tf_op jit(solution)/shard_map/ppermute | solution.py:386
  109.6 1.8 collective-permute-done.11
  112.4 1.6 collective-permute-start.13
  114.0 1.4 collective-permute-start.14
  115.4 3.7 %collective-permute-done.12 = bf16[4,8,2688]{2,1,0:T(8,128)(2,1)S(1)} collective-permute-done((bf16[4,8,2688]{2,1,0:T(8,128)(2,1)S(1)}, bf16[4,8,2688]{2,1,0:T(8,128)(2,1)S(1)}, u32[]{:S(2)}, u32[]{:S(2)}) %collective-permute-start.12) | collective-permute-done | bytes 172064 | tf_op jit(solution)/shard_map/ppermute | solution.py:386
  119.1 2.5 %collective-permute-done.13 = bf16[4,8,2688]{2,1,0:T(8,128)(2,1)S(1)} collective-permute-done((bf16[4,8,2688]{2,1,0:T(8,128)(2,1)S(1)}, bf16[4,8,2688]{2,1,0:T(8,128)(2,1)S(1)}, u32[]{:S(2)}, u32[]{:S(2)}) %collective-permute-start.13) | collective-permute-done | bytes 172064 | tf_op jit(solution)/shard_map/ppermute | solution.py:386
  121.6 1.6 collective-permute-done.14
  123.3 2.6 %collective-permute-start.15 = (bf16[1,8,2688]{2,1,0:T(8,128)(2,1)S(1)}, bf16[1,8,2688]{2,1,0:T(8,128)(2,1)S(1)}, u32[]{:S(2)}, u32[]{:S(2)}) collective-permute-start(bf16[1,8,2688]{2,1,0:T(8,128)(2,1)S(1)} %get-tuple-element.148), channel_id=1, source_target_pairs={{0,2},{1,3},{2,0},{3,1},{4,6},{5,7},{6,4},{7,5},{8,10},{9,11},{10,... | collective-permute-start | bytes 129032 | tf_op jit(solution)/shard_map/ppermute | solution.py:386
  125.9 3.9 %collective-permute-start.16 = (bf16[1,8,2688]{2,1,0:T(8,128)(2,1)S(1)}, bf16[1,8,2688]{2,1,0:T(8,128)(2,1)S(1)}, u32[]{:S(2)}, u32[]{:S(2)}) collective-permute-start(bf16[1,8,2688]{2,1,0:T(8,128)(2,1)S(1)} %get-tuple-element.150), channel_id=1, source_target_pairs={{0,4},{1,5},{2,6},{3,7},{4,0},{5,1},{6,2},{7,3},{8,12},{9,13},{10,... | collective-permute-start | bytes 129032 | tf_op jit(solution)/shard_map/ppermute | solution.py:386
  129.8 2.5 %collective-permute-done.16 = bf16[1,8,2688]{2,1,0:T(8,128)(2,1)S(1)} collective-permute-done((bf16[1,8,2688]{2,1,0:T(8,128)(2,1)S(1)}, bf16[1,8,2688]{2,1,0:T(8,128)(2,1)S(1)}, u32[]{:S(2)}, u32[]{:S(2)}) %collective-permute-start.16) | collective-permute-done | bytes 43040 | tf_op jit(solution)/shard_map/ppermute | solution.py:386
  132.3 3.3 %collective-permute-done.17 = bf16[1,8,2688]{2,1,0:T(8,128)(2,1)S(1)} collective-permute-done((bf16[1,8,2688]{2,1,0:T(8,128)(2,1)S(1)}, bf16[1,8,2688]{2,1,0:T(8,128)(2,1)S(1)}, u32[]{:S(2)}, u32[]{:S(2)}) %collective-permute-start.17) | collective-permute-done | bytes 43040 | tf_op jit(solution)/shard_map/ppermute | solution.py:386
  136.4 0.7 multiply_reduce_fusion.1
  137.1 0.6 multiply_reduce_fusion
  137.7 2.7 %concatenate.40 = f32[15]{0:T(128)S(1)} concatenate(f32[1]{0:T(128)} %bitcast.29, f32[1]{0:T(128)} %bitcast.30, f32[1]{0:T(128)} %bitcast.31, f32[1]{0:T(128)} %bitcast.37, f32[11]{0:T(128)S(1)} %get-tuple-element.112), dimensions={0} | concatenate | bytes 120 | tf_op jit(solution)/shard_map/concatenate | solution.py:428
  140.4 2.7 %concatenate.38 = f32[15]{0:T(128)S(1)} concatenate(f32[1]{0:T(128)} %bitcast.24, f32[1]{0:T(128)} %bitcast.25, f32[1]{0:T(128)} %bitcast.26, f32[1]{0:T(128)} %bitcast.27, f32[11]{0:T(128)S(1)} %get-tuple-element.113), dimensions={0} | concatenate | bytes 120 | tf_op jit(solution)/shard_map/concatenate | solution.py:428
  143.1 37.2 %all-reduce.2 = (f32[8,128]{1,0:T(8,128)S(1)}, f32[15]{0:T(128)S(1)}, f32[15]{0:T(128)S(1)}) all-reduce(f32[8,128]{1,0:T(8,128)S(1)} %copy-done.21, f32[15]{0:T(128)S(1)} %concatenate.38, f32[15]{0:T(128)S(1)} %concatenate.40), channel_id=1, replica_groups=mesh['maps'=4,'band'=8] {'maps','band'}, use_global_device_ids=true, to_apply=%region_13.14 | all-reduce | flops 1054 | bytes 8432 | tf_op jit(solution)/shard_map/psum | solution.py:602
  (185 shorter events, 16.2 us)
Async XLA Ops:
  0.7 14.5 %copy-start.63 = (s32[32]{0:T(128)S(1)}, s32[32]{0:T(128)}, u32[]{:S(2)}) copy-start(s32[32]{0:T(128)} %constant.70.clone) | copy-start | bytes 388
  0.7 15.6 %copy-start.25 = (s32[32]{0:T(128)S(1)}, s32[32]{0:T(128)}, u32[]{:S(2)}) copy-start(s32[32]{0:T(128)} %constant.61.clone) | copy-start | bytes 388
  4.3 12.6 %collective-permute-start.2 = (bf16[1,8,2688]{2,1,0:T(8,128)(2,1)S(1)}, bf16[1,8,2688]{2,1,0:T(8,128)(2,1)S(1)}, u32[]{:S(2)}, u32[]{:S(2)}) collective-permute-start(bf16[1,8,2688]{2,1,0:T(8,128)(2,1)S(1)} %bitcast.96), channel_id=1, source_target_pairs={{0,2},{1,3},{2,0},{3,1},{4,6},{5,7},{6,4},{7,5},{8,10},{9,11},{10,... | collective-permute-start | bytes 129032 | tf_op jit(solution)/shard_map/ppermute | solution.py:386
  7.4 9.6 %collective-permute-start.3 = (bf16[1,8,2688]{2,1,0:T(8,128)(2,1)S(1)}, bf16[1,8,2688]{2,1,0:T(8,128)(2,1)S(1)}, u32[]{:S(2)}, u32[]{:S(2)}) collective-permute-start(bf16[1,8,2688]{2,1,0:T(8,128)(2,1)S(1)} %bitcast.97), channel_id=1, source_target_pairs={{0,4},{1,5},{2,6},{3,7},{4,0},{5,1},{6,2},{7,3},{8,12},{9,13},{10,... | collective-permute-start | bytes 129032 | tf_op jit(solution)/shard_map/ppermute | solution.py:386
  10.0 7.0 %collective-permute-start.4 = (bf16[1,8,2688]{2,1,0:T(8,128)(2,1)S(1)}, bf16[1,8,2688]{2,1,0:T(8,128)(2,1)S(1)}, u32[]{:S(2)}, u32[]{:S(2)}) collective-permute-start(bf16[1,8,2688]{2,1,0:T(8,128)(2,1)S(1)} %bitcast.98), channel_id=1, source_target_pairs={{0,6},{1,7},{2,4},{3,5},{4,2},{5,3},{6,0},{7,1},{8,14},{9,15},{10,... | collective-permute-start | bytes 129032 | tf_op jit(solution)/shard_map/ppermute | solution.py:386
  11.9 32.5 %collective-permute-start = (bf16[12,48,256]{2,1,0:T(8,128)(2,1)}, bf16[12,48,256]{2,1,0:T(8,128)(2,1)S(1)}, u32[]{:S(2)}, u32[]{:S(2)}) collective-permute-start(bf16[12,48,256]{2,1,0:T(8,128)(2,1)} %get-tuple-element.147), channel_id=1, source_target_pairs={{0,1},{1,2},{2,3},{3,4},{4,5},{5,6},{6,7},{8,9},{9,10},{10,11},{11... | collective-permute-start | bytes 884744 | tf_op jit(solution)/shard_map/ppermute | solution.py:473
  13.2 31.2 %collective-permute-start.1 = (bf16[12,48,256]{2,1,0:T(8,128)(2,1)}, bf16[12,48,256]{2,1,0:T(8,128)(2,1)S(1)}, u32[]{:S(2)}, u32[]{:S(2)}) collective-permute-start(bf16[12,48,256]{2,1,0:T(8,128)(2,1)} %get-tuple-element.146), channel_id=1, source_target_pairs={{1,0},{2,1},{3,2},{4,3},{5,4},{6,5},{7,6},{9,8},{10,9},{11,10},{12... | collective-permute-start | bytes 884744 | tf_op jit(solution)/shard_map/ppermute | solution.py:474
  16.3 15.0 %copy-start.61 = (s32[1,2]{1,0:T(1,128)S(1)}, s32[1,2]{1,0:T(1,128)}, u32[]{:S(2)}) copy-start(s32[1,2]{1,0:T(1,128)} %param.29) | copy-start | bytes 28
  17.0 6.0 %collective-permute-start.5 = (bf16[4,8,2688]{2,1,0:T(8,128)(2,1)S(1)}, bf16[4,8,2688]{2,1,0:T(8,128)(2,1)S(1)}, u32[]{:S(2)}, u32[]{:S(2)}) collective-permute-start(bf16[4,8,2688]{2,1,0:T(8,128)(2,1)S(1)} %pad_maximum_fusion), channel_id=1, source_target_pairs={{0,8},{1,9},{2,10},{3,11},{4,12},{5,13},{6,14},{7,15},{8,0},{9,1},... | collective-permute-start | bytes 516104 | tf_op jit(solution)/shard_map/ppermute | solution.py:386
  18.8 9.2 %collective-permute-start.6 = (bf16[4,8,2688]{2,1,0:T(8,128)(2,1)S(1)}, bf16[4,8,2688]{2,1,0:T(8,128)(2,1)S(1)}, u32[]{:S(2)}, u32[]{:S(2)}) collective-permute-start(bf16[4,8,2688]{2,1,0:T(8,128)(2,1)S(1)} %pad_maximum_fusion), channel_id=1, source_target_pairs={{0,16},{1,17},{2,18},{3,19},{4,20},{5,21},{6,22},{7,23},{8,24},{9,... | collective-permute-start | bytes 516104 | tf_op jit(solution)/shard_map/ppermute | solution.py:386
  20.3 8.5 %collective-permute-start.7 = (bf16[4,8,2688]{2,1,0:T(8,128)(2,1)S(1)}, bf16[4,8,2688]{2,1,0:T(8,128)(2,1)S(1)}, u32[]{:S(2)}, u32[]{:S(2)}) collective-permute-start(bf16[4,8,2688]{2,1,0:T(8,128)(2,1)S(1)} %pad_maximum_fusion), channel_id=1, source_target_pairs={{0,24},{1,25},{2,26},{3,27},{4,28},{5,29},{6,30},{7,31},{8,16},{9,... | collective-permute-start | bytes 516104 | tf_op jit(solution)/shard_map/ppermute | solution.py:386
  29.5 3.7 %collective-permute-start.8 = (bf16[16,8,2688]{2,1,0:T(8,128)(2,1)}, bf16[16,8,2688]{2,1,0:T(8,128)(2,1)S(1)}, u32[]{:S(2)}, u32[]{:S(2)}) collective-permute-start(bf16[16,8,2688]{2,1,0:T(8,128)(2,1)} %get-tuple-element.151), channel_id=1, source_target_pairs={{0,1},{1,0},{2,3},{3,2},{4,5},{5,4},{6,7},{7,6},{8,9},{9,8},{10,11... | collective-permute-start | bytes 2064392 | tf_op jit(solution)/shard_map/ppermute | solution.py:386
  41.0 2.6 %slice-start = ((bf16[256,2688]{0,1:T(8,128)(2,1)}), bf16[256,256]{0,1:T(8,128)(2,1)S(1)}, s32[]{:S(2)}) async-start(bf16[256,2688]{0,1:T(8,128)(2,1)} %copy-done.26), calls=%async_computation | async-start | bytes 262144 | tf_op jit(solution)/shard_map/slice | solution.py:486
  41.0 3.4 %copy-start = (bf16[16,48,256]{2,1,0:T(8,128)(2,1)S(1)}, bf16[16,48,256]{2,1,0:T(8,128)(2,1)}, u32[]{:S(2)}) copy-start(bf16[16,48,256]{2,1,0:T(8,128)(2,1)} %x_ref.3) | copy-start | bytes 1179652
  41.0 3.4 %copy-start.14 = (bf16[192,192]{1,0:T(8,128)(2,1)S(1)}, bf16[192,192]{1,0:T(8,128)(2,1)}, u32[]{:S(2)}) copy-start(bf16[192,192]{1,0:T(8,128)(2,1)} %constant.62.clone.po_ref) | copy-start | bytes 221188
  41.0 3.4 %copy-start.16 = (f32[8,49]{1,0:T(8,128)S(1)}, f32[8,49]{1,0:T(8,128)}, u32[]{:S(2)}) copy-start(f32[8,49]{1,0:T(8,128)} %table_ref.1) | copy-start | bytes 4708
  41.0 3.4 %copy-start.22 = (bf16[16,48,256]{2,1,0:T(8,128)(2,1)S(1)}, bf16[16,48,256]{2,1,0:T(8,128)(2,1)}, u32[]{:S(2)}) copy-start(bf16[16,48,256]{2,1,0:T(8,128)(2,1)} %cot_ref.1) | copy-start | bytes 1179652
  41.0 3.4 %copy-start.23 = (bf16[512,480]{1,0:T(8,128)(2,1)S(1)}, bf16[512,480]{1,0:T(8,128)(2,1)}, u32[]{:S(2)}) copy-start(bf16[512,480]{1,0:T(8,128)(2,1)} %constant.63.clone.pk_ref) | copy-start | bytes 1474564
  79.8 9.6 %copy-start.1 = (f32[768,512]{1,0:T(8,128)S(1)}, f32[768,512]{1,0:T(8,128)}, u32[]{:S(2)}) copy-start(f32[768,512]{1,0:T(8,128)} %get-tuple-element.42.own_ref) | copy-start | bytes 4718596
  79.8 8.8 %collective-permute-start.10 = (bf16[640,512]{1,0:T(8,128)(2,1)}, bf16[640,512]{1,0:T(8,128)(2,1)S(1)}, u32[]{:S(2)}, u32[]{:S(2)}) collective-permute-start(bf16[640,512]{1,0:T(8,128)(2,1)} %get-tuple-element.44), channel_id=1, source_target_pairs={{1,0},{2,1},{3,2},{4,3},{5,4},{6,5},{7,6},{9,8},{10,9},{11,10},{12... | collective-permute-start | bytes 1966088 | tf_op jit(solution)/shard_map/ppermute | solution.py:561
  81.2 8.2 %collective-permute-start.9 = (bf16[640,512]{1,0:T(8,128)(2,1)}, bf16[640,512]{1,0:T(8,128)(2,1)}, u32[]{:S(2)}, u32[]{:S(2)}) collective-permute-start(bf16[640,512]{1,0:T(8,128)(2,1)} %get-tuple-element.43), channel_id=1, source_target_pairs={{0,1},{1,2},{2,3},{3,4},{4,5},{5,6},{6,7},{8,9},{9,10},{10,11},{11... | collective-permute-start | bytes 1966088 | tf_op jit(solution)/shard_map/ppermute | solution.py:560
  85.7 3.7 %copy-start.2 = (f32[768,256]{1,0:T(8,128)S(1)}, f32[768,256]{1,0:T(8,128)}, u32[]{:S(2)}) copy-start(f32[768,256]{1,0:T(8,128)} %get-tuple-element.46.dx1_ref) | copy-start | bytes 2359300
  92.4 4.3 %copy-start.19 = (f32[8,256]{1,0:T(8,128)S(1)}, f32[8,256]{1,0:T(8,128)}, u32[]{:S(2)}) copy-start(f32[8,256]{1,0:T(8,128)} %copy-done.18) | copy-start | bytes 24580
  92.4 4.3 %copy-start.49 = (f32[3,256]{1,0:T(4,128)S(1)}, f32[3,256]{1,0:T(4,128)}, u32[]{:S(2)}) copy-start(f32[3,256]{1,0:T(4,128)} %reshape.172) | copy-start | bytes 9220
  101.6 2.6 %copy-start.60 = (pred[32]{0:T(512)(128)(4,1)S(1)}, pred[32]{0:T(512)(128)(4,1)}, u32[]{:S(2)}) copy-start(pred[32]{0:T(512)(128)(4,1)} %get-tuple-element.138) | copy-start | bytes 100
  104.5 6.8 %collective-permute-start.11 = (bf16[16,8,2688]{2,1,0:T(8,128)(2,1)S(1)}, bf16[16,8,2688]{2,1,0:T(8,128)(2,1)S(1)}, u32[]{:S(2)}, u32[]{:S(2)}) collective-permute-start(bf16[16,8,2688]{2,1,0:T(8,128)(2,1)S(1)} %slice.185), channel_id=1, source_target_pairs={{0,1},{1,0},{2,3},{3,2},{4,5},{5,4},{6,7},{7,6},{8,9},{9,8},{10,11... | collective-permute-start | bytes 2064392 | tf_op jit(solution)/shard_map/ppermute | solution.py:386
  111.5 18.2 %copy-start.62 = (s32[49]{0:T(128)S(1)}, s32[49]{0:T(128)}, u32[]{:S(2)}) copy-start(s32[49]{0:T(128)} %constant.160) | copy-start | bytes 592
  111.6 24.0 %copy-start.39 = (f32[8,256]{1,0:T(8,128)S(1)}, f32[8,256]{1,0:T(8,128)}, u32[]{:S(2)}) copy-start(f32[8,256]{1,0:T(8,128)} %param.31) | copy-start | bytes 24580
  111.6 24.0 %copy-start.54 = (f32[8,256]{1,0:T(8,128)S(1)}, f32[8,256]{1,0:T(8,128)}, u32[]{:S(2)}) copy-start(f32[8,256]{1,0:T(8,128)} %param.38) | copy-start | bytes 24580
  111.6 24.0 %copy-start.55 = (f32[8,256]{1,0:T(8,128)S(1)}, f32[8,256]{1,0:T(8,128)}, u32[]{:S(2)}) copy-start(f32[8,256]{1,0:T(8,128)} %param.39) | copy-start | bytes 24580
  111.6 24.7 %copy-start.40 = (f32[11,8]{0,1:T(8,128)S(1)}, f32[11,8]{0,1:T(8,128)}, u32[]{:S(2)}) copy-start(f32[11,8]{0,1:T(8,128)} %param.34) | copy-start | bytes 1060
  111.6 24.6 %copy-start.56 = (f32[11,8]{0,1:T(8,128)S(1)}, f32[11,8]{0,1:T(8,128)}, u32[]{:S(2)}) copy-start(f32[11,8]{0,1:T(8,128)} %param.44) | copy-start | bytes 1060
  111.6 24.6 %copy-start.57 = (f32[11,8]{0,1:T(8,128)S(1)}, f32[11,8]{0,1:T(8,128)}, u32[]{:S(2)}) copy-start(f32[11,8]{0,1:T(8,128)} %param.45) | copy-start | bytes 1060
  111.6 24.7 %copy-start.31 = (f32[8,768]{1,0:T(8,128)S(1)}, f32[8,768]{1,0:T(8,128)}, u32[]{:S(2)}) copy-start(f32[8,768]{1,0:T(8,128)} %param.32) | copy-start | bytes 73732
  111.6 24.7 %copy-start.32 = (f32[8,768]{1,0:T(8,128)S(1)}, f32[8,768]{1,0:T(8,128)}, u32[]{:S(2)}) copy-start(f32[8,768]{1,0:T(8,128)} %param.30) | copy-start | bytes 73732
  111.7 24.7 %copy-start.45 = (f32[8,768]{1,0:T(8,128)S(1)}, f32[8,768]{1,0:T(8,128)}, u32[]{:S(2)}) copy-start(f32[8,768]{1,0:T(8,128)} %param.40) | copy-start | bytes 73732
  111.7 24.7 %copy-start.46 = (f32[8,768]{1,0:T(8,128)S(1)}, f32[8,768]{1,0:T(8,128)}, u32[]{:S(2)}) copy-start(f32[8,768]{1,0:T(8,128)} %param.41) | copy-start | bytes 73732
  111.7 24.7 %copy-start.47 = (f32[8,768]{1,0:T(8,128)S(1)}, f32[8,768]{1,0:T(8,128)}, u32[]{:S(2)}) copy-start(f32[8,768]{1,0:T(8,128)} %param.37) | copy-start | bytes 73732
  111.7 24.7 %copy-start.48 = (f32[8,768]{1,0:T(8,128)S(1)}, f32[8,768]{1,0:T(8,128)}, u32[]{:S(2)}) copy-start(f32[8,768]{1,0:T(8,128)} %param.36) | copy-start | bytes 73732
  111.8 25.3 %copy-start.30 = (f32[24,256]{1,0:T(8,128)S(1)}, f32[24,256]{1,0:T(8,128)}, u32[]{:S(2)}) copy-start(f32[24,256]{1,0:T(8,128)} %param.33) | copy-start | bytes 73732
  111.8 25.3 %copy-start.43 = (f32[24,256]{1,0:T(8,128)S(1)}, f32[24,256]{1,0:T(8,128)}, u32[]{:S(2)}) copy-start(f32[24,256]{1,0:T(8,128)} %param.42) | copy-start | bytes 73732
  111.8 25.3 %copy-start.44 = (f32[24,256]{1,0:T(8,128)S(1)}, f32[24,256]{1,0:T(8,128)}, u32[]{:S(2)}) copy-start(f32[24,256]{1,0:T(8,128)} %param.43) | copy-start | bytes 73732
  111.8 31.3 %copy-start.21 = (f32[8,128]{1,0:T(8,128)S(1)}, f32[8,128]{1,0:T(8,128)}, u32[]{:S(2)}) copy-start(f32[8,128]{1,0:T(8,128)} %copy-done.20) | copy-start | bytes 12292
  111.8 69.2 %copy-start.17 = (f32[8,49]{1,0:T(8,128)S(1)}, f32[8,49]{1,0:T(8,128)}, u32[]{:S(2)}) copy-start(f32[8,49]{1,0:T(8,128)} %table_ref.1) | copy-start | bytes 4708
  111.8 69.2 %copy-start.58 = (f32[8,49]{1,0:T(8,128)S(1)}, f32[8,49]{1,0:T(8,128)}, u32[]{:S(2)}) copy-start(f32[8,49]{1,0:T(8,128)} %param.46) | copy-start | bytes 4708
  111.8 69.2 %copy-start.59 = (f32[8,49]{1,0:T(8,128)S(1)}, f32[8,49]{1,0:T(8,128)}, u32[]{:S(2)}) copy-start(f32[8,49]{1,0:T(8,128)} %param.47) | copy-start | bytes 4708
  111.8 7.3 %collective-permute-start.12 = (bf16[4,8,2688]{2,1,0:T(8,128)(2,1)S(1)}, bf16[4,8,2688]{2,1,0:T(8,128)(2,1)S(1)}, u32[]{:S(2)}, u32[]{:S(2)}) collective-permute-start(bf16[4,8,2688]{2,1,0:T(8,128)(2,1)S(1)} %get-tuple-element.143), channel_id=1, source_target_pairs={{0,8},{1,9},{2,10},{3,11},{4,12},{5,13},{6,14},{7,15},{8,0},{9,1},... | collective-permute-start | bytes 516104 | tf_op jit(solution)/shard_map/ppermute | solution.py:386
  112.4 9.2 %collective-permute-start.13 = (bf16[4,8,2688]{2,1,0:T(8,128)(2,1)S(1)}, bf16[4,8,2688]{2,1,0:T(8,128)(2,1)S(1)}, u32[]{:S(2)}, u32[]{:S(2)}) collective-permute-start(bf16[4,8,2688]{2,1,0:T(8,128)(2,1)S(1)} %get-tuple-element.145), channel_id=1, source_target_pairs={{0,16},{1,17},{2,18},{3,19},{4,20},{5,21},{6,22},{7,23},{8,24},{9,... | collective-permute-start | bytes 516104 | tf_op jit(solution)/shard_map/ppermute | solution.py:386
  114.0 9.2 %collective-permute-start.14 = (bf16[4,8,2688]{2,1,0:T(8,128)(2,1)S(1)}, bf16[4,8,2688]{2,1,0:T(8,128)(2,1)S(1)}, u32[]{:S(2)}, u32[]{:S(2)}) collective-permute-start(bf16[4,8,2688]{2,1,0:T(8,128)(2,1)S(1)} %get-tuple-element.144), channel_id=1, source_target_pairs={{0,24},{1,25},{2,26},{3,27},{4,28},{5,29},{6,30},{7,31},{8,16},{9,... | collective-permute-start | bytes 516104 | tf_op jit(solution)/shard_map/ppermute | solution.py:386
  123.3 6.4 %collective-permute-start.15 = (bf16[1,8,2688]{2,1,0:T(8,128)(2,1)S(1)}, bf16[1,8,2688]{2,1,0:T(8,128)(2,1)S(1)}, u32[]{:S(2)}, u32[]{:S(2)}) collective-permute-start(bf16[1,8,2688]{2,1,0:T(8,128)(2,1)S(1)} %get-tuple-element.148), channel_id=1, source_target_pairs={{0,2},{1,3},{2,0},{3,1},{4,6},{5,7},{6,4},{7,5},{8,10},{9,11},{10,... | collective-permute-start | bytes 129032 | tf_op jit(solution)/shard_map/ppermute | solution.py:386
  125.9 6.4 %collective-permute-start.16 = (bf16[1,8,2688]{2,1,0:T(8,128)(2,1)S(1)}, bf16[1,8,2688]{2,1,0:T(8,128)(2,1)S(1)}, u32[]{:S(2)}, u32[]{:S(2)}) collective-permute-start(bf16[1,8,2688]{2,1,0:T(8,128)(2,1)S(1)} %get-tuple-element.150), channel_id=1, source_target_pairs={{0,4},{1,5},{2,6},{3,7},{4,0},{5,1},{6,2},{7,3},{8,12},{9,13},{10,... | collective-permute-start | bytes 129032 | tf_op jit(solution)/shard_map/ppermute | solution.py:386
  129.7 5.8 %collective-permute-start.17 = (bf16[1,8,2688]{2,1,0:T(8,128)(2,1)S(1)}, bf16[1,8,2688]{2,1,0:T(8,128)(2,1)S(1)}, u32[]{:S(2)}, u32[]{:S(2)}) collective-permute-start(bf16[1,8,2688]{2,1,0:T(8,128)(2,1)S(1)} %get-tuple-element.149), channel_id=1, source_target_pairs={{0,6},{1,7},{2,4},{3,5},{4,2},{5,3},{6,0},{7,1},{8,14},{9,15},{10,... | collective-permute-start | bytes 129032 | tf_op jit(solution)/shard_map/ppermute | solution.py:386
  136.3 55.1 %copy-start.41 = (f32[8,256]{1,0:T(8,128)}, f32[8,256]{1,0:T(8,128)S(1)}, u32[]{:S(2)}) copy-start(f32[8,256]{1,0:T(8,128)S(1)} %get-tuple-element.130) | copy-start | bytes 24580
  136.3 55.1 %copy-start.42 = (f32[8,256]{1,0:T(8,128)}, f32[8,256]{1,0:T(8,128)S(1)}, u32[]{:S(2)}) copy-start(f32[8,256]{1,0:T(8,128)S(1)} %get-tuple-element.131) | copy-start | bytes 24580
  136.4 55.0 %copy-start.50 = (f32[11,8]{0,1:T(8,128)}, f32[11,8]{0,1:T(8,128)S(1)}, u32[]{:S(2)}) copy-start(f32[11,8]{0,1:T(8,128)S(1)} %get-tuple-element.124) | copy-start | bytes 1060
  136.4 55.0 %copy-start.51 = (f32[11,8]{0,1:T(8,128)}, f32[11,8]{0,1:T(8,128)S(1)}, u32[]{:S(2)}) copy-start(f32[11,8]{0,1:T(8,128)S(1)} %get-tuple-element.125) | copy-start | bytes 1060
  137.1 54.3 %copy-start.35 = (f32[8,768]{1,0:T(8,128)}, f32[8,768]{1,0:T(8,128)S(1)}, u32[]{:S(2)}) copy-start(f32[8,768]{1,0:T(8,128)S(1)} %get-tuple-element.128) | copy-start | bytes 73732
  137.1 54.3 %copy-start.36 = (f32[8,768]{1,0:T(8,128)}, f32[8,768]{1,0:T(8,128)S(1)}, u32[]{:S(2)}) copy-start(f32[8,768]{1,0:T(8,128)S(1)} %get-tuple-element.129) | copy-start | bytes 73732
  137.1 54.3 %copy-start.37 = (f32[8,768]{1,0:T(8,128)}, f32[8,768]{1,0:T(8,128)S(1)}, u32[]{:S(2)}) copy-start(f32[8,768]{1,0:T(8,128)S(1)} %get-tuple-element.160) | copy-start | bytes 73732
  137.1 54.3 %copy-start.38 = (f32[8,768]{1,0:T(8,128)}, f32[8,768]{1,0:T(8,128)S(1)}, u32[]{:S(2)}) copy-start(f32[8,768]{1,0:T(8,128)S(1)} %get-tuple-element.161) | copy-start | bytes 73732
  137.7 53.7 %copy-start.33 = (f32[24,256]{1,0:T(8,128)}, f32[24,256]{1,0:T(8,128)S(1)}, u32[]{:S(2)}) copy-start(f32[24,256]{1,0:T(8,128)S(1)} %get-tuple-element.126) | copy-start | bytes 73732
  137.7 53.7 %copy-start.34 = (f32[24,256]{1,0:T(8,128)}, f32[24,256]{1,0:T(8,128)S(1)}, u32[]{:S(2)}) copy-start(f32[24,256]{1,0:T(8,128)S(1)} %get-tuple-element.127) | copy-start | bytes 73732
  181.7 9.7 %copy-start.52 = (f32[8,49]{1,0:T(8,128)}, f32[8,49]{1,0:T(8,128)S(1)}, u32[]{:S(2)}) copy-start(f32[8,49]{1,0:T(8,128)S(1)} %get-tuple-element.122) | copy-start | bytes 4708
  181.7 9.8 %copy-start.53 = (f32[8,49]{1,0:T(8,128)}, f32[8,49]{1,0:T(8,128)S(1)}, u32[]{:S(2)}) copy-start(f32[8,49]{1,0:T(8,128)S(1)} %get-tuple-element.123) | copy-start | bytes 4708
  (19 other events, 21.2 us)

commit v2 on v1

--- a/solution.py
+++ b/solution.py
@@ -139,7 +139,6 @@
     v_ref,
     bias_ref,
     p_ref,
-    x1_ref,
     dmix_ref,
     tacc_ref,
 ):
@@ -357,7 +356,160 @@
     lax.fori_loop(0, 4, block, 0)
 
 
-def call(kernel, out_shape, scratch, *args, smem=0, flops=10**8):
+EARLY = 896
+LATE = 512
+
+
+def pack_kernel(wqkv_ref, wo_ref, wu_ref, wd_ref, vec_ref, out_ref):
+    vrows = vec_ref.shape[0]
+    lane = lax.broadcasted_iota(jnp.int32, (vrows, 128), 1)
+    row = lax.broadcasted_iota(jnp.int32, (vrows, 128), 0)
+    turned = dot_tn(vec_ref[...].astype(BF), (lane == row).astype(BF))
+    top = [wd_ref[8 * b : 8 * b + 8, :] for b in range(3)]
+    top += [wo_ref[:, 0:128], wqkv_ref[:, 0:512]]
+    low = [wu_ref[...], wo_ref[:, 128:256], wqkv_ref[:, 512:768], turned, jnp.zeros((8, 128), F32)]
+    both = jnp.concatenate([jnp.concatenate(top, axis=1), jnp.concatenate(low, axis=1)], axis=0)
+    out_ref[...] = both.astype(BF)
+
+
+def unpack(me, blocks, refs):
+    wqkv_ref, wo_ref, wu_ref, wd_ref, vec_ref, fq, fo, fu, fd, fv = refs
+    for index, block in enumerate(blocks):
+        core, across = divmod(index, 4)
+        for z in range(4):
+            o = me ^ (core | (z << 1) | (across << 3))
+            slab = block[z].astype(F32)
+            at = pl.ds(pl.multiple_of(o * 8, 8), 8)
+            for b in range(3):
+                fd[pl.ds(pl.multiple_of(o * 24 + 8 * b, 8), 8), :] = slab[0:8, 256 * b : 256 * b + 256]
+            fo[at, 0:128] = slab[0:8, 768:896]
+            fo[at, 128:256] = slab[8:16, 768:896]
+            fu[at, :] = slab[8:16, 0:768]
+            fq[at, 0:512] = slab[0:8, 896:1408]
+            fq[at, 512:768] = slab[8:16, 896:1152]
+            fv[at, :] = slab[8:16, 1152:1280]
+    wqkv_ref[...] = fq[...].astype(BF)
+    wo_ref[...] = fo[...].astype(BF)
+    wu_ref[...] = fu[...].astype(BF)
+    wd_ref[...] = fd[...].astype(BF)
+    vec_ref[...] = fv[...].T[0 : vec_ref.shape[0]]
+
+
+def layer_packed(
+    where_ref, x_ref, xb_ref, xa_ref, cot_ref, b0, b1, b2, b3, b4, b5, b6, b7, table_ref, po_ref, pk_ref, *rest
+):
+    weights = rest[-10:]
+    unpack(where_ref[3], (b0, b1, b2, b3, b4, b5, b6, b7), weights)
+    outs, scratch = rest[:16], rest[18:-10]
+    rest[16][...] = weights[0][...]
+    rest[17][...] = weights[4][...]
+    layer_kernel(
+        where_ref, x_ref, xb_ref, xa_ref, cot_ref, *weights[:5], table_ref, po_ref, pk_ref, *outs, *scratch
+    )
+
+
+def frame_slot(me, o):
+    m = me ^ o
+    return (m & 1) * 16 + (m >> 3) * 4 + ((m >> 1) & 3)
+
+
+def early_kernel(where_ref, act_ref, dy_ref, a2_ref, dz_ref, mixed_ref, da_ref, out_ref, fd, fu, fo):
+    fd[...] = dot_tn(act_ref[...], dy_ref[...])
+    fu[...] = dot_tn(a2_ref[...], dz_ref[...])
+    fo[...] = dot_tn(mixed_ref[...], da_ref[...])
+    me = where_ref[3]
+    for o in range(32):
+        at = slice(8 * o, 8 * o + 8)
+        top = [fd[24 * o + 8 * b : 24 * o + 8 * b + 8, :] for b in range(3)] + [fo[at, 0:128]]
+        low = [fu[at, :], fo[at, 128:256]]
+        both = jnp.concatenate([jnp.concatenate(top, axis=1), jnp.concatenate(low, axis=1)], axis=0)
+        out_ref[frame_slot(me, o)] = both.astype(BF)
+
+
+def late_kernel(where_ref, *refs):
+    own, fa, fb, dq, dx1, x, wqkv, vec, po, a1, sums, zsum, tgrad = refs[:13]
+    tok_ref, out_ref, dqkv, sums2, fq, fv = refs[13:]
+    finish_kernel(own, fa, fb, dq, dx1, x, wqkv, vec, po, tok_ref, dqkv, sums2)
+    fq[...] = dot_tn(a1[...], dqkv[...])
+    lines = jnp.concatenate(
+        [sums[...] + sums2[...]]
+        + [zsum[:, 256 * i : 256 * i + 256] for i in range(3)]
+        + [jnp.zeros((117, 256), F32)],
+        axis=0,
+    )
+    fv[...] = lines.T
+    table = tgrad[...]
+    me = where_ref[3]
+    for o in range(32):
+        at = slice(8 * o, 8 * o + 8)
+        low = jnp.concatenate([fq[at, 512:768], fv[at, :], table], axis=1)
+        out_ref[frame_slot(me, o)] = jnp.concatenate([fq[at, 0:512], low], axis=0).astype(BF)
+
+
+def adam_kernel(*refs):
+    w, first, second = refs[4:10], refs[10:16], refs[16:22]
+    outs = refs[22:]
+    total = refs[0][...] + sum(ref[...].astype(F32) for ref in refs[1:4])
+    early, late = total[:, :EARLY], total[:, EARLY:]
+    vrows = w[4].shape[0]
+    grads = [
+        jnp.concatenate([late[0:8], late[8:16, 0:256]], axis=1),
+        jnp.concatenate([early[0:8, 768:896], early[8:16, 768:896]], axis=1),
+        early[8:16, 0:768],
+        jnp.concatenate([early[0:8, 256 * b : 256 * b + 256] for b in range(3)], axis=0),
+        late[8:16, 256:384].T[0:vrows],
+        lax.dot_general(
+            late[8:16, 384:512],
+            table_slots(),
+            (((1,), (1,)), ((), ())),
+            precision=lax.Precision.HIGHEST,
+            preferred_element_type=F32,
+        ),
+    ]
+    row = lax.broadcasted_iota(jnp.int32, (16, 128), 0)
+    lane = lax.broadcasted_iota(jnp.int32, (16, 128), 1)
+    norms = jnp.zeros((16, 128), F32)
+    for i in range(6):
+        new_first, new_second, update = adam_parts(w[i][...], grads[i], first[i][...], second[i][...])
+        outs[3 * i][...] = new_first
+        outs[3 * i + 1][...] = new_second
+        outs[3 * i + 2][...] = update
+        for col, v in ((0, w[i][...]), (1, update)):
+            if i == 4:
+                per_row = jnp.sum(v * v, axis=1, keepdims=True)
+                tall = jnp.concatenate([jnp.zeros((4, 1), F32), per_row, jnp.zeros((12 - vrows, 1), F32)], axis=0)
+                norms = jnp.where((lane == col) & (row >= 4) & (row < 4 + vrows), tall, norms)
+            else:
+                total = jnp.sum(v * v)
+                at = i if i < 4 else 4 + vrows
+                norms = jnp.where((lane == col) & (row == at), total, norms)
+    outs[18][...] = norms
+
+
+def step_kernel(mine_ref, a_ref, b_ref, c_ref, d_ref, *refs):
+    w, update, outs = refs[0:6], refs[6:12], refs[12:]
+    vrows = w[4].shape[0]
+    total = a_ref[...] + b_ref[...] + c_ref[...] + d_ref[...]
+    row = lax.broadcasted_iota(jnp.int32, (16, 128), 0)
+    norms = jnp.sqrt(jnp.where(row == 4 + vrows, mine_ref[...], total))
+    turned = norms.T
+    outs[6][...] = turned[0:1]
+    outs[7][...] = turned[1:2]
+    rate = LEARN_RATE * norms[:, 0:1] / (norms[:, 1:2] + RATIO_EPS)
+    for i in range(6):
+        if i == 4:
+            r = rate[4 : 4 + vrows]
+        else:
+            r = rate[i : i + 1] if i < 4 else rate[4 + vrows : 5 + vrows]
+        outs[i][...] = w[i][...] - r * update[i][...]
+
+
+def stack_kernel(*refs):
+    for i, ref in enumerate(refs[:-1]):
+        refs[-1][i] = ref[...]
+
+
+def call(kernel, out_shape, scratch, *args, smem=0, flops=10**8, vmem=16):
     vm = pl.BlockSpec(memory_space=pltpu.VMEM)
     specs = [pl.BlockSpec(memory_space=pltpu.SMEM)] * smem + [vm] * (len(args) - smem)
     return pl.pallas_call(
@@ -366,7 +518,7 @@
         in_specs=specs,
         out_specs=jax.tree.map(lambda _: vm, out_shape),
         scratch_shapes=scratch,
-        compiler_params=pltpu.CompilerParams(vmem_limit_bytes=48 * 2**20),
+        compiler_params=pltpu.CompilerParams(vmem_limit_bytes=vmem * 2**20),
         cost_estimate=pl.CostEstimate(flops=flops, bytes_accessed=10**6, transcendentals=0),
     )(*args)
 
@@ -404,11 +556,7 @@
 
 def scatter_sum(grads, groups, count):
     for lo, bits in reversed(groups):
-        low = grads.astype(BF).reshape((1 << bits, -1) + grads.shape[1:])
-        total = grads.reshape(low.shape)[0].astype(F32)
-        for d in range(1, 1 << bits):
-            total = total + swap(low[d], d << lo, count).astype(F32)
-        grads = total
+        grads = add_stage(grads, lo, bits, count)
     return grads[0]
 
 
@@ -431,6 +579,135 @@
             jnp.sum(rowwise * rowwise, axis=1),
         ]
     )
+
+
+def layer_outputs():
+    return (
+        sds((16, 48, 256)),
+        sds((768, 768)),
+        sds((768, 256)),
+        sds((768, 768)),
+        sds((768, 256)),
+        sds((768, 256)),
+        sds((768, 256)),
+        sds((768, 256)),
+        sds((768, 256)),
+        sds((768, 256), F32),
+        sds((768, 512), F32),
+        sds((CLS * RIM, 512)),
+        sds((CLS * RIM, 512)),
+        sds((HEADS, KN), F32),
+        sds((8, 256), F32),
+        sds((1, 768), F32),
+    )
+
+
+def layer_scratch():
+    return [
+        pltpu.VMEM((768, 256), F32),
+        pltpu.VMEM((768, 256), BF),
+        pltpu.VMEM((CLS * KN, 256), BF),
+        pltpu.VMEM((CLS * KN, 256), BF),
+        pltpu.VMEM((KN, 384), F32),
+        pltpu.VMEM((CLS * KN, 384), F32),
+        pltpu.VMEM((768, 256), BF),
+        pltpu.VMEM((KN, 384), F32),
+    ]
+
+
+def packed_step(tokens_in, cotangent, map_sizes, weights, firsts, seconds):
+    count = 32
+    me = lax.axis_index(AXES)
+    band_index = lax.axis_index("band")
+    vrows = weights[4].shape[0]
+    up = [(i, i + 1) for i in range(7)]
+    down = [(i + 1, i) for i in range(7)]
+    x_before = lax.ppermute(tokens_in[-12:], "band", up)
+    x_after = lax.ppermute(tokens_in[:12], "band", down)
+
+    slab = call(pack_kernel, sds((16, EARLY + LATE)), [], *weights[:5])
+    column = call(
+        stack_kernel,
+        sds((4, 16, EARLY + LATE)),
+        [],
+        slab,
+        *[swap(slab, d << 1, count) for d in (1, 2, 3)],
+    )
+    blocks = [column] + [swap(column, d << 3, count) for d in (1, 2, 3)]
+    blocks += [swap(block, 1, count) for block in blocks]
+
+    po = jnp.asarray(order_own(), BF)
+    pk = jnp.asarray(order_keys(), BF)
+    place = jnp.stack([band_index, map_sizes[0, 0], map_sizes[0, 1], me]).astype(jnp.int32)
+    matrices = [(256, 768), (256, 256), (256, 768), (768, 256)]
+    (
+        layer_out, act, dy, dz, a2, mixed, da, a1, dq, dx1, own, rim_a, rim_b, tgrad, sums, zsum, big_qkv, vec,
+    ) = call(
+        layer_packed,
+        layer_outputs() + (sds((256, 768)), sds((vrows, 256), F32)),
+        layer_scratch()
+        + [pltpu.VMEM(m, BF) for m in matrices]
+        + [pltpu.VMEM((vrows, 256), F32)]
+        + [pltpu.VMEM(m, F32) for m in matrices]
+        + [pltpu.VMEM((256, 128), F32)],
+        place, tokens_in, x_before, x_after, cotangent, *blocks, weights[5], po, pk,
+        smem=1, flops=6 * 10**9, vmem=24,
+    )
+    from_prev = lax.ppermute(rim_a, "band", up)
+    from_next = lax.ppermute(rim_b, "band", down)
+    early = call(
+        early_kernel,
+        sds((count, 16, EARLY)),
+        [pltpu.VMEM((768, 256), F32), pltpu.VMEM((256, 768), F32), pltpu.VMEM((256, 256), F32)],
+        place, act, dy, a2, dz, mixed, da,
+        smem=1, flops=10**9,
+    )
+    tokens_grad, late = call(
+        late_kernel,
+        (sds((16, 48, 256)), sds((count, 16, LATE))),
+        [
+            pltpu.VMEM((768, 768), BF),
+            pltpu.VMEM((8, 256), F32),
+            pltpu.VMEM((256, 768), F32),
+            pltpu.VMEM((256, 128), F32),
+        ],
+        place, own, from_prev, from_next, dq, dx1, tokens_in, big_qkv, vec, po, a1, sums, zsum, tgrad,
+        smem=1, flops=10**9,
+    )
+    early = add_stage(add_stage(early, 0, 1, count), 3, 2, count)
+    late = add_stage(add_stage(late, 0, 1, count), 3, 2, count)
+    grads = jnp.concatenate([early, late], axis=-1)
+    low = grads.astype(BF)
+    parts = [grads[0]] + [swap(low[d], d << 1, count) for d in (1, 2, 3)]
+
+    shapes = [sds(w.shape, F32) for w in weights]
+    moments = call(
+        adam_kernel,
+        tuple(shape for shape in shapes for _ in range(3)) + (sds((16, 128), F32),),
+        [],
+        *parts, *weights, *firsts, *seconds,
+    )
+    mine = moments[18]
+    squares = mine + swap(mine, 1, count)
+    squares = squares + swap(squares, 8, count) + swap(squares, 16, count) + swap(squares, 24, count)
+    news = call(
+        step_kernel,
+        tuple(shapes) + (sds((1, 16), F32),) * 2,
+        [],
+        mine, squares, *[swap(squares, d << 1, count) for d in (1, 2, 3)], *weights, *moments[2:18:3],
+    )
+    results = [layer_out, tokens_grad]
+    for i in range(6):
+        results += [moments[3 * i], moments[3 * i + 1], news[i]]
+    return tuple(results) + (news[6].reshape(16), news[7].reshape(16))
+
+
+def add_stage(grads, lo, bits, count):
+    low = grads.astype(BF).reshape((1 << bits, -1) + grads.shape[1:])
+    total = grads.reshape(low.shape)[0].astype(F32)
+    for d in range(1, 1 << bits):
+        total = total + swap(low[d], d << lo, count).astype(F32)
+    return total
 
 
 def per_device(
@@ -458,6 +735,13 @@
     first_table,
     second_table,
 ):
+    if w_qkv.shape[0] == 8 and (maps, band) == (4, 8):
+        return packed_step(
+            tokens_in, cotangent, map_sizes,
+            (w_qkv, w_out, w_up, w_down, vectors, pos_table),
+            (first_qkv, first_out, first_up, first_down, first_vectors, first_table),
+            (second_qkv, second_out, second_up, second_down, second_vectors, second_table),
+        )
     count = maps * band
     rows = w_qkv.shape[0]
     vrows = vectors.shape[0]
@@ -512,35 +796,8 @@
         zsum,
     ) = call(
         layer_kernel,
-        (
-            sds((16, 48, 256)),
-            sds((768, 768)),
-            sds((768, 256)),
-            sds((768, 768)),
-            sds((768, 256)),
-            sds((768, 256)),
-            sds((768, 256)),
-            sds((768, 256)),
-            sds((768, 256)),
-            sds((768, 256), F32),
-            sds((768, 512), F32),
-            sds((CLS * RIM, 512)),
-            sds((CLS * RIM, 512)),
-            sds((HEADS, KN), F32),
-            sds((8, 256), F32),
-            sds((1, 768), F32),
-        ),
-        [
-            pltpu.VMEM((768, 256), F32),
-            pltpu.VMEM((768, 256), BF),
-            pltpu.VMEM((CLS * KN, 256), BF),
-            pltpu.VMEM((CLS * KN, 256), BF),
-            pltpu.VMEM((KN, 384), F32),
-            pltpu.VMEM((CLS * KN, 384), F32),
-            pltpu.VMEM((768, 256), F32),
-            pltpu.VMEM((768, 256), BF),
-            pltpu.VMEM((KN, 384), F32),
-        ],
+        layer_outputs(),
+        layer_scratch(),
         place,
         tokens_in,
         x_before,

time: 193 us -> 132 us (0.68)
  blocking collectives: 37.2 us -> 0 us
  local copies, waits for them, and re-layouts: 39.2 us -> 24.8 us
  other arithmetic: 15.9 us -> 2.74 us
  starting transfers between devices: 33.7 us -> 46 us
  matrix products: 5.28 us -> 0 us
  between operations: 6.12 us -> 1.26 us
    psum x1 -> x0, blocking collectives: 37.2 us -> none  [per_device(): table_total = lax.psum(table_grad, AXES)[:, lanes]]
    ppermute x14 -> x28, starting transfers between devices: 25.8 us -> 38.6 us  [swap(): return lax.ppermute(block, AXES, [(k, k ^ mask) for k in range(count)])]
    gather x6 -> x0, local copies, waits for them, and re-layouts: 7.62 us -> none  [the longest x2 3.63 us: per_device(): whole = jnp.take(block, order, axis=0).reshape(256, -1)]
    concatenate x6 -> x0, local copies, waits for them, and re-layouts: 7.04 us -> none  [the longest x2 5.35 us: squares_of(): jnp.concatenate([jnp.stack([jnp.sum(matrix * matrix) for matrix in matric...]
    unnamed x137 -> x108, local copies, waits for them, and re-layouts: 16.4 us -> 22.3 us
    dot_general x4 -> x0, matrix products: 5.28 us -> none  [dot_tn(): lax.dot_general(a, b, (((0,), (0,)), ((), ())), preferred_element_type=F32)]
    slice x13 -> x6, local copies, waits for them, and re-layouts: 6.98 us -> 2.54 us  [the longest x1 1.09 us: packed_step(): x_after = lax.ppermute(tokens_in[:12], 'band', down)]
    sub x6 -> x0, other arithmetic: 3.74 us -> none  [the longest x1 0.63 us: per_device(): next_down = w_down - LEARN_RATE * ratios[3] * part_down[2]]
  transfers between devices with their start and end apart: 18 -> 32, of which waited for: 8 -> 13; matrix products, arithmetic and copies ran while one was open for 13% -> 7% of each run, Pallas kernels for 0% -> 5%
where the time goes in v2:
time: 132 us; the launch traced here: 131 us
  starting transfers between devices  46 us (35%)
  Pallas kernels  35.8 us (27%)
  local copies, waits for them, and re-layouts  24.8 us (19%)
  waiting for transfers between devices  20.3 us (15%)
  other arithmetic  2.74 us (2%)
    ppermute x28, starting transfers between devices, swap(): return lax.ppermute(block, AXES, [(k, k ^ mask) for k in range(count)])  38.6 us
    pallas_call x7, Pallas kernels, call(): pl.pallas_call(kernel, out_shape=out_shape, in_specs=specs, out_specs=jax...  35.8 us
    unnamed x108, local copies, waits for them, and re-layouts  22.3 us
    ppermute x28, waiting for transfers between devices, swap(): return lax.ppermute(block, AXES, [(k, k ^ mask) for k in range(count)])  20.3 us
  transfers between devices with their start and end apart: 32, of which 13 were waited for; matrix products, arithmetic and copies ran while one was open for 7% of the time, Pallas kernels for 5%

profile of v2, /device:TPU:0, one launch (start us, length us, event | category | flops | bytes accessed | tf_op | source)
XLA Modules:
  0.0 130.9 jit_solution(9344311275439459204)
XLA Ops:
  0.7 0.8 copy.45.vec_ref.refs_8_.refs_4_
  1.5 0.7 copy-done.18
  2.2 0.7 copy-done.20
  3.0 0.7 copy-done.22
  3.7 0.7 copy-done.28
  4.6 3.0 %collective-permute-start.2 = (bf16[16,1408]{1,0:T(8,128)(2,1)S(1)}, bf16[16,1408]{1,0:T(8,128)(2,1)S(1)}, u32[]{:S(2)}, u32[]{:S(2)}) collective-permute-start(bf16[16,1408]{1,0:T(8,128)(2,1)S(1)} %shard_map.390.refs_0_), channel_id=1, source_target_pairs={{0,2},{1,3},{2,0},{3,1},{4,6},{5,7},{6,4},{7,5},{8,10},{9,11},{10,... | collective-permute-start | bytes 135176 | tf_op jit(solution)/shard_map/ppermute | solution.py:538
  7.6 2.6 %collective-permute-start.3 = (bf16[16,1408]{1,0:T(8,128)(2,1)S(1)}, bf16[16,1408]{1,0:T(8,128)(2,1)S(1)}, u32[]{:S(2)}, u32[]{:S(2)}) collective-permute-start(bf16[16,1408]{1,0:T(8,128)(2,1)S(1)} %shard_map.390.refs_0_), channel_id=1, source_target_pairs={{0,4},{1,5},{2,6},{3,7},{4,0},{5,1},{6,2},{7,3},{8,12},{9,13},{10,... | collective-permute-start | bytes 135176 | tf_op jit(solution)/shard_map/ppermute | solution.py:538
  10.2 3.2 %collective-permute-done.3.refs_2_ = bf16[16,1408]{1,0:T(8,128)(2,1)S(1)} collective-permute-done((bf16[16,1408]{1,0:T(8,128)(2,1)S(1)}, bf16[16,1408]{1,0:T(8,128)(2,1)S(1)}, u32[]{:S(2)}, u32[]{:S(2)}) %collective-permute-start.3) | collective-permute-done | bytes 45088 | tf_op jit(solution)/shard_map/ppermute | solution.py:538
  13.4 2.6 %collective-permute-done.4.refs_3_ = bf16[16,1408]{1,0:T(8,128)(2,1)S(1)} collective-permute-done((bf16[16,1408]{1,0:T(8,128)(2,1)S(1)}, bf16[16,1408]{1,0:T(8,128)(2,1)S(1)}, u32[]{:S(2)}, u32[]{:S(2)}) %collective-permute-start.4) | collective-permute-done | bytes 45088 | tf_op jit(solution)/shard_map/ppermute | solution.py:538
  16.1 1.6 %collective-permute-start.6 = (bf16[4,16,1408]{2,1,0:T(8,128)(2,1)S(1)}, bf16[4,16,1408]{2,1,0:T(8,128)(2,1)S(1)}, u32[]{:S(2)}, u32[]{:S(2)}) collective-permute-start(bf16[4,16,1408]{2,1,0:T(8,128)(2,1)S(1)} %shard_map.391.b0), channel_id=1, source_target_pairs={{0,16},{1,17},{2,18},{3,19},{4,20},{5,21},{6,22},{7,23},{8,24},{9,... | collective-permute-start | bytes 540680 | tf_op jit(solution)/shard_map/ppermute | solution.py:538
  17.7 1.4 %collective-permute-start.7 = (bf16[4,16,1408]{2,1,0:T(8,128)(2,1)S(1)}, bf16[4,16,1408]{2,1,0:T(8,128)(2,1)S(1)}, u32[]{:S(2)}, u32[]{:S(2)}) collective-permute-start(bf16[4,16,1408]{2,1,0:T(8,128)(2,1)S(1)} %shard_map.391.b0), channel_id=1, source_target_pairs={{0,24},{1,25},{2,26},{3,27},{4,28},{5,29},{6,30},{7,31},{8,16},{9,... | collective-permute-start | bytes 540680 | tf_op jit(solution)/shard_map/ppermute | solution.py:538
  19.6 1.1 fusion.10
  20.7 2.4 %collective-permute-start = (bf16[12,48,256]{2,1,0:T(8,128)(2,1)S(1)}, bf16[12,48,256]{2,1,0:T(8,128)(2,1)S(1)}, u32[]{:S(2)}, u32[]{:S(2)}) collective-permute-start(bf16[12,48,256]{2,1,0:T(8,128)(2,1)S(1)} %get-tuple-element.146), channel_id=1, source_target_pairs={{0,1},{1,2},{2,3},{3,4},{4,5},{5,6},{6,7},{8,9},{9,10},{10,11},{11... | collective-permute-start | bytes 884744 | tf_op jit(solution)/shard_map/ppermute | solution.py:625
  23.7 1.3 collective-permute-start.1
  25.0 1.2 collective-permute-start.10
  29.3 1.4 %pad_add_fusion.where_ref = s32[4]{0:T(128)S(1)} fusion(s32[1]{0:T(128)} %bitcast.3, s32[1]{0:T(128)} %bitcast.2, s32[1]{0:T(128)} %bitcast.1, s32[1]{0:T(128)} %bitcast), kind=kLoop, calls=%fused_computation.18 | loop fusion | flops 12 | bytes 32 | tf_op jit(solution)/shard_map/stack | solution.py:641
  30.8 0.9 copy-done.44
  31.7 0.9 copy-done.46
  32.6 0.9 copy-done.48
  33.6 1.0 copy-done.49
  34.6 27.7 %shard_map.392 = (bf16[16,48,256]{2,1,0:T(8,128)(2,1)}, bf16[768,768]{1,0:T(8,128)(2,1)S(1)}, bf16[768,256]{1,0:T(8,128)(2,1)S(1)}, bf16[768,768]{1,0:T(8,128)(2...) custom-call(s32[4]{0:T(128)S(1)} %pad_add_fusion.where_ref, ...), custom_call_target="tpu_custom_call" | custom-call | flops 6000000000 | bytes 1000000 | tf_op jit(solution)/shard_map/pallas_call | solution.py:515
  62.4 2.4 %collective-permute-start.12 = (bf16[640,512]{1,0:T(8,128)(2,1)}, bf16[640,512]{1,0:T(8,128)(2,1)S(1)}, u32[]{:S(2)}, u32[]{:S(2)}) collective-permute-start(bf16[640,512]{1,0:T(8,128)(2,1)} %get-tuple-element.71), channel_id=1, source_target_pairs={{0,1},{1,2},{2,3},{3,4},{4,5},{5,6},{6,7},{8,9},{9,10},{10,11},{11... | collective-permute-start | bytes 1966088 | tf_op jit(solution)/shard_map/ppermute | solution.py:656
  64.8 1.3 collective-permute-start.13
  66.1 1.5 %shard_map.394 = bf16[32,16,896]{2,1,0:T(8,128)(2,1)S(1)} custom-call(s32[4]{0:T(128)S(1)} %pad_add_fusion.where_ref, bf16[768,768]{1,0:T(8,128)(2,1)S(1)} %get-tuple-element.82.act_ref, bf16[768,256]{1,0:T(8,128)(2,1)S(1)} %get-tuple-element.83.dy_ref, bf16[768,256]{1,0:T(8,128)(2,1)S(1)} %get-tuple-element.84.a2_ref, ...), custom_call_target="tpu_custom_call" | custom-call | flops 1000000000 | bytes 1000000 | tf_op jit(solution)/shard_map/pallas_call | solution.py:515
  67.7 0.8 slice.93
  68.5 1.1 collective-permute-start.14
  69.7 0.8 copy.47.refs_14_
  70.4 1.4 %copy.48.refs_20_ = f32[11,8]{1,0:T(8,128)} copy(f32[11,8]{0,1:T(8,128)} %param.41) | data formatting | bytes 704 | tf_op args[18]
  71.8 1.1 copy-done.2
  72.9 1.0 copy-done.4
  73.9 1.0 copy-done.6
  74.9 1.0 copy-done.8
  75.9 0.9 copy-done.10
  76.8 0.7 copy-done.25
  77.5 0.7 copy-done.31
  78.9 0.7 copy-done.39
  79.6 0.7 copy-done.41
  80.3 4.7 %shard_map.393 = (bf16[16,48,256]{2,1,0:T(8,128)(2,1)}, bf16[32,16,512]{2,1,0:T(8,128)(2,1)S(1)}) custom-call(s32[4]{0:T(128)S(1)} %copy-done.33, f32[768,512]{1,0:T(8,128)S(1)} %get-tuple-element.70.refs_0_, bf16[640,512]{1,0:T(8,128)(2,1)S(1)} %collective-permute-done.12.refs_1_, bf16[640,512]{1,0:T(8,128)(2,1)} %collective-permute-done.13.refs_2_, ...), custom_call_target="tpu_custom_call" | custom-call | flops 1000000000 | bytes 1000000 | tf_op jit(solution)/shard_map/pallas_call | solution.py:515
  85.0 5.6 %collective-permute-start.18 = (bf16[16,16,512]{2,1,0:T(8,128)(2,1)S(1)}, bf16[16,16,512]{2,1,0:T(8,128)(2,1)S(1)}, u32[]{:S(2)}, u32[]{:S(2)}) collective-permute-start(bf16[16,16,512]{2,1,0:T(8,128)(2,1)S(1)} %slice.83), channel_id=1, source_target_pairs={{0,1},{1,0},{2,3},{3,2},{4,5},{5,4},{6,7},{7,6},{8,9},{9,8},{10,11... | collective-permute-start | bytes 786440 | tf_op jit(solution)/shard_map/ppermute | solution.py:538
  90.6 1.1 fusion.8
  91.8 1.6 %collective-permute-start.15 = (bf16[4,16,896]{2,1,0:T(8,128)(2,1)S(1)}, bf16[4,16,896]{2,1,0:T(8,128)(2,1)S(1)}, u32[]{:S(2)}, u32[]{:S(2)}) collective-permute-start(bf16[4,16,896]{2,1,0:T(8,128)(2,1)S(1)} %get-tuple-element.142), channel_id=1, source_target_pairs={{0,8},{1,9},{2,10},{3,11},{4,12},{5,13},{6,14},{7,15},{8,0},{9,1},... | collective-permute-start | bytes 344072 | tf_op jit(solution)/shard_map/ppermute | solution.py:538
  93.3 1.8 %collective-permute-start.16 = (bf16[4,16,896]{2,1,0:T(8,128)(2,1)S(1)}, bf16[4,16,896]{2,1,0:T(8,128)(2,1)S(1)}, u32[]{:S(2)}, u32[]{:S(2)}) collective-permute-start(bf16[4,16,896]{2,1,0:T(8,128)(2,1)S(1)} %get-tuple-element.144), channel_id=1, source_target_pairs={{0,16},{1,17},{2,18},{3,19},{4,20},{5,21},{6,22},{7,23},{8,24},{9,... | collective-permute-start | bytes 344072 | tf_op jit(solution)/shard_map/ppermute | solution.py:538
  95.5 1.6 %collective-permute-start.19 = (bf16[4,16,512]{2,1,0:T(8,128)(2,1)S(1)}, bf16[4,16,512]{2,1,0:T(8,128)(2,1)S(1)}, u32[]{:S(2)}, u32[]{:S(2)}) collective-permute-start(bf16[4,16,512]{2,1,0:T(8,128)(2,1)S(1)} %get-tuple-element.147), channel_id=1, source_target_pairs={{0,8},{1,9},{2,10},{3,11},{4,12},{5,13},{6,14},{7,15},{8,0},{9,1},... | collective-permute-start | bytes 196616 | tf_op jit(solution)/shard_map/ppermute | solution.py:538
  97.0 1.8 %collective-permute-start.20 = (bf16[4,16,512]{2,1,0:T(8,128)(2,1)S(1)}, bf16[4,16,512]{2,1,0:T(8,128)(2,1)S(1)}, u32[]{:S(2)}, u32[]{:S(2)}) collective-permute-start(bf16[4,16,512]{2,1,0:T(8,128)(2,1)S(1)} %get-tuple-element.149), channel_id=1, source_target_pairs={{0,16},{1,17},{2,18},{3,19},{4,20},{5,21},{6,22},{7,23},{8,24},{9,... | collective-permute-start | bytes 196616 | tf_op jit(solution)/shard_map/ppermute | solution.py:538
  98.8 1.8 %collective-permute-start.21 = (bf16[4,16,512]{2,1,0:T(8,128)(2,1)S(1)}, bf16[4,16,512]{2,1,0:T(8,128)(2,1)S(1)}, u32[]{:S(2)}, u32[]{:S(2)}) collective-permute-start(bf16[4,16,512]{2,1,0:T(8,128)(2,1)S(1)} %get-tuple-element.148), channel_id=1, source_target_pairs={{0,24},{1,25},{2,26},{3,27},{4,28},{5,29},{6,30},{7,31},{8,16},{9,... | collective-permute-start | bytes 196616 | tf_op jit(solution)/shard_map/ppermute | solution.py:538
  100.6 1.5 %collective-permute-done.16 = bf16[4,16,896]{2,1,0:T(8,128)(2,1)S(1)} collective-permute-done((bf16[4,16,896]{2,1,0:T(8,128)(2,1)S(1)}, bf16[4,16,896]{2,1,0:T(8,128)(2,1)S(1)}, u32[]{:S(2)}, u32[]{:S(2)}) %collective-permute-start.16) | collective-permute-done | bytes 114720 | tf_op jit(solution)/shard_map/ppermute | solution.py:538
  102.7 1.2 collective-permute-done.21
  104.2 1.4 %collective-permute-start.23 = (bf16[16,1408]{1,0:T(8,128)(2,1)S(1)}, bf16[16,1408]{1,0:T(8,128)(2,1)S(1)}, u32[]{:S(2)}, u32[]{:S(2)}) collective-permute-start(bf16[16,1408]{1,0:T(8,128)(2,1)S(1)} %get-tuple-element.151), channel_id=1, source_target_pairs={{0,4},{1,5},{2,6},{3,7},{4,0},{5,1},{6,2},{7,3},{8,12},{9,13},{10,... | collective-permute-start | bytes 135176 | tf_op jit(solution)/shard_map/ppermute | solution.py:538
  105.5 3.0 %collective-permute-start.24 = (bf16[16,1408]{1,0:T(8,128)(2,1)S(1)}, bf16[16,1408]{1,0:T(8,128)(2,1)S(1)}, u32[]{:S(2)}, u32[]{:S(2)}) collective-permute-start(bf16[16,1408]{1,0:T(8,128)(2,1)S(1)} %get-tuple-element.150), channel_id=1, source_target_pairs={{0,6},{1,7},{2,4},{3,5},{4,2},{5,3},{6,0},{7,1},{8,14},{9,15},{10,... | collective-permute-start | bytes 135176 | tf_op jit(solution)/shard_map/ppermute | solution.py:538
  108.5 0.8 collective-permute-done.23.refs_2_
  109.3 2.1 %collective-permute-done.24.refs_3_ = bf16[16,1408]{1,0:T(8,128)(2,1)S(1)} collective-permute-done((bf16[16,1408]{1,0:T(8,128)(2,1)S(1)}, bf16[16,1408]{1,0:T(8,128)(2,1)S(1)}, u32[]{:S(2)}, u32[]{:S(2)}) %collective-permute-start.24) | collective-permute-done | bytes 45088 | tf_op jit(solution)/shard_map/ppermute | solution.py:538
  111.6 0.9 shard_map.395
  112.5 1.2 collective-permute-done.25
  113.6 1.0 collective-permute-start.26
  114.7 1.3 collective-permute-start.27
  115.9 1.2 collective-permute-start.28
  117.3 1.0 collective-permute-done.27
  118.3 2.2 %collective-permute-done.28 = f32[16,128]{1,0:T(8,128)S(1)} collective-permute-done((f32[16,128]{1,0:T(8,128)S(1)}, f32[16,128]{1,0:T(8,128)S(1)}, u32[]{:S(2)}, u32[]{:S(2)}) %collective-permute-start.28) | collective-permute-done | bytes 8224 | tf_op jit(solution)/shard_map/ppermute | solution.py:538
  121.2 2.9 %collective-permute-start.30 = (f32[16,128]{1,0:T(8,128)S(1)}, f32[16,128]{1,0:T(8,128)S(1)}, u32[]{:S(2)}, u32[]{:S(2)}) collective-permute-start(f32[16,128]{1,0:T(8,128)S(1)} %add_add_fusion.a_ref), channel_id=1, source_target_pairs={{0,4},{1,5},{2,6},{3,7},{4,0},{5,1},{6,2},{7,3},{8,12},{9,13},{10,... | collective-permute-start | bytes 24584 | tf_op jit(solution)/shard_map/ppermute | solution.py:538
  124.0 0.9 collective-permute-start.31
  124.9 0.7 copy.50
  126.2 3.2 %collective-permute-done.31.d_ref = f32[16,128]{1,0:T(8,128)S(1)} collective-permute-done((f32[16,128]{1,0:T(8,128)S(1)}, f32[16,128]{1,0:T(8,128)S(1)}, u32[]{:S(2)}, u32[]{:S(2)}) %collective-permute-start.31) | collective-permute-done | bytes 8224 | tf_op jit(solution)/shard_map/ppermute | solution.py:538
  129.5 0.8 shard_map.396
  130.2 0.7 copy.52
  (131 shorter events, 7.8 us)
Async XLA Ops:
  0.7 30.1 %copy-start.9 = (bf16[192,192]{1,0:T(8,128)(2,1)S(1)}, bf16[192,192]{1,0:T(8,128)(2,1)}, u32[]{:S(2)}) copy-start(bf16[192,192]{1,0:T(8,128)(2,1)} %constant.14.clone.po_ref.refs_8_) | copy-start | bytes 221188
  0.7 30.1 %copy-start = (bf16[16,48,256]{2,1,0:T(8,128)(2,1)S(1)}, bf16[16,48,256]{2,1,0:T(8,128)(2,1)}, u32[]{:S(2)}) copy-start(bf16[16,48,256]{2,1,0:T(8,128)(2,1)} %refs_5_.3) | copy-start | bytes 1179652
  4.4 24.3 %copy-start.50 = (s32[1,2]{1,0:T(1,128)S(1)}, s32[1,2]{1,0:T(1,128)}, u32[]{:S(2)}) copy-start(s32[1,2]{1,0:T(1,128)} %param.25) | copy-start | bytes 28
  4.4 26.4 %copy-start.36 = (f32[8,49]{1,0:T(8,128)S(1)}, f32[8,49]{1,0:T(8,128)}, u32[]{:S(2)}) copy-start(f32[8,49]{1,0:T(8,128)} %refs_5_.5) | copy-start | bytes 4708
  4.4 26.4 %copy-start.42 = (bf16[16,48,256]{2,1,0:T(8,128)(2,1)S(1)}, bf16[16,48,256]{2,1,0:T(8,128)(2,1)}, u32[]{:S(2)}) copy-start(bf16[16,48,256]{2,1,0:T(8,128)(2,1)} %cot_ref.1) | copy-start | bytes 1179652
  4.6 5.6 %collective-permute-start.2 = (bf16[16,1408]{1,0:T(8,128)(2,1)S(1)}, bf16[16,1408]{1,0:T(8,128)(2,1)S(1)}, u32[]{:S(2)}, u32[]{:S(2)}) collective-permute-start(bf16[16,1408]{1,0:T(8,128)(2,1)S(1)} %shard_map.390.refs_0_), channel_id=1, source_target_pairs={{0,2},{1,3},{2,0},{3,1},{4,6},{5,7},{6,4},{7,5},{8,10},{9,11},{10,... | collective-permute-start | bytes 135176 | tf_op jit(solution)/shard_map/ppermute | solution.py:538
  7.6 5.8 %collective-permute-start.3 = (bf16[16,1408]{1,0:T(8,128)(2,1)S(1)}, bf16[16,1408]{1,0:T(8,128)(2,1)S(1)}, u32[]{:S(2)}, u32[]{:S(2)}) collective-permute-start(bf16[16,1408]{1,0:T(8,128)(2,1)S(1)} %shard_map.390.refs_0_), channel_id=1, source_target_pairs={{0,4},{1,5},{2,6},{3,7},{4,0},{5,1},{6,2},{7,3},{8,12},{9,13},{10,... | collective-permute-start | bytes 135176 | tf_op jit(solution)/shard_map/ppermute | solution.py:538
  10.2 5.8 %collective-permute-start.4 = (bf16[16,1408]{1,0:T(8,128)(2,1)S(1)}, bf16[16,1408]{1,0:T(8,128)(2,1)S(1)}, u32[]{:S(2)}, u32[]{:S(2)}) collective-permute-start(bf16[16,1408]{1,0:T(8,128)(2,1)S(1)} %shard_map.390.refs_0_), channel_id=1, source_target_pairs={{0,6},{1,7},{2,4},{3,5},{4,2},{5,3},{6,0},{7,1},{8,14},{9,15},{10,... | collective-permute-start | bytes 135176 | tf_op jit(solution)/shard_map/ppermute | solution.py:538
  16.1 7.7 %collective-permute-start.6 = (bf16[4,16,1408]{2,1,0:T(8,128)(2,1)S(1)}, bf16[4,16,1408]{2,1,0:T(8,128)(2,1)S(1)}, u32[]{:S(2)}, u32[]{:S(2)}) collective-permute-start(bf16[4,16,1408]{2,1,0:T(8,128)(2,1)S(1)} %shard_map.391.b0), channel_id=1, source_target_pairs={{0,16},{1,17},{2,18},{3,19},{4,20},{5,21},{6,22},{7,23},{8,24},{9,... | collective-permute-start | bytes 540680 | tf_op jit(solution)/shard_map/ppermute | solution.py:538
  17.7 7.4 %collective-permute-start.7 = (bf16[4,16,1408]{2,1,0:T(8,128)(2,1)S(1)}, bf16[4,16,1408]{2,1,0:T(8,128)(2,1)S(1)}, u32[]{:S(2)}, u32[]{:S(2)}) collective-permute-start(bf16[4,16,1408]{2,1,0:T(8,128)(2,1)S(1)} %shard_map.391.b0), channel_id=1, source_target_pairs={{0,24},{1,25},{2,26},{3,27},{4,28},{5,29},{6,30},{7,31},{8,16},{9,... | collective-permute-start | bytes 540680 | tf_op jit(solution)/shard_map/ppermute | solution.py:538
  19.1 7.1 %collective-permute-start.5 = (bf16[4,16,1408]{2,1,0:T(8,128)(2,1)S(1)}, bf16[4,16,1408]{2,1,0:T(8,128)(2,1)S(1)}, u32[]{:S(2)}, u32[]{:S(2)}) collective-permute-start(bf16[4,16,1408]{2,1,0:T(8,128)(2,1)S(1)} %shard_map.391.b0), channel_id=1, source_target_pairs={{0,8},{1,9},{2,10},{3,11},{4,12},{5,13},{6,14},{7,15},{8,0},{9,1},... | collective-permute-start | bytes 540680 | tf_op jit(solution)/shard_map/ppermute | solution.py:538
  19.6 7.4 %collective-permute-start.8 = (bf16[4,16,1408]{2,1,0:T(8,128)(2,1)S(1)}, bf16[4,16,1408]{2,1,0:T(8,128)(2,1)S(1)}, u32[]{:S(2)}, u32[]{:S(2)}) collective-permute-start(bf16[4,16,1408]{2,1,0:T(8,128)(2,1)S(1)} %shard_map.391.b0), channel_id=1, source_target_pairs={{0,1},{1,0},{2,3},{3,2},{4,5},{5,4},{6,7},{7,6},{8,9},{9,8},{10,11... | collective-permute-start | bytes 540680 | tf_op jit(solution)/shard_map/ppermute | solution.py:538
  20.7 10.0 %collective-permute-start = (bf16[12,48,256]{2,1,0:T(8,128)(2,1)S(1)}, bf16[12,48,256]{2,1,0:T(8,128)(2,1)S(1)}, u32[]{:S(2)}, u32[]{:S(2)}) collective-permute-start(bf16[12,48,256]{2,1,0:T(8,128)(2,1)S(1)} %get-tuple-element.146), channel_id=1, source_target_pairs={{0,1},{1,2},{2,3},{3,4},{4,5},{5,6},{6,7},{8,9},{9,10},{10,11},{11... | collective-permute-start | bytes 884744 | tf_op jit(solution)/shard_map/ppermute | solution.py:625
  23.7 7.0 %collective-permute-start.1 = (bf16[12,48,256]{2,1,0:T(8,128)(2,1)S(1)}, bf16[12,48,256]{2,1,0:T(8,128)(2,1)S(1)}, u32[]{:S(2)}, u32[]{:S(2)}) collective-permute-start(bf16[12,48,256]{2,1,0:T(8,128)(2,1)S(1)} %get-tuple-element.145), channel_id=1, source_target_pairs={{1,0},{2,1},{3,2},{4,3},{5,4},{6,5},{7,6},{9,8},{10,9},{11,10},{12... | collective-permute-start | bytes 884744 | tf_op jit(solution)/shard_map/ppermute | solution.py:626
  25.0 5.7 %collective-permute-start.10 = (bf16[4,16,1408]{2,1,0:T(8,128)(2,1)S(1)}, bf16[4,16,1408]{2,1,0:T(8,128)(2,1)S(1)}, u32[]{:S(2)}, u32[]{:S(2)}) collective-permute-start(bf16[4,16,1408]{2,1,0:T(8,128)(2,1)S(1)} %collective-permute-done.6.b2), channel_id=1, source_target_pairs={{0,1},{1,0},{2,3},{3,2},{4,5},{5,4},{6,7},{7,6},{8,9},{9,8},{10,11... | collective-permute-start | bytes 540680 | tf_op jit(solution)/shard_map/ppermute | solution.py:538
  26.2 4.5 %collective-permute-start.11 = (bf16[4,16,1408]{2,1,0:T(8,128)(2,1)S(1)}, bf16[4,16,1408]{2,1,0:T(8,128)(2,1)S(1)}, u32[]{:S(2)}, u32[]{:S(2)}) collective-permute-start(bf16[4,16,1408]{2,1,0:T(8,128)(2,1)S(1)} %collective-permute-done.7.b3), channel_id=1, source_target_pairs={{0,1},{1,0},{2,3},{3,2},{4,5},{5,4},{6,7},{7,6},{8,9},{9,8},{10,11... | collective-permute-start | bytes 540680 | tf_op jit(solution)/shard_map/ppermute | solution.py:538
  27.7 3.1 %collective-permute-start.9 = (bf16[4,16,1408]{2,1,0:T(8,128)(2,1)S(1)}, bf16[4,16,1408]{2,1,0:T(8,128)(2,1)S(1)}, u32[]{:S(2)}, u32[]{:S(2)}) collective-permute-start(bf16[4,16,1408]{2,1,0:T(8,128)(2,1)S(1)} %collective-permute-done.5.b1), channel_id=1, source_target_pairs={{0,1},{1,0},{2,3},{3,2},{4,5},{5,4},{6,7},{7,6},{8,9},{9,8},{10,11... | collective-permute-start | bytes 540680 | tf_op jit(solution)/shard_map/ppermute | solution.py:538
  30.7 35.4 %copy-start.32 = (s32[4]{0:T(128)}, s32[4]{0:T(128)S(1)}, u32[]{:S(2)}) copy-start(s32[4]{0:T(128)S(1)} %pad_add_fusion.where_ref) | copy-start | bytes 52
  33.6 1.0 copy-start.49
  62.3 5.3 %copy-start.1 = (f32[768,256]{1,0:T(8,128)}, f32[768,256]{1,0:T(8,128)S(1)}, u32[]{:S(2)}) copy-start(f32[768,256]{1,0:T(8,128)S(1)} %get-tuple-element.74.refs_4_) | copy-start | bytes 2359300
  62.3 5.3 %copy-start.3 = (bf16[768,256]{1,0:T(8,128)(2,1)}, bf16[768,256]{1,0:T(8,128)(2,1)S(1)}, u32[]{:S(2)}) copy-start(bf16[768,256]{1,0:T(8,128)(2,1)S(1)} %get-tuple-element.77.refs_9_) | copy-start | bytes 1179652
  62.3 5.3 %copy-start.5 = (bf16[768,256]{1,0:T(8,128)(2,1)}, bf16[768,256]{1,0:T(8,128)(2,1)S(1)}, u32[]{:S(2)}) copy-start(bf16[768,256]{1,0:T(8,128)(2,1)S(1)} %get-tuple-element.73.refs_3_) | copy-start | bytes 1179652
  62.3 5.3 %copy-start.7 = (bf16[256,768]{1,0:T(8,128)(2,1)}, bf16[256,768]{1,0:T(8,128)(2,1)S(1)}, u32[]{:S(2)}) copy-start(bf16[256,768]{1,0:T(8,128)(2,1)S(1)} %get-tuple-element.75.refs_6_) | copy-start | bytes 1179652
  62.4 5.3 %copy-start.24 = (f32[11,256]{1,0:T(8,128)}, f32[11,256]{1,0:T(8,128)S(1)}, u32[]{:S(2)}) copy-start(f32[11,256]{1,0:T(8,128)S(1)} %get-tuple-element.76.refs_7_) | copy-start | bytes 33796
  62.4 5.3 %copy-start.30 = (f32[8,256]{1,0:T(8,128)}, f32[8,256]{1,0:T(8,128)S(1)}, u32[]{:S(2)}) copy-start(f32[8,256]{1,0:T(8,128)S(1)} %get-tuple-element.78.refs_10_) | copy-start | bytes 24580
  62.4 5.3 %copy-start.38 = (f32[8,128]{1,0:T(8,128)}, f32[8,128]{1,0:T(8,128)S(1)}, u32[]{:S(2)}) copy-start(f32[8,128]{1,0:T(8,128)S(1)} %get-tuple-element.80.refs_12_) | copy-start | bytes 12292
  62.4 5.3 %copy-start.40 = (f32[1,768]{1,0:T(1,128)}, f32[1,768]{1,0:T(1,128)S(1)}, u32[]{:S(2)}) copy-start(f32[1,768]{1,0:T(1,128)S(1)} %get-tuple-element.79.refs_11_) | copy-start | bytes 9220
  62.4 9.4 %collective-permute-start.12 = (bf16[640,512]{1,0:T(8,128)(2,1)}, bf16[640,512]{1,0:T(8,128)(2,1)S(1)}, u32[]{:S(2)}, u32[]{:S(2)}) collective-permute-start(bf16[640,512]{1,0:T(8,128)(2,1)} %get-tuple-element.71), channel_id=1, source_target_pairs={{0,1},{1,2},{2,3},{3,4},{4,5},{5,6},{6,7},{8,9},{9,10},{10,11},{11... | collective-permute-start | bytes 1966088 | tf_op jit(solution)/shard_map/ppermute | solution.py:656
  64.8 7.0 %collective-permute-start.13 = (bf16[640,512]{1,0:T(8,128)(2,1)}, bf16[640,512]{1,0:T(8,128)(2,1)}, u32[]{:S(2)}, u32[]{:S(2)}) collective-permute-start(bf16[640,512]{1,0:T(8,128)(2,1)} %get-tuple-element.72), channel_id=1, source_target_pairs={{1,0},{2,1},{3,2},{4,3},{5,4},{6,5},{7,6},{9,8},{10,9},{11,10},{12... | collective-permute-start | bytes 1966088 | tf_op jit(solution)/shard_map/ppermute | solution.py:657
  68.5 22.1 %collective-permute-start.14 = (bf16[16,16,896]{2,1,0:T(8,128)(2,1)}, bf16[16,16,896]{2,1,0:T(8,128)(2,1)}, u32[]{:S(2)}, u32[]{:S(2)}) collective-permute-start(bf16[16,16,896]{2,1,0:T(8,128)(2,1)} %slice.93), channel_id=1, source_target_pairs={{0,1},{1,0},{2,3},{3,2},{4,5},{5,4},{6,7},{7,6},{8,9},{9,8},{10,11... | collective-permute-start | bytes 1376264 | tf_op jit(solution)/shard_map/ppermute | solution.py:538
  71.8 1.1 copy-start.2
  85.0 10.3 %collective-permute-start.18 = (bf16[16,16,512]{2,1,0:T(8,128)(2,1)S(1)}, bf16[16,16,512]{2,1,0:T(8,128)(2,1)S(1)}, u32[]{:S(2)}, u32[]{:S(2)}) collective-permute-start(bf16[16,16,512]{2,1,0:T(8,128)(2,1)S(1)} %slice.83), channel_id=1, source_target_pairs={{0,1},{1,0},{2,3},{3,2},{4,5},{5,4},{6,7},{7,6},{8,9},{9,8},{10,11... | collective-permute-start | bytes 786440 | tf_op jit(solution)/shard_map/ppermute | solution.py:538
  91.8 7.0 %collective-permute-start.15 = (bf16[4,16,896]{2,1,0:T(8,128)(2,1)S(1)}, bf16[4,16,896]{2,1,0:T(8,128)(2,1)S(1)}, u32[]{:S(2)}, u32[]{:S(2)}) collective-permute-start(bf16[4,16,896]{2,1,0:T(8,128)(2,1)S(1)} %get-tuple-element.142), channel_id=1, source_target_pairs={{0,8},{1,9},{2,10},{3,11},{4,12},{5,13},{6,14},{7,15},{8,0},{9,1},... | collective-permute-start | bytes 344072 | tf_op jit(solution)/shard_map/ppermute | solution.py:538
  93.3 8.7 %collective-permute-start.16 = (bf16[4,16,896]{2,1,0:T(8,128)(2,1)S(1)}, bf16[4,16,896]{2,1,0:T(8,128)(2,1)S(1)}, u32[]{:S(2)}, u32[]{:S(2)}) collective-permute-start(bf16[4,16,896]{2,1,0:T(8,128)(2,1)S(1)} %get-tuple-element.144), channel_id=1, source_target_pairs={{0,16},{1,17},{2,18},{3,19},{4,20},{5,21},{6,22},{7,23},{8,24},{9,... | collective-permute-start | bytes 344072 | tf_op jit(solution)/shard_map/ppermute | solution.py:538
  95.1 6.9 %collective-permute-start.17 = (bf16[4,16,896]{2,1,0:T(8,128)(2,1)S(1)}, bf16[4,16,896]{2,1,0:T(8,128)(2,1)S(1)}, u32[]{:S(2)}, u32[]{:S(2)}) collective-permute-start(bf16[4,16,896]{2,1,0:T(8,128)(2,1)S(1)} %get-tuple-element.143), channel_id=1, source_target_pairs={{0,24},{1,25},{2,26},{3,27},{4,28},{5,29},{6,30},{7,31},{8,16},{9,... | collective-permute-start | bytes 344072 | tf_op jit(solution)/shard_map/ppermute | solution.py:538
  95.5 6.8 %collective-permute-start.19 = (bf16[4,16,512]{2,1,0:T(8,128)(2,1)S(1)}, bf16[4,16,512]{2,1,0:T(8,128)(2,1)S(1)}, u32[]{:S(2)}, u32[]{:S(2)}) collective-permute-start(bf16[4,16,512]{2,1,0:T(8,128)(2,1)S(1)} %get-tuple-element.147), channel_id=1, source_target_pairs={{0,8},{1,9},{2,10},{3,11},{4,12},{5,13},{6,14},{7,15},{8,0},{9,1},... | collective-permute-start | bytes 196616 | tf_op jit(solution)/shard_map/ppermute | solution.py:538
  97.0 5.7 %collective-permute-start.20 = (bf16[4,16,512]{2,1,0:T(8,128)(2,1)S(1)}, bf16[4,16,512]{2,1,0:T(8,128)(2,1)S(1)}, u32[]{:S(2)}, u32[]{:S(2)}) collective-permute-start(bf16[4,16,512]{2,1,0:T(8,128)(2,1)S(1)} %get-tuple-element.149), channel_id=1, source_target_pairs={{0,16},{1,17},{2,18},{3,19},{4,20},{5,21},{6,22},{7,23},{8,24},{9,... | collective-permute-start | bytes 196616 | tf_op jit(solution)/shard_map/ppermute | solution.py:538
  98.8 5.2 %collective-permute-start.21 = (bf16[4,16,512]{2,1,0:T(8,128)(2,1)S(1)}, bf16[4,16,512]{2,1,0:T(8,128)(2,1)S(1)}, u32[]{:S(2)}, u32[]{:S(2)}) collective-permute-start(bf16[4,16,512]{2,1,0:T(8,128)(2,1)S(1)} %get-tuple-element.148), channel_id=1, source_target_pairs={{0,24},{1,25},{2,26},{3,27},{4,28},{5,29},{6,30},{7,31},{8,16},{9,... | collective-permute-start | bytes 196616 | tf_op jit(solution)/shard_map/ppermute | solution.py:538
  102.0 9.4 %copy-start.11 = (f32[11,8]{1,0:T(8,128)S(1)}, f32[11,8]{1,0:T(8,128)}, u32[]{:S(2)}) copy-start(f32[11,8]{1,0:T(8,128)} %copy.48.refs_20_) | copy-start | bytes 1060
  102.0 9.4 %copy-start.12 = (f32[8,768]{1,0:T(8,128)S(1)}, f32[8,768]{1,0:T(8,128)}, u32[]{:S(2)}) copy-start(f32[8,768]{1,0:T(8,128)} %refs_10_.1) | copy-start | bytes 73732
  102.0 9.4 %copy-start.13 = (f32[8,768]{1,0:T(8,128)S(1)}, f32[8,768]{1,0:T(8,128)}, u32[]{:S(2)}) copy-start(f32[8,768]{1,0:T(8,128)} %refs_12_.1) | copy-start | bytes 73732
  102.0 9.4 %copy-start.14 = (f32[24,256]{1,0:T(8,128)S(1)}, f32[24,256]{1,0:T(8,128)}, u32[]{:S(2)}) copy-start(f32[24,256]{1,0:T(8,128)} %refs_13_.1) | copy-start | bytes 73732
  102.1 9.4 %copy-start.15 = (f32[8,768]{1,0:T(8,128)S(1)}, f32[8,768]{1,0:T(8,128)}, u32[]{:S(2)}) copy-start(f32[8,768]{1,0:T(8,128)} %refs_16_.1) | copy-start | bytes 73732
  102.1 9.4 %copy-start.16 = (f32[8,768]{1,0:T(8,128)S(1)}, f32[8,768]{1,0:T(8,128)}, u32[]{:S(2)}) copy-start(f32[8,768]{1,0:T(8,128)} %refs_18_.1) | copy-start | bytes 73732
  102.1 9.4 %copy-start.17 = (f32[24,256]{1,0:T(8,128)S(1)}, f32[24,256]{1,0:T(8,128)}, u32[]{:S(2)}) copy-start(f32[24,256]{1,0:T(8,128)} %refs_19_.1) | copy-start | bytes 73732
  102.1 9.4 %copy-start.19 = (f32[8,768]{1,0:T(8,128)S(1)}, f32[8,768]{1,0:T(8,128)}, u32[]{:S(2)}) copy-start(f32[8,768]{1,0:T(8,128)} %refs_0_.1) | copy-start | bytes 73732
  102.1 9.4 %copy-start.21 = (f32[8,768]{1,0:T(8,128)S(1)}, f32[8,768]{1,0:T(8,128)}, u32[]{:S(2)}) copy-start(f32[8,768]{1,0:T(8,128)} %refs_2_.1) | copy-start | bytes 73732
  102.1 9.4 %copy-start.23 = (f32[24,256]{1,0:T(8,128)S(1)}, f32[24,256]{1,0:T(8,128)}, u32[]{:S(2)}) copy-start(f32[24,256]{1,0:T(8,128)} %refs_3_.1) | copy-start | bytes 73732
  102.1 9.4 %copy-start.26 = (f32[8,256]{1,0:T(8,128)S(1)}, f32[8,256]{1,0:T(8,128)}, u32[]{:S(2)}) copy-start(f32[8,256]{1,0:T(8,128)} %refs_11_.1) | copy-start | bytes 24580
  102.1 9.4 %copy-start.27 = (f32[8,256]{1,0:T(8,128)S(1)}, f32[8,256]{1,0:T(8,128)}, u32[]{:S(2)}) copy-start(f32[8,256]{1,0:T(8,128)} %refs_17_.1) | copy-start | bytes 24580
  102.2 9.4 %copy-start.29 = (f32[8,256]{1,0:T(8,128)S(1)}, f32[8,256]{1,0:T(8,128)}, u32[]{:S(2)}) copy-start(f32[8,256]{1,0:T(8,128)} %refs_1_.1) | copy-start | bytes 24580
  102.2 9.4 %copy-start.34 = (f32[8,49]{1,0:T(8,128)S(1)}, f32[8,49]{1,0:T(8,128)}, u32[]{:S(2)}) copy-start(f32[8,49]{1,0:T(8,128)} %refs_15_.1) | copy-start | bytes 4708
  102.2 9.4 %copy-start.35 = (f32[8,49]{1,0:T(8,128)S(1)}, f32[8,49]{1,0:T(8,128)}, u32[]{:S(2)}) copy-start(f32[8,49]{1,0:T(8,128)} %refs_21_.1) | copy-start | bytes 4708
  102.2 9.4 %copy-start.37 = (f32[8,49]{1,0:T(8,128)S(1)}, f32[8,49]{1,0:T(8,128)}, u32[]{:S(2)}) copy-start(f32[8,49]{1,0:T(8,128)} %refs_5_.5) | copy-start | bytes 4708
  104.1 4.5 %collective-permute-start.22 = (bf16[16,1408]{1,0:T(8,128)(2,1)S(1)}, bf16[16,1408]{1,0:T(8,128)(2,1)S(1)}, u32[]{:S(2)}, u32[]{:S(2)}) collective-permute-start(bf16[16,1408]{1,0:T(8,128)(2,1)S(1)} %get-tuple-element.152), channel_id=1, source_target_pairs={{0,2},{1,3},{2,0},{3,1},{4,6},{5,7},{6,4},{7,5},{8,10},{9,11},{10,... | collective-permute-start | bytes 135176 | tf_op jit(solution)/shard_map/ppermute | solution.py:538
  104.2 5.2 %collective-permute-start.23 = (bf16[16,1408]{1,0:T(8,128)(2,1)S(1)}, bf16[16,1408]{1,0:T(8,128)(2,1)S(1)}, u32[]{:S(2)}, u32[]{:S(2)}) collective-permute-start(bf16[16,1408]{1,0:T(8,128)(2,1)S(1)} %get-tuple-element.151), channel_id=1, source_target_pairs={{0,4},{1,5},{2,6},{3,7},{4,0},{5,1},{6,2},{7,3},{8,12},{9,13},{10,... | collective-permute-start | bytes 135176 | tf_op jit(solution)/shard_map/ppermute | solution.py:538
  105.5 5.9 %collective-permute-start.24 = (bf16[16,1408]{1,0:T(8,128)(2,1)S(1)}, bf16[16,1408]{1,0:T(8,128)(2,1)S(1)}, u32[]{:S(2)}, u32[]{:S(2)}) collective-permute-start(bf16[16,1408]{1,0:T(8,128)(2,1)S(1)} %get-tuple-element.150), channel_id=1, source_target_pairs={{0,6},{1,7},{2,4},{3,5},{4,2},{5,3},{6,0},{7,1},{8,14},{9,15},{10,... | collective-permute-start | bytes 135176 | tf_op jit(solution)/shard_map/ppermute | solution.py:538
  112.4 1.2 collective-permute-start.25
  113.6 3.7 %collective-permute-start.26 = (f32[16,128]{1,0:T(8,128)S(1)}, f32[16,128]{1,0:T(8,128)S(1)}, u32[]{:S(2)}, u32[]{:S(2)}) collective-permute-start(f32[16,128]{1,0:T(8,128)S(1)} %add.48), channel_id=1, source_target_pairs={{0,8},{1,9},{2,10},{3,11},{4,12},{5,13},{6,14},{7,15},{8,0},{9,1},... | collective-permute-start | bytes 24584 | tf_op jit(solution)/shard_map/ppermute | solution.py:538
  114.7 3.7 %collective-permute-start.27 = (f32[16,128]{1,0:T(8,128)S(1)}, f32[16,128]{1,0:T(8,128)S(1)}, u32[]{:S(2)}, u32[]{:S(2)}) collective-permute-start(f32[16,128]{1,0:T(8,128)S(1)} %add.48), channel_id=1, source_target_pairs={{0,16},{1,17},{2,18},{3,19},{4,20},{5,21},{6,22},{7,23},{8,24},{9,... | collective-permute-start | bytes 24584 | tf_op jit(solution)/shard_map/ppermute | solution.py:538
  115.9 4.5 %collective-permute-start.28 = (f32[16,128]{1,0:T(8,128)S(1)}, f32[16,128]{1,0:T(8,128)S(1)}, u32[]{:S(2)}, u32[]{:S(2)}) collective-permute-start(f32[16,128]{1,0:T(8,128)S(1)} %add.48), channel_id=1, source_target_pairs={{0,24},{1,25},{2,26},{3,27},{4,28},{5,29},{6,30},{7,31},{8,16},{9,... | collective-permute-start | bytes 24584 | tf_op jit(solution)/shard_map/ppermute | solution.py:538
  120.5 5.7 %collective-permute-start.29 = (f32[16,128]{1,0:T(8,128)S(1)}, f32[16,128]{1,0:T(8,128)S(1)}, u32[]{:S(2)}, u32[]{:S(2)}) collective-permute-start(f32[16,128]{1,0:T(8,128)S(1)} %add_add_fusion.a_ref), channel_id=1, source_target_pairs={{0,2},{1,3},{2,0},{3,1},{4,6},{5,7},{6,4},{7,5},{8,10},{9,11},{10,... | collective-permute-start | bytes 24584 | tf_op jit(solution)/shard_map/ppermute | solution.py:538
  121.2 5.1 %collective-permute-start.30 = (f32[16,128]{1,0:T(8,128)S(1)}, f32[16,128]{1,0:T(8,128)S(1)}, u32[]{:S(2)}, u32[]{:S(2)}) collective-permute-start(f32[16,128]{1,0:T(8,128)S(1)} %add_add_fusion.a_ref), channel_id=1, source_target_pairs={{0,4},{1,5},{2,6},{3,7},{4,0},{5,1},{6,2},{7,3},{8,12},{9,13},{10,... | collective-permute-start | bytes 24584 | tf_op jit(solution)/shard_map/ppermute | solution.py:538
  124.0 5.4 %collective-permute-start.31 = (f32[16,128]{1,0:T(8,128)S(1)}, f32[16,128]{1,0:T(8,128)S(1)}, u32[]{:S(2)}, u32[]{:S(2)}) collective-permute-start(f32[16,128]{1,0:T(8,128)S(1)} %add_add_fusion.a_ref), channel_id=1, source_target_pairs={{0,6},{1,7},{2,4},{3,5},{4,2},{5,3},{6,0},{7,1},{8,14},{9,15},{10,... | collective-permute-start | bytes 24584 | tf_op jit(solution)/shard_map/ppermute | solution.py:538
  (19 other events, 15.0 us)

commit v3 on v2

--- a/solution.py
+++ b/solution.py
@@ -104,7 +104,7 @@
 
 
 def layer_kernel(
-    where_ref,
+    sizes_ref,
     x_ref,
     xb_ref,
     xa_ref,
@@ -142,9 +142,9 @@
     dmix_ref,
     tacc_ref,
 ):
-    row0 = where_ref[0] * 16
-    height = where_ref[1]
-    wide = where_ref[2]
+    row0 = lax.axis_index("band") * 16
+    height = sizes_ref[0, 0]
+    wide = sizes_ref[0, 1]
     scale = 32 ** (-0.5)
     lane_head = lax.broadcasted_iota(jnp.int32, (QN, 256), 1) >> 5
 
@@ -360,14 +360,14 @@
 LATE = 512
 
 
+def widen(v):
+    return jnp.concatenate([v, jnp.zeros((v.shape[0], 128 - v.shape[1]), F32)], axis=1)
+
+
 def pack_kernel(wqkv_ref, wo_ref, wu_ref, wd_ref, vec_ref, out_ref):
-    vrows = vec_ref.shape[0]
-    lane = lax.broadcasted_iota(jnp.int32, (vrows, 128), 1)
-    row = lax.broadcasted_iota(jnp.int32, (vrows, 128), 0)
-    turned = dot_tn(vec_ref[...].astype(BF), (lane == row).astype(BF))
     top = [wd_ref[8 * b : 8 * b + 8, :] for b in range(3)]
     top += [wo_ref[:, 0:128], wqkv_ref[:, 0:512]]
-    low = [wu_ref[...], wo_ref[:, 128:256], wqkv_ref[:, 512:768], turned, jnp.zeros((8, 128), F32)]
+    low = [wu_ref[...], wo_ref[:, 128:256], wqkv_ref[:, 512:768], widen(vec_ref[...]), jnp.zeros((8, 128), F32)]
     both = jnp.concatenate([jnp.concatenate(top, axis=1), jnp.concatenate(low, axis=1)], axis=0)
     out_ref[...] = both.astype(BF)
 
@@ -395,16 +395,20 @@
     vec_ref[...] = fv[...].T[0 : vec_ref.shape[0]]
 
 
+def own_index():
+    return lax.axis_index("maps") * 8 + lax.axis_index("band")
+
+
 def layer_packed(
-    where_ref, x_ref, xb_ref, xa_ref, cot_ref, b0, b1, b2, b3, b4, b5, b6, b7, table_ref, po_ref, pk_ref, *rest
+    sizes_ref, x_ref, xb_ref, xa_ref, cot_ref, b0, b1, b2, b3, b4, b5, b6, b7, table_ref, po_ref, pk_ref, *rest
 ):
     weights = rest[-10:]
-    unpack(where_ref[3], (b0, b1, b2, b3, b4, b5, b6, b7), weights)
+    unpack(own_index(), (b0, b1, b2, b3, b4, b5, b6, b7), weights)
     outs, scratch = rest[:16], rest[18:-10]
     rest[16][...] = weights[0][...]
     rest[17][...] = weights[4][...]
     layer_kernel(
-        where_ref, x_ref, xb_ref, xa_ref, cot_ref, *weights[:5], table_ref, po_ref, pk_ref, *outs, *scratch
+        sizes_ref, x_ref, xb_ref, xa_ref, cot_ref, *weights[:5], table_ref, po_ref, pk_ref, *outs, *scratch
     )
 
 
@@ -413,11 +417,11 @@
     return (m & 1) * 16 + (m >> 3) * 4 + ((m >> 1) & 3)
 
 
-def early_kernel(where_ref, act_ref, dy_ref, a2_ref, dz_ref, mixed_ref, da_ref, out_ref, fd, fu, fo):
+def early_kernel(act_ref, dy_ref, a2_ref, dz_ref, mixed_ref, da_ref, out_ref, fd, fu, fo):
     fd[...] = dot_tn(act_ref[...], dy_ref[...])
     fu[...] = dot_tn(a2_ref[...], dz_ref[...])
     fo[...] = dot_tn(mixed_ref[...], da_ref[...])
-    me = where_ref[3]
+    me = own_index()
     for o in range(32):
         at = slice(8 * o, 8 * o + 8)
         top = [fd[24 * o + 8 * b : 24 * o + 8 * b + 8, :] for b in range(3)] + [fo[at, 0:128]]
@@ -426,7 +430,7 @@
         out_ref[frame_slot(me, o)] = both.astype(BF)
 
 
-def late_kernel(where_ref, *refs):
+def late_kernel(*refs):
     own, fa, fb, dq, dx1, x, wqkv, vec, po, a1, sums, zsum, tgrad = refs[:13]
     tok_ref, out_ref, dqkv, sums2, fq, fv = refs[13:]
     finish_kernel(own, fa, fb, dq, dx1, x, wqkv, vec, po, tok_ref, dqkv, sums2)
@@ -439,7 +443,7 @@
     )
     fv[...] = lines.T
     table = tgrad[...]
-    me = where_ref[3]
+    me = own_index()
     for o in range(32):
         at = slice(8 * o, 8 * o + 8)
         low = jnp.concatenate([fq[at, 512:768], fv[at, :], table], axis=1)
@@ -451,13 +455,13 @@
     outs = refs[22:]
     total = refs[0][...] + sum(ref[...].astype(F32) for ref in refs[1:4])
     early, late = total[:, :EARLY], total[:, EARLY:]
-    vrows = w[4].shape[0]
+    vrows = w[4].shape[1]
     grads = [
         jnp.concatenate([late[0:8], late[8:16, 0:256]], axis=1),
         jnp.concatenate([early[0:8, 768:896], early[8:16, 768:896]], axis=1),
         early[8:16, 0:768],
         jnp.concatenate([early[0:8, 256 * b : 256 * b + 256] for b in range(3)], axis=0),
-        late[8:16, 256:384].T[0:vrows],
+        late[8:16, 256 : 256 + vrows],
         lax.dot_general(
             late[8:16, 384:512],
             table_slots(),
@@ -466,41 +470,39 @@
             preferred_element_type=F32,
         ),
     ]
-    row = lax.broadcasted_iota(jnp.int32, (16, 128), 0)
-    lane = lax.broadcasted_iota(jnp.int32, (16, 128), 1)
-    norms = jnp.zeros((16, 128), F32)
+    row = lax.broadcasted_iota(jnp.int32, (8, 128), 0)
+    lane = lax.broadcasted_iota(jnp.int32, (8, 128), 1)
+    norms = jnp.zeros((8, 128), F32)
     for i in range(6):
         new_first, new_second, update = adam_parts(w[i][...], grads[i], first[i][...], second[i][...])
         outs[3 * i][...] = new_first
         outs[3 * i + 1][...] = new_second
         outs[3 * i + 2][...] = update
-        for col, v in ((0, w[i][...]), (1, update)):
+        for line, v in ((0, w[i][...]), (1, update)):
             if i == 4:
-                per_row = jnp.sum(v * v, axis=1, keepdims=True)
-                tall = jnp.concatenate([jnp.zeros((4, 1), F32), per_row, jnp.zeros((12 - vrows, 1), F32)], axis=0)
-                norms = jnp.where((lane == col) & (row >= 4) & (row < 4 + vrows), tall, norms)
+                sums = pltpu.roll(widen(jnp.sum(v * v, axis=0, keepdims=True)), 4, 1)
+                norms = jnp.where((row == line) & (lane >= 4) & (lane < 4 + vrows), sums, norms)
             else:
-                total = jnp.sum(v * v)
                 at = i if i < 4 else 4 + vrows
-                norms = jnp.where((lane == col) & (row == at), total, norms)
+                norms = jnp.where((row == line) & (lane == at), jnp.sum(v * v), norms)
     outs[18][...] = norms
 
 
 def step_kernel(mine_ref, a_ref, b_ref, c_ref, d_ref, *refs):
     w, update, outs = refs[0:6], refs[6:12], refs[12:]
-    vrows = w[4].shape[0]
+    vrows = w[4].shape[1]
     total = a_ref[...] + b_ref[...] + c_ref[...] + d_ref[...]
-    row = lax.broadcasted_iota(jnp.int32, (16, 128), 0)
-    norms = jnp.sqrt(jnp.where(row == 4 + vrows, mine_ref[...], total))
-    turned = norms.T
-    outs[6][...] = turned[0:1]
-    outs[7][...] = turned[1:2]
-    rate = LEARN_RATE * norms[:, 0:1] / (norms[:, 1:2] + RATIO_EPS)
+    lane = lax.broadcasted_iota(jnp.int32, (8, 128), 1)
+    norms = jnp.sqrt(jnp.where(lane == 4 + vrows, mine_ref[...], total))
+    outs[6][...] = norms[0:1, 0:16]
+    outs[7][...] = norms[1:2, 0:16]
+    rate = LEARN_RATE * norms[0:1] / (norms[1:2] + RATIO_EPS)
     for i in range(6):
         if i == 4:
-            r = rate[4 : 4 + vrows]
+            r = pltpu.roll(rate, 124, 1)[:, 0:vrows]
         else:
-            r = rate[i : i + 1] if i < 4 else rate[4 + vrows : 5 + vrows]
+            at = i if i < 4 else 4 + vrows
+            r = rate[:, at : at + 1]
         outs[i][...] = w[i][...] - r * update[i][...]
 
 
@@ -617,9 +619,9 @@
 
 def packed_step(tokens_in, cotangent, map_sizes, weights, firsts, seconds):
     count = 32
-    me = lax.axis_index(AXES)
-    band_index = lax.axis_index("band")
     vrows = weights[4].shape[0]
+    turn = lambda arrays: tuple(a.T if i == 4 else a for i, a in enumerate(arrays))
+    weights, firsts, seconds = turn(weights), turn(firsts), turn(seconds)
     up = [(i, i + 1) for i in range(7)]
     down = [(i + 1, i) for i in range(7)]
     x_before = lax.ppermute(tokens_in[-12:], "band", up)
@@ -638,7 +640,6 @@
 
     po = jnp.asarray(order_own(), BF)
     pk = jnp.asarray(order_keys(), BF)
-    place = jnp.stack([band_index, map_sizes[0, 0], map_sizes[0, 1], me]).astype(jnp.int32)
     matrices = [(256, 768), (256, 256), (256, 768), (768, 256)]
     (
         layer_out, act, dy, dz, a2, mixed, da, a1, dq, dx1, own, rim_a, rim_b, tgrad, sums, zsum, big_qkv, vec,
@@ -650,7 +651,7 @@
         + [pltpu.VMEM((vrows, 256), F32)]
         + [pltpu.VMEM(m, F32) for m in matrices]
         + [pltpu.VMEM((256, 128), F32)],
-        place, tokens_in, x_before, x_after, cotangent, *blocks, weights[5], po, pk,
+        map_sizes, tokens_in, x_before, x_after, cotangent, *blocks, weights[5], po, pk,
         smem=1, flops=6 * 10**9, vmem=24,
     )
     from_prev = lax.ppermute(rim_a, "band", up)
@@ -659,8 +660,8 @@
         early_kernel,
         sds((count, 16, EARLY)),
         [pltpu.VMEM((768, 256), F32), pltpu.VMEM((256, 768), F32), pltpu.VMEM((256, 256), F32)],
-        place, act, dy, a2, dz, mixed, da,
-        smem=1, flops=10**9,
+        act, dy, a2, dz, mixed, da,
+        flops=10**9,
     )
     tokens_grad, late = call(
         late_kernel,
@@ -671,8 +672,8 @@
             pltpu.VMEM((256, 768), F32),
             pltpu.VMEM((256, 128), F32),
         ],
-        place, own, from_prev, from_next, dq, dx1, tokens_in, big_qkv, vec, po, a1, sums, zsum, tgrad,
-        smem=1, flops=10**9,
+        own, from_prev, from_next, dq, dx1, tokens_in, big_qkv, vec, po, a1, sums, zsum, tgrad,
+        flops=10**9,
     )
     early = add_stage(add_stage(early, 0, 1, count), 3, 2, count)
     late = add_stage(add_stage(late, 0, 1, count), 3, 2, count)
@@ -683,7 +684,7 @@
     shapes = [sds(w.shape, F32) for w in weights]
     moments = call(
         adam_kernel,
-        tuple(shape for shape in shapes for _ in range(3)) + (sds((16, 128), F32),),
+        tuple(shape for shape in shapes for _ in range(3)) + (sds((8, 128), F32),),
         [],
         *parts, *weights, *firsts, *seconds,
     )
@@ -698,7 +699,8 @@
     )
     results = [layer_out, tokens_grad]
     for i in range(6):
-        results += [moments[3 * i], moments[3 * i + 1], news[i]]
+        three = (moments[3 * i], moments[3 * i + 1], news[i])
+        results += [a.T for a in three] if i == 4 else three
     return tuple(results) + (news[6].reshape(16), news[7].reshape(16))
 
 
@@ -749,7 +751,6 @@
     masks = np.array(frame_masks(groups))
     inverse = np.argsort(masks)
     me = lax.axis_index(AXES)
-    band_index = lax.axis_index("band")
     reach = 3 * DIL
 
     up = [(i, i + 1) for i in range(band - 1)]
@@ -776,7 +777,6 @@
 
     po = jnp.asarray(order_own(), BF)
     pk = jnp.asarray(order_keys(), BF)
-    place = jnp.stack([band_index, map_sizes[0, 0], map_sizes[0, 1]]).astype(jnp.int32)
     (
         layer_out,
         act,
@@ -798,7 +798,7 @@
         layer_kernel,
         layer_outputs(),
         layer_scratch(),
-        place,
+        map_sizes,
         tokens_in,
         x_before,
         x_after,

time: 132 us -> 113 us (0.86)
  local copies, waits for them, and re-layouts: 24.8 us -> 4.97 us
  starting transfers between devices: 46 us -> 49.9 us
  other arithmetic: 2.74 us -> 0.36 us
  Pallas kernels: 35.8 us -> 33.7 us
  waiting for transfers between devices: 20.3 us -> 22.2 us
    unnamed x108 -> x56, local copies, waits for them, and re-layouts: 22.3 us -> 3.77 us
    ppermute x28, starting transfers between devices: 38.6 us -> 42 us  [swap(): return lax.ppermute(block, AXES, [(k, k ^ mask) for k in range(count)])]
    pallas_call x7, Pallas kernels: 35.8 us -> 33.7 us  [call(): pl.pallas_call(kernel, out_shape=out_shape, in_specs=specs, out_specs=jax...]
    ppermute x28, waiting for transfers between devices: 20.3 us -> 21.7 us  [swap(): return lax.ppermute(block, AXES, [(k, k ^ mask) for k in range(count)])]
    another operation x1 -> x0, other arithmetic: 1.37 us -> none  [packed_step(): jnp.stack([band_index, map_sizes[0, 0], map_sizes[0, 1], me])]
  transfers between devices with their start and end apart: 32 -> 32, of which waited for: 13 -> 18; matrix products, arithmetic and copies ran while one was open for 7% -> 1% of each run, Pallas kernels for 5% -> 4%
where the time goes in v3:
time: 113 us; the launch traced here: 112 us
  starting transfers between devices  49.9 us (44%)
  Pallas kernels  33.7 us (30%)
  waiting for transfers between devices  22.2 us (20%)
  local copies, waits for them, and re-layouts  4.97 us (4%)
  between operations  1.15 us (1%)
    ppermute x28, starting transfers between devices, swap(): return lax.ppermute(block, AXES, [(k, k ^ mask) for k in range(count)])  42 us
    pallas_call x7, Pallas kernels, call(): pl.pallas_call(kernel, out_shape=out_shape, in_specs=specs, out_specs=jax...  33.7 us
    ppermute x28, waiting for transfers between devices, swap(): return lax.ppermute(block, AXES, [(k, k ^ mask) for k in range(count)])  21.7 us
    unnamed x56, local copies, waits for them, and re-layouts  3.77 us
    ppermute x1, starting transfers between devices, packed_step(): x_before = lax.ppermute(tokens_in[-12:], 'band', up)  3.05 us
  transfers between devices with their start and end apart: 32, of which 18 were waited for; matrix products, arithmetic and copies ran while one was open for 1% of the time, Pallas kernels for 4%

profile of v3, /device:TPU:0, one launch (start us, length us, event | category | flops | bytes accessed | tf_op | source)
XLA Modules:
  0.0 112.3 jit_solution(4411617738070524193)
XLA Ops:
  0.7 0.0 copy-start.1
  0.7 0.8 copy-done.8
  1.5 0.7 copy-done.10
  2.2 0.7 copy-done.12
  3.0 0.7 copy-done.16
  3.7 0.7 copy-done.22
  4.4 5.1 %collective-permute-start.4 = (bf16[16,1408]{1,0:T(8,128)(2,1)S(1)}, bf16[16,1408]{1,0:T(8,128)(2,1)S(1)}, u32[]{:S(2)}, u32[]{:S(2)}) collective-permute-start(bf16[16,1408]{1,0:T(8,128)(2,1)S(1)} %shard_map.390.refs_0_), channel_id=1, source_target_pairs={{0,6},{1,7},{2,4},{3,5},{4,2},{5,3},{6,0},{7,1},{8,14},{9,15},{10,... | collective-permute-start | bytes 135176 | tf_op jit(solution)/shard_map/ppermute | solution.py:540
  9.5 0.6 collective-permute-start.2
  10.1 1.4 %collective-permute-done.4.refs_3_ = bf16[16,1408]{1,0:T(8,128)(2,1)S(1)} collective-permute-done((bf16[16,1408]{1,0:T(8,128)(2,1)S(1)}, bf16[16,1408]{1,0:T(8,128)(2,1)S(1)}, u32[]{:S(2)}, u32[]{:S(2)}) %collective-permute-start.4) | collective-permute-done | bytes 45088 | tf_op jit(solution)/shard_map/ppermute | solution.py:540
  11.6 2.9 %collective-permute-done.3.refs_2_ = bf16[16,1408]{1,0:T(8,128)(2,1)S(1)} collective-permute-done((bf16[16,1408]{1,0:T(8,128)(2,1)S(1)}, bf16[16,1408]{1,0:T(8,128)(2,1)S(1)}, u32[]{:S(2)}, u32[]{:S(2)}) %collective-permute-start.3) | collective-permute-done | bytes 45088 | tf_op jit(solution)/shard_map/ppermute | solution.py:540
  14.4 0.1 collective-permute-start.8
  14.5 2.5 %collective-permute-start.7 = (bf16[4,16,1408]{2,1,0:T(8,128)(2,1)S(1)}, bf16[4,16,1408]{2,1,0:T(8,128)(2,1)S(1)}, u32[]{:S(2)}, u32[]{:S(2)}) collective-permute-start(bf16[4,16,1408]{2,1,0:T(8,128)(2,1)S(1)} %shard_map.391.b0), channel_id=1, source_target_pairs={{0,24},{1,25},{2,26},{3,27},{4,28},{5,29},{6,30},{7,31},{8,16},{9,... | collective-permute-start | bytes 540680 | tf_op jit(solution)/shard_map/ppermute | solution.py:540
  17.0 0.5 collective-permute-start.6
  17.5 0.5 collective-permute-start.5
  18.1 1.1 fusion.10
  19.2 1.3 %collective-permute-start.1 = (bf16[12,48,256]{2,1,0:T(8,128)(2,1)S(1)}, bf16[12,48,256]{2,1,0:T(8,128)(2,1)S(1)}, u32[]{:S(2)}, u32[]{:S(2)}) collective-permute-start(bf16[12,48,256]{2,1,0:T(8,128)(2,1)S(1)} %get-tuple-element.123), channel_id=1, source_target_pairs={{1,0},{2,1},{3,2},{4,3},{5,4},{6,5},{7,6},{9,8},{10,9},{11,10},{12... | collective-permute-start | bytes 884744 | tf_op jit(solution)/shard_map/ppermute | solution.py:628
  20.5 3.0 %collective-permute-start = (bf16[12,48,256]{2,1,0:T(8,128)(2,1)S(1)}, bf16[12,48,256]{2,1,0:T(8,128)(2,1)S(1)}, u32[]{:S(2)}, u32[]{:S(2)}) collective-permute-start(bf16[12,48,256]{2,1,0:T(8,128)(2,1)S(1)} %get-tuple-element.124), channel_id=1, source_target_pairs={{0,1},{1,2},{2,3},{3,4},{4,5},{5,6},{6,7},{8,9},{9,10},{10,11},{11... | collective-permute-start | bytes 884744 | tf_op jit(solution)/shard_map/ppermute | solution.py:627
  23.6 0.9 collective-permute-start.11
  24.4 1.8 %collective-permute-done.6.b2 = bf16[4,16,1408]{2,1,0:T(8,128)(2,1)S(1)} collective-permute-done((bf16[4,16,1408]{2,1,0:T(8,128)(2,1)S(1)}, bf16[4,16,1408]{2,1,0:T(8,128)(2,1)S(1)}, u32[]{:S(2)}, u32[]{:S(2)}) %collective-permute-start.6) | collective-permute-done | bytes 180256 | tf_op jit(solution)/shard_map/ppermute | solution.py:540
  26.3 0.0 collective-permute-start.10
  26.3 0.1 collective-permute-done.5.b1
  26.4 0.4 collective-permute-start.9
  26.8 0.9 collective-permute-done.10.b6
  27.7 0.3 collective-permute-done.9.b5
  28.0 27.5 %shard_map.392 = (bf16[16,48,256]{2,1,0:T(8,128)(2,1)}, bf16[768,768]{1,0:T(8,128)(2,1)S(1)}, bf16[768,256]{1,0:T(8,128)(2,1)S(1)}, bf16[768,768]{1,0:T(8,128)(2...) custom-call(s32[1,2]{1,0:T(1,128)S(1)} %copy-done.26, ...), custom_call_target="tpu_custom_call" | custom-call | flops 6000000000 | bytes 1000000 | tf_op jit(solution)/shard_map/pallas_call | solution.py:517
  55.5 2.2 %collective-permute-start.12 = (bf16[640,512]{1,0:T(8,128)(2,1)S(1)}, bf16[640,512]{1,0:T(8,128)(2,1)S(1)}, u32[]{:S(2)}, u32[]{:S(2)}) collective-permute-start(bf16[640,512]{1,0:T(8,128)(2,1)S(1)} %get-tuple-element.71), channel_id=1, source_target_pairs={{0,1},{1,2},{2,3},{3,4},{4,5},{5,6},{6,7},{8,9},{9,10},{10,11},{11... | collective-permute-start | bytes 1966088 | tf_op jit(solution)/shard_map/ppermute | solution.py:657
  57.7 1.3 %collective-permute-start.13 = (bf16[640,512]{1,0:T(8,128)(2,1)S(1)}, bf16[640,512]{1,0:T(8,128)(2,1)S(1)}, u32[]{:S(2)}, u32[]{:S(2)}) collective-permute-start(bf16[640,512]{1,0:T(8,128)(2,1)S(1)} %get-tuple-element.72), channel_id=1, source_target_pairs={{1,0},{2,1},{3,2},{4,3},{5,4},{6,5},{7,6},{9,8},{10,9},{11,10},{12... | collective-permute-start | bytes 1966088 | tf_op jit(solution)/shard_map/ppermute | solution.py:658
  59.0 1.0 shard_map.394
  60.0 3.0 %collective-permute-start.14 = (bf16[16,16,896]{2,1,0:T(8,128)(2,1)S(1)}, bf16[16,16,896]{2,1,0:T(8,128)(2,1)S(1)}, u32[]{:S(2)}, u32[]{:S(2)}) collective-permute-start(bf16[16,16,896]{2,1,0:T(8,128)(2,1)S(1)} %slice.85), channel_id=1, source_target_pairs={{0,1},{1,0},{2,3},{3,2},{4,5},{5,4},{6,7},{7,6},{8,9},{9,8},{10,11... | collective-permute-start | bytes 1376264 | tf_op jit(solution)/shard_map/ppermute | solution.py:540
  63.0 0.5 collective-permute-done.13.refs_2_
  63.5 3.6 %shard_map.393 = (bf16[16,48,256]{2,1,0:T(8,128)(2,1)}, bf16[32,16,512]{2,1,0:T(8,128)(2,1)S(1)}) custom-call(f32[768,512]{1,0:T(8,128)S(1)} %get-tuple-element.70.refs_0_, bf16[640,512]{1,0:T(8,128)(2,1)S(1)} %collective-permute-done.12.refs_1_, bf16[640,512]{1,0:T(8,128)(2,1)S(1)} %collective-permute-done.13.refs_2_, ...), custom_call_target="tpu_custom_call" | custom-call | flops 1000000000 | bytes 1000000 | tf_op jit(solution)/shard_map/pallas_call | solution.py:517
  67.1 8.5 %collective-permute-start.18 = (bf16[16,16,512]{2,1,0:T(8,128)(2,1)S(1)}, bf16[16,16,512]{2,1,0:T(8,128)(2,1)S(1)}, u32[]{:S(2)}, u32[]{:S(2)}) collective-permute-start(bf16[16,16,512]{2,1,0:T(8,128)(2,1)S(1)} %slice.75), channel_id=1, source_target_pairs={{0,1},{1,0},{2,3},{3,2},{4,5},{5,4},{6,7},{7,6},{8,9},{9,8},{10,11... | collective-permute-start | bytes 786440 | tf_op jit(solution)/shard_map/ppermute | solution.py:540
  75.6 0.1 fusion.8
  75.8 1.6 %collective-permute-start.15 = (bf16[4,16,896]{2,1,0:T(8,128)(2,1)S(1)}, bf16[4,16,896]{2,1,0:T(8,128)(2,1)S(1)}, u32[]{:S(2)}, u32[]{:S(2)}) collective-permute-start(bf16[4,16,896]{2,1,0:T(8,128)(2,1)S(1)} %get-tuple-element.120), channel_id=1, source_target_pairs={{0,8},{1,9},{2,10},{3,11},{4,12},{5,13},{6,14},{7,15},{8,0},{9,1},... | collective-permute-start | bytes 344072 | tf_op jit(solution)/shard_map/ppermute | solution.py:540
  77.3 1.5 %collective-permute-start.17 = (bf16[4,16,896]{2,1,0:T(8,128)(2,1)S(1)}, bf16[4,16,896]{2,1,0:T(8,128)(2,1)S(1)}, u32[]{:S(2)}, u32[]{:S(2)}) collective-permute-start(bf16[4,16,896]{2,1,0:T(8,128)(2,1)S(1)} %get-tuple-element.121), channel_id=1, source_target_pairs={{0,24},{1,25},{2,26},{3,27},{4,28},{5,29},{6,30},{7,31},{8,16},{9,... | collective-permute-start | bytes 344072 | tf_op jit(solution)/shard_map/ppermute | solution.py:540
  78.8 0.5 collective-permute-start.16
  79.3 0.1 fusion.7
  79.4 1.6 %collective-permute-start.19 = (bf16[4,16,512]{2,1,0:T(8,128)(2,1)S(1)}, bf16[4,16,512]{2,1,0:T(8,128)(2,1)S(1)}, u32[]{:S(2)}, u32[]{:S(2)}) collective-permute-start(bf16[4,16,512]{2,1,0:T(8,128)(2,1)S(1)} %get-tuple-element.125), channel_id=1, source_target_pairs={{0,8},{1,9},{2,10},{3,11},{4,12},{5,13},{6,14},{7,15},{8,0},{9,1},... | collective-permute-start | bytes 196616 | tf_op jit(solution)/shard_map/ppermute | solution.py:540
  81.0 1.5 %collective-permute-start.21 = (bf16[4,16,512]{2,1,0:T(8,128)(2,1)S(1)}, bf16[4,16,512]{2,1,0:T(8,128)(2,1)S(1)}, u32[]{:S(2)}, u32[]{:S(2)}) collective-permute-start(bf16[4,16,512]{2,1,0:T(8,128)(2,1)S(1)} %get-tuple-element.126), channel_id=1, source_target_pairs={{0,24},{1,25},{2,26},{3,27},{4,28},{5,29},{6,30},{7,31},{8,16},{9,... | collective-permute-start | bytes 196616 | tf_op jit(solution)/shard_map/ppermute | solution.py:540
  82.5 0.9 collective-permute-start.20
  83.4 1.9 %collective-permute-done.17 = bf16[4,16,896]{2,1,0:T(8,128)(2,1)S(1)} collective-permute-done((bf16[4,16,896]{2,1,0:T(8,128)(2,1)S(1)}, bf16[4,16,896]{2,1,0:T(8,128)(2,1)S(1)}, u32[]{:S(2)}, u32[]{:S(2)}) %collective-permute-start.17) | collective-permute-done | bytes 114720 | tf_op jit(solution)/shard_map/ppermute | solution.py:540
  85.3 2.6 %collective-permute-done.16 = bf16[4,16,896]{2,1,0:T(8,128)(2,1)S(1)} collective-permute-done((bf16[4,16,896]{2,1,0:T(8,128)(2,1)S(1)}, bf16[4,16,896]{2,1,0:T(8,128)(2,1)S(1)}, u32[]{:S(2)}, u32[]{:S(2)}) %collective-permute-start.16) | collective-permute-done | bytes 114720 | tf_op jit(solution)/shard_map/ppermute | solution.py:540
  88.1 0.1 fusion.2
  88.1 0.4 collective-permute-done.20
  88.7 1.7 %collective-permute-start.24 = (bf16[16,1408]{1,0:T(8,128)(2,1)S(1)}, bf16[16,1408]{1,0:T(8,128)(2,1)S(1)}, u32[]{:S(2)}, u32[]{:S(2)}) collective-permute-start(bf16[16,1408]{1,0:T(8,128)(2,1)S(1)} %get-tuple-element.128), channel_id=1, source_target_pairs={{0,6},{1,7},{2,4},{3,5},{4,2},{5,3},{6,0},{7,1},{8,14},{9,15},{10,... | collective-permute-start | bytes 135176 | tf_op jit(solution)/shard_map/ppermute | solution.py:540
  90.4 1.2 %collective-permute-start.23 = (bf16[16,1408]{1,0:T(8,128)(2,1)S(1)}, bf16[16,1408]{1,0:T(8,128)(2,1)S(1)}, u32[]{:S(2)}, u32[]{:S(2)}) collective-permute-start(bf16[16,1408]{1,0:T(8,128)(2,1)S(1)} %get-tuple-element.129), channel_id=1, source_target_pairs={{0,4},{1,5},{2,6},{3,7},{4,0},{5,1},{6,2},{7,3},{8,12},{9,13},{10,... | collective-permute-start | bytes 135176 | tf_op jit(solution)/shard_map/ppermute | solution.py:540
  91.6 1.6 %collective-permute-start.22 = (bf16[16,1408]{1,0:T(8,128)(2,1)S(1)}, bf16[16,1408]{1,0:T(8,128)(2,1)S(1)}, u32[]{:S(2)}, u32[]{:S(2)}) collective-permute-start(bf16[16,1408]{1,0:T(8,128)(2,1)S(1)} %get-tuple-element.130), channel_id=1, source_target_pairs={{0,2},{1,3},{2,0},{3,1},{4,6},{5,7},{6,4},{7,5},{8,10},{9,11},{10,... | collective-permute-start | bytes 135176 | tf_op jit(solution)/shard_map/ppermute | solution.py:540
  93.1 1.9 %collective-permute-done.24.refs_3_ = bf16[16,1408]{1,0:T(8,128)(2,1)S(1)} collective-permute-done((bf16[16,1408]{1,0:T(8,128)(2,1)S(1)}, bf16[16,1408]{1,0:T(8,128)(2,1)S(1)}, u32[]{:S(2)}, u32[]{:S(2)}) %collective-permute-start.24) | collective-permute-done | bytes 45088 | tf_op jit(solution)/shard_map/ppermute | solution.py:540
  95.1 0.9 collective-permute-done.23.refs_2_
  96.1 0.9 shard_map.395
  97.0 0.1 collective-permute-start.25
  97.1 1.2 %collective-permute-done.25 = f32[8,128]{1,0:T(8,128)S(1)} collective-permute-done((f32[8,128]{1,0:T(8,128)S(1)}, f32[8,128]{1,0:T(8,128)S(1)}, u32[]{:S(2)}, u32[]{:S(2)}) %collective-permute-start.25) | collective-permute-done | bytes 4128 | tf_op jit(solution)/shard_map/ppermute | solution.py:540
  98.2 1.4 %collective-permute-start.28 = (f32[8,128]{1,0:T(8,128)S(1)}, f32[8,128]{1,0:T(8,128)S(1)}, u32[]{:S(2)}, u32[]{:S(2)}) collective-permute-start(f32[8,128]{1,0:T(8,128)S(1)} %add.44), channel_id=1, source_target_pairs={{0,24},{1,25},{2,26},{3,27},{4,28},{5,29},{6,30},{7,31},{8,16},{9,... | collective-permute-start | bytes 12296 | tf_op jit(solution)/shard_map/ppermute | solution.py:540
  99.7 1.5 %collective-permute-start.27 = (f32[8,128]{1,0:T(8,128)S(1)}, f32[8,128]{1,0:T(8,128)S(1)}, u32[]{:S(2)}, u32[]{:S(2)}) collective-permute-start(f32[8,128]{1,0:T(8,128)S(1)} %add.44), channel_id=1, source_target_pairs={{0,16},{1,17},{2,18},{3,19},{4,20},{5,21},{6,22},{7,23},{8,24},{9,... | collective-permute-start | bytes 12296 | tf_op jit(solution)/shard_map/ppermute | solution.py:540
  101.2 0.5 collective-permute-start.26
  101.7 1.0 collective-permute-done.28
  102.7 0.5 collective-permute-done.27
  103.3 1.5 %collective-permute-done.26 = f32[8,128]{1,0:T(8,128)S(1)} collective-permute-done((f32[8,128]{1,0:T(8,128)S(1)}, f32[8,128]{1,0:T(8,128)S(1)}, u32[]{:S(2)}, u32[]{:S(2)}) %collective-permute-start.26) | collective-permute-done | bytes 4128 | tf_op jit(solution)/shard_map/ppermute | solution.py:540
  104.8 2.3 %collective-permute-start.31 = (f32[8,128]{1,0:T(8,128)S(1)}, f32[8,128]{1,0:T(8,128)S(1)}, u32[]{:S(2)}, u32[]{:S(2)}) collective-permute-start(f32[8,128]{1,0:T(8,128)S(1)} %add_add_fusion.a_ref), channel_id=1, source_target_pairs={{0,6},{1,7},{2,4},{3,5},{4,2},{5,3},{6,0},{7,1},{8,14},{9,15},{10,... | collective-permute-start | bytes 12296 | tf_op jit(solution)/shard_map/ppermute | solution.py:540
  107.0 0.4 collective-permute-start.30
  107.5 1.7 %collective-permute-start.29 = (f32[8,128]{1,0:T(8,128)S(1)}, f32[8,128]{1,0:T(8,128)S(1)}, u32[]{:S(2)}, u32[]{:S(2)}) collective-permute-start(f32[8,128]{1,0:T(8,128)S(1)} %add_add_fusion.a_ref), channel_id=1, source_target_pairs={{0,2},{1,3},{2,0},{3,1},{4,6},{5,7},{6,4},{7,5},{8,10},{9,11},{10,... | collective-permute-start | bytes 12296 | tf_op jit(solution)/shard_map/ppermute | solution.py:540
  109.2 1.0 collective-permute-done.31.d_ref
  110.2 1.4 %collective-permute-done.30.c_ref = f32[8,128]{1,0:T(8,128)S(1)} collective-permute-done((f32[8,128]{1,0:T(8,128)S(1)}, f32[8,128]{1,0:T(8,128)S(1)}, u32[]{:S(2)}, u32[]{:S(2)}) %collective-permute-start.30) | collective-permute-done | bytes 4128 | tf_op jit(solution)/shard_map/ppermute | solution.py:540
  111.6 0.8 shard_map.396
  (77 shorter events, 0.4 us)
Async XLA Ops:
  0.7 27.3 %copy-start.1 = (bf16[192,192]{1,0:T(8,128)(2,1)S(1)}, bf16[192,192]{1,0:T(8,128)(2,1)}, u32[]{:S(2)}) copy-start(bf16[192,192]{1,0:T(8,128)(2,1)} %constant.4.clone.po_ref.refs_8_) | copy-start | bytes 221188
  0.7 27.3 %copy-start = (bf16[16,48,256]{2,1,0:T(8,128)(2,1)S(1)}, bf16[16,48,256]{2,1,0:T(8,128)(2,1)}, u32[]{:S(2)}) copy-start(bf16[16,48,256]{2,1,0:T(8,128)(2,1)} %refs_5_.3) | copy-start | bytes 1179652
  0.7 0.8 copy-start.8
  1.5 0.7 copy-start.10
  2.2 0.7 copy-start.12
  3.0 0.7 copy-start.16
  3.7 0.7 copy-start.22
  4.3 23.6 %copy-start.24 = (f32[8,49]{1,0:T(8,128)S(1)}, f32[8,49]{1,0:T(8,128)}, u32[]{:S(2)}) copy-start(f32[8,49]{1,0:T(8,128)} %refs_5_.5) | copy-start | bytes 4708
  4.3 23.6 %copy-start.25 = (bf16[16,48,256]{2,1,0:T(8,128)(2,1)S(1)}, bf16[16,48,256]{2,1,0:T(8,128)(2,1)}, u32[]{:S(2)}) copy-start(bf16[16,48,256]{2,1,0:T(8,128)(2,1)} %cot_ref.1) | copy-start | bytes 1179652
  4.3 23.6 %copy-start.26 = (s32[1,2]{1,0:T(1,128)S(1)}, s32[1,2]{1,0:T(1,128)}, u32[]{:S(2)}) copy-start(s32[1,2]{1,0:T(1,128)} %sizes_ref.1) | copy-start | bytes 28
  4.3 23.6 %copy-start.27 = (bf16[512,480]{1,0:T(8,128)(2,1)S(1)}, bf16[512,480]{1,0:T(8,128)(2,1)}, u32[]{:S(2)}) copy-start(bf16[512,480]{1,0:T(8,128)(2,1)} %constant.5.clone.pk_ref) | copy-start | bytes 1474564
  4.4 7.2 %collective-permute-start.4 = (bf16[16,1408]{1,0:T(8,128)(2,1)S(1)}, bf16[16,1408]{1,0:T(8,128)(2,1)S(1)}, u32[]{:S(2)}, u32[]{:S(2)}) collective-permute-start(bf16[16,1408]{1,0:T(8,128)(2,1)S(1)} %shard_map.390.refs_0_), channel_id=1, source_target_pairs={{0,6},{1,7},{2,4},{3,5},{4,2},{5,3},{6,0},{7,1},{8,14},{9,15},{10,... | collective-permute-start | bytes 135176 | tf_op jit(solution)/shard_map/ppermute | solution.py:540
  9.5 4.9 %collective-permute-start.3 = (bf16[16,1408]{1,0:T(8,128)(2,1)S(1)}, bf16[16,1408]{1,0:T(8,128)(2,1)S(1)}, u32[]{:S(2)}, u32[]{:S(2)}) collective-permute-start(bf16[16,1408]{1,0:T(8,128)(2,1)S(1)} %shard_map.390.refs_0_), channel_id=1, source_target_pairs={{0,4},{1,5},{2,6},{3,7},{4,0},{5,1},{6,2},{7,3},{8,12},{9,13},{10,... | collective-permute-start | bytes 135176 | tf_op jit(solution)/shard_map/ppermute | solution.py:540
  9.5 4.9 %collective-permute-start.2 = (bf16[16,1408]{1,0:T(8,128)(2,1)S(1)}, bf16[16,1408]{1,0:T(8,128)(2,1)S(1)}, u32[]{:S(2)}, u32[]{:S(2)}) collective-permute-start(bf16[16,1408]{1,0:T(8,128)(2,1)S(1)} %shard_map.390.refs_0_), channel_id=1, source_target_pairs={{0,2},{1,3},{2,0},{3,1},{4,6},{5,7},{6,4},{7,5},{8,10},{9,11},{10,... | collective-permute-start | bytes 135176 | tf_op jit(solution)/shard_map/ppermute | solution.py:540
  14.4 6.0 %collective-permute-start.8 = (bf16[4,16,1408]{2,1,0:T(8,128)(2,1)S(1)}, bf16[4,16,1408]{2,1,0:T(8,128)(2,1)S(1)}, u32[]{:S(2)}, u32[]{:S(2)}) collective-permute-start(bf16[4,16,1408]{2,1,0:T(8,128)(2,1)S(1)} %shard_map.391.b0), channel_id=1, source_target_pairs={{0,1},{1,0},{2,3},{3,2},{4,5},{5,4},{6,7},{7,6},{8,9},{9,8},{10,11... | collective-permute-start | bytes 540680 | tf_op jit(solution)/shard_map/ppermute | solution.py:540
  14.5 9.0 %collective-permute-start.7 = (bf16[4,16,1408]{2,1,0:T(8,128)(2,1)S(1)}, bf16[4,16,1408]{2,1,0:T(8,128)(2,1)S(1)}, u32[]{:S(2)}, u32[]{:S(2)}) collective-permute-start(bf16[4,16,1408]{2,1,0:T(8,128)(2,1)S(1)} %shard_map.391.b0), channel_id=1, source_target_pairs={{0,24},{1,25},{2,26},{3,27},{4,28},{5,29},{6,30},{7,31},{8,16},{9,... | collective-permute-start | bytes 540680 | tf_op jit(solution)/shard_map/ppermute | solution.py:540
  17.0 9.2 %collective-permute-start.6 = (bf16[4,16,1408]{2,1,0:T(8,128)(2,1)S(1)}, bf16[4,16,1408]{2,1,0:T(8,128)(2,1)S(1)}, u32[]{:S(2)}, u32[]{:S(2)}) collective-permute-start(bf16[4,16,1408]{2,1,0:T(8,128)(2,1)S(1)} %shard_map.391.b0), channel_id=1, source_target_pairs={{0,16},{1,17},{2,18},{3,19},{4,20},{5,21},{6,22},{7,23},{8,24},{9,... | collective-permute-start | bytes 540680 | tf_op jit(solution)/shard_map/ppermute | solution.py:540
  17.5 8.8 %collective-permute-start.5 = (bf16[4,16,1408]{2,1,0:T(8,128)(2,1)S(1)}, bf16[4,16,1408]{2,1,0:T(8,128)(2,1)S(1)}, u32[]{:S(2)}, u32[]{:S(2)}) collective-permute-start(bf16[4,16,1408]{2,1,0:T(8,128)(2,1)S(1)} %shard_map.391.b0), channel_id=1, source_target_pairs={{0,8},{1,9},{2,10},{3,11},{4,12},{5,13},{6,14},{7,15},{8,0},{9,1},... | collective-permute-start | bytes 540680 | tf_op jit(solution)/shard_map/ppermute | solution.py:540
  19.2 7.6 %collective-permute-start.1 = (bf16[12,48,256]{2,1,0:T(8,128)(2,1)S(1)}, bf16[12,48,256]{2,1,0:T(8,128)(2,1)S(1)}, u32[]{:S(2)}, u32[]{:S(2)}) collective-permute-start(bf16[12,48,256]{2,1,0:T(8,128)(2,1)S(1)} %get-tuple-element.123), channel_id=1, source_target_pairs={{1,0},{2,1},{3,2},{4,3},{5,4},{6,5},{7,6},{9,8},{10,9},{11,10},{12... | collective-permute-start | bytes 884744 | tf_op jit(solution)/shard_map/ppermute | solution.py:628
  20.5 6.3 %collective-permute-start = (bf16[12,48,256]{2,1,0:T(8,128)(2,1)S(1)}, bf16[12,48,256]{2,1,0:T(8,128)(2,1)S(1)}, u32[]{:S(2)}, u32[]{:S(2)}) collective-permute-start(bf16[12,48,256]{2,1,0:T(8,128)(2,1)S(1)} %get-tuple-element.124), channel_id=1, source_target_pairs={{0,1},{1,2},{2,3},{3,4},{4,5},{5,6},{6,7},{8,9},{9,10},{10,11},{11... | collective-permute-start | bytes 884744 | tf_op jit(solution)/shard_map/ppermute | solution.py:627
  23.6 3.2 %collective-permute-start.11 = (bf16[4,16,1408]{2,1,0:T(8,128)(2,1)S(1)}, bf16[4,16,1408]{2,1,0:T(8,128)(2,1)S(1)}, u32[]{:S(2)}, u32[]{:S(2)}) collective-permute-start(bf16[4,16,1408]{2,1,0:T(8,128)(2,1)S(1)} %collective-permute-done.7.b3), channel_id=1, source_target_pairs={{0,1},{1,0},{2,3},{3,2},{4,5},{5,4},{6,7},{7,6},{8,9},{9,8},{10,11... | collective-permute-start | bytes 540680 | tf_op jit(solution)/shard_map/ppermute | solution.py:540
  26.3 1.4 %collective-permute-start.10 = (bf16[4,16,1408]{2,1,0:T(8,128)(2,1)S(1)}, bf16[4,16,1408]{2,1,0:T(8,128)(2,1)S(1)}, u32[]{:S(2)}, u32[]{:S(2)}) collective-permute-start(bf16[4,16,1408]{2,1,0:T(8,128)(2,1)S(1)} %collective-permute-done.6.b2), channel_id=1, source_target_pairs={{0,1},{1,0},{2,3},{3,2},{4,5},{5,4},{6,7},{7,6},{8,9},{9,8},{10,11... | collective-permute-start | bytes 540680 | tf_op jit(solution)/shard_map/ppermute | solution.py:540
  26.4 1.6 %collective-permute-start.9 = (bf16[4,16,1408]{2,1,0:T(8,128)(2,1)S(1)}, bf16[4,16,1408]{2,1,0:T(8,128)(2,1)S(1)}, u32[]{:S(2)}, u32[]{:S(2)}) collective-permute-start(bf16[4,16,1408]{2,1,0:T(8,128)(2,1)S(1)} %collective-permute-done.5.b1), channel_id=1, source_target_pairs={{0,1},{1,0},{2,3},{3,2},{4,5},{5,4},{6,7},{7,6},{8,9},{9,8},{10,11... | collective-permute-start | bytes 540680 | tf_op jit(solution)/shard_map/ppermute | solution.py:540
  55.5 7.5 %collective-permute-start.12 = (bf16[640,512]{1,0:T(8,128)(2,1)S(1)}, bf16[640,512]{1,0:T(8,128)(2,1)S(1)}, u32[]{:S(2)}, u32[]{:S(2)}) collective-permute-start(bf16[640,512]{1,0:T(8,128)(2,1)S(1)} %get-tuple-element.71), channel_id=1, source_target_pairs={{0,1},{1,2},{2,3},{3,4},{4,5},{5,6},{6,7},{8,9},{9,10},{10,11},{11... | collective-permute-start | bytes 1966088 | tf_op jit(solution)/shard_map/ppermute | solution.py:657
  57.7 5.8 %collective-permute-start.13 = (bf16[640,512]{1,0:T(8,128)(2,1)S(1)}, bf16[640,512]{1,0:T(8,128)(2,1)S(1)}, u32[]{:S(2)}, u32[]{:S(2)}) collective-permute-start(bf16[640,512]{1,0:T(8,128)(2,1)S(1)} %get-tuple-element.72), channel_id=1, source_target_pairs={{1,0},{2,1},{3,2},{4,3},{5,4},{6,5},{7,6},{9,8},{10,9},{11,10},{12... | collective-permute-start | bytes 1966088 | tf_op jit(solution)/shard_map/ppermute | solution.py:658
  60.0 15.6 %collective-permute-start.14 = (bf16[16,16,896]{2,1,0:T(8,128)(2,1)S(1)}, bf16[16,16,896]{2,1,0:T(8,128)(2,1)S(1)}, u32[]{:S(2)}, u32[]{:S(2)}) collective-permute-start(bf16[16,16,896]{2,1,0:T(8,128)(2,1)S(1)} %slice.85), channel_id=1, source_target_pairs={{0,1},{1,0},{2,3},{3,2},{4,5},{5,4},{6,7},{7,6},{8,9},{9,8},{10,11... | collective-permute-start | bytes 1376264 | tf_op jit(solution)/shard_map/ppermute | solution.py:540
  67.1 12.2 %collective-permute-start.18 = (bf16[16,16,512]{2,1,0:T(8,128)(2,1)S(1)}, bf16[16,16,512]{2,1,0:T(8,128)(2,1)S(1)}, u32[]{:S(2)}, u32[]{:S(2)}) collective-permute-start(bf16[16,16,512]{2,1,0:T(8,128)(2,1)S(1)} %slice.75), channel_id=1, source_target_pairs={{0,1},{1,0},{2,3},{3,2},{4,5},{5,4},{6,7},{7,6},{8,9},{9,8},{10,11... | collective-permute-start | bytes 786440 | tf_op jit(solution)/shard_map/ppermute | solution.py:540
  75.8 6.7 %collective-permute-start.15 = (bf16[4,16,896]{2,1,0:T(8,128)(2,1)S(1)}, bf16[4,16,896]{2,1,0:T(8,128)(2,1)S(1)}, u32[]{:S(2)}, u32[]{:S(2)}) collective-permute-start(bf16[4,16,896]{2,1,0:T(8,128)(2,1)S(1)} %get-tuple-element.120), channel_id=1, source_target_pairs={{0,8},{1,9},{2,10},{3,11},{4,12},{5,13},{6,14},{7,15},{8,0},{9,1},... | collective-permute-start | bytes 344072 | tf_op jit(solution)/shard_map/ppermute | solution.py:540
  77.3 8.0 %collective-permute-start.17 = (bf16[4,16,896]{2,1,0:T(8,128)(2,1)S(1)}, bf16[4,16,896]{2,1,0:T(8,128)(2,1)S(1)}, u32[]{:S(2)}, u32[]{:S(2)}) collective-permute-start(bf16[4,16,896]{2,1,0:T(8,128)(2,1)S(1)} %get-tuple-element.121), channel_id=1, source_target_pairs={{0,24},{1,25},{2,26},{3,27},{4,28},{5,29},{6,30},{7,31},{8,16},{9,... | collective-permute-start | bytes 344072 | tf_op jit(solution)/shard_map/ppermute | solution.py:540
  78.8 9.1 %collective-permute-start.16 = (bf16[4,16,896]{2,1,0:T(8,128)(2,1)S(1)}, bf16[4,16,896]{2,1,0:T(8,128)(2,1)S(1)}, u32[]{:S(2)}, u32[]{:S(2)}) collective-permute-start(bf16[4,16,896]{2,1,0:T(8,128)(2,1)S(1)} %get-tuple-element.122), channel_id=1, source_target_pairs={{0,16},{1,17},{2,18},{3,19},{4,20},{5,21},{6,22},{7,23},{8,24},{9,... | collective-permute-start | bytes 344072 | tf_op jit(solution)/shard_map/ppermute | solution.py:540
  79.4 8.7 %collective-permute-start.19 = (bf16[4,16,512]{2,1,0:T(8,128)(2,1)S(1)}, bf16[4,16,512]{2,1,0:T(8,128)(2,1)S(1)}, u32[]{:S(2)}, u32[]{:S(2)}) collective-permute-start(bf16[4,16,512]{2,1,0:T(8,128)(2,1)S(1)} %get-tuple-element.125), channel_id=1, source_target_pairs={{0,8},{1,9},{2,10},{3,11},{4,12},{5,13},{6,14},{7,15},{8,0},{9,1},... | collective-permute-start | bytes 196616 | tf_op jit(solution)/shard_map/ppermute | solution.py:540
  81.0 7.1 %collective-permute-start.21 = (bf16[4,16,512]{2,1,0:T(8,128)(2,1)S(1)}, bf16[4,16,512]{2,1,0:T(8,128)(2,1)S(1)}, u32[]{:S(2)}, u32[]{:S(2)}) collective-permute-start(bf16[4,16,512]{2,1,0:T(8,128)(2,1)S(1)} %get-tuple-element.126), channel_id=1, source_target_pairs={{0,24},{1,25},{2,26},{3,27},{4,28},{5,29},{6,30},{7,31},{8,16},{9,... | collective-permute-start | bytes 196616 | tf_op jit(solution)/shard_map/ppermute | solution.py:540
  82.5 6.1 %collective-permute-start.20 = (bf16[4,16,512]{2,1,0:T(8,128)(2,1)S(1)}, bf16[4,16,512]{2,1,0:T(8,128)(2,1)S(1)}, u32[]{:S(2)}, u32[]{:S(2)}) collective-permute-start(bf16[4,16,512]{2,1,0:T(8,128)(2,1)S(1)} %get-tuple-element.127), channel_id=1, source_target_pairs={{0,16},{1,17},{2,18},{3,19},{4,20},{5,21},{6,22},{7,23},{8,24},{9,... | collective-permute-start | bytes 196616 | tf_op jit(solution)/shard_map/ppermute | solution.py:540
  87.9 8.1 %copy-start.2 = (f32[8,768]{1,0:T(8,128)S(1)}, f32[8,768]{1,0:T(8,128)}, u32[]{:S(2)}) copy-start(f32[8,768]{1,0:T(8,128)} %refs_10_.1) | copy-start | bytes 73732
  87.9 8.1 %copy-start.3 = (f32[8,768]{1,0:T(8,128)S(1)}, f32[8,768]{1,0:T(8,128)}, u32[]{:S(2)}) copy-start(f32[8,768]{1,0:T(8,128)} %refs_12_.1) | copy-start | bytes 73732
  87.9 8.1 %copy-start.4 = (f32[24,256]{1,0:T(8,128)S(1)}, f32[24,256]{1,0:T(8,128)}, u32[]{:S(2)}) copy-start(f32[24,256]{1,0:T(8,128)} %refs_13_.1) | copy-start | bytes 73732
  87.9 8.1 %copy-start.5 = (f32[8,768]{1,0:T(8,128)S(1)}, f32[8,768]{1,0:T(8,128)}, u32[]{:S(2)}) copy-start(f32[8,768]{1,0:T(8,128)} %refs_16_.1) | copy-start | bytes 73732
  87.9 8.1 %copy-start.6 = (f32[8,768]{1,0:T(8,128)S(1)}, f32[8,768]{1,0:T(8,128)}, u32[]{:S(2)}) copy-start(f32[8,768]{1,0:T(8,128)} %refs_18_.1) | copy-start | bytes 73732
  87.9 8.1 %copy-start.7 = (f32[24,256]{1,0:T(8,128)S(1)}, f32[24,256]{1,0:T(8,128)}, u32[]{:S(2)}) copy-start(f32[24,256]{1,0:T(8,128)} %refs_19_.1) | copy-start | bytes 73732
  87.9 8.1 %copy-start.9 = (f32[8,768]{1,0:T(8,128)S(1)}, f32[8,768]{1,0:T(8,128)}, u32[]{:S(2)}) copy-start(f32[8,768]{1,0:T(8,128)} %refs_0_.1) | copy-start | bytes 73732
  87.9 8.1 %copy-start.11 = (f32[8,768]{1,0:T(8,128)S(1)}, f32[8,768]{1,0:T(8,128)}, u32[]{:S(2)}) copy-start(f32[8,768]{1,0:T(8,128)} %refs_2_.1) | copy-start | bytes 73732
  87.9 8.1 %copy-start.13 = (f32[24,256]{1,0:T(8,128)S(1)}, f32[24,256]{1,0:T(8,128)}, u32[]{:S(2)}) copy-start(f32[24,256]{1,0:T(8,128)} %refs_3_.1) | copy-start | bytes 73732
  88.0 8.1 %copy-start.14 = (f32[8,256]{1,0:T(8,128)S(1)}, f32[8,256]{1,0:T(8,128)}, u32[]{:S(2)}) copy-start(f32[8,256]{1,0:T(8,128)} %refs_11_.1) | copy-start | bytes 24580
  88.0 8.1 %copy-start.15 = (f32[8,256]{1,0:T(8,128)S(1)}, f32[8,256]{1,0:T(8,128)}, u32[]{:S(2)}) copy-start(f32[8,256]{1,0:T(8,128)} %refs_17_.1) | copy-start | bytes 24580
  88.0 8.1 %copy-start.17 = (f32[8,256]{1,0:T(8,128)S(1)}, f32[8,256]{1,0:T(8,128)}, u32[]{:S(2)}) copy-start(f32[8,256]{1,0:T(8,128)} %refs_1_.1) | copy-start | bytes 24580
  88.0 8.1 %copy-start.18 = (f32[11,8]{0,1:T(8,128)S(1)}, f32[11,8]{0,1:T(8,128)}, u32[]{:S(2)}) copy-start(f32[11,8]{0,1:T(8,128)} %param.40) | copy-start | bytes 1060
  88.0 8.1 %copy-start.19 = (f32[8,49]{1,0:T(8,128)S(1)}, f32[8,49]{1,0:T(8,128)}, u32[]{:S(2)}) copy-start(f32[8,49]{1,0:T(8,128)} %refs_15_.1) | copy-start | bytes 4708
  88.0 8.1 %copy-start.20 = (f32[11,8]{0,1:T(8,128)S(1)}, f32[11,8]{0,1:T(8,128)}, u32[]{:S(2)}) copy-start(f32[11,8]{0,1:T(8,128)} %param.41) | copy-start | bytes 1060
  88.0 8.1 %copy-start.21 = (f32[8,49]{1,0:T(8,128)S(1)}, f32[8,49]{1,0:T(8,128)}, u32[]{:S(2)}) copy-start(f32[8,49]{1,0:T(8,128)} %refs_21_.1) | copy-start | bytes 4708
  88.0 8.1 %copy-start.23 = (f32[11,8]{0,1:T(8,128)S(1)}, f32[11,8]{0,1:T(8,128)}, u32[]{:S(2)}) copy-start(f32[11,8]{0,1:T(8,128)} %param.30) | copy-start | bytes 1060
  88.7 6.4 %collective-permute-start.24 = (bf16[16,1408]{1,0:T(8,128)(2,1)S(1)}, bf16[16,1408]{1,0:T(8,128)(2,1)S(1)}, u32[]{:S(2)}, u32[]{:S(2)}) collective-permute-start(bf16[16,1408]{1,0:T(8,128)(2,1)S(1)} %get-tuple-element.128), channel_id=1, source_target_pairs={{0,6},{1,7},{2,4},{3,5},{4,2},{5,3},{6,0},{7,1},{8,14},{9,15},{10,... | collective-permute-start | bytes 135176 | tf_op jit(solution)/shard_map/ppermute | solution.py:540
  90.4 5.5 %collective-permute-start.23 = (bf16[16,1408]{1,0:T(8,128)(2,1)S(1)}, bf16[16,1408]{1,0:T(8,128)(2,1)S(1)}, u32[]{:S(2)}, u32[]{:S(2)}) collective-permute-start(bf16[16,1408]{1,0:T(8,128)(2,1)S(1)} %get-tuple-element.129), channel_id=1, source_target_pairs={{0,4},{1,5},{2,6},{3,7},{4,0},{5,1},{6,2},{7,3},{8,12},{9,13},{10,... | collective-permute-start | bytes 135176 | tf_op jit(solution)/shard_map/ppermute | solution.py:540
  91.6 4.4 %collective-permute-start.22 = (bf16[16,1408]{1,0:T(8,128)(2,1)S(1)}, bf16[16,1408]{1,0:T(8,128)(2,1)S(1)}, u32[]{:S(2)}, u32[]{:S(2)}) collective-permute-start(bf16[16,1408]{1,0:T(8,128)(2,1)S(1)} %get-tuple-element.130), channel_id=1, source_target_pairs={{0,2},{1,3},{2,0},{3,1},{4,6},{5,7},{6,4},{7,5},{8,10},{9,11},{10,... | collective-permute-start | bytes 135176 | tf_op jit(solution)/shard_map/ppermute | solution.py:540
  97.0 1.2 %collective-permute-start.25 = (f32[8,128]{1,0:T(8,128)S(1)}, f32[8,128]{1,0:T(8,128)S(1)}, u32[]{:S(2)}, u32[]{:S(2)}) collective-permute-start(f32[8,128]{1,0:T(8,128)S(1)} %get-tuple-element.91.mine_ref), channel_id=1, source_target_pairs={{0,1},{1,0},{2,3},{3,2},{4,5},{5,4},{6,7},{7,6},{8,9},{9,8},{10,11... | collective-permute-start | bytes 12296 | tf_op jit(solution)/shard_map/ppermute | solution.py:540
  98.2 4.5 %collective-permute-start.28 = (f32[8,128]{1,0:T(8,128)S(1)}, f32[8,128]{1,0:T(8,128)S(1)}, u32[]{:S(2)}, u32[]{:S(2)}) collective-permute-start(f32[8,128]{1,0:T(8,128)S(1)} %add.44), channel_id=1, source_target_pairs={{0,24},{1,25},{2,26},{3,27},{4,28},{5,29},{6,30},{7,31},{8,16},{9,... | collective-permute-start | bytes 12296 | tf_op jit(solution)/shard_map/ppermute | solution.py:540
  99.7 3.6 %collective-permute-start.27 = (f32[8,128]{1,0:T(8,128)S(1)}, f32[8,128]{1,0:T(8,128)S(1)}, u32[]{:S(2)}, u32[]{:S(2)}) collective-permute-start(f32[8,128]{1,0:T(8,128)S(1)} %add.44), channel_id=1, source_target_pairs={{0,16},{1,17},{2,18},{3,19},{4,20},{5,21},{6,22},{7,23},{8,24},{9,... | collective-permute-start | bytes 12296 | tf_op jit(solution)/shard_map/ppermute | solution.py:540
  101.2 3.6 %collective-permute-start.26 = (f32[8,128]{1,0:T(8,128)S(1)}, f32[8,128]{1,0:T(8,128)S(1)}, u32[]{:S(2)}, u32[]{:S(2)}) collective-permute-start(f32[8,128]{1,0:T(8,128)S(1)} %add.44), channel_id=1, source_target_pairs={{0,8},{1,9},{2,10},{3,11},{4,12},{5,13},{6,14},{7,15},{8,0},{9,1},... | collective-permute-start | bytes 12296 | tf_op jit(solution)/shard_map/ppermute | solution.py:540
  104.8 5.4 %collective-permute-start.31 = (f32[8,128]{1,0:T(8,128)S(1)}, f32[8,128]{1,0:T(8,128)S(1)}, u32[]{:S(2)}, u32[]{:S(2)}) collective-permute-start(f32[8,128]{1,0:T(8,128)S(1)} %add_add_fusion.a_ref), channel_id=1, source_target_pairs={{0,6},{1,7},{2,4},{3,5},{4,2},{5,3},{6,0},{7,1},{8,14},{9,15},{10,... | collective-permute-start | bytes 12296 | tf_op jit(solution)/shard_map/ppermute | solution.py:540
  107.0 4.5 %collective-permute-start.30 = (f32[8,128]{1,0:T(8,128)S(1)}, f32[8,128]{1,0:T(8,128)S(1)}, u32[]{:S(2)}, u32[]{:S(2)}) collective-permute-start(f32[8,128]{1,0:T(8,128)S(1)} %add_add_fusion.a_ref), channel_id=1, source_target_pairs={{0,4},{1,5},{2,6},{3,7},{4,0},{5,1},{6,2},{7,3},{8,12},{9,13},{10,... | collective-permute-start | bytes 12296 | tf_op jit(solution)/shard_map/ppermute | solution.py:540
  107.5 4.1 %collective-permute-start.29 = (f32[8,128]{1,0:T(8,128)S(1)}, f32[8,128]{1,0:T(8,128)S(1)}, u32[]{:S(2)}, u32[]{:S(2)}) collective-permute-start(f32[8,128]{1,0:T(8,128)S(1)} %add_add_fusion.a_ref), channel_id=1, source_target_pairs={{0,2},{1,3},{2,0},{3,1},{4,6},{5,7},{6,4},{7,5},{8,10},{9,11},{10,... | collective-permute-start | bytes 12296 | tf_op jit(solution)/shard_map/ppermute | solution.py:540

commit v4 on v3

--- a/solution.py
+++ b/solution.py
@@ -44,24 +44,21 @@
     return lax.dot_general(a, b, (((0,), (0,)), ((), ())), preferred_element_type=F32)
 
 
-def order_own():
-    sel = np.zeros((4 * QN, 4 * 48), np.float32)
-    for o in range(4 * QN):
-        cc, rest = divmod(o, QN)
-        qr, qc = divmod(rest, 12)
-        sel[o, qr * 48 + qc * 4 + cc] = 1
-    return sel
-
-
-def order_keys():
-    sel = np.zeros((4 * KN, 480), np.float32)
-    for o in range(4 * KN):
-        cc, slot = divmod(o, KN)
-        j = (slot + 36) % KN
-        if j < 120:
-            kr, kc = divmod(j, 12)
-            sel[o, kr * 48 + kc * 4 + cc] = 1
-    return sel
+def select(shape, source):
+    o = lax.broadcasted_iota(jnp.int32, shape, 0)
+    return (source(o) == lax.broadcasted_iota(jnp.int32, shape, 1)).astype(F32).astype(BF)
+
+
+def own_source(o):
+    cc = (o * 171) >> 13
+    qr, qc = split12(o - QN * cc)
+    return qr * 48 + qc * 4 + cc
+
+
+def key_source(o):
+    j = ((o & (KN - 1)) + 36) & (KN - 1)
+    kr, kc = split12(j)
+    return jnp.where(j < 120, kr * 48 + kc * 4 + (o >> 7), -1)
 
 
 def normed(v):
@@ -103,53 +100,11 @@
     return (((12 * (nr - 3) + nc - 3) & (KN - 1)) == lane).astype(F32)
 
 
-def layer_kernel(
-    sizes_ref,
-    x_ref,
-    xb_ref,
-    xa_ref,
-    cot_ref,
-    wqkv_ref,
-    wo_ref,
-    wu_ref,
-    wd_ref,
-    vec_ref,
-    table_ref,
-    po_ref,
-    pk_ref,
-    out_ref,
-    act_ref,
-    dy_ref,
-    dz_ref,
-    a2_ref,
-    mixed_ref,
-    da_ref,
-    a1_ref,
-    dq_ref,
-    dx1_ref,
-    own_ref,
-    rima_ref,
-    rimb_ref,
-    tgrad_ref,
-    sums_ref,
-    zsum_ref,
-    xp_ref,
-    q_ref,
-    k_ref,
-    v_ref,
-    bias_ref,
-    p_ref,
-    dmix_ref,
-    tacc_ref,
-):
-    row0 = lax.axis_index("band") * 16
-    height = sizes_ref[0, 0]
-    wide = sizes_ref[0, 1]
-    scale = 32 ** (-0.5)
-    lane_head = lax.broadcasted_iota(jnp.int32, (QN, 256), 1) >> 5
-
-    def vrow(i):
-        return vec_ref[i : i + 1, :]
+def prep_kernel(sizes_ref, table_ref, x_ref, bias_ref, limits_ref, po_ref, pk_ref, xp_ref, xhat_ref, rstd_ref):
+    po_ref[...] = select((4 * QN, 4 * 48), own_source)
+    pk_ref[...] = select((4 * KN, 10 * 48), key_source)
+    row = lax.broadcasted_iota(jnp.int32, (8, 128), 0)
+    limits_ref[...] = jnp.where(row == 0, sizes_ref[0, 0] - lax.axis_index("band") * 16, sizes_ref[0, 1])
 
     slots = lax.dot_general(
         table_ref[...],
@@ -171,29 +126,56 @@
         rows.append(jnp.where(window, line, MASKED))
     bias_ref[...] = jnp.concatenate(rows, axis=0).T
 
-    def project(rc, _):
-        own = jnp.concatenate([x_ref[4 * i + rc] for i in range(4)], axis=0)
-        xp = dot(po_ref[...], own)
+    def block(rc, _):
         at = pl.ds(pl.multiple_of(rc * 192, 192), 192)
+        xp = dot(po_ref[...], jnp.concatenate([x_ref[4 * i + rc] for i in range(4)], axis=0))
         xp_ref[at, :] = xp
-        a1 = (normed(xp)[0] * vrow(0) + vrow(1)).astype(BF)
+        xhat, rstd = normed(xp)
+        xhat_ref[at, :] = xhat
+        rstd_ref[at, :] = jnp.broadcast_to(rstd, (192, 128))
+        return 0
+
+    lax.fori_loop(0, 4, block, 0, unroll=2)
+
+
+def halo_kernel(x_ref, xc_ref, xz_ref, pk_ref, xk_ref):
+    odd = (lax.axis_index("band") & 1) == 1
+
+    def block(rc, _):
+        rows = [jnp.where(odd, xc_ref[4 + 4 * i + rc], xz_ref[4 + 4 * i + rc]) for i in range(3)]
+        rows += [x_ref[4 * i + rc] for i in range(4)]
+        rows += [jnp.where(odd, xz_ref[4 * i + rc], xc_ref[4 * i + rc]) for i in range(3)]
+        xk = dot(pk_ref[...], jnp.concatenate(rows, axis=0))
+        xk_ref[pl.ds(pl.multiple_of(rc * 512, 512), 512), :] = normed(xk)[0]
+        return 0
+
+    lax.fori_loop(0, 4, block, 0, unroll=2)
+
+
+def project_kernel(xhat_ref, xk_ref, wqkv_ref, vec_ref, a1_ref, q_ref, k_ref, v_ref):
+    def vrow(i):
+        return vec_ref[i : i + 1, :]
+
+    def block(rc, _):
+        at = pl.ds(pl.multiple_of(rc * 192, 192), 192)
+        a1 = (xhat_ref[at, :] * vrow(0) + vrow(1)).astype(BF)
         a1_ref[at, :] = a1
         q_ref[at, :] = (dot(a1, wqkv_ref[:, 0:256]) + vrow(2)).astype(BF)
-        around = jnp.concatenate(
-            [xb_ref[4 * i + rc] for i in range(3)]
-            + [own]
-            + [xa_ref[4 * i + rc] for i in range(3)],
-            axis=0,
-        )
-        xk = dot(pk_ref[...], around)
-        a1k = (normed(xk)[0] * vrow(0) + vrow(1)).astype(BF)
         at = pl.ds(pl.multiple_of(rc * 512, 512), 512)
+        a1k = (xk_ref[at, :] * vrow(0) + vrow(1)).astype(BF)
         k_ref[at, :] = dot(a1k, wqkv_ref[:, 256:512]).astype(BF)
         v_ref[at, :] = (dot(a1k, wqkv_ref[:, 512:768]) + vrow(3)).astype(BF)
         return 0
 
-    lax.fori_loop(0, 4, project, 0)
-
+    lax.fori_loop(0, 4, block, 0, unroll=2)
+
+
+def attend_kernel(limits_ref, bias_ref, q_ref, k_ref, v_ref, mixed_ref, p_ref):
+    scale = 32 ** (-0.5)
+    lane_head = lax.broadcasted_iota(jnp.int32, (QN, 256), 1) >> 5
+    row0 = lax.axis_index("band") * 16
+    height = limits_ref[0:1, 0:1]
+    wide = limits_ref[1:2, 0:1]
     ks = lax.broadcasted_iota(jnp.int32, (KN, 384), 0)
     ql = lax.broadcasted_iota(jnp.int32, (KN, 384), 1)
     kj = (ks + 36) & (KN - 1)
@@ -208,9 +190,9 @@
         at_k = pl.ds(pl.multiple_of(k * KN, KN), KN)
         qbd = spread_heads(q_ref[at_q, :], lane_head)
         s = dot_nt(k_ref[at_k, :], qbd) * (scale * LOG2E) + bias_ref[...]
-        r = krow * 4 + (row0 + rc - 12)
+        r = krow * 4 + (rc - 12)
         c = kcol * 4 + cc
-        okay = ((r >= 0) & (r < height) & (c < wide)) | same
+        okay = ((r >= -row0) & (r < height) & (c < wide)) | same
         s = jnp.where(okay, s, MASKED)
         top = jnp.max(s, axis=0, keepdims=True)
         e = jnp.exp2(s - top)
@@ -220,7 +202,44 @@
         mixed_ref[at_q, :] = pick_heads(full, lane_head).astype(BF)
         return 0
 
-    lax.fori_loop(0, CLS, attend, 0)
+    lax.fori_loop(0, CLS, attend, 0, unroll=4)
+
+
+def feed_kernel(
+    cot_ref,
+    mixed_ref,
+    xp_ref,
+    q_ref,
+    k_ref,
+    v_ref,
+    p_ref,
+    wo_ref,
+    wu_ref,
+    wd_ref,
+    vec_ref,
+    po_ref,
+    act_ref,
+    dy_ref,
+    dz_ref,
+    a2_ref,
+    da_ref,
+    dx1_ref,
+    x1_ref,
+    own_ref,
+    rimc_ref,
+    rimz_ref,
+    dsl_ref,
+    tacc_ref,
+    sums_ref,
+    zsum_ref,
+    dmix_ref,
+):
+    odd = (lax.axis_index("band") & 1) == 1
+    scale = 32 ** (-0.5)
+    lane_head = lax.broadcasted_iota(jnp.int32, (QN, 256), 1) >> 5
+
+    def vrow(i):
+        return vec_ref[i : i + 1, :]
 
     sums_ref[...] = jnp.zeros_like(sums_ref)
     zsum_ref[...] = jnp.zeros_like(zsum_ref)
@@ -228,6 +247,7 @@
     def feed(rc, _):
         at = pl.ds(pl.multiple_of(rc * 192, 192), 192)
         x1 = xp_ref[at, :] + (dot(mixed_ref[at, :], wo_ref[...]) + vrow(4))
+        x1_ref[at, :] = x1
         xhat, rstd = normed(x1)
         a2 = (xhat * vrow(5) + vrow(6)).astype(BF)
         a2_ref[at, :] = a2
@@ -236,17 +256,13 @@
         c0 = 0.7978845608028654
         c1 = 0.044715
         z2 = z * z
-        t = jnp.tanh(c0 * (z + c1 * z2 * z))
-        act = (0.5 * z * (1.0 + t)).astype(BF)
-        act_ref[at, :] = act
-        res = x1 + dot(act, wd_ref[...]) + vrow(7)
-        back = dot_tn(po_ref[...], res.astype(BF)).astype(BF)
-        for i in range(4):
-            out_ref[4 * i + rc] = back[48 * i : 48 * i + 48]
+        t = jnp.tanh(z * (c0 + c0 * c1 * z2))
+        hz = 0.5 * z
+        act_ref[at, :] = (hz + hz * t).astype(BF)
         dyf = dot(po_ref[...], jnp.concatenate([cot_ref[4 * i + rc] for i in range(4)], axis=0))
         dy = dyf.astype(BF)
         dy_ref[at, :] = dy
-        slope = 0.5 * (1.0 + t) + 0.5 * z * (1.0 - t * t) * (c0 * (1.0 + 3.0 * c1 * z2))
+        slope = (0.5 + 0.5 * t) + (hz - hz * (t * t)) * (c0 + 3.0 * c0 * c1 * z2)
         dz = (dot_nt(dy, wd_ref[...]) * slope).astype(BF)
         dz_ref[at, :] = dz
         zsum_ref[...] += jnp.sum(dz.astype(F32), axis=0, keepdims=True)
@@ -262,7 +278,7 @@
         sums_ref[7:8, :] += jnp.sum(dyf, axis=0, keepdims=True)
         return 0
 
-    lax.fori_loop(0, 4, feed, 0)
+    lax.fori_loop(0, 4, feed, 0, unroll=2)
 
     tacc_ref[...] = jnp.zeros_like(tacc_ref)
 
@@ -278,9 +294,8 @@
         ds = pdp - p * jnp.sum(pdp, axis=0, keepdims=True)
         tacc_ref[...] += ds
         dsl = ds.astype(BF)
+        dsl_ref[at_k, :] = dsl
         dk = dot(dsl, qbd) * scale
-        dq = pick_heads(dot_tn(dsl, k_ref[at_k, :]), lane_head) * scale
-        dq_ref[at_q, :] = dq.astype(BF)
         own_ref[at_q, 0:256] = dk[0:QN]
         own_ref[at_q, 256:512] = dv[0:QN]
         after = jnp.concatenate([dk[QN : QN + RIM], dv[QN : QN + RIM]], axis=1)
@@ -291,14 +306,67 @@
         after0, before0 = back_class(pair * 2)
         after1, before1 = back_class(pair * 2 + 1)
         at = pl.ds(pl.multiple_of(pair * 2 * RIM, 2 * RIM), 2 * RIM)
-        rima_ref[at, :] = jnp.concatenate([after0, after1], axis=0).astype(BF)
-        rimb_ref[at, :] = jnp.concatenate([before0, before1], axis=0).astype(BF)
+        after = jnp.concatenate([after0, after1], axis=0)
+        before = jnp.concatenate([before0, before1], axis=0)
+        rimc_ref[at, :] = jnp.where(odd, before, after).astype(BF)
+        rimz_ref[at, :] = jnp.where(odd, after, before).astype(BF)
         return 0
 
-    lax.fori_loop(0, CLS // 2, attend_back, 0)
-    sums_ref[2:3, :] = jnp.sum(dq_ref[...].astype(F32), axis=0, keepdims=True)
+    lax.fori_loop(0, CLS // 2, attend_back, 0, unroll=2)
+
+
+def early_grads(act_ref, dy_ref, a2_ref, dz_ref, mixed_ref, da_ref, fd, fu, fo):
+    fd[...] = dot_tn(act_ref[...], dy_ref[...])
+    fu[...] = dot_tn(a2_ref[...], dz_ref[...])
+    fo[...] = dot_tn(mixed_ref[...], da_ref[...])
+
+
+def window_kernel(
+    x1_ref,
+    act_ref,
+    dsl_ref,
+    k_ref,
+    tacc_ref,
+    a1_ref,
+    wd_ref,
+    wqkv_ref,
+    vec_ref,
+    po_ref,
+    out_ref,
+    dnq_ref,
+    fwq_ref,
+    tgrad_ref,
+    qsum_ref,
+    dq_ref,
+):
+    scale = 32 ** (-0.5)
+    lane_head = lax.broadcasted_iota(jnp.int32, (QN, 256), 1) >> 5
+
+    def query(k, _):
+        at_q = pl.ds(pl.multiple_of(k * QN, QN), QN)
+        at_k = pl.ds(pl.multiple_of(k * KN, KN), KN)
+        dq = pick_heads(dot_tn(dsl_ref[at_k, :], k_ref[at_k, :]), lane_head) * scale
+        dq_ref[at_q, :] = dq.astype(BF)
+        return 0
+
+    lax.fori_loop(0, CLS, query, 0, unroll=4)
+    dq = dq_ref[...]
+    qsum_ref[...] = jnp.sum(dq.astype(F32), axis=0, keepdims=True)
+    fwq_ref[...] = dot_tn(a1_ref[...], dq)
+    dnq_ref[...] = dot_nt(dq, wqkv_ref[:, 0:256])
+
+    def result(rc, _):
+        at = pl.ds(pl.multiple_of(rc * 192, 192), 192)
+        res = x1_ref[at, :] + dot(act_ref[at, :], wd_ref[...]) + vec_ref[7:8, :]
+        back = dot_tn(po_ref[...], res.astype(BF)).astype(BF)
+        for i in range(4):
+            out_ref[4 * i + rc] = back[48 * i : 48 * i + 48]
+        return 0
+
+    lax.fori_loop(0, 4, result, 0, unroll=2)
 
     flat = tacc_ref[...].T
+    qi = lax.broadcasted_iota(jnp.int32, (QN, KN), 0)
     lines = []
     for h in range(HEADS):
         part = flat[h * QN : (h + 1) * QN]
@@ -311,28 +379,31 @@
 
 def finish_kernel(
     own_ref,
-    fa_ref,
-    fb_ref,
-    dq_ref,
+    gotc_ref,
+    gotz_ref,
+    dnq_ref,
     dx1_ref,
-    x_ref,
+    xhat_ref,
+    rstd_ref,
     wqkv_ref,
     vec_ref,
     po_ref,
+    a1_ref,
     tok_ref,
-    dqkv_ref,
+    fkv_ref,
     sums_ref,
+    dkv_ref,
 ):
+    odd = (lax.axis_index("band") & 1) == 1
     sums_ref[...] = jnp.zeros_like(sums_ref)
 
     def block(rc, _):
-        own = jnp.concatenate([x_ref[4 * i + rc] for i in range(4)], axis=0)
-        xp = dot(po_ref[...], own)
-        xhat, rstd = normed(xp)
         at = pl.ds(pl.multiple_of(rc * 192, 192), 192)
         mine = own_ref[at, :]
-        got_a = fa_ref[pl.ds(pl.multiple_of(rc * 160, 160), 160), :].astype(F32)
-        got_b = fb_ref[pl.ds(pl.multiple_of(rc * 160, 160), 160), :].astype(F32)
+        got_c = gotc_ref[pl.ds(pl.multiple_of(rc * 160, 160), 160), :].astype(F32)
+        got_z = gotz_ref[pl.ds(pl.multiple_of(rc * 160, 160), 160), :].astype(F32)
+        got_a = jnp.where(odd, got_c, got_z)
+        got_b = jnp.where(odd, got_z, got_c)
         gap = jnp.zeros((QN - RIM, 512), F32)
         parts = []
         for i in range(4):
@@ -340,11 +411,10 @@
             b = jnp.concatenate([gap, got_b[i * RIM : (i + 1) * RIM]], axis=0)
             parts.append(mine[i * QN : (i + 1) * QN] + a + b)
         dkv = jnp.concatenate(parts, axis=0).astype(BF)
-        dqkv = jnp.concatenate([dq_ref[at, :], dkv], axis=1)
-        dqkv_ref[at, :] = dqkv
-        dn = dot_nt(dqkv, wqkv_ref[...])
-        gain = vec_ref[0:1, :]
-        dx = dx1_ref[at, :] + norm_back(dn * gain, xhat, rstd)
+        dkv_ref[at, :] = dkv
+        dn = dnq_ref[at, :] + dot_nt(dkv, wqkv_ref[:, 256:768])
+        xhat = xhat_ref[at, :]
+        dx = dx1_ref[at, :] + norm_back(dn * vec_ref[0:1, :], xhat, rstd_ref[at, 0:1])
         back = dot_tn(po_ref[...], dx.astype(BF)).astype(BF)
         for i in range(4):
             tok_ref[4 * i + rc] = back[48 * i : 48 * i + 48]
@@ -353,7 +423,8 @@
         sums_ref[3:4, :] += jnp.sum(dkv[:, 256:512].astype(F32), axis=0, keepdims=True)
         return 0
 
-    lax.fori_loop(0, 4, block, 0)
+    lax.fori_loop(0, 4, block, 0, unroll=2)
+    fkv_ref[...] = dot_tn(a1_ref[...], dkv_ref[...])
 
 
 EARLY = 896
@@ -364,51 +435,61 @@
     return jnp.concatenate([v, jnp.zeros((v.shape[0], 128 - v.shape[1]), F32)], axis=1)
 
 
-def pack_kernel(wqkv_ref, wo_ref, wu_ref, wd_ref, vec_ref, out_ref):
-    top = [wd_ref[8 * b : 8 * b + 8, :] for b in range(3)]
-    top += [wo_ref[:, 0:128], wqkv_ref[:, 0:512]]
-    low = [wu_ref[...], wo_ref[:, 128:256], wqkv_ref[:, 512:768], widen(vec_ref[...]), jnp.zeros((8, 128), F32)]
-    both = jnp.concatenate([jnp.concatenate(top, axis=1), jnp.concatenate(low, axis=1)], axis=0)
-    out_ref[...] = both.astype(BF)
-
-
-def unpack(me, blocks, refs):
-    wqkv_ref, wo_ref, wu_ref, wd_ref, vec_ref, fq, fo, fu, fd, fv = refs
+def pack(wqkv, wo, wu, wd, vec):
+    pieces = [(wqkv, 0, 0), (wo, 0, 768), (wd, 0, 1024), (vec, 0, 1280)]
+    pieces += [(wu, 8, 0), (wd, 0, 768), (wd, -8, 1024)]
+    total = 0.0
+    for p, row, lane in pieces:
+        rows, lanes = p.shape
+        zero = jnp.zeros((), F32)
+        if rows == 24 and lane == 1024 and row == 0:
+            p = lax.pad(p, zero, ((0, -16, 0), (0, 0, 0)))
+            rows = 8
+        elif rows == 24:
+            p = lax.pad(p, zero, ((-8 + row, -8 - row, 0), (0, 0, 0)))
+            row, rows = 8, 8
+        total = total + lax.pad(p, zero, ((row, 16 - row - rows, 0), (lane, EARLY + LATE - lane - lanes, 0)))
+    return total.astype(BF)
+
+
+def own_index():
+    return lax.axis_index("maps") * 8 + lax.axis_index("band")
+
+
+def sorted_slabs(blocks):
+    me = own_index()
     for index, block in enumerate(blocks):
         core, across = divmod(index, 4)
         for z in range(4):
-            o = me ^ (core | (z << 1) | (across << 3))
-            slab = block[z].astype(F32)
-            at = pl.ds(pl.multiple_of(o * 8, 8), 8)
-            for b in range(3):
-                fd[pl.ds(pl.multiple_of(o * 24 + 8 * b, 8), 8), :] = slab[0:8, 256 * b : 256 * b + 256]
-            fo[at, 0:128] = slab[0:8, 768:896]
-            fo[at, 128:256] = slab[8:16, 768:896]
-            fu[at, :] = slab[8:16, 0:768]
-            fq[at, 0:512] = slab[0:8, 896:1408]
-            fq[at, 512:768] = slab[8:16, 896:1152]
-            fv[at, :] = slab[8:16, 1152:1280]
-    wqkv_ref[...] = fq[...].astype(BF)
-    wo_ref[...] = fo[...].astype(BF)
-    wu_ref[...] = fu[...].astype(BF)
-    wd_ref[...] = fd[...].astype(BF)
-    vec_ref[...] = fv[...].T[0 : vec_ref.shape[0]]
-
-
-def own_index():
-    return lax.axis_index("maps") * 8 + lax.axis_index("band")
-
-
-def layer_packed(
-    sizes_ref, x_ref, xb_ref, xa_ref, cot_ref, b0, b1, b2, b3, b4, b5, b6, b7, table_ref, po_ref, pk_ref, *rest
+            yield me ^ (core | (z << 1) | (across << 3)), block[z].astype(F32)
+
+
+def project_packed(xhat_ref, xk_ref, b0, b1, b2, b3, b4, b5, b6, b7, *rest):
+    outs, big_qkv, vec, fq, fv = rest[:4], *rest[4:]
+    for o, slab in sorted_slabs((b0, b1, b2, b3, b4, b5, b6, b7)):
+        at = pl.ds(pl.multiple_of(o * 8, 8), 8)
+        fq[at, :] = slab[0:8, 0:768]
+        fv[at, :] = slab[0:8, 1280:1408]
+    big_qkv[...] = fq[...].astype(BF)
+    vec[...] = fv[...].T[0 : vec.shape[0]]
+    project_kernel(xhat_ref, xk_ref, big_qkv, vec, *outs)
+
+
+def feed_packed(
+    cot_ref, mixed_ref, xp_ref, q_ref, k_ref, v_ref, p_ref, vec_ref, po_ref, b0, b1, b2, b3, b4, b5, b6, b7, *rest
 ):
-    weights = rest[-10:]
-    unpack(own_index(), (b0, b1, b2, b3, b4, b5, b6, b7), weights)
-    outs, scratch = rest[:16], rest[18:-10]
-    rest[16][...] = weights[0][...]
-    rest[17][...] = weights[4][...]
-    layer_kernel(
-        sizes_ref, x_ref, xb_ref, xa_ref, cot_ref, *weights[:5], table_ref, po_ref, pk_ref, *outs, *scratch
+    outs, big_down, (dmix, big_out, big_up, fo, fu, fd) = rest[:14], rest[14], rest[15:]
+    for o, slab in sorted_slabs((b0, b1, b2, b3, b4, b5, b6, b7)):
+        at = pl.ds(pl.multiple_of(o * 8, 8), 8)
+        for b, rows in enumerate((slab[0:8, 1024:1280], slab[8:16, 768:1024], slab[8:16, 1024:1280])):
+            fd[pl.ds(pl.multiple_of(o * 24 + 8 * b, 8), 8), :] = rows
+        fo[at, :] = slab[0:8, 768:1024]
+        fu[at, :] = slab[8:16, 0:768]
+    big_out[...] = fo[...].astype(BF)
+    big_up[...] = fu[...].astype(BF)
+    big_down[...] = fd[...].astype(BF)
+    feed_kernel(
+        cot_ref, mixed_ref, xp_ref, q_ref, k_ref, v_ref, p_ref, big_out, big_up, big_down, vec_ref, po_ref, *outs, dmix
     )
 
 
@@ -417,10 +498,9 @@
     return (m & 1) * 16 + (m >> 3) * 4 + ((m >> 1) & 3)
 
 
-def early_kernel(act_ref, dy_ref, a2_ref, dz_ref, mixed_ref, da_ref, out_ref, fd, fu, fo):
-    fd[...] = dot_tn(act_ref[...], dy_ref[...])
-    fu[...] = dot_tn(a2_ref[...], dz_ref[...])
-    fo[...] = dot_tn(mixed_ref[...], da_ref[...])
+def early_kernel(*refs):
+    out_ref, fd, fu, fo = refs[6:]
+    early_grads(*refs[:6], fd, fu, fo)
     me = own_index()
     for o in range(32):
         at = slice(8 * o, 8 * o + 8)
@@ -430,13 +510,16 @@
         out_ref[frame_slot(me, o)] = both.astype(BF)
 
 
+def qrow(line):
+    return jnp.where(lax.broadcasted_iota(jnp.int32, (8, 256), 0) == 2, line, 0.0)
+
+
 def late_kernel(*refs):
-    own, fa, fb, dq, dx1, x, wqkv, vec, po, a1, sums, zsum, tgrad = refs[:13]
-    tok_ref, out_ref, dqkv, sums2, fq, fv = refs[13:]
-    finish_kernel(own, fa, fb, dq, dx1, x, wqkv, vec, po, tok_ref, dqkv, sums2)
-    fq[...] = dot_tn(a1[...], dqkv[...])
+    sums, zsum, qsum, fwq, tgrad = refs[11:16]
+    tok_ref, out_ref, fkv, sums2, dkv, fv = refs[16:]
+    finish_kernel(*refs[:11], tok_ref, fkv, sums2, dkv)
     lines = jnp.concatenate(
-        [sums[...] + sums2[...]]
+        [sums[...] + sums2[...] + qrow(qsum[...])]
         + [zsum[:, 256 * i : 256 * i + 256] for i in range(3)]
         + [jnp.zeros((117, 256), F32)],
         axis=0,
@@ -446,8 +529,9 @@
     me = own_index()
     for o in range(32):
         at = slice(8 * o, 8 * o + 8)
-        low = jnp.concatenate([fq[at, 512:768], fv[at, :], table], axis=1)
-        out_ref[frame_slot(me, o)] = jnp.concatenate([fq[at, 0:512], low], axis=0).astype(BF)
+        top = jnp.concatenate([fwq[at, :], fkv[at, 0:256]], axis=1)
+        low = jnp.concatenate([fkv[at, 256:512], fv[at, :], table], axis=1)
+        out_ref[frame_slot(me, o)] = jnp.concatenate([top, low], axis=0).astype(BF)
 
 
 def adam_kernel(*refs):
@@ -507,8 +591,8 @@
 
 
 def stack_kernel(*refs):
-    for i, ref in enumerate(refs[:-1]):
-        refs[-1][i] = ref[...]
+    for i, ref in enumerate(refs[:4]):
+        refs[4][i] = ref[...]
 
 
 def call(kernel, out_shape, scratch, *args, smem=0, flops=10**8, vmem=16):
@@ -583,38 +667,61 @@
     )
 
 
-def layer_outputs():
+def prep_outputs():
     return (
-        sds((16, 48, 256)),
+        sds((KN, 384), F32),
+        sds((8, 128), jnp.int32),
+        sds((4 * QN, 4 * 48)),
+        sds((4 * KN, 10 * 48)),
+        sds((768, 256), F32),
+        sds((768, 256), F32),
+        sds((768, 128), F32),
+    )
+
+
+def project_outputs():
+    return (sds((768, 256)), sds((768, 256)), sds((CLS * KN, 256)), sds((CLS * KN, 256)))
+
+
+def attend_outputs():
+    return (sds((768, 256)), sds((CLS * KN, 384), F32))
+
+
+def feed_outputs():
+    return (
         sds((768, 768)),
         sds((768, 256)),
         sds((768, 768)),
         sds((768, 256)),
         sds((768, 256)),
-        sds((768, 256)),
-        sds((768, 256)),
-        sds((768, 256)),
+        sds((768, 256), F32),
         sds((768, 256), F32),
         sds((768, 512), F32),
         sds((CLS * RIM, 512)),
         sds((CLS * RIM, 512)),
-        sds((HEADS, KN), F32),
+        sds((CLS * KN, 384)),
+        sds((KN, 384), F32),
         sds((8, 256), F32),
         sds((1, 768), F32),
     )
 
 
-def layer_scratch():
-    return [
-        pltpu.VMEM((768, 256), F32),
-        pltpu.VMEM((768, 256), BF),
-        pltpu.VMEM((CLS * KN, 256), BF),
-        pltpu.VMEM((CLS * KN, 256), BF),
-        pltpu.VMEM((KN, 384), F32),
-        pltpu.VMEM((CLS * KN, 384), F32),
-        pltpu.VMEM((768, 256), BF),
-        pltpu.VMEM((KN, 384), F32),
-    ]
+def window_outputs():
+    return (
+        sds((16, 48, 256)),
+        sds((768, 256), F32),
+        sds((256, 256), F32),
+        sds((HEADS, KN), F32),
+        sds((1, 256), F32),
+    )
+
+
+def beside(block, band):
+    touching = [(b, b + 1 if b % 2 else b - 1) for b in range(band)]
+    return (
+        lax.ppermute(block[0], "band", [(b, b ^ 1) for b in range(band)]),
+        lax.ppermute(block[1], "band", [(b, to) for b, to in touching if 0 <= to < band]),
+    )
 
 
 def packed_step(tokens_in, cotangent, map_sizes, weights, firsts, seconds):
@@ -622,40 +729,45 @@
     vrows = weights[4].shape[0]
     turn = lambda arrays: tuple(a.T if i == 4 else a for i, a in enumerate(arrays))
     weights, firsts, seconds = turn(weights), turn(firsts), turn(seconds)
-    up = [(i, i + 1) for i in range(7)]
-    down = [(i + 1, i) for i in range(7)]
-    x_before = lax.ppermute(tokens_in[-12:], "band", up)
-    x_after = lax.ppermute(tokens_in[:12], "band", down)
-
-    slab = call(pack_kernel, sds((16, EARLY + LATE)), [], *weights[:5])
+    slab = pack(*weights[:5])
     column = call(
         stack_kernel,
         sds((4, 16, EARLY + LATE)),
         [],
         slab,
         *[swap(slab, d << 1, count) for d in (1, 2, 3)],
-    )
+        vmem=4,
+    )
+    column, x = lax.optimization_barrier((column, tokens_in))
     blocks = [column] + [swap(column, d << 3, count) for d in (1, 2, 3)]
-    blocks += [swap(block, 1, count) for block in blocks]
-
-    po = jnp.asarray(order_own(), BF)
-    pk = jnp.asarray(order_keys(), BF)
-    matrices = [(256, 768), (256, 256), (256, 768), (768, 256)]
+    x_core, x_next = beside((x, x), 8)
+    bias, limits, po, pk, xp, xhat, rstd = call(
+        prep_kernel, prep_outputs(), [], map_sizes, weights[5], x, smem=1, flops=2 * 10**9, vmem=8
+    )
+    xk = call(halo_kernel, sds((CLS * KN, 256), F32), [], x, x_core, x_next, pk, flops=10**9, vmem=8)
+    *far, xk = lax.optimization_barrier((*blocks[1:], xk))
+    blocks = [blocks[0]] + far + [swap(block, 1, count) for block in [blocks[0]] + far]
+    a1, queries, keys, values, big_qkv, vec = call(
+        project_packed,
+        project_outputs() + (sds((256, 768)), sds((vrows, 256), F32)),
+        [pltpu.VMEM((256, 768), F32), pltpu.VMEM((256, 128), F32)],
+        xhat, xk, *blocks,
+        flops=10**9, vmem=8,
+    )
+    mixed, probs = call(
+        attend_kernel, attend_outputs(), [], limits, bias, queries, keys, values, flops=3 * 10**9, vmem=8
+    )
     (
-        layer_out, act, dy, dz, a2, mixed, da, a1, dq, dx1, own, rim_a, rim_b, tgrad, sums, zsum, big_qkv, vec,
+        act, dy, dz, a2, da, dx1, x1, own, rim_c, rim_z, dsl, tacc, sums, zsum, big_down,
     ) = call(
-        layer_packed,
-        layer_outputs() + (sds((256, 768)), sds((vrows, 256), F32)),
-        layer_scratch()
-        + [pltpu.VMEM(m, BF) for m in matrices]
-        + [pltpu.VMEM((vrows, 256), F32)]
-        + [pltpu.VMEM(m, F32) for m in matrices]
-        + [pltpu.VMEM((256, 128), F32)],
-        map_sizes, tokens_in, x_before, x_after, cotangent, *blocks, weights[5], po, pk,
-        smem=1, flops=6 * 10**9, vmem=24,
-    )
-    from_prev = lax.ppermute(rim_a, "band", up)
-    from_next = lax.ppermute(rim_b, "band", down)
+        feed_packed,
+        feed_outputs() + (sds((768, 256)),),
+        [pltpu.VMEM((768, 256), BF), pltpu.VMEM((256, 256), BF), pltpu.VMEM((256, 768), BF)]
+        + [pltpu.VMEM(m, F32) for m in ((256, 256), (256, 768), (768, 256))],
+        cotangent, mixed, xp, queries, keys, values, probs, vec, po, *blocks,
+        flops=4 * 10**9,
+    )
+    got_c, got_z = beside((rim_c, rim_z), 8)
     early = call(
         early_kernel,
         sds((count, 16, EARLY)),
@@ -663,19 +775,29 @@
         act, dy, a2, dz, mixed, da,
         flops=10**9,
     )
+    early = add_stage(early, 0, 1, count)
+    early, tacc = lax.optimization_barrier((early, tacc))
+    layer_out, dnq, fwq, tgrad, qsum = call(
+        window_kernel,
+        window_outputs(),
+        [pltpu.VMEM((768, 256), BF)],
+        x1, act, dsl, keys, tacc, a1, big_down, big_qkv, vec, po,
+        flops=3 * 10**9,
+    )
+    early = add_stage(early, 3, 2, count)
+    early, own = lax.optimization_barrier((early, own))
     tokens_grad, late = call(
         late_kernel,
         (sds((16, 48, 256)), sds((count, 16, LATE))),
         [
-            pltpu.VMEM((768, 768), BF),
+            pltpu.VMEM((256, 512), F32),
             pltpu.VMEM((8, 256), F32),
-            pltpu.VMEM((256, 768), F32),
+            pltpu.VMEM((768, 512), BF),
             pltpu.VMEM((256, 128), F32),
         ],
-        own, from_prev, from_next, dq, dx1, tokens_in, big_qkv, vec, po, a1, sums, zsum, tgrad,
+        own, got_c, got_z, dnq, dx1, xhat, rstd, big_qkv, vec, po, a1, sums, zsum, qsum, fwq, tgrad,
         flops=10**9,
     )
-    early = add_stage(add_stage(early, 0, 1, count), 3, 2, count)
     late = add_stage(add_stage(late, 0, 1, count), 3, 2, count)
     grads = jnp.concatenate([early, late], axis=-1)
     low = grads.astype(BF)
@@ -751,12 +873,7 @@
     masks = np.array(frame_masks(groups))
     inverse = np.argsort(masks)
     me = lax.axis_index(AXES)
-    reach = 3 * DIL
-
-    up = [(i, i + 1) for i in range(band - 1)]
-    down = [(i + 1, i) for i in range(band - 1)]
-    x_before = lax.ppermute(tokens_in[-reach:], "band", up)
-    x_after = lax.ppermute(tokens_in[:reach], "band", down)
+    x_core, x_next = beside((tokens_in, tokens_in), band)
 
     def pack(qkv, out, upw, dnw, vec):
         dn = dnw.reshape(3, rows, 256).transpose(1, 0, 2).reshape(rows, 768)
@@ -775,65 +892,43 @@
     )
     vec = whole[:, 2560 : 2560 + vrows].T.astype(F32)
 
-    po = jnp.asarray(order_own(), BF)
-    pk = jnp.asarray(order_keys(), BF)
-    (
-        layer_out,
-        act,
-        dy,
-        dz,
-        a2,
-        mixed,
-        da,
-        a1,
-        dq,
-        dx1,
-        own,
-        rim_a,
-        rim_b,
-        table_grad,
-        sums,
-        zsum,
-    ) = call(
-        layer_kernel,
-        layer_outputs(),
-        layer_scratch(),
-        map_sizes,
-        tokens_in,
-        x_before,
-        x_after,
-        cotangent,
-        big_qkv,
-        big_out,
-        big_up,
-        big_down,
-        vec,
-        pos_table,
-        po,
-        pk,
-        smem=1,
-        flops=6 * 10**9,
-    )
-    from_prev = lax.ppermute(rim_a, "band", up)
-    from_next = lax.ppermute(rim_b, "band", down)
-    grad_down = dot_tn(act, dy)
-    grad_up = dot_tn(a2, dz)
-    grad_out = dot_tn(mixed, da)
-    tokens_grad, dqkv, sums2 = call(
+    bias, limits, po, pk, xp, xhat, rstd = call(
+        prep_kernel, prep_outputs(), [], map_sizes, pos_table, tokens_in, smem=1, flops=2 * 10**9
+    )
+    xk = call(halo_kernel, sds((CLS * KN, 256), F32), [], tokens_in, x_core, x_next, pk, flops=10**9)
+    a1, queries, keys, values = call(project_kernel, project_outputs(), [], xhat, xk, big_qkv, vec, flops=10**9)
+    mixed, probs = call(attend_kernel, attend_outputs(), [], limits, bias, queries, keys, values, flops=3 * 10**9)
+    act, dy, dz, a2, da, dx1, x1, own, rim_c, rim_z, dsl, tacc, sums, zsum = call(
+        feed_kernel,
+        feed_outputs(),
+        [pltpu.VMEM((768, 256), BF)],
+        cotangent, mixed, xp, queries, keys, values, probs, big_out, big_up, big_down, vec, po,
+        flops=4 * 10**9,
+    )
+    got_c, got_z = beside((rim_c, rim_z), band)
+    grad_down, grad_up, grad_out = call(
+        early_grads,
+        (sds((768, 256), F32), sds((256, 768), F32), sds((256, 256), F32)),
+        [],
+        act, dy, a2, dz, mixed, da,
+        flops=10**9,
+    )
+    layer_out, dnq, fwq, table_grad, qsum = call(
+        window_kernel,
+        window_outputs(),
+        [pltpu.VMEM((768, 256), BF)],
+        x1, act, dsl, keys, tacc, a1, big_down, big_qkv, vec, po,
+        flops=3 * 10**9,
+    )
+    tokens_grad, fkv, sums2 = call(
         finish_kernel,
-        (sds((16, 48, 256)), sds((768, 768)), sds((8, 256), F32)),
-        [],
-        own,
-        from_prev,
-        from_next,
-        dq,
-        dx1,
-        tokens_in,
-        big_qkv,
-        vec,
-        po,
-    )
-    grad_qkv = dot_tn(a1, dqkv)
+        (sds((16, 48, 256)), sds((256, 512), F32), sds((8, 256), F32)),
+        [pltpu.VMEM((768, 512), BF)],
+        own, got_c, got_z, dnq, dx1, xhat, rstd, big_qkv, vec, po, a1,
+        flops=10**9,
+    )
+    grad_qkv = jnp.concatenate([fwq, fkv], axis=1)
+    sums2 = sums2.at[2:3].add(qsum)
     grad_vec = jnp.concatenate([sums + sums2, zsum.reshape(3, 256)], axis=0)
 
     packed = jnp.concatenate(

time: 113 us -> 93.1 us (0.82)
  starting transfers between devices: 49.9 us -> 34.1 us
  Pallas kernels: 33.7 us -> 28 us
  waiting for transfers between devices: 22.2 us -> 25 us
  local copies, waits for them, and re-layouts: 4.97 us -> 3.31 us
    ppermute x28, starting transfers between devices: 42 us -> 30.6 us  [swap(): return lax.ppermute(block, AXES, [(k, k ^ mask) for k in range(count)])]
    pallas_call x7 -> x11, Pallas kernels: 33.7 us -> 28 us  [call(): pl.pallas_call(kernel, out_shape=out_shape, in_specs=specs, out_specs=jax...]
    ppermute x4, starting transfers between devices: 7.84 us -> 3.6 us  [the longest x2 2.04 us: beside(): lax.ppermute(block[0], 'band', [(b, b ^ 1) for b in range(band)])]
    ppermute x28, waiting for transfers between devices: 21.7 us -> 25 us  [swap(): return lax.ppermute(block, AXES, [(k, k ^ mask) for k in range(count)])]
    unnamed x56 -> x44, local copies, waits for them, and re-layouts: 3.77 us -> 2.46 us
  transfers between devices with their start and end apart: 32 -> 32, of which waited for: 18 -> 23; matrix products, arithmetic and copies ran while one was open for 1% -> 0% of each run, Pallas kernels for 4% -> 8%
where the time goes in v4:
time: 93.1 us; the launch traced here: 92.8 us
  starting transfers between devices  34.1 us (37%)
  Pallas kernels  28 us (30%)
  waiting for transfers between devices  25 us (27%)
  local copies, waits for them, and re-layouts  3.31 us (4%)
  other arithmetic  1.17 us (1%)
  between operations  1.17 us (1%)
    ppermute x28, starting transfers between devices, swap(): return lax.ppermute(block, AXES, [(k, k ^ mask) for k in range(count)])  30.6 us
    pallas_call x11, Pallas kernels, call(): pl.pallas_call(kernel, out_shape=out_shape, in_specs=specs, out_specs=jax...  28 us
    ppermute x28, waiting for transfers between devices, swap(): return lax.ppermute(block, AXES, [(k, k ^ mask) for k in range(count)])  25 us
    unnamed x44, local copies, waits for them, and re-layouts  2.46 us
    ppermute x2, starting transfers between devices, beside(): lax.ppermute(block[0], 'band', [(b, b ^ 1) for b in range(band)])  2.04 us
  transfers between devices with their start and end apart: 32, of which 23 were waited for; matrix products, arithmetic and copies ran while one was open for 0% of the time, Pallas kernels for 8%

profile of v4, /device:TPU:0, one launch (start us, length us, event | category | flops | bytes accessed | tf_op | source)
XLA Modules:
  0.0 92.8 jit_solution(1237992782919293174)
XLA Ops:
  0.7 0.7 fusion.8
  1.4 0.8 add_convert_fusion.refs_0_
  2.2 5.1 %collective-permute-start.2 = (bf16[16,1408]{1,0:T(8,128)(2,1)S(1)}, bf16[16,1408]{1,0:T(8,128)(2,1)S(1)}, u32[]{:S(2)}, u32[]{:S(2)}) collective-permute-start(bf16[16,1408]{1,0:T(8,128)(2,1)S(1)} %add_convert_fusion.refs_0_), channel_id=1, source_target_pairs={{0,6},{1,7},{2,4},{3,5},{4,2},{5,3},{6,0},{7,1},{8,14},{9,15},{10,... | collective-permute-start | bytes 135176 | tf_op jit(solution)/shard_map/ppermute | solution.py:624
  7.3 0.6 collective-permute-start
  7.9 1.4 %collective-permute-done.2.refs_3_ = bf16[16,1408]{1,0:T(8,128)(2,1)S(1)} collective-permute-done((bf16[16,1408]{1,0:T(8,128)(2,1)S(1)}, bf16[16,1408]{1,0:T(8,128)(2,1)S(1)}, u32[]{:S(2)}, u32[]{:S(2)}) %collective-permute-start.2) | collective-permute-done | bytes 45088 | tf_op jit(solution)/shard_map/ppermute | solution.py:624
  9.4 2.9 %collective-permute-done.1.refs_2_ = bf16[16,1408]{1,0:T(8,128)(2,1)S(1)} collective-permute-done((bf16[16,1408]{1,0:T(8,128)(2,1)S(1)}, bf16[16,1408]{1,0:T(8,128)(2,1)S(1)}, u32[]{:S(2)}, u32[]{:S(2)}) %collective-permute-start.1) | collective-permute-done | bytes 45088 | tf_op jit(solution)/shard_map/ppermute | solution.py:624
  12.2 0.7 collective-permute-start.7
  12.9 1.8 %collective-permute-start.6 = (bf16[16,48,256]{2,1,0:T(8,128)(2,1)}, bf16[16,48,256]{2,1,0:T(8,128)(2,1)S(1)}, u32[]{:S(2)}, u32[]{:S(2)}) collective-permute-start(bf16[16,48,256]{2,1,0:T(8,128)(2,1)} %x_ref.1), channel_id=1, source_target_pairs={{0,1},{1,0},{2,3},{3,2},{4,5},{5,4},{6,7},{7,6},{8,9},{9,8},{10,11... | collective-permute-start | bytes 1179656 | tf_op jit(solution)/shard_map/ppermute | solution.py:722
  14.7 2.4 %collective-permute-start.5 = (bf16[4,16,1408]{2,1,0:T(8,128)(2,1)S(1)}, bf16[4,16,1408]{2,1,0:T(8,128)(2,1)S(1)}, u32[]{:S(2)}, u32[]{:S(2)}) collective-permute-start(bf16[4,16,1408]{2,1,0:T(8,128)(2,1)S(1)} %shard_map.372.b0), channel_id=1, source_target_pairs={{0,24},{1,25},{2,26},{3,27},{4,28},{5,29},{6,30},{7,31},{8,16},{9,... | collective-permute-start | bytes 540680 | tf_op jit(solution)/shard_map/ppermute | solution.py:624
  17.2 0.5 collective-permute-start.4
  17.7 0.5 collective-permute-start.3
  18.2 1.0 %copy-done = bf16[16,48,256]{2,1,0:T(8,128)(2,1)S(1)} copy-done((bf16[16,48,256]{2,1,0:T(8,128)(2,1)S(1)}, bf16[16,48,256]{2,1,0:T(8,128)(2,1)}, u32[]{:S(2)}) %copy-start) | copy-done | bytes 393240
  19.2 0.7 copy-done.18
  19.9 0.7 copy-done.21
  20.5 2.1 %shard_map.373 = (f32[128,384]{1,0:T(8,128)S(1)}, s32[8,128]{1,0:T(8,128)S(1)}, bf16[192,192]{1,0:T(8,128)(2,1)S(1)}, bf16[512,480]{1,0:T(8,128)(2,1)S(1)}, f32[...) custom-call(s32[1,2]{1,0:T(1,128)S(1)} %copy-done.21, f32[8,49]{1,0:T(8,128)S(1)} %copy-done.18, ...), custom_call_target="tpu_custom_call" | custom-call | flops 2000000000 | bytes 1000000 | tf_op jit(solution)/shard_map/pallas_call | solution.py:601
  22.7 1.4 %shard_map.374.xk_ref = f32[2048,256]{1,0:T(8,128)S(1)} custom-call(bf16[16,48,256]{2,1,0:T(8,128)(2,1)S(1)} %copy-done, bf16[16,48,256]{2,1,0:T(8,128)(2,1)S(1)} %collective-permute-done.6.xc_ref, bf16[16,48,256]{2,1,0:T(8,128)(2,1)S(1)} %collective-permute-done.7.xz_ref, bf16[512,480]{1,0:T(8,128)(2,1)S(1)} %get-tuple-element.101.pk_ref), custom_call_target="tpu_custom_call" | custom-call | flops 1000000000 | bytes 1000000 | tf_op jit(solution)/shard_map/pallas_call | solution.py:601
  24.2 1.9 %collective-permute-done.4.b2 = bf16[4,16,1408]{2,1,0:T(8,128)(2,1)S(1)} collective-permute-done((bf16[4,16,1408]{2,1,0:T(8,128)(2,1)S(1)}, bf16[4,16,1408]{2,1,0:T(8,128)(2,1)S(1)}, u32[]{:S(2)}, u32[]{:S(2)}) %collective-permute-start.4) | collective-permute-done | bytes 180256 | tf_op jit(solution)/shard_map/ppermute | solution.py:624
  26.0 0.1 collective-permute-done.3.b1
  26.1 0.5 collective-permute-start.10
  26.6 0.9 collective-permute-done.9.b5
  27.5 0.3 collective-permute-done.10.b6
  27.8 0.3 collective-permute-done.11.b7
  28.1 1.2 %shard_map.375 = (bf16[768,256]{1,0:T(8,128)(2,1)S(1)}, bf16[768,256]{1,0:T(8,128)(2,1)S(1)}, bf16[2048,256]{1,0:T(8,128)(2,1)S(1)}, bf16[2048,256]{1,0:T(8,128)...) custom-call(f32[768,256]{1,0:T(8,128)S(1)} %get-tuple-element.99.xhat_ref.refs_5_, ...), custom_call_target="tpu_custom_call" | custom-call | flops 1000000000 | bytes 1000000 | tf_op jit(solution)/shard_map/pallas_call | solution.py:601
  29.3 3.8 %shard_map.376 = (bf16[768,256]{1,0:T(8,128)(2,1)S(1)}, f32[2048,384]{1,0:T(8,128)S(1)}) custom-call(s32[8,128]{1,0:T(8,128)S(1)} %get-tuple-element.97.limits_ref, f32[128,384]{1,0:T(8,128)S(1)} %get-tuple-element.98.bias_ref, bf16[768,256]{1,0:T(8,128)(2,1)S(1)} %get-tuple-element.106.q_ref, bf16[2048,256]{1,0:T(8,128)(2,1)S(1)} %get-tuple-element.107.k_ref, ...), custom_call_target="tpu_custom_call" | custom-call | flops 3000000000 | bytes 1000000 | tf_op jit(solution)/shard_map/pallas_call | solution.py:601
  33.1 9.5 %shard_map.377 = (bf16[768,768]{1,0:T(8,128)(2,1)S(1)}, bf16[768,256]{1,0:T(8,128)(2,1)S(1)}, bf16[768,768]{1,0:T(8,128)(2,1)S(1)}, bf16[768,256]{1,0:T(8,128)(2...) custom-call(bf16[16,48,256]{2,1,0:T(8,128)(2,1)S(1)} %copy-done.20, ...), custom_call_target="tpu_custom_call" | custom-call | flops 4000000000 | bytes 1000000 | tf_op jit(solution)/shard_map/pallas_call | solution.py:601
  42.6 0.9 %shard_map.378 = bf16[32,16,896]{2,1,0:T(8,128)(2,1)S(1)} custom-call(bf16[768,768]{1,0:T(8,128)(2,1)S(1)} %get-tuple-element.115.refs_0_.act_ref, bf16[768,256]{1,0:T(8,128)(2,1)S(1)} %get-tuple-element.117.refs_1_, bf16[768,256]{1,0:T(8,128)(2,1)S(1)} %get-tuple-element.118.refs_2_, bf16[768,768]{1,0:T(8,128)(2,1)S(1)} %get-tuple-element.119.refs_3_, ...), custom_call_target="tpu_custom_call" | custom-call | flops 1000000000 | bytes 1000000 | tf_op jit(solution)/shard_map/pallas_call | solution.py:601
  43.6 0.3 collective-permute-start.12
  43.9 0.3 collective-permute-start.16
  44.1 0.9 collective-permute-start.17
  45.0 0.4 collective-permute-done.12
  45.6 1.6 %collective-permute-start.13 = (bf16[4,16,896]{2,1,0:T(8,128)(2,1)S(1)}, bf16[4,16,896]{2,1,0:T(8,128)(2,1)S(1)}, u32[]{:S(2)}, u32[]{:S(2)}) collective-permute-start(bf16[4,16,896]{2,1,0:T(8,128)(2,1)S(1)} %get-tuple-element.172), channel_id=1, source_target_pairs={{0,8},{1,9},{2,10},{3,11},{4,12},{5,13},{6,14},{7,15},{8,0},{9,1},... | collective-permute-start | bytes 344072 | tf_op jit(solution)/shard_map/ppermute | solution.py:624
  47.2 1.4 %collective-permute-start.15 = (bf16[4,16,896]{2,1,0:T(8,128)(2,1)S(1)}, bf16[4,16,896]{2,1,0:T(8,128)(2,1)S(1)}, u32[]{:S(2)}, u32[]{:S(2)}) collective-permute-start(bf16[4,16,896]{2,1,0:T(8,128)(2,1)S(1)} %get-tuple-element.173), channel_id=1, source_target_pairs={{0,24},{1,25},{2,26},{3,27},{4,28},{5,29},{6,30},{7,31},{8,16},{9,... | collective-permute-start | bytes 344072 | tf_op jit(solution)/shard_map/ppermute | solution.py:624
  48.6 0.6 collective-permute-start.14
  49.2 4.4 %shard_map.379 = (bf16[16,48,256]{2,1,0:T(8,128)(2,1)}, f32[768,256]{1,0:T(8,128)S(1)}, f32[256,256]{1,0:T(8,128)S(1)}, f32[8,128]{1,0:T(8,128)S(1)}, f32[1,256]{1,0:T(1,128)S(1)}) custom-call(f32[768,256]{1,0:T(8,128)S(1)} %get-tuple-element.114.x1_ref, bf16[768,768]{1,0:T(8,128)(2,1)S(1)} %get-tuple-element.115.refs_0_.act_ref, ...), custom_call_target="tpu_custom_call" | custom-call | flops 3000000000 | bytes 1000000 | tf_op jit(solution)/shard_map/pallas_call | solution.py:601
  53.6 2.1 %collective-permute-done.14 = bf16[4,16,896]{2,1,0:T(8,128)(2,1)S(1)} collective-permute-done((bf16[4,16,896]{2,1,0:T(8,128)(2,1)S(1)}, bf16[4,16,896]{2,1,0:T(8,128)(2,1)S(1)}, u32[]{:S(2)}, u32[]{:S(2)}) %collective-permute-start.14) | collective-permute-done | bytes 114720 | tf_op jit(solution)/shard_map/ppermute | solution.py:624
  55.7 3.1 %shard_map.380 = (bf16[16,48,256]{2,1,0:T(8,128)(2,1)}, bf16[32,16,512]{2,1,0:T(8,128)(2,1)S(1)}) custom-call(f32[768,512]{1,0:T(8,128)S(1)} %get-tuple-element.129.refs_0_, bf16[640,512]{1,0:T(8,128)(2,1)S(1)} %collective-permute-done.16.refs_1_, bf16[640,512]{1,0:T(8,128)(2,1)S(1)} %collective-permute-done.17.refs_2_, ...), custom_call_target="tpu_custom_call" | custom-call | flops 1000000000 | bytes 1000000 | tf_op jit(solution)/shard_map/pallas_call | solution.py:601
  59.0 0.9 collective-permute-start.18
  59.9 1.2 %collective-permute-done.18 = bf16[16,16,512]{2,1,0:T(8,128)(2,1)S(1)} collective-permute-done((bf16[16,16,512]{2,1,0:T(8,128)(2,1)S(1)}, bf16[16,16,512]{2,1,0:T(8,128)(2,1)S(1)}, u32[]{:S(2)}, u32[]{:S(2)}) %collective-permute-start.18) | collective-permute-done | bytes 262176 | tf_op jit(solution)/shard_map/ppermute | solution.py:624
  61.2 1.6 %collective-permute-start.19 = (bf16[4,16,512]{2,1,0:T(8,128)(2,1)S(1)}, bf16[4,16,512]{2,1,0:T(8,128)(2,1)S(1)}, u32[]{:S(2)}, u32[]{:S(2)}) collective-permute-start(bf16[4,16,512]{2,1,0:T(8,128)(2,1)S(1)} %get-tuple-element.175), channel_id=1, source_target_pairs={{0,8},{1,9},{2,10},{3,11},{4,12},{5,13},{6,14},{7,15},{8,0},{9,1},... | collective-permute-start | bytes 196616 | tf_op jit(solution)/shard_map/ppermute | solution.py:624
  62.8 1.4 %collective-permute-start.21 = (bf16[4,16,512]{2,1,0:T(8,128)(2,1)S(1)}, bf16[4,16,512]{2,1,0:T(8,128)(2,1)S(1)}, u32[]{:S(2)}, u32[]{:S(2)}) collective-permute-start(bf16[4,16,512]{2,1,0:T(8,128)(2,1)S(1)} %get-tuple-element.176), channel_id=1, source_target_pairs={{0,24},{1,25},{2,26},{3,27},{4,28},{5,29},{6,30},{7,31},{8,16},{9,... | collective-permute-start | bytes 196616 | tf_op jit(solution)/shard_map/ppermute | solution.py:624
  64.2 0.6 collective-permute-start.20
  64.8 0.9 collective-permute-done.19
  65.7 2.4 %collective-permute-done.21 = bf16[4,16,512]{2,1,0:T(8,128)(2,1)S(1)} collective-permute-done((bf16[4,16,512]{2,1,0:T(8,128)(2,1)S(1)}, bf16[4,16,512]{2,1,0:T(8,128)(2,1)S(1)}, u32[]{:S(2)}, u32[]{:S(2)}) %collective-permute-start.21) | collective-permute-done | bytes 65568 | tf_op jit(solution)/shard_map/ppermute | solution.py:624
  68.1 1.2 %collective-permute-done.20 = bf16[4,16,512]{2,1,0:T(8,128)(2,1)S(1)} collective-permute-done((bf16[4,16,512]{2,1,0:T(8,128)(2,1)S(1)}, bf16[4,16,512]{2,1,0:T(8,128)(2,1)S(1)}, u32[]{:S(2)}, u32[]{:S(2)}) %collective-permute-start.20) | collective-permute-done | bytes 65568 | tf_op jit(solution)/shard_map/ppermute | solution.py:624
  69.4 1.4 %collective-permute-start.24 = (bf16[16,1408]{1,0:T(8,128)(2,1)S(1)}, bf16[16,1408]{1,0:T(8,128)(2,1)S(1)}, u32[]{:S(2)}, u32[]{:S(2)}) collective-permute-start(bf16[16,1408]{1,0:T(8,128)(2,1)S(1)} %get-tuple-element.178), channel_id=1, source_target_pairs={{0,6},{1,7},{2,4},{3,5},{4,2},{5,3},{6,0},{7,1},{8,14},{9,15},{10,... | collective-permute-start | bytes 135176 | tf_op jit(solution)/shard_map/ppermute | solution.py:624
  70.8 2.0 %collective-permute-start.23 = (bf16[16,1408]{1,0:T(8,128)(2,1)S(1)}, bf16[16,1408]{1,0:T(8,128)(2,1)S(1)}, u32[]{:S(2)}, u32[]{:S(2)}) collective-permute-start(bf16[16,1408]{1,0:T(8,128)(2,1)S(1)} %get-tuple-element.179), channel_id=1, source_target_pairs={{0,4},{1,5},{2,6},{3,7},{4,0},{5,1},{6,2},{7,3},{8,12},{9,13},{10,... | collective-permute-start | bytes 135176 | tf_op jit(solution)/shard_map/ppermute | solution.py:624
  72.8 1.0 %collective-permute-start.22 = (bf16[16,1408]{1,0:T(8,128)(2,1)S(1)}, bf16[16,1408]{1,0:T(8,128)(2,1)S(1)}, u32[]{:S(2)}, u32[]{:S(2)}) collective-permute-start(bf16[16,1408]{1,0:T(8,128)(2,1)S(1)} %get-tuple-element.180), channel_id=1, source_target_pairs={{0,2},{1,3},{2,0},{3,1},{4,6},{5,7},{6,4},{7,5},{8,10},{9,11},{10,... | collective-permute-start | bytes 135176 | tf_op jit(solution)/shard_map/ppermute | solution.py:624
  73.8 1.9 %collective-permute-done.24.refs_3_ = bf16[16,1408]{1,0:T(8,128)(2,1)S(1)} collective-permute-done((bf16[16,1408]{1,0:T(8,128)(2,1)S(1)}, bf16[16,1408]{1,0:T(8,128)(2,1)S(1)}, u32[]{:S(2)}, u32[]{:S(2)}) %collective-permute-start.24) | collective-permute-done | bytes 45088 | tf_op jit(solution)/shard_map/ppermute | solution.py:624
  75.8 1.4 %collective-permute-done.23.refs_2_ = bf16[16,1408]{1,0:T(8,128)(2,1)S(1)} collective-permute-done((bf16[16,1408]{1,0:T(8,128)(2,1)S(1)}, bf16[16,1408]{1,0:T(8,128)(2,1)S(1)}, u32[]{:S(2)}, u32[]{:S(2)}) %collective-permute-start.23) | collective-permute-done | bytes 45088 | tf_op jit(solution)/shard_map/ppermute | solution.py:624
  77.1 0.2 collective-permute-done.22.refs_1_
  77.5 0.9 shard_map.381
  78.5 1.2 %collective-permute-done.25 = f32[8,128]{1,0:T(8,128)S(1)} collective-permute-done((f32[8,128]{1,0:T(8,128)S(1)}, f32[8,128]{1,0:T(8,128)S(1)}, u32[]{:S(2)}, u32[]{:S(2)}) %collective-permute-start.25) | collective-permute-done | bytes 4128 | tf_op jit(solution)/shard_map/ppermute | solution.py:624
  79.6 1.6 %collective-permute-start.28 = (f32[8,128]{1,0:T(8,128)S(1)}, f32[8,128]{1,0:T(8,128)S(1)}, u32[]{:S(2)}, u32[]{:S(2)}) collective-permute-start(f32[8,128]{1,0:T(8,128)S(1)} %add.82), channel_id=1, source_target_pairs={{0,24},{1,25},{2,26},{3,27},{4,28},{5,29},{6,30},{7,31},{8,16},{9,... | collective-permute-start | bytes 12296 | tf_op jit(solution)/shard_map/ppermute | solution.py:624
  81.2 1.3 %collective-permute-start.27 = (f32[8,128]{1,0:T(8,128)S(1)}, f32[8,128]{1,0:T(8,128)S(1)}, u32[]{:S(2)}, u32[]{:S(2)}) collective-permute-start(f32[8,128]{1,0:T(8,128)S(1)} %add.82), channel_id=1, source_target_pairs={{0,16},{1,17},{2,18},{3,19},{4,20},{5,21},{6,22},{7,23},{8,24},{9,... | collective-permute-start | bytes 12296 | tf_op jit(solution)/shard_map/ppermute | solution.py:624
  82.4 0.7 collective-permute-start.26
  83.1 1.0 %collective-permute-done.28 = f32[8,128]{1,0:T(8,128)S(1)} collective-permute-done((f32[8,128]{1,0:T(8,128)S(1)}, f32[8,128]{1,0:T(8,128)S(1)}, u32[]{:S(2)}, u32[]{:S(2)}) %collective-permute-start.28) | collective-permute-done | bytes 4128 | tf_op jit(solution)/shard_map/ppermute | solution.py:624
  84.1 0.7 collective-permute-done.27
  84.8 1.3 %collective-permute-done.26 = f32[8,128]{1,0:T(8,128)S(1)} collective-permute-done((f32[8,128]{1,0:T(8,128)S(1)}, f32[8,128]{1,0:T(8,128)S(1)}, u32[]{:S(2)}, u32[]{:S(2)}) %collective-permute-start.26) | collective-permute-done | bytes 4128 | tf_op jit(solution)/shard_map/ppermute | solution.py:624
  86.1 0.9 %collective-permute-start.31 = (f32[8,128]{1,0:T(8,128)S(1)}, f32[8,128]{1,0:T(8,128)S(1)}, u32[]{:S(2)}, u32[]{:S(2)}) collective-permute-start(f32[8,128]{1,0:T(8,128)S(1)} %add_add_fusion.a_ref), channel_id=1, source_target_pairs={{0,6},{1,7},{2,4},{3,5},{4,2},{5,3},{6,0},{7,1},{8,14},{9,15},{10,... | collective-permute-start | bytes 12296 | tf_op jit(solution)/shard_map/ppermute | solution.py:624
  87.0 0.5 collective-permute-start.30
  87.5 2.9 %collective-permute-start.29 = (f32[8,128]{1,0:T(8,128)S(1)}, f32[8,128]{1,0:T(8,128)S(1)}, u32[]{:S(2)}, u32[]{:S(2)}) collective-permute-start(f32[8,128]{1,0:T(8,128)S(1)} %add_add_fusion.a_ref), channel_id=1, source_target_pairs={{0,2},{1,3},{2,0},{3,1},{4,6},{5,7},{6,4},{7,5},{8,10},{9,11},{10,... | collective-permute-start | bytes 12296 | tf_op jit(solution)/shard_map/ppermute | solution.py:624
  90.4 1.0 %collective-permute-done.31.d_ref = f32[8,128]{1,0:T(8,128)S(1)} collective-permute-done((f32[8,128]{1,0:T(8,128)S(1)}, f32[8,128]{1,0:T(8,128)S(1)}, u32[]{:S(2)}, u32[]{:S(2)}) %collective-permute-start.31) | collective-permute-done | bytes 4128 | tf_op jit(solution)/shard_map/ppermute | solution.py:624
  91.5 0.5 collective-permute-done.29.b_ref
  92.0 0.8 shard_map.382
  (71 shorter events, 0.9 us)
Async XLA Ops:
  2.2 7.2 %collective-permute-start.2 = (bf16[16,1408]{1,0:T(8,128)(2,1)S(1)}, bf16[16,1408]{1,0:T(8,128)(2,1)S(1)}, u32[]{:S(2)}, u32[]{:S(2)}) collective-permute-start(bf16[16,1408]{1,0:T(8,128)(2,1)S(1)} %add_convert_fusion.refs_0_), channel_id=1, source_target_pairs={{0,6},{1,7},{2,4},{3,5},{4,2},{5,3},{6,0},{7,1},{8,14},{9,15},{10,... | collective-permute-start | bytes 135176 | tf_op jit(solution)/shard_map/ppermute | solution.py:624
  7.3 4.9 %collective-permute-start.1 = (bf16[16,1408]{1,0:T(8,128)(2,1)S(1)}, bf16[16,1408]{1,0:T(8,128)(2,1)S(1)}, u32[]{:S(2)}, u32[]{:S(2)}) collective-permute-start(bf16[16,1408]{1,0:T(8,128)(2,1)S(1)} %add_convert_fusion.refs_0_), channel_id=1, source_target_pairs={{0,4},{1,5},{2,6},{3,7},{4,0},{5,1},{6,2},{7,3},{8,12},{9,13},{10,... | collective-permute-start | bytes 135176 | tf_op jit(solution)/shard_map/ppermute | solution.py:624
  7.3 4.9 %collective-permute-start = (bf16[16,1408]{1,0:T(8,128)(2,1)S(1)}, bf16[16,1408]{1,0:T(8,128)(2,1)S(1)}, u32[]{:S(2)}, u32[]{:S(2)}) collective-permute-start(bf16[16,1408]{1,0:T(8,128)(2,1)S(1)} %add_convert_fusion.refs_0_), channel_id=1, source_target_pairs={{0,2},{1,3},{2,0},{3,1},{4,6},{5,7},{6,4},{7,5},{8,10},{9,11},{10,... | collective-permute-start | bytes 135176 | tf_op jit(solution)/shard_map/ppermute | solution.py:624
  12.2 10.4 %collective-permute-start.7 = (bf16[16,48,256]{2,1,0:T(8,128)(2,1)}, bf16[16,48,256]{2,1,0:T(8,128)(2,1)S(1)}, u32[]{:S(2)}, u32[]{:S(2)}) collective-permute-start(bf16[16,48,256]{2,1,0:T(8,128)(2,1)} %x_ref.1), channel_id=1, source_target_pairs={{1,2},{2,1},{3,4},{4,3},{5,6},{6,5},{9,10},{10,9},{11,12},{12,11},... | collective-permute-start | bytes 1179656 | tf_op jit(solution)/shard_map/ppermute | solution.py:723
  12.9 9.8 %collective-permute-start.6 = (bf16[16,48,256]{2,1,0:T(8,128)(2,1)}, bf16[16,48,256]{2,1,0:T(8,128)(2,1)S(1)}, u32[]{:S(2)}, u32[]{:S(2)}) collective-permute-start(bf16[16,48,256]{2,1,0:T(8,128)(2,1)} %x_ref.1), channel_id=1, source_target_pairs={{0,1},{1,0},{2,3},{3,2},{4,5},{5,4},{6,7},{7,6},{8,9},{9,8},{10,11... | collective-permute-start | bytes 1179656 | tf_op jit(solution)/shard_map/ppermute | solution.py:722
  14.7 9.4 %collective-permute-start.5 = (bf16[4,16,1408]{2,1,0:T(8,128)(2,1)S(1)}, bf16[4,16,1408]{2,1,0:T(8,128)(2,1)S(1)}, u32[]{:S(2)}, u32[]{:S(2)}) collective-permute-start(bf16[4,16,1408]{2,1,0:T(8,128)(2,1)S(1)} %shard_map.372.b0), channel_id=1, source_target_pairs={{0,24},{1,25},{2,26},{3,27},{4,28},{5,29},{6,30},{7,31},{8,16},{9,... | collective-permute-start | bytes 540680 | tf_op jit(solution)/shard_map/ppermute | solution.py:624
  17.2 8.8 %collective-permute-start.4 = (bf16[4,16,1408]{2,1,0:T(8,128)(2,1)S(1)}, bf16[4,16,1408]{2,1,0:T(8,128)(2,1)S(1)}, u32[]{:S(2)}, u32[]{:S(2)}) collective-permute-start(bf16[4,16,1408]{2,1,0:T(8,128)(2,1)S(1)} %shard_map.372.b0), channel_id=1, source_target_pairs={{0,16},{1,17},{2,18},{3,19},{4,20},{5,21},{6,22},{7,23},{8,24},{9,... | collective-permute-start | bytes 540680 | tf_op jit(solution)/shard_map/ppermute | solution.py:624
  17.7 8.4 %collective-permute-start.3 = (bf16[4,16,1408]{2,1,0:T(8,128)(2,1)S(1)}, bf16[4,16,1408]{2,1,0:T(8,128)(2,1)S(1)}, u32[]{:S(2)}, u32[]{:S(2)}) collective-permute-start(bf16[4,16,1408]{2,1,0:T(8,128)(2,1)S(1)} %shard_map.372.b0), channel_id=1, source_target_pairs={{0,8},{1,9},{2,10},{3,11},{4,12},{5,13},{6,14},{7,15},{8,0},{9,1},... | collective-permute-start | bytes 540680 | tf_op jit(solution)/shard_map/ppermute | solution.py:624
  18.2 1.0 %copy-start = (bf16[16,48,256]{2,1,0:T(8,128)(2,1)S(1)}, bf16[16,48,256]{2,1,0:T(8,128)(2,1)}, u32[]{:S(2)}) copy-start(bf16[16,48,256]{2,1,0:T(8,128)(2,1)} %x_ref.1) | copy-start | bytes 1179652
  19.2 0.7 copy-start.18
  19.9 0.7 copy-start.21
  22.6 4.0 %collective-permute-start.8 = (bf16[4,16,1408]{2,1,0:T(8,128)(2,1)S(1)}, bf16[4,16,1408]{2,1,0:T(8,128)(2,1)S(1)}, u32[]{:S(2)}, u32[]{:S(2)}) collective-permute-start(bf16[4,16,1408]{2,1,0:T(8,128)(2,1)S(1)} %shard_map.372.b0), channel_id=1, source_target_pairs={{0,1},{1,0},{2,3},{3,2},{4,5},{5,4},{6,7},{7,6},{8,9},{9,8},{10,11... | collective-permute-start | bytes 540680 | tf_op jit(solution)/shard_map/ppermute | solution.py:624
  26.1 1.4 %collective-permute-start.9 = (bf16[4,16,1408]{2,1,0:T(8,128)(2,1)S(1)}, bf16[4,16,1408]{2,1,0:T(8,128)(2,1)S(1)}, u32[]{:S(2)}, u32[]{:S(2)}) collective-permute-start(bf16[4,16,1408]{2,1,0:T(8,128)(2,1)S(1)} %collective-permute-done.3.b1), channel_id=1, source_target_pairs={{0,1},{1,0},{2,3},{3,2},{4,5},{5,4},{6,7},{7,6},{8,9},{9,8},{10,11... | collective-permute-start | bytes 540680 | tf_op jit(solution)/shard_map/ppermute | solution.py:624
  26.1 1.7 %collective-permute-start.10 = (bf16[4,16,1408]{2,1,0:T(8,128)(2,1)S(1)}, bf16[4,16,1408]{2,1,0:T(8,128)(2,1)S(1)}, u32[]{:S(2)}, u32[]{:S(2)}) collective-permute-start(bf16[4,16,1408]{2,1,0:T(8,128)(2,1)S(1)} %collective-permute-done.4.b2), channel_id=1, source_target_pairs={{0,1},{1,0},{2,3},{3,2},{4,5},{5,4},{6,7},{7,6},{8,9},{9,8},{10,11... | collective-permute-start | bytes 540680 | tf_op jit(solution)/shard_map/ppermute | solution.py:624
  26.6 1.4 %collective-permute-start.11 = (bf16[4,16,1408]{2,1,0:T(8,128)(2,1)S(1)}, bf16[4,16,1408]{2,1,0:T(8,128)(2,1)S(1)}, u32[]{:S(2)}, u32[]{:S(2)}) collective-permute-start(bf16[4,16,1408]{2,1,0:T(8,128)(2,1)S(1)} %collective-permute-done.5.b3), channel_id=1, source_target_pairs={{0,1},{1,0},{2,3},{3,2},{4,5},{5,4},{6,7},{7,6},{8,9},{9,8},{10,11... | collective-permute-start | bytes 540680 | tf_op jit(solution)/shard_map/ppermute | solution.py:624
  29.3 3.8 %copy-start.20 = (bf16[16,48,256]{2,1,0:T(8,128)(2,1)S(1)}, bf16[16,48,256]{2,1,0:T(8,128)(2,1)}, u32[]{:S(2)}) copy-start(bf16[16,48,256]{2,1,0:T(8,128)(2,1)} %cot_ref.1) | copy-start | bytes 1179652
  43.6 1.9 %collective-permute-start.12 = (bf16[16,16,896]{2,1,0:T(8,128)(2,1)S(1)}, bf16[16,16,896]{2,1,0:T(8,128)(2,1)S(1)}, u32[]{:S(2)}, u32[]{:S(2)}) collective-permute-start(bf16[16,16,896]{2,1,0:T(8,128)(2,1)S(1)} %slice.80), channel_id=1, source_target_pairs={{0,1},{1,0},{2,3},{3,2},{4,5},{5,4},{6,7},{7,6},{8,9},{9,8},{10,11... | collective-permute-start | bytes 1376264 | tf_op jit(solution)/shard_map/ppermute | solution.py:624
  43.9 11.8 %collective-permute-start.16 = (bf16[640,512]{1,0:T(8,128)(2,1)S(1)}, bf16[640,512]{1,0:T(8,128)(2,1)S(1)}, u32[]{:S(2)}, u32[]{:S(2)}) collective-permute-start(bf16[640,512]{1,0:T(8,128)(2,1)S(1)} %get-tuple-element.130), channel_id=1, source_target_pairs={{0,1},{1,0},{2,3},{3,2},{4,5},{5,4},{6,7},{7,6},{8,9},{9,8},{10,11... | collective-permute-start | bytes 1966088 | tf_op jit(solution)/shard_map/ppermute | solution.py:722
  44.1 11.6 %collective-permute-start.17 = (bf16[640,512]{1,0:T(8,128)(2,1)S(1)}, bf16[640,512]{1,0:T(8,128)(2,1)S(1)}, u32[]{:S(2)}, u32[]{:S(2)}) collective-permute-start(bf16[640,512]{1,0:T(8,128)(2,1)S(1)} %get-tuple-element.131), channel_id=1, source_target_pairs={{1,2},{2,1},{3,4},{4,3},{5,6},{6,5},{9,10},{10,9},{11,12},{12,11},... | collective-permute-start | bytes 1966088 | tf_op jit(solution)/shard_map/ppermute | solution.py:723
  45.6 7.9 %collective-permute-start.13 = (bf16[4,16,896]{2,1,0:T(8,128)(2,1)S(1)}, bf16[4,16,896]{2,1,0:T(8,128)(2,1)S(1)}, u32[]{:S(2)}, u32[]{:S(2)}) collective-permute-start(bf16[4,16,896]{2,1,0:T(8,128)(2,1)S(1)} %get-tuple-element.172), channel_id=1, source_target_pairs={{0,8},{1,9},{2,10},{3,11},{4,12},{5,13},{6,14},{7,15},{8,0},{9,1},... | collective-permute-start | bytes 344072 | tf_op jit(solution)/shard_map/ppermute | solution.py:624
  47.2 6.4 %collective-permute-start.15 = (bf16[4,16,896]{2,1,0:T(8,128)(2,1)S(1)}, bf16[4,16,896]{2,1,0:T(8,128)(2,1)S(1)}, u32[]{:S(2)}, u32[]{:S(2)}) collective-permute-start(bf16[4,16,896]{2,1,0:T(8,128)(2,1)S(1)} %get-tuple-element.173), channel_id=1, source_target_pairs={{0,24},{1,25},{2,26},{3,27},{4,28},{5,29},{6,30},{7,31},{8,16},{9,... | collective-permute-start | bytes 344072 | tf_op jit(solution)/shard_map/ppermute | solution.py:624
  48.6 7.1 %collective-permute-start.14 = (bf16[4,16,896]{2,1,0:T(8,128)(2,1)S(1)}, bf16[4,16,896]{2,1,0:T(8,128)(2,1)S(1)}, u32[]{:S(2)}, u32[]{:S(2)}) collective-permute-start(bf16[4,16,896]{2,1,0:T(8,128)(2,1)S(1)} %get-tuple-element.174), channel_id=1, source_target_pairs={{0,16},{1,17},{2,18},{3,19},{4,20},{5,21},{6,22},{7,23},{8,24},{9,... | collective-permute-start | bytes 344072 | tf_op jit(solution)/shard_map/ppermute | solution.py:624
  58.8 18.5 %copy-start.1 = (f32[8,768]{1,0:T(8,128)S(1)}, f32[8,768]{1,0:T(8,128)}, u32[]{:S(2)}) copy-start(f32[8,768]{1,0:T(8,128)} %refs_2_.1) | copy-start | bytes 73732
  58.8 18.5 %copy-start.2 = (f32[8,768]{1,0:T(8,128)S(1)}, f32[8,768]{1,0:T(8,128)}, u32[]{:S(2)}) copy-start(f32[8,768]{1,0:T(8,128)} %refs_0_.1) | copy-start | bytes 73732
  58.8 18.5 %copy-start.3 = (f32[24,256]{1,0:T(8,128)S(1)}, f32[24,256]{1,0:T(8,128)}, u32[]{:S(2)}) copy-start(f32[24,256]{1,0:T(8,128)} %refs_3_.1) | copy-start | bytes 73732
  58.8 18.5 %copy-start.4 = (f32[8,256]{1,0:T(8,128)S(1)}, f32[8,256]{1,0:T(8,128)}, u32[]{:S(2)}) copy-start(f32[8,256]{1,0:T(8,128)} %refs_1_.1) | copy-start | bytes 24580
  58.9 18.5 %copy-start.5 = (f32[8,768]{1,0:T(8,128)S(1)}, f32[8,768]{1,0:T(8,128)}, u32[]{:S(2)}) copy-start(f32[8,768]{1,0:T(8,128)} %refs_10_.1) | copy-start | bytes 73732
  58.9 18.5 %copy-start.6 = (f32[8,768]{1,0:T(8,128)S(1)}, f32[8,768]{1,0:T(8,128)}, u32[]{:S(2)}) copy-start(f32[8,768]{1,0:T(8,128)} %refs_12_.1) | copy-start | bytes 73732
  58.9 18.5 %copy-start.7 = (f32[24,256]{1,0:T(8,128)S(1)}, f32[24,256]{1,0:T(8,128)}, u32[]{:S(2)}) copy-start(f32[24,256]{1,0:T(8,128)} %refs_13_.1) | copy-start | bytes 73732
  58.9 18.5 %copy-start.8 = (f32[8,768]{1,0:T(8,128)S(1)}, f32[8,768]{1,0:T(8,128)}, u32[]{:S(2)}) copy-start(f32[8,768]{1,0:T(8,128)} %refs_16_.1) | copy-start | bytes 73732
  58.9 18.5 %copy-start.9 = (f32[8,768]{1,0:T(8,128)S(1)}, f32[8,768]{1,0:T(8,128)}, u32[]{:S(2)}) copy-start(f32[8,768]{1,0:T(8,128)} %refs_18_.1) | copy-start | bytes 73732
  58.9 18.5 %copy-start.10 = (f32[24,256]{1,0:T(8,128)S(1)}, f32[24,256]{1,0:T(8,128)}, u32[]{:S(2)}) copy-start(f32[24,256]{1,0:T(8,128)} %refs_19_.1) | copy-start | bytes 73732
  58.9 18.5 %copy-start.11 = (f32[11,8]{0,1:T(8,128)S(1)}, f32[11,8]{0,1:T(8,128)}, u32[]{:S(2)}) copy-start(f32[11,8]{0,1:T(8,128)} %param.28) | copy-start | bytes 1060
  58.9 18.5 %copy-start.12 = (f32[8,256]{1,0:T(8,128)S(1)}, f32[8,256]{1,0:T(8,128)}, u32[]{:S(2)}) copy-start(f32[8,256]{1,0:T(8,128)} %refs_11_.1) | copy-start | bytes 24580
  58.9 18.5 %copy-start.13 = (f32[8,256]{1,0:T(8,128)S(1)}, f32[8,256]{1,0:T(8,128)}, u32[]{:S(2)}) copy-start(f32[8,256]{1,0:T(8,128)} %refs_17_.1) | copy-start | bytes 24580
  59.0 18.5 %copy-start.14 = (f32[11,8]{0,1:T(8,128)S(1)}, f32[11,8]{0,1:T(8,128)}, u32[]{:S(2)}) copy-start(f32[11,8]{0,1:T(8,128)} %param.38) | copy-start | bytes 1060
  59.0 18.5 %copy-start.15 = (f32[8,49]{1,0:T(8,128)S(1)}, f32[8,49]{1,0:T(8,128)}, u32[]{:S(2)}) copy-start(f32[8,49]{1,0:T(8,128)} %refs_15_.1) | copy-start | bytes 4708
  59.0 18.5 %copy-start.16 = (f32[11,8]{0,1:T(8,128)S(1)}, f32[11,8]{0,1:T(8,128)}, u32[]{:S(2)}) copy-start(f32[11,8]{0,1:T(8,128)} %param.39) | copy-start | bytes 1060
  59.0 18.5 %copy-start.17 = (f32[8,49]{1,0:T(8,128)S(1)}, f32[8,49]{1,0:T(8,128)}, u32[]{:S(2)}) copy-start(f32[8,49]{1,0:T(8,128)} %refs_21_.1) | copy-start | bytes 4708
  59.0 18.5 %copy-start.19 = (f32[8,49]{1,0:T(8,128)S(1)}, f32[8,49]{1,0:T(8,128)}, u32[]{:S(2)}) copy-start(f32[8,49]{1,0:T(8,128)} %refs_5_.3) | copy-start | bytes 4708
  59.0 2.1 %collective-permute-start.18 = (bf16[16,16,512]{2,1,0:T(8,128)(2,1)S(1)}, bf16[16,16,512]{2,1,0:T(8,128)(2,1)S(1)}, u32[]{:S(2)}, u32[]{:S(2)}) collective-permute-start(bf16[16,16,512]{2,1,0:T(8,128)(2,1)S(1)} %slice.70), channel_id=1, source_target_pairs={{0,1},{1,0},{2,3},{3,2},{4,5},{5,4},{6,7},{7,6},{8,9},{9,8},{10,11... | collective-permute-start | bytes 786440 | tf_op jit(solution)/shard_map/ppermute | solution.py:624
  61.2 4.5 %collective-permute-start.19 = (bf16[4,16,512]{2,1,0:T(8,128)(2,1)S(1)}, bf16[4,16,512]{2,1,0:T(8,128)(2,1)S(1)}, u32[]{:S(2)}, u32[]{:S(2)}) collective-permute-start(bf16[4,16,512]{2,1,0:T(8,128)(2,1)S(1)} %get-tuple-element.175), channel_id=1, source_target_pairs={{0,8},{1,9},{2,10},{3,11},{4,12},{5,13},{6,14},{7,15},{8,0},{9,1},... | collective-permute-start | bytes 196616 | tf_op jit(solution)/shard_map/ppermute | solution.py:624
  62.8 5.2 %collective-permute-start.21 = (bf16[4,16,512]{2,1,0:T(8,128)(2,1)S(1)}, bf16[4,16,512]{2,1,0:T(8,128)(2,1)S(1)}, u32[]{:S(2)}, u32[]{:S(2)}) collective-permute-start(bf16[4,16,512]{2,1,0:T(8,128)(2,1)S(1)} %get-tuple-element.176), channel_id=1, source_target_pairs={{0,24},{1,25},{2,26},{3,27},{4,28},{5,29},{6,30},{7,31},{8,16},{9,... | collective-permute-start | bytes 196616 | tf_op jit(solution)/shard_map/ppermute | solution.py:624
  64.2 5.1 %collective-permute-start.20 = (bf16[4,16,512]{2,1,0:T(8,128)(2,1)S(1)}, bf16[4,16,512]{2,1,0:T(8,128)(2,1)S(1)}, u32[]{:S(2)}, u32[]{:S(2)}) collective-permute-start(bf16[4,16,512]{2,1,0:T(8,128)(2,1)S(1)} %get-tuple-element.177), channel_id=1, source_target_pairs={{0,16},{1,17},{2,18},{3,19},{4,20},{5,21},{6,22},{7,23},{8,24},{9,... | collective-permute-start | bytes 196616 | tf_op jit(solution)/shard_map/ppermute | solution.py:624
  69.4 6.4 %collective-permute-start.24 = (bf16[16,1408]{1,0:T(8,128)(2,1)S(1)}, bf16[16,1408]{1,0:T(8,128)(2,1)S(1)}, u32[]{:S(2)}, u32[]{:S(2)}) collective-permute-start(bf16[16,1408]{1,0:T(8,128)(2,1)S(1)} %get-tuple-element.178), channel_id=1, source_target_pairs={{0,6},{1,7},{2,4},{3,5},{4,2},{5,3},{6,0},{7,1},{8,14},{9,15},{10,... | collective-permute-start | bytes 135176 | tf_op jit(solution)/shard_map/ppermute | solution.py:624
  70.8 6.4 %collective-permute-start.23 = (bf16[16,1408]{1,0:T(8,128)(2,1)S(1)}, bf16[16,1408]{1,0:T(8,128)(2,1)S(1)}, u32[]{:S(2)}, u32[]{:S(2)}) collective-permute-start(bf16[16,1408]{1,0:T(8,128)(2,1)S(1)} %get-tuple-element.179), channel_id=1, source_target_pairs={{0,4},{1,5},{2,6},{3,7},{4,0},{5,1},{6,2},{7,3},{8,12},{9,13},{10,... | collective-permute-start | bytes 135176 | tf_op jit(solution)/shard_map/ppermute | solution.py:624
  72.8 4.5 %collective-permute-start.22 = (bf16[16,1408]{1,0:T(8,128)(2,1)S(1)}, bf16[16,1408]{1,0:T(8,128)(2,1)S(1)}, u32[]{:S(2)}, u32[]{:S(2)}) collective-permute-start(bf16[16,1408]{1,0:T(8,128)(2,1)S(1)} %get-tuple-element.180), channel_id=1, source_target_pairs={{0,2},{1,3},{2,0},{3,1},{4,6},{5,7},{6,4},{7,5},{8,10},{9,11},{10,... | collective-permute-start | bytes 135176 | tf_op jit(solution)/shard_map/ppermute | solution.py:624
  78.4 1.2 %collective-permute-start.25 = (f32[8,128]{1,0:T(8,128)S(1)}, f32[8,128]{1,0:T(8,128)S(1)}, u32[]{:S(2)}, u32[]{:S(2)}) collective-permute-start(f32[8,128]{1,0:T(8,128)S(1)} %get-tuple-element.145.mine_ref), channel_id=1, source_target_pairs={{0,1},{1,0},{2,3},{3,2},{4,5},{5,4},{6,7},{7,6},{8,9},{9,8},{10,11... | collective-permute-start | bytes 12296 | tf_op jit(solution)/shard_map/ppermute | solution.py:624
  79.6 4.5 %collective-permute-start.28 = (f32[8,128]{1,0:T(8,128)S(1)}, f32[8,128]{1,0:T(8,128)S(1)}, u32[]{:S(2)}, u32[]{:S(2)}) collective-permute-start(f32[8,128]{1,0:T(8,128)S(1)} %add.82), channel_id=1, source_target_pairs={{0,24},{1,25},{2,26},{3,27},{4,28},{5,29},{6,30},{7,31},{8,16},{9,... | collective-permute-start | bytes 12296 | tf_op jit(solution)/shard_map/ppermute | solution.py:624
  81.2 3.6 %collective-permute-start.27 = (f32[8,128]{1,0:T(8,128)S(1)}, f32[8,128]{1,0:T(8,128)S(1)}, u32[]{:S(2)}, u32[]{:S(2)}) collective-permute-start(f32[8,128]{1,0:T(8,128)S(1)} %add.82), channel_id=1, source_target_pairs={{0,16},{1,17},{2,18},{3,19},{4,20},{5,21},{6,22},{7,23},{8,24},{9,... | collective-permute-start | bytes 12296 | tf_op jit(solution)/shard_map/ppermute | solution.py:624
  82.4 3.6 %collective-permute-start.26 = (f32[8,128]{1,0:T(8,128)S(1)}, f32[8,128]{1,0:T(8,128)S(1)}, u32[]{:S(2)}, u32[]{:S(2)}) collective-permute-start(f32[8,128]{1,0:T(8,128)S(1)} %add.82), channel_id=1, source_target_pairs={{0,8},{1,9},{2,10},{3,11},{4,12},{5,13},{6,14},{7,15},{8,0},{9,1},... | collective-permute-start | bytes 12296 | tf_op jit(solution)/shard_map/ppermute | solution.py:624
  86.1 5.4 %collective-permute-start.31 = (f32[8,128]{1,0:T(8,128)S(1)}, f32[8,128]{1,0:T(8,128)S(1)}, u32[]{:S(2)}, u32[]{:S(2)}) collective-permute-start(f32[8,128]{1,0:T(8,128)S(1)} %add_add_fusion.a_ref), channel_id=1, source_target_pairs={{0,6},{1,7},{2,4},{3,5},{4,2},{5,3},{6,0},{7,1},{8,14},{9,15},{10,... | collective-permute-start | bytes 12296 | tf_op jit(solution)/shard_map/ppermute | solution.py:624
  87.0 4.6 %collective-permute-start.30 = (f32[8,128]{1,0:T(8,128)S(1)}, f32[8,128]{1,0:T(8,128)S(1)}, u32[]{:S(2)}, u32[]{:S(2)}) collective-permute-start(f32[8,128]{1,0:T(8,128)S(1)} %add_add_fusion.a_ref), channel_id=1, source_target_pairs={{0,4},{1,5},{2,6},{3,7},{4,0},{5,1},{6,2},{7,3},{8,12},{9,13},{10,... | collective-permute-start | bytes 12296 | tf_op jit(solution)/shard_map/ppermute | solution.py:624
  87.5 4.5 %collective-permute-start.29 = (f32[8,128]{1,0:T(8,128)S(1)}, f32[8,128]{1,0:T(8,128)S(1)}, u32[]{:S(2)}, u32[]{:S(2)}) collective-permute-start(f32[8,128]{1,0:T(8,128)S(1)} %add_add_fusion.a_ref), channel_id=1, source_target_pairs={{0,2},{1,3},{2,0},{3,1},{4,6},{5,7},{6,4},{7,5},{8,10},{9,11},{10,... | collective-permute-start | bytes 12296 | tf_op jit(solution)/shard_map/ppermute | solution.py:624

commit v5 on v4

--- a/solution.py
+++ b/solution.py
@@ -21,6 +21,8 @@
 RATIO_EPS = 1e-06
 MASKED = -1e30
 LOG2E = 1.4426950408889634
+GELU0 = 0.7978845608028654
+GELU1 = 0.044715
 AXES = ("maps", "band")
 
 BF = jnp.bfloat16
@@ -100,7 +102,9 @@
     return (((12 * (nr - 3) + nc - 3) & (KN - 1)) == lane).astype(F32)
 
 
-def prep_kernel(sizes_ref, table_ref, x_ref, bias_ref, limits_ref, po_ref, pk_ref, xp_ref, xhat_ref, rstd_ref):
+def prep_kernel(
+    sizes_ref, table_ref, x_ref, cot_ref, bias_ref, limits_ref, po_ref, pk_ref, xp_ref, xhat_ref, rstd_ref, dy_ref, dysum_ref
+):
     po_ref[...] = select((4 * QN, 4 * 48), own_source)
     pk_ref[...] = select((4 * KN, 10 * 48), key_source)
     row = lax.broadcasted_iota(jnp.int32, (8, 128), 0)
@@ -133,9 +137,13 @@
         xhat, rstd = normed(xp)
         xhat_ref[at, :] = xhat
         rstd_ref[at, :] = jnp.broadcast_to(rstd, (192, 128))
+        dy = dot(po_ref[...], jnp.concatenate([cot_ref[4 * i + rc] for i in range(4)], axis=0))
+        dy_ref[at, :] = dy.astype(BF)
+        dysum_ref[...] += jnp.sum(dy, axis=0, keepdims=True)
         return 0
 
-    lax.fori_loop(0, 4, block, 0, unroll=2)
+    dysum_ref[...] = jnp.zeros_like(dysum_ref)
+    lax.fori_loop(0, 4, block, 0, unroll=4)
 
 
 def halo_kernel(x_ref, xc_ref, xz_ref, pk_ref, xk_ref):
@@ -202,46 +210,33 @@
         mixed_ref[at_q, :] = pick_heads(full, lane_head).astype(BF)
         return 0
 
-    lax.fori_loop(0, CLS, attend, 0, unroll=4)
+    lax.fori_loop(0, CLS, attend, 0, unroll=CLS)
 
 
 def feed_kernel(
-    cot_ref,
+    dy_ref,
+    dysum_ref,
     mixed_ref,
     xp_ref,
-    q_ref,
-    k_ref,
-    v_ref,
-    p_ref,
     wo_ref,
     wu_ref,
     wd_ref,
     vec_ref,
-    po_ref,
     act_ref,
-    dy_ref,
     dz_ref,
     a2_ref,
     da_ref,
     dx1_ref,
     x1_ref,
-    own_ref,
-    rimc_ref,
-    rimz_ref,
-    dsl_ref,
-    tacc_ref,
+    dmix_ref,
     sums_ref,
     zsum_ref,
-    dmix_ref,
 ):
-    odd = (lax.axis_index("band") & 1) == 1
-    scale = 32 ** (-0.5)
-    lane_head = lax.broadcasted_iota(jnp.int32, (QN, 256), 1) >> 5
-
     def vrow(i):
         return vec_ref[i : i + 1, :]
 
     sums_ref[...] = jnp.zeros_like(sums_ref)
+    sums_ref[7:8, :] = dysum_ref[...]
     zsum_ref[...] = jnp.zeros_like(zsum_ref)
 
     def feed(rc, _):
@@ -251,22 +246,21 @@
         xhat, rstd = normed(x1)
         a2 = (xhat * vrow(5) + vrow(6)).astype(BF)
         a2_ref[at, :] = a2
-        bias = jnp.concatenate([vrow(8), vrow(9), vrow(10)], axis=1)
-        z = dot(a2, wu_ref[...]) + bias
-        c0 = 0.7978845608028654
-        c1 = 0.044715
-        z2 = z * z
-        t = jnp.tanh(z * (c0 + c0 * c1 * z2))
-        hz = 0.5 * z
-        act_ref[at, :] = (hz + hz * t).astype(BF)
-        dyf = dot(po_ref[...], jnp.concatenate([cot_ref[4 * i + rc] for i in range(4)], axis=0))
-        dy = dyf.astype(BF)
-        dy_ref[at, :] = dy
-        slope = (0.5 + 0.5 * t) + (hz - hz * (t * t)) * (c0 + 3.0 * c0 * c1 * z2)
-        dz = (dot_nt(dy, wd_ref[...]) * slope).astype(BF)
-        dz_ref[at, :] = dz
-        zsum_ref[...] += jnp.sum(dz.astype(F32), axis=0, keepdims=True)
-        dn = dot_nt(dz, wu_ref[...])
+        dy = dy_ref[at, :]
+        dn = jnp.zeros((192, 256), F32)
+        for part in range(3):
+            cols = slice(256 * part, 256 * part + 256)
+            z = dot(a2, wu_ref[:, cols]) + vrow(8 + part)
+            cube = (GELU0 * GELU1) * (z * z)
+            up = 1.0 + jnp.tanh(z * (GELU0 + cube))
+            hz = 0.5 * z
+            act_ref[at, cols] = (hz * up).astype(BF)
+            slope = up * (0.5 + hz * (2.0 - up) * (GELU0 + 3.0 * cube))
+            dz = (dot_nt(dy, wd_ref[cols, :]) * slope).astype(BF)
+            dz_ref[at, cols] = dz
+            zsum_ref[:, cols] += jnp.sum(dz.astype(F32), axis=0, keepdims=True)
+            dn = dn + dot_nt(dz, wu_ref[:, cols])
+        dyf = dy.astype(F32)
         dx1 = dyf + norm_back(dn * vrow(5), xhat, rstd)
         dx1_ref[at, :] = dx1
         da = dx1.astype(BF)
@@ -275,11 +269,25 @@
         sums_ref[4:5, :] += jnp.sum(da.astype(F32), axis=0, keepdims=True)
         sums_ref[5:6, :] += jnp.sum(dn * xhat, axis=0, keepdims=True)
         sums_ref[6:7, :] += jnp.sum(dn, axis=0, keepdims=True)
-        sums_ref[7:8, :] += jnp.sum(dyf, axis=0, keepdims=True)
         return 0
 
-    lax.fori_loop(0, 4, feed, 0, unroll=2)
-
+    lax.fori_loop(0, 4, feed, 0, unroll=4)
+
+
+def back_kernel(
+    q_ref,
+    v_ref,
+    p_ref,
+    dmix_ref,
+    own_ref,
+    rimc_ref,
+    rimz_ref,
+    dsl_ref,
+    tacc_ref,
+):
+    odd = (lax.axis_index("band") & 1) == 1
+    scale = 32 ** (-0.5)
+    lane_head = lax.broadcasted_iota(jnp.int32, (QN, 256), 1) >> 5
     tacc_ref[...] = jnp.zeros_like(tacc_ref)
 
     def back_class(k):
@@ -312,7 +320,7 @@
         rimz_ref[at, :] = jnp.where(odd, after, before).astype(BF)
         return 0
 
-    lax.fori_loop(0, CLS // 2, attend_back, 0, unroll=2)
+    lax.fori_loop(0, CLS // 2, attend_back, 0, unroll=8)
 
 
 def early_grads(act_ref, dy_ref, a2_ref, dz_ref, mixed_ref, da_ref, fd, fu, fo):
@@ -349,7 +357,7 @@
         dq_ref[at_q, :] = dq.astype(BF)
         return 0
 
-    lax.fori_loop(0, CLS, query, 0, unroll=4)
+    lax.fori_loop(0, CLS, query, 0, unroll=16)
     dq = dq_ref[...]
     qsum_ref[...] = jnp.sum(dq.astype(F32), axis=0, keepdims=True)
     fwq_ref[...] = dot_tn(a1_ref[...], dq)
@@ -382,14 +390,10 @@
     gotc_ref,
     gotz_ref,
     dnq_ref,
-    dx1_ref,
     xhat_ref,
-    rstd_ref,
     wqkv_ref,
-    vec_ref,
-    po_ref,
     a1_ref,
-    tok_ref,
+    dn_ref,
     fkv_ref,
     sums_ref,
     dkv_ref,
@@ -413,18 +417,26 @@
         dkv = jnp.concatenate(parts, axis=0).astype(BF)
         dkv_ref[at, :] = dkv
         dn = dnq_ref[at, :] + dot_nt(dkv, wqkv_ref[:, 256:768])
-        xhat = xhat_ref[at, :]
-        dx = dx1_ref[at, :] + norm_back(dn * vec_ref[0:1, :], xhat, rstd_ref[at, 0:1])
+        dn_ref[at, :] = dn
+        sums_ref[0:1, :] += jnp.sum(dn * xhat_ref[at, :], axis=0, keepdims=True)
+        sums_ref[1:2, :] += jnp.sum(dn, axis=0, keepdims=True)
+        sums_ref[3:4, :] += jnp.sum(dkv[:, 256:512].astype(F32), axis=0, keepdims=True)
+        return 0
+
+    lax.fori_loop(0, 4, block, 0, unroll=4)
+    fkv_ref[...] = dot_tn(a1_ref[...], dkv_ref[...])
+
+
+def input_kernel(dn_ref, dx1_ref, xhat_ref, rstd_ref, vec_ref, po_ref, tok_ref):
+    def block(rc, _):
+        at = pl.ds(pl.multiple_of(rc * 192, 192), 192)
+        dx = dx1_ref[at, :] + norm_back(dn_ref[at, :] * vec_ref[0:1, :], xhat_ref[at, :], rstd_ref[at, 0:1])
         back = dot_tn(po_ref[...], dx.astype(BF)).astype(BF)
         for i in range(4):
             tok_ref[4 * i + rc] = back[48 * i : 48 * i + 48]
-        sums_ref[0:1, :] += jnp.sum(dn * xhat, axis=0, keepdims=True)
-        sums_ref[1:2, :] += jnp.sum(dn, axis=0, keepdims=True)
-        sums_ref[3:4, :] += jnp.sum(dkv[:, 256:512].astype(F32), axis=0, keepdims=True)
         return 0
 
-    lax.fori_loop(0, 4, block, 0, unroll=2)
-    fkv_ref[...] = dot_tn(a1_ref[...], dkv_ref[...])
+    lax.fori_loop(0, 4, block, 0, unroll=4)
 
 
 EARLY = 896
@@ -475,10 +487,8 @@
     project_kernel(xhat_ref, xk_ref, big_qkv, vec, *outs)
 
 
-def feed_packed(
-    cot_ref, mixed_ref, xp_ref, q_ref, k_ref, v_ref, p_ref, vec_ref, po_ref, b0, b1, b2, b3, b4, b5, b6, b7, *rest
-):
-    outs, big_down, (dmix, big_out, big_up, fo, fu, fd) = rest[:14], rest[14], rest[15:]
+def feed_packed(dy_ref, dysum_ref, mixed_ref, xp_ref, vec_ref, b0, b1, b2, b3, b4, b5, b6, b7, *rest):
+    outs, big_down, (big_out, big_up, fo, fu, fd) = rest[:9], rest[9], rest[10:]
     for o, slab in sorted_slabs((b0, b1, b2, b3, b4, b5, b6, b7)):
         at = pl.ds(pl.multiple_of(o * 8, 8), 8)
         for b, rows in enumerate((slab[0:8, 1024:1280], slab[8:16, 768:1024], slab[8:16, 1024:1280])):
@@ -488,9 +498,7 @@
     big_out[...] = fo[...].astype(BF)
     big_up[...] = fu[...].astype(BF)
     big_down[...] = fd[...].astype(BF)
-    feed_kernel(
-        cot_ref, mixed_ref, xp_ref, q_ref, k_ref, v_ref, p_ref, big_out, big_up, big_down, vec_ref, po_ref, *outs, dmix
-    )
+    feed_kernel(dy_ref, dysum_ref, mixed_ref, xp_ref, big_out, big_up, big_down, vec_ref, *outs)
 
 
 def frame_slot(me, o):
@@ -515,9 +523,9 @@
 
 
 def late_kernel(*refs):
-    sums, zsum, qsum, fwq, tgrad = refs[11:16]
-    tok_ref, out_ref, fkv, sums2, dkv, fv = refs[16:]
-    finish_kernel(*refs[:11], tok_ref, fkv, sums2, dkv)
+    sums, zsum, qsum, fwq, tgrad = refs[7:12]
+    dn_ref, out_ref, fkv, sums2, dkv, fv = refs[12:]
+    finish_kernel(*refs[:7], dn_ref, fkv, sums2, dkv)
     lines = jnp.concatenate(
         [sums[...] + sums2[...] + qrow(qsum[...])]
         + [zsum[:, 256 * i : 256 * i + 256] for i in range(3)]
@@ -676,6 +684,8 @@
         sds((768, 256), F32),
         sds((768, 256), F32),
         sds((768, 128), F32),
+        sds((768, 256)),
+        sds((1, 256), F32),
     )
 
 
@@ -690,19 +700,24 @@
 def feed_outputs():
     return (
         sds((768, 768)),
-        sds((768, 256)),
         sds((768, 768)),
         sds((768, 256)),
         sds((768, 256)),
         sds((768, 256), F32),
         sds((768, 256), F32),
+        sds((768, 256)),
+        sds((8, 256), F32),
+        sds((1, 768), F32),
+    )
+
+
+def back_outputs():
+    return (
         sds((768, 512), F32),
         sds((CLS * RIM, 512)),
         sds((CLS * RIM, 512)),
         sds((CLS * KN, 384)),
         sds((KN, 384), F32),
-        sds((8, 256), F32),
-        sds((1, 768), F32),
     )
 
 
@@ -741,11 +756,11 @@
     column, x = lax.optimization_barrier((column, tokens_in))
     blocks = [column] + [swap(column, d << 3, count) for d in (1, 2, 3)]
     x_core, x_next = beside((x, x), 8)
-    bias, limits, po, pk, xp, xhat, rstd = call(
-        prep_kernel, prep_outputs(), [], map_sizes, weights[5], x, smem=1, flops=2 * 10**9, vmem=8
-    )
+    bias, limits, po, pk, xp, xhat, rstd, dy, dysum = call(
+        prep_kernel, prep_outputs(), [], map_sizes, weights[5], x, cotangent, smem=1, flops=2 * 10**9, vmem=8
+    )
+    *far, pk = lax.optimization_barrier((*blocks[1:], pk))
     xk = call(halo_kernel, sds((CLS * KN, 256), F32), [], x, x_core, x_next, pk, flops=10**9, vmem=8)
-    *far, xk = lax.optimization_barrier((*blocks[1:], xk))
     blocks = [blocks[0]] + far + [swap(block, 1, count) for block in [blocks[0]] + far]
     a1, queries, keys, values, big_qkv, vec = call(
         project_packed,
@@ -757,24 +772,26 @@
     mixed, probs = call(
         attend_kernel, attend_outputs(), [], limits, bias, queries, keys, values, flops=3 * 10**9, vmem=8
     )
-    (
-        act, dy, dz, a2, da, dx1, x1, own, rim_c, rim_z, dsl, tacc, sums, zsum, big_down,
-    ) = call(
+    act, dz, a2, da, dx1, x1, dmix, sums, zsum, big_down = call(
         feed_packed,
         feed_outputs() + (sds((768, 256)),),
-        [pltpu.VMEM((768, 256), BF), pltpu.VMEM((256, 256), BF), pltpu.VMEM((256, 768), BF)]
+        [pltpu.VMEM((256, 256), BF), pltpu.VMEM((256, 768), BF)]
         + [pltpu.VMEM(m, F32) for m in ((256, 256), (256, 768), (768, 256))],
-        cotangent, mixed, xp, queries, keys, values, probs, vec, po, *blocks,
-        flops=4 * 10**9,
-    )
-    got_c, got_z = beside((rim_c, rim_z), 8)
+        dy, dysum, mixed, xp, vec, *blocks,
+        flops=4 * 10**9, vmem=8,
+    )
     early = call(
         early_kernel,
         sds((count, 16, EARLY)),
         [pltpu.VMEM((768, 256), F32), pltpu.VMEM((256, 768), F32), pltpu.VMEM((256, 256), F32)],
         act, dy, a2, dz, mixed, da,
-        flops=10**9,
-    )
+        flops=10**9, vmem=8,
+    )
+    early, dmix = lax.optimization_barrier((early, dmix))
+    own, rim_c, rim_z, dsl, tacc = call(
+        back_kernel, back_outputs(), [], queries, values, probs, dmix, flops=4 * 10**9, vmem=8
+    )
+    got_c, got_z = beside((rim_c, rim_z), 8)
     early = add_stage(early, 0, 1, count)
     early, tacc = lax.optimization_barrier((early, tacc))
     layer_out, dnq, fwq, tgrad, qsum = call(
@@ -786,18 +803,19 @@
     )
     early = add_stage(early, 3, 2, count)
     early, own = lax.optimization_barrier((early, own))
-    tokens_grad, late = call(
+    dn, late = call(
         late_kernel,
-        (sds((16, 48, 256)), sds((count, 16, LATE))),
+        (sds((768, 256), F32), sds((count, 16, LATE))),
         [
             pltpu.VMEM((256, 512), F32),
             pltpu.VMEM((8, 256), F32),
             pltpu.VMEM((768, 512), BF),
             pltpu.VMEM((256, 128), F32),
         ],
-        own, got_c, got_z, dnq, dx1, xhat, rstd, big_qkv, vec, po, a1, sums, zsum, qsum, fwq, tgrad,
-        flops=10**9,
-    )
+        own, got_c, got_z, dnq, xhat, big_qkv, a1, sums, zsum, qsum, fwq, tgrad,
+        flops=10**9, vmem=8,
+    )
+    tokens_grad = call(input_kernel, sds((16, 48, 256)), [], dn, dx1, xhat, rstd, vec, po, flops=10**9, vmem=8)
     late = add_stage(add_stage(late, 0, 1, count), 3, 2, count)
     grads = jnp.concatenate([early, late], axis=-1)
     low = grads.astype(BF)
@@ -892,19 +910,20 @@
     )
     vec = whole[:, 2560 : 2560 + vrows].T.astype(F32)
 
-    bias, limits, po, pk, xp, xhat, rstd = call(
-        prep_kernel, prep_outputs(), [], map_sizes, pos_table, tokens_in, smem=1, flops=2 * 10**9
+    bias, limits, po, pk, xp, xhat, rstd, dy, dysum = call(
+        prep_kernel, prep_outputs(), [], map_sizes, pos_table, tokens_in, cotangent, smem=1, flops=2 * 10**9
     )
     xk = call(halo_kernel, sds((CLS * KN, 256), F32), [], tokens_in, x_core, x_next, pk, flops=10**9)
     a1, queries, keys, values = call(project_kernel, project_outputs(), [], xhat, xk, big_qkv, vec, flops=10**9)
     mixed, probs = call(attend_kernel, attend_outputs(), [], limits, bias, queries, keys, values, flops=3 * 10**9)
-    act, dy, dz, a2, da, dx1, x1, own, rim_c, rim_z, dsl, tacc, sums, zsum = call(
+    act, dz, a2, da, dx1, x1, dmix, sums, zsum = call(
         feed_kernel,
         feed_outputs(),
-        [pltpu.VMEM((768, 256), BF)],
-        cotangent, mixed, xp, queries, keys, values, probs, big_out, big_up, big_down, vec, po,
+        [],
+        dy, dysum, mixed, xp, big_out, big_up, big_down, vec,
         flops=4 * 10**9,
     )
+    own, rim_c, rim_z, dsl, tacc = call(back_kernel, back_outputs(), [], queries, values, probs, dmix, flops=4 * 10**9)
     got_c, got_z = beside((rim_c, rim_z), band)
     grad_down, grad_up, grad_out = call(
         early_grads,
@@ -920,13 +939,14 @@
         x1, act, dsl, keys, tacc, a1, big_down, big_qkv, vec, po,
         flops=3 * 10**9,
     )
-    tokens_grad, fkv, sums2 = call(
+    dn, fkv, sums2 = call(
         finish_kernel,
-        (sds((16, 48, 256)), sds((256, 512), F32), sds((8, 256), F32)),
+        (sds((768, 256), F32), sds((256, 512), F32), sds((8, 256), F32)),
         [pltpu.VMEM((768, 512), BF)],
-        own, got_c, got_z, dnq, dx1, xhat, rstd, big_qkv, vec, po, a1,
+        own, got_c, got_z, dnq, xhat, big_qkv, a1,
         flops=10**9,
     )
+    tokens_grad = call(input_kernel, sds((16, 48, 256)), [], dn, dx1, xhat, rstd, vec, po, flops=10**9)
     grad_qkv = jnp.concatenate([fwq, fkv], axis=1)
     sums2 = sums2.at[2:3].add(qsum)
     grad_vec = jnp.concatenate([sums + sums2, zsum.reshape(3, 256)], axis=0)

time: 93.1 us -> 88.4 us (0.950)
  Pallas kernels: 28 us -> 23.3 us
  waiting for transfers between devices: 25 us -> 21.9 us
  starting transfers between devices: 34.1 us -> 36.2 us
  local copies, waits for them, and re-layouts: 3.31 us -> 4.3 us
    pallas_call x11 -> x13, Pallas kernels: 28 us -> 23.3 us  [call(): pl.pallas_call(kernel, out_shape=out_shape, in_specs=specs, out_specs=jax...]
    ppermute x28, waiting for transfers between devices: 25 us -> 21.9 us  [swap(): return lax.ppermute(block, AXES, [(k, k ^ mask) for k in range(count)])]
    ppermute x28, starting transfers between devices: 30.6 us -> 32.8 us  [swap(): return lax.ppermute(block, AXES, [(k, k ^ mask) for k in range(count)])]
    unnamed x44, local copies, waits for them, and re-layouts: 2.46 us -> 3.45 us
  transfers between devices with their start and end apart: 32 -> 32, of which waited for: 23 -> 17; matrix products, arithmetic and copies ran while one was open for 0% -> 0% of each run, Pallas kernels for 8% -> 13%
where the time goes in v5:
time: 88.4 us; the launch traced here: 88 us
  starting transfers between devices  36.2 us (41%)
  Pallas kernels  23.3 us (26%)
  waiting for transfers between devices  21.9 us (25%)
  local copies, waits for them, and re-layouts  4.3 us (5%)
  between operations  1.2 us (1%)
  other arithmetic  1.17 us (1%)
    ppermute x28, starting transfers between devices, swap(): return lax.ppermute(block, AXES, [(k, k ^ mask) for k in range(count)])  32.8 us
    pallas_call x13, Pallas kernels, call(): pl.pallas_call(kernel, out_shape=out_shape, in_specs=specs, out_specs=jax...  23.3 us
    ppermute x28, waiting for transfers between devices, swap(): return lax.ppermute(block, AXES, [(k, k ^ mask) for k in range(count)])  21.9 us
    unnamed x44, local copies, waits for them, and re-layouts  3.45 us
    ppermute x2, starting transfers between devices, beside(): lax.ppermute(block[0], 'band', [(b, b ^ 1) for b in range(band)])  1.86 us
  transfers between devices with their start and end apart: 32, of which 17 were waited for; matrix products, arithmetic and copies ran while one was open for 0% of the time, Pallas kernels for 13%

profile of v5, /device:TPU:0, one launch (start us, length us, event | category | flops | bytes accessed | tf_op | source)
XLA Modules:
  0.0 88.0 jit_solution(9522731314602172309)
XLA Ops:
  0.7 0.7 fusion.8
  1.4 0.8 add_convert_fusion.refs_0_
  2.2 5.1 %collective-permute-start.2 = (bf16[16,1408]{1,0:T(8,128)(2,1)S(1)}, bf16[16,1408]{1,0:T(8,128)(2,1)S(1)}, u32[]{:S(2)}, u32[]{:S(2)}) collective-permute-start(bf16[16,1408]{1,0:T(8,128)(2,1)S(1)} %add_convert_fusion.refs_0_), channel_id=1, source_target_pairs={{0,6},{1,7},{2,4},{3,5},{4,2},{5,3},{6,0},{7,1},{8,14},{9,15},{10,... | collective-permute-start | bytes 135176 | tf_op jit(solution)/shard_map/ppermute | solution.py:632
  7.3 0.6 collective-permute-start
  7.9 1.4 %collective-permute-done.2.refs_3_ = bf16[16,1408]{1,0:T(8,128)(2,1)S(1)} collective-permute-done((bf16[16,1408]{1,0:T(8,128)(2,1)S(1)}, bf16[16,1408]{1,0:T(8,128)(2,1)S(1)}, u32[]{:S(2)}, u32[]{:S(2)}) %collective-permute-start.2) | collective-permute-done | bytes 45088 | tf_op jit(solution)/shard_map/ppermute | solution.py:632
  9.4 2.9 %collective-permute-done.1.refs_2_ = bf16[16,1408]{1,0:T(8,128)(2,1)S(1)} collective-permute-done((bf16[16,1408]{1,0:T(8,128)(2,1)S(1)}, bf16[16,1408]{1,0:T(8,128)(2,1)S(1)}, u32[]{:S(2)}, u32[]{:S(2)}) %collective-permute-start.1) | collective-permute-done | bytes 45088 | tf_op jit(solution)/shard_map/ppermute | solution.py:632
  12.2 0.7 collective-permute-start.4
  12.9 1.8 %collective-permute-start.3 = (bf16[16,48,256]{2,1,0:T(8,128)(2,1)}, bf16[16,48,256]{2,1,0:T(8,128)(2,1)S(1)}, u32[]{:S(2)}, u32[]{:S(2)}) collective-permute-start(bf16[16,48,256]{2,1,0:T(8,128)(2,1)} %x_ref.1), channel_id=1, source_target_pairs={{0,1},{1,0},{2,3},{3,2},{4,5},{5,4},{6,7},{7,6},{8,9},{9,8},{10,11... | collective-permute-start | bytes 1179656 | tf_op jit(solution)/shard_map/ppermute | solution.py:737
  14.7 2.4 %collective-permute-start.7 = (bf16[4,16,1408]{2,1,0:T(8,128)(2,1)S(1)}, bf16[4,16,1408]{2,1,0:T(8,128)(2,1)S(1)}, u32[]{:S(2)}, u32[]{:S(2)}) collective-permute-start(bf16[4,16,1408]{2,1,0:T(8,128)(2,1)S(1)} %shard_map.372.b0), channel_id=1, source_target_pairs={{0,24},{1,25},{2,26},{3,27},{4,28},{5,29},{6,30},{7,31},{8,16},{9,... | collective-permute-start | bytes 540680 | tf_op jit(solution)/shard_map/ppermute | solution.py:632
  17.2 0.5 collective-permute-start.6
  17.7 0.5 collective-permute-start.5
  18.2 1.0 %copy-done = bf16[16,48,256]{2,1,0:T(8,128)(2,1)S(1)} copy-done((bf16[16,48,256]{2,1,0:T(8,128)(2,1)S(1)}, bf16[16,48,256]{2,1,0:T(8,128)(2,1)}, u32[]{:S(2)}) %copy-start) | copy-done | bytes 393240
  19.2 0.7 copy-done.18
  19.9 1.0 %copy-done.20 = bf16[16,48,256]{2,1,0:T(8,128)(2,1)S(1)} copy-done((bf16[16,48,256]{2,1,0:T(8,128)(2,1)S(1)}, bf16[16,48,256]{2,1,0:T(8,128)(2,1)}, u32[]{:S(2)}) %copy-start.20) | copy-done | bytes 393240
  20.9 0.7 copy-done.21
  21.5 1.5 %shard_map.373 = (f32[128,384]{1,0:T(8,128)S(1)}, s32[8,128]{1,0:T(8,128)S(1)}, bf16[192,192]{1,0:T(8,128)(2,1)S(1)}, bf16[512,480]{1,0:T(8,128)(2,1)S(1)}, f32[...) custom-call(s32[1,2]{1,0:T(1,128)S(1)} %copy-done.21, ...), custom_call_target="tpu_custom_call" | custom-call | flops 2000000000 | bytes 1000000 | tf_op jit(solution)/shard_map/pallas_call | solution.py:609
  23.2 2.8 %collective-permute-done.6.b2 = bf16[4,16,1408]{2,1,0:T(8,128)(2,1)S(1)} collective-permute-done((bf16[4,16,1408]{2,1,0:T(8,128)(2,1)S(1)}, bf16[4,16,1408]{2,1,0:T(8,128)(2,1)S(1)}, u32[]{:S(2)}, u32[]{:S(2)}) %collective-permute-start.6) | collective-permute-done | bytes 180256 | tf_op jit(solution)/shard_map/ppermute | solution.py:632
  26.0 0.1 collective-permute-done.5.b1
  26.1 0.5 collective-permute-start.10
  26.6 1.4 %shard_map.374.xk_ref = f32[2048,256]{1,0:T(8,128)S(1)} custom-call(bf16[16,48,256]{2,1,0:T(8,128)(2,1)S(1)} %copy-done, bf16[16,48,256]{2,1,0:T(8,128)(2,1)S(1)} %collective-permute-done.3.xc_ref, bf16[16,48,256]{2,1,0:T(8,128)(2,1)S(1)} %collective-permute-done.4.xz_ref, bf16[512,480]{1,0:T(8,128)(2,1)S(1)} %get-tuple-element.108.pk_ref), custom_call_target="tpu_custom_call" | custom-call | flops 1000000000 | bytes 1000000 | tf_op jit(solution)/shard_map/pallas_call | solution.py:609
  28.1 1.2 %shard_map.375 = (bf16[768,256]{1,0:T(8,128)(2,1)S(1)}, bf16[768,256]{1,0:T(8,128)(2,1)S(1)}, bf16[2048,256]{1,0:T(8,128)(2,1)S(1)}, bf16[2048,256]{1,0:T(8,128)...) custom-call(f32[768,256]{1,0:T(8,128)S(1)} %get-tuple-element.105.xhat_ref.refs_4_, ...), custom_call_target="tpu_custom_call" | custom-call | flops 1000000000 | bytes 1000000 | tf_op jit(solution)/shard_map/pallas_call | solution.py:609
  29.4 2.6 %shard_map.376 = (bf16[768,256]{1,0:T(8,128)(2,1)S(1)}, f32[2048,384]{1,0:T(8,128)S(1)}) custom-call(s32[8,128]{1,0:T(8,128)S(1)} %get-tuple-element.103.limits_ref, f32[128,384]{1,0:T(8,128)S(1)} %get-tuple-element.104.bias_ref, bf16[768,256]{1,0:T(8,128)(2,1)S(1)} %get-tuple-element.112.q_ref, bf16[2048,256]{1,0:T(8,128)(2,1)S(1)} %get-tuple-element.113.k_ref, ...), custom_call_target="tpu_custom_call" | custom-call | flops 3000000000 | bytes 1000000 | tf_op jit(solution)/shard_map/pallas_call | solution.py:609
  32.0 4.4 %shard_map.377 = (bf16[768,768]{1,0:T(8,128)(2,1)S(1)}, bf16[768,768]{1,0:T(8,128)(2,1)S(1)}, bf16[768,256]{1,0:T(8,128)(2,1)S(1)}, bf16[768,256]{1,0:T(8,128)(2...) custom-call(bf16[768,256]{1,0:T(8,128)(2,1)S(1)} %get-tuple-element., ...), custom_call_target="tpu_custom_call" | custom-call | flops 4000000000 | bytes 1000000 | tf_op jit(solution)/shard_map/pallas_call | solution.py:609
  36.4 0.9 %shard_map.378 = bf16[32,16,896]{2,1,0:T(8,128)(2,1)S(1)} custom-call(bf16[768,768]{1,0:T(8,128)(2,1)S(1)} %get-tuple-element.119.refs_0_.act_ref, bf16[768,256]{1,0:T(8,128)(2,1)S(1)} %get-tuple-element.101.dy_ref.refs_1_, bf16[768,256]{1,0:T(8,128)(2,1)S(1)} %get-tuple-element.121.refs_2_, bf16[768,768]{1,0:T(8,128)(2,1)S(1)} %get-tuple-element.122.refs_3_, ...), custom_call_target="tpu_custom_call" | custom-call | flops 1000000000 | bytes 1000000 | tf_op jit(solution)/shard_map/pallas_call | solution.py:609
  37.4 0.6 collective-permute-start.12
  38.0 3.5 %shard_map.379 = (f32[768,512]{1,0:T(8,128)S(1)}, bf16[640,512]{1,0:T(8,128)(2,1)S(1)}, bf16[640,512]{1,0:T(8,128)(2,1)S(1)}, bf16[2048,384]{1,0:T(8,128)(2,1)S(1)}, f32[128,384]{1,0:T(8,128)S(1)}) custom-call(bf16[768,256]{1,0:T(8,128)(2,1)S(1)} %get-tuple-element.112.q_ref, bf16[2048,256]{1,0:T(8,128)(2,1)S(1)} %get-tuple-element.114.v_ref, ...), custom_call_target="tpu_custom_call" | custom-call | flops 4000000000 | bytes 1000000 | tf_op jit(solution)/shard_map/pallas_call | solution.py:609
  41.4 0.1 collective-permute-start.16
  41.5 0.9 collective-permute-start.17
  42.4 0.1 convert_add_fusion
  42.6 1.6 %collective-permute-start.13 = (bf16[4,16,896]{2,1,0:T(8,128)(2,1)S(1)}, bf16[4,16,896]{2,1,0:T(8,128)(2,1)S(1)}, u32[]{:S(2)}, u32[]{:S(2)}) collective-permute-start(bf16[4,16,896]{2,1,0:T(8,128)(2,1)S(1)} %get-tuple-element.180), channel_id=1, source_target_pairs={{0,8},{1,9},{2,10},{3,11},{4,12},{5,13},{6,14},{7,15},{8,0},{9,1},... | collective-permute-start | bytes 344072 | tf_op jit(solution)/shard_map/ppermute | solution.py:632
  44.2 1.4 %collective-permute-start.15 = (bf16[4,16,896]{2,1,0:T(8,128)(2,1)S(1)}, bf16[4,16,896]{2,1,0:T(8,128)(2,1)S(1)}, u32[]{:S(2)}, u32[]{:S(2)}) collective-permute-start(bf16[4,16,896]{2,1,0:T(8,128)(2,1)S(1)} %get-tuple-element.181), channel_id=1, source_target_pairs={{0,24},{1,25},{2,26},{3,27},{4,28},{5,29},{6,30},{7,31},{8,16},{9,... | collective-permute-start | bytes 344072 | tf_op jit(solution)/shard_map/ppermute | solution.py:632
  45.6 0.6 collective-permute-start.14
  46.2 3.6 %shard_map.380 = (bf16[16,48,256]{2,1,0:T(8,128)(2,1)}, f32[768,256]{1,0:T(8,128)S(1)}, f32[256,256]{1,0:T(8,128)S(1)}, f32[8,128]{1,0:T(8,128)S(1)}, f32[1,256]{1,0:T(1,128)S(1)}) custom-call(f32[768,256]{1,0:T(8,128)S(1)} %get-tuple-element.118.x1_ref, bf16[768,768]{1,0:T(8,128)(2,1)S(1)} %get-tuple-element.119.refs_0_.act_ref, ...), custom_call_target="tpu_custom_call" | custom-call | flops 3000000000 | bytes 1000000 | tf_op jit(solution)/shard_map/pallas_call | solution.py:609
  49.7 0.3 collective-permute-done.15
  50.0 1.0 %collective-permute-done.14 = bf16[4,16,896]{2,1,0:T(8,128)(2,1)S(1)} collective-permute-done((bf16[4,16,896]{2,1,0:T(8,128)(2,1)S(1)}, bf16[4,16,896]{2,1,0:T(8,128)(2,1)S(1)}, u32[]{:S(2)}, u32[]{:S(2)}) %collective-permute-start.14) | collective-permute-done | bytes 114720 | tf_op jit(solution)/shard_map/ppermute | solution.py:632
  51.2 0.9 %shard_map.381 = (f32[768,256]{1,0:T(8,128)S(1)}, bf16[32,16,512]{2,1,0:T(8,128)(2,1)S(1)}) custom-call(f32[768,512]{1,0:T(8,128)S(1)} %get-tuple-element.137.refs_0_, bf16[640,512]{1,0:T(8,128)(2,1)S(1)} %collective-permute-done.16.refs_1_, bf16[640,512]{1,0:T(8,128)(2,1)S(1)} %collective-permute-done.17.refs_2_, ...), custom_call_target="tpu_custom_call" | custom-call | flops 1000000000 | bytes 1000000 | tf_op jit(solution)/shard_map/pallas_call | solution.py:609
  52.3 2.9 %collective-permute-start.18 = (bf16[16,16,512]{2,1,0:T(8,128)(2,1)S(1)}, bf16[16,16,512]{2,1,0:T(8,128)(2,1)S(1)}, u32[]{:S(2)}, u32[]{:S(2)}) collective-permute-start(bf16[16,16,512]{2,1,0:T(8,128)(2,1)S(1)} %slice.70), channel_id=1, source_target_pairs={{0,1},{1,0},{2,3},{3,2},{4,5},{5,4},{6,7},{7,6},{8,9},{9,8},{10,11... | collective-permute-start | bytes 786440 | tf_op jit(solution)/shard_map/ppermute | solution.py:632
  55.2 1.2 %collective-permute-done.18 = bf16[16,16,512]{2,1,0:T(8,128)(2,1)S(1)} collective-permute-done((bf16[16,16,512]{2,1,0:T(8,128)(2,1)S(1)}, bf16[16,16,512]{2,1,0:T(8,128)(2,1)S(1)}, u32[]{:S(2)}, u32[]{:S(2)}) %collective-permute-start.18) | collective-permute-done | bytes 262176 | tf_op jit(solution)/shard_map/ppermute | solution.py:632
  56.4 0.1 fusion.5
  56.5 1.6 %collective-permute-start.19 = (bf16[4,16,512]{2,1,0:T(8,128)(2,1)S(1)}, bf16[4,16,512]{2,1,0:T(8,128)(2,1)S(1)}, u32[]{:S(2)}, u32[]{:S(2)}) collective-permute-start(bf16[4,16,512]{2,1,0:T(8,128)(2,1)S(1)} %get-tuple-element.183), channel_id=1, source_target_pairs={{0,8},{1,9},{2,10},{3,11},{4,12},{5,13},{6,14},{7,15},{8,0},{9,1},... | collective-permute-start | bytes 196616 | tf_op jit(solution)/shard_map/ppermute | solution.py:632
  58.1 1.4 %collective-permute-start.21 = (bf16[4,16,512]{2,1,0:T(8,128)(2,1)S(1)}, bf16[4,16,512]{2,1,0:T(8,128)(2,1)S(1)}, u32[]{:S(2)}, u32[]{:S(2)}) collective-permute-start(bf16[4,16,512]{2,1,0:T(8,128)(2,1)S(1)} %get-tuple-element.184), channel_id=1, source_target_pairs={{0,24},{1,25},{2,26},{3,27},{4,28},{5,29},{6,30},{7,31},{8,16},{9,... | collective-permute-start | bytes 196616 | tf_op jit(solution)/shard_map/ppermute | solution.py:632
  59.5 0.6 collective-permute-start.20
  60.1 0.9 %collective-permute-done.19 = bf16[4,16,512]{2,1,0:T(8,128)(2,1)S(1)} collective-permute-done((bf16[4,16,512]{2,1,0:T(8,128)(2,1)S(1)}, bf16[4,16,512]{2,1,0:T(8,128)(2,1)S(1)}, u32[]{:S(2)}, u32[]{:S(2)}) %collective-permute-start.19) | collective-permute-done | bytes 65568 | tf_op jit(solution)/shard_map/ppermute | solution.py:632
  61.0 2.3 %collective-permute-done.21 = bf16[4,16,512]{2,1,0:T(8,128)(2,1)S(1)} collective-permute-done((bf16[4,16,512]{2,1,0:T(8,128)(2,1)S(1)}, bf16[4,16,512]{2,1,0:T(8,128)(2,1)S(1)}, u32[]{:S(2)}, u32[]{:S(2)}) %collective-permute-start.21) | collective-permute-done | bytes 65568 | tf_op jit(solution)/shard_map/ppermute | solution.py:632
  63.3 1.2 %collective-permute-done.20 = bf16[4,16,512]{2,1,0:T(8,128)(2,1)S(1)} collective-permute-done((bf16[4,16,512]{2,1,0:T(8,128)(2,1)S(1)}, bf16[4,16,512]{2,1,0:T(8,128)(2,1)S(1)}, u32[]{:S(2)}, u32[]{:S(2)}) %collective-permute-start.20) | collective-permute-done | bytes 65568 | tf_op jit(solution)/shard_map/ppermute | solution.py:632
  64.6 1.4 %collective-permute-start.24 = (bf16[16,1408]{1,0:T(8,128)(2,1)S(1)}, bf16[16,1408]{1,0:T(8,128)(2,1)S(1)}, u32[]{:S(2)}, u32[]{:S(2)}) collective-permute-start(bf16[16,1408]{1,0:T(8,128)(2,1)S(1)} %get-tuple-element.186), channel_id=1, source_target_pairs={{0,6},{1,7},{2,4},{3,5},{4,2},{5,3},{6,0},{7,1},{8,14},{9,15},{10,... | collective-permute-start | bytes 135176 | tf_op jit(solution)/shard_map/ppermute | solution.py:632
  66.1 2.2 %collective-permute-start.23 = (bf16[16,1408]{1,0:T(8,128)(2,1)S(1)}, bf16[16,1408]{1,0:T(8,128)(2,1)S(1)}, u32[]{:S(2)}, u32[]{:S(2)}) collective-permute-start(bf16[16,1408]{1,0:T(8,128)(2,1)S(1)} %get-tuple-element.187), channel_id=1, source_target_pairs={{0,4},{1,5},{2,6},{3,7},{4,0},{5,1},{6,2},{7,3},{8,12},{9,13},{10,... | collective-permute-start | bytes 135176 | tf_op jit(solution)/shard_map/ppermute | solution.py:632
  68.3 0.8 collective-permute-start.22
  69.1 1.9 %collective-permute-done.24.refs_3_ = bf16[16,1408]{1,0:T(8,128)(2,1)S(1)} collective-permute-done((bf16[16,1408]{1,0:T(8,128)(2,1)S(1)}, bf16[16,1408]{1,0:T(8,128)(2,1)S(1)}, u32[]{:S(2)}, u32[]{:S(2)}) %collective-permute-start.24) | collective-permute-done | bytes 45088 | tf_op jit(solution)/shard_map/ppermute | solution.py:632
  71.0 1.6 %collective-permute-done.23.refs_2_ = bf16[16,1408]{1,0:T(8,128)(2,1)S(1)} collective-permute-done((bf16[16,1408]{1,0:T(8,128)(2,1)S(1)}, bf16[16,1408]{1,0:T(8,128)(2,1)S(1)}, u32[]{:S(2)}, u32[]{:S(2)}) %collective-permute-start.23) | collective-permute-done | bytes 45088 | tf_op jit(solution)/shard_map/ppermute | solution.py:632
  72.6 0.2 collective-permute-done.22.refs_1_
  73.0 0.9 %shard_map.383 = (f32[8,768]{1,0:T(8,128)}, f32[8,768]{1,0:T(8,128)}, f32[8,768]{1,0:T(8,128)S(1)}, f32[8,256]{1,0:T(8,128)}, f32[8,256]{1,0:T(8,128)}, /*index=...) custom-call(f32[16,1408]{1,0:T(8,128)S(1)} %fusion.4.refs_0_, ...), custom_call_target="tpu_custom_call" | custom-call | flops 100000000 | bytes 1000000 | tf_op jit(solution)/shard_map/pallas_call | solution.py:609
  74.0 1.2 %collective-permute-done.25 = f32[8,128]{1,0:T(8,128)S(1)} collective-permute-done((f32[8,128]{1,0:T(8,128)S(1)}, f32[8,128]{1,0:T(8,128)S(1)}, u32[]{:S(2)}, u32[]{:S(2)}) %collective-permute-start.25) | collective-permute-done | bytes 4128 | tf_op jit(solution)/shard_map/ppermute | solution.py:632
  75.2 1.4 %collective-permute-start.28 = (f32[8,128]{1,0:T(8,128)S(1)}, f32[8,128]{1,0:T(8,128)S(1)}, u32[]{:S(2)}, u32[]{:S(2)}) collective-permute-start(f32[8,128]{1,0:T(8,128)S(1)} %add.82), channel_id=1, source_target_pairs={{0,24},{1,25},{2,26},{3,27},{4,28},{5,29},{6,30},{7,31},{8,16},{9,... | collective-permute-start | bytes 12296 | tf_op jit(solution)/shard_map/ppermute | solution.py:632
  76.6 1.1 %collective-permute-start.27 = (f32[8,128]{1,0:T(8,128)S(1)}, f32[8,128]{1,0:T(8,128)S(1)}, u32[]{:S(2)}, u32[]{:S(2)}) collective-permute-start(f32[8,128]{1,0:T(8,128)S(1)} %add.82), channel_id=1, source_target_pairs={{0,16},{1,17},{2,18},{3,19},{4,20},{5,21},{6,22},{7,23},{8,24},{9,... | collective-permute-start | bytes 12296 | tf_op jit(solution)/shard_map/ppermute | solution.py:632
  77.7 1.0 %collective-permute-start.26 = (f32[8,128]{1,0:T(8,128)S(1)}, f32[8,128]{1,0:T(8,128)S(1)}, u32[]{:S(2)}, u32[]{:S(2)}) collective-permute-start(f32[8,128]{1,0:T(8,128)S(1)} %add.82), channel_id=1, source_target_pairs={{0,8},{1,9},{2,10},{3,11},{4,12},{5,13},{6,14},{7,15},{8,0},{9,1},... | collective-permute-start | bytes 12296 | tf_op jit(solution)/shard_map/ppermute | solution.py:632
  78.7 1.0 %collective-permute-done.28 = f32[8,128]{1,0:T(8,128)S(1)} collective-permute-done((f32[8,128]{1,0:T(8,128)S(1)}, f32[8,128]{1,0:T(8,128)S(1)}, u32[]{:S(2)}, u32[]{:S(2)}) %collective-permute-start.28) | collective-permute-done | bytes 4128 | tf_op jit(solution)/shard_map/ppermute | solution.py:632
  79.7 0.5 collective-permute-done.27
  80.2 1.1 %collective-permute-done.26 = f32[8,128]{1,0:T(8,128)S(1)} collective-permute-done((f32[8,128]{1,0:T(8,128)S(1)}, f32[8,128]{1,0:T(8,128)S(1)}, u32[]{:S(2)}, u32[]{:S(2)}) %collective-permute-start.26) | collective-permute-done | bytes 4128 | tf_op jit(solution)/shard_map/ppermute | solution.py:632
  81.3 1.0 %collective-permute-start.31 = (f32[8,128]{1,0:T(8,128)S(1)}, f32[8,128]{1,0:T(8,128)S(1)}, u32[]{:S(2)}, u32[]{:S(2)}) collective-permute-start(f32[8,128]{1,0:T(8,128)S(1)} %add_add_fusion.a_ref), channel_id=1, source_target_pairs={{0,6},{1,7},{2,4},{3,5},{4,2},{5,3},{6,0},{7,1},{8,14},{9,15},{10,... | collective-permute-start | bytes 12296 | tf_op jit(solution)/shard_map/ppermute | solution.py:632
  82.3 0.5 collective-permute-start.30
  82.8 2.9 %collective-permute-start.29 = (f32[8,128]{1,0:T(8,128)S(1)}, f32[8,128]{1,0:T(8,128)S(1)}, u32[]{:S(2)}, u32[]{:S(2)}) collective-permute-start(f32[8,128]{1,0:T(8,128)S(1)} %add_add_fusion.a_ref), channel_id=1, source_target_pairs={{0,2},{1,3},{2,0},{3,1},{4,6},{5,7},{6,4},{7,5},{8,10},{9,11},{10,... | collective-permute-start | bytes 12296 | tf_op jit(solution)/shard_map/ppermute | solution.py:632
  85.7 1.6 %shard_map.382 = bf16[16,48,256]{2,1,0:T(8,128)(2,1)} custom-call(f32[768,256]{1,0:T(8,128)S(1)} %get-tuple-element.146.dn_ref, f32[768,256]{1,0:T(8,128)S(1)} %get-tuple-element.147.dx1_ref, f32[768,256]{1,0:T(8,128)S(1)} %get-tuple-element.105.xhat_ref.refs_4_, f32[768,128]{1,0:T(8,128)S(1)} %get-tuple-element.148.rstd_ref, ...), custom_call_target="tpu_custom_call" | custom-call | flops 1000000000 | bytes 1000000 | tf_op jit(solution)/shard_map/pallas_call | solution.py:609
  87.3 0.8 shard_map.384
  (73 shorter events, 0.6 us)
Async XLA Ops:
  2.2 7.2 %collective-permute-start.2 = (bf16[16,1408]{1,0:T(8,128)(2,1)S(1)}, bf16[16,1408]{1,0:T(8,128)(2,1)S(1)}, u32[]{:S(2)}, u32[]{:S(2)}) collective-permute-start(bf16[16,1408]{1,0:T(8,128)(2,1)S(1)} %add_convert_fusion.refs_0_), channel_id=1, source_target_pairs={{0,6},{1,7},{2,4},{3,5},{4,2},{5,3},{6,0},{7,1},{8,14},{9,15},{10,... | collective-permute-start | bytes 135176 | tf_op jit(solution)/shard_map/ppermute | solution.py:632
  7.3 4.9 %collective-permute-start.1 = (bf16[16,1408]{1,0:T(8,128)(2,1)S(1)}, bf16[16,1408]{1,0:T(8,128)(2,1)S(1)}, u32[]{:S(2)}, u32[]{:S(2)}) collective-permute-start(bf16[16,1408]{1,0:T(8,128)(2,1)S(1)} %add_convert_fusion.refs_0_), channel_id=1, source_target_pairs={{0,4},{1,5},{2,6},{3,7},{4,0},{5,1},{6,2},{7,3},{8,12},{9,13},{10,... | collective-permute-start | bytes 135176 | tf_op jit(solution)/shard_map/ppermute | solution.py:632
  7.3 4.9 %collective-permute-start = (bf16[16,1408]{1,0:T(8,128)(2,1)S(1)}, bf16[16,1408]{1,0:T(8,128)(2,1)S(1)}, u32[]{:S(2)}, u32[]{:S(2)}) collective-permute-start(bf16[16,1408]{1,0:T(8,128)(2,1)S(1)} %add_convert_fusion.refs_0_), channel_id=1, source_target_pairs={{0,2},{1,3},{2,0},{3,1},{4,6},{5,7},{6,4},{7,5},{8,10},{9,11},{10,... | collective-permute-start | bytes 135176 | tf_op jit(solution)/shard_map/ppermute | solution.py:632
  12.2 14.4 %collective-permute-start.4 = (bf16[16,48,256]{2,1,0:T(8,128)(2,1)}, bf16[16,48,256]{2,1,0:T(8,128)(2,1)S(1)}, u32[]{:S(2)}, u32[]{:S(2)}) collective-permute-start(bf16[16,48,256]{2,1,0:T(8,128)(2,1)} %x_ref.1), channel_id=1, source_target_pairs={{1,2},{2,1},{3,4},{4,3},{5,6},{6,5},{9,10},{10,9},{11,12},{12,11},... | collective-permute-start | bytes 1179656 | tf_op jit(solution)/shard_map/ppermute | solution.py:738
  12.9 13.7 %collective-permute-start.3 = (bf16[16,48,256]{2,1,0:T(8,128)(2,1)}, bf16[16,48,256]{2,1,0:T(8,128)(2,1)S(1)}, u32[]{:S(2)}, u32[]{:S(2)}) collective-permute-start(bf16[16,48,256]{2,1,0:T(8,128)(2,1)} %x_ref.1), channel_id=1, source_target_pairs={{0,1},{1,0},{2,3},{3,2},{4,5},{5,4},{6,7},{7,6},{8,9},{9,8},{10,11... | collective-permute-start | bytes 1179656 | tf_op jit(solution)/shard_map/ppermute | solution.py:737
  14.7 8.4 %collective-permute-start.7 = (bf16[4,16,1408]{2,1,0:T(8,128)(2,1)S(1)}, bf16[4,16,1408]{2,1,0:T(8,128)(2,1)S(1)}, u32[]{:S(2)}, u32[]{:S(2)}) collective-permute-start(bf16[4,16,1408]{2,1,0:T(8,128)(2,1)S(1)} %shard_map.372.b0), channel_id=1, source_target_pairs={{0,24},{1,25},{2,26},{3,27},{4,28},{5,29},{6,30},{7,31},{8,16},{9,... | collective-permute-start | bytes 540680 | tf_op jit(solution)/shard_map/ppermute | solution.py:632
  17.2 8.8 %collective-permute-start.6 = (bf16[4,16,1408]{2,1,0:T(8,128)(2,1)S(1)}, bf16[4,16,1408]{2,1,0:T(8,128)(2,1)S(1)}, u32[]{:S(2)}, u32[]{:S(2)}) collective-permute-start(bf16[4,16,1408]{2,1,0:T(8,128)(2,1)S(1)} %shard_map.372.b0), channel_id=1, source_target_pairs={{0,16},{1,17},{2,18},{3,19},{4,20},{5,21},{6,22},{7,23},{8,24},{9,... | collective-permute-start | bytes 540680 | tf_op jit(solution)/shard_map/ppermute | solution.py:632
  17.7 8.4 %collective-permute-start.5 = (bf16[4,16,1408]{2,1,0:T(8,128)(2,1)S(1)}, bf16[4,16,1408]{2,1,0:T(8,128)(2,1)S(1)}, u32[]{:S(2)}, u32[]{:S(2)}) collective-permute-start(bf16[4,16,1408]{2,1,0:T(8,128)(2,1)S(1)} %shard_map.372.b0), channel_id=1, source_target_pairs={{0,8},{1,9},{2,10},{3,11},{4,12},{5,13},{6,14},{7,15},{8,0},{9,1},... | collective-permute-start | bytes 540680 | tf_op jit(solution)/shard_map/ppermute | solution.py:632
  18.2 1.0 %copy-start = (bf16[16,48,256]{2,1,0:T(8,128)(2,1)S(1)}, bf16[16,48,256]{2,1,0:T(8,128)(2,1)}, u32[]{:S(2)}) copy-start(bf16[16,48,256]{2,1,0:T(8,128)(2,1)} %x_ref.1) | copy-start | bytes 1179652
  19.2 0.7 copy-start.18
  19.9 1.0 %copy-start.20 = (bf16[16,48,256]{2,1,0:T(8,128)(2,1)S(1)}, bf16[16,48,256]{2,1,0:T(8,128)(2,1)}, u32[]{:S(2)}) copy-start(bf16[16,48,256]{2,1,0:T(8,128)(2,1)} %cot_ref.1) | copy-start | bytes 1179652
  20.9 0.7 copy-start.21
  23.1 5.0 %collective-permute-start.8 = (bf16[4,16,1408]{2,1,0:T(8,128)(2,1)S(1)}, bf16[4,16,1408]{2,1,0:T(8,128)(2,1)S(1)}, u32[]{:S(2)}, u32[]{:S(2)}) collective-permute-start(bf16[4,16,1408]{2,1,0:T(8,128)(2,1)S(1)} %shard_map.372.b0), channel_id=1, source_target_pairs={{0,1},{1,0},{2,3},{3,2},{4,5},{5,4},{6,7},{7,6},{8,9},{9,8},{10,11... | collective-permute-start | bytes 540680 | tf_op jit(solution)/shard_map/ppermute | solution.py:632
  26.1 2.0 %collective-permute-start.9 = (bf16[4,16,1408]{2,1,0:T(8,128)(2,1)S(1)}, bf16[4,16,1408]{2,1,0:T(8,128)(2,1)S(1)}, u32[]{:S(2)}, u32[]{:S(2)}) collective-permute-start(bf16[4,16,1408]{2,1,0:T(8,128)(2,1)S(1)} %collective-permute-done.5.b1), channel_id=1, source_target_pairs={{0,1},{1,0},{2,3},{3,2},{4,5},{5,4},{6,7},{7,6},{8,9},{9,8},{10,11... | collective-permute-start | bytes 540680 | tf_op jit(solution)/shard_map/ppermute | solution.py:632
  26.1 2.0 %collective-permute-start.10 = (bf16[4,16,1408]{2,1,0:T(8,128)(2,1)S(1)}, bf16[4,16,1408]{2,1,0:T(8,128)(2,1)S(1)}, u32[]{:S(2)}, u32[]{:S(2)}) collective-permute-start(bf16[4,16,1408]{2,1,0:T(8,128)(2,1)S(1)} %collective-permute-done.6.b2), channel_id=1, source_target_pairs={{0,1},{1,0},{2,3},{3,2},{4,5},{5,4},{6,7},{7,6},{8,9},{9,8},{10,11... | collective-permute-start | bytes 540680 | tf_op jit(solution)/shard_map/ppermute | solution.py:632
  26.6 1.5 %collective-permute-start.11 = (bf16[4,16,1408]{2,1,0:T(8,128)(2,1)S(1)}, bf16[4,16,1408]{2,1,0:T(8,128)(2,1)S(1)}, u32[]{:S(2)}, u32[]{:S(2)}) collective-permute-start(bf16[4,16,1408]{2,1,0:T(8,128)(2,1)S(1)} %collective-permute-done.7.b3), channel_id=1, source_target_pairs={{0,1},{1,0},{2,3},{3,2},{4,5},{5,4},{6,7},{7,6},{8,9},{9,8},{10,11... | collective-permute-start | bytes 540680 | tf_op jit(solution)/shard_map/ppermute | solution.py:632
  37.4 5.0 %collective-permute-start.12 = (bf16[16,16,896]{2,1,0:T(8,128)(2,1)S(1)}, bf16[16,16,896]{2,1,0:T(8,128)(2,1)S(1)}, u32[]{:S(2)}, u32[]{:S(2)}) collective-permute-start(bf16[16,16,896]{2,1,0:T(8,128)(2,1)S(1)} %slice.64), channel_id=1, source_target_pairs={{0,1},{1,0},{2,3},{3,2},{4,5},{5,4},{6,7},{7,6},{8,9},{9,8},{10,11... | collective-permute-start | bytes 1376264 | tf_op jit(solution)/shard_map/ppermute | solution.py:632
  41.4 9.7 %collective-permute-start.16 = (bf16[640,512]{1,0:T(8,128)(2,1)S(1)}, bf16[640,512]{1,0:T(8,128)(2,1)S(1)}, u32[]{:S(2)}, u32[]{:S(2)}) collective-permute-start(bf16[640,512]{1,0:T(8,128)(2,1)S(1)} %get-tuple-element.138), channel_id=1, source_target_pairs={{0,1},{1,0},{2,3},{3,2},{4,5},{5,4},{6,7},{7,6},{8,9},{9,8},{10,11... | collective-permute-start | bytes 1966088 | tf_op jit(solution)/shard_map/ppermute | solution.py:737
  41.5 9.6 %collective-permute-start.17 = (bf16[640,512]{1,0:T(8,128)(2,1)S(1)}, bf16[640,512]{1,0:T(8,128)(2,1)S(1)}, u32[]{:S(2)}, u32[]{:S(2)}) collective-permute-start(bf16[640,512]{1,0:T(8,128)(2,1)S(1)} %get-tuple-element.139), channel_id=1, source_target_pairs={{1,2},{2,1},{3,4},{4,3},{5,6},{6,5},{9,10},{10,9},{11,12},{12,11},... | collective-permute-start | bytes 1966088 | tf_op jit(solution)/shard_map/ppermute | solution.py:738
  42.6 7.1 %collective-permute-start.13 = (bf16[4,16,896]{2,1,0:T(8,128)(2,1)S(1)}, bf16[4,16,896]{2,1,0:T(8,128)(2,1)S(1)}, u32[]{:S(2)}, u32[]{:S(2)}) collective-permute-start(bf16[4,16,896]{2,1,0:T(8,128)(2,1)S(1)} %get-tuple-element.180), channel_id=1, source_target_pairs={{0,8},{1,9},{2,10},{3,11},{4,12},{5,13},{6,14},{7,15},{8,0},{9,1},... | collective-permute-start | bytes 344072 | tf_op jit(solution)/shard_map/ppermute | solution.py:632
  44.2 5.9 %collective-permute-start.15 = (bf16[4,16,896]{2,1,0:T(8,128)(2,1)S(1)}, bf16[4,16,896]{2,1,0:T(8,128)(2,1)S(1)}, u32[]{:S(2)}, u32[]{:S(2)}) collective-permute-start(bf16[4,16,896]{2,1,0:T(8,128)(2,1)S(1)} %get-tuple-element.181), channel_id=1, source_target_pairs={{0,24},{1,25},{2,26},{3,27},{4,28},{5,29},{6,30},{7,31},{8,16},{9,... | collective-permute-start | bytes 344072 | tf_op jit(solution)/shard_map/ppermute | solution.py:632
  45.6 5.5 %collective-permute-start.14 = (bf16[4,16,896]{2,1,0:T(8,128)(2,1)S(1)}, bf16[4,16,896]{2,1,0:T(8,128)(2,1)S(1)}, u32[]{:S(2)}, u32[]{:S(2)}) collective-permute-start(bf16[4,16,896]{2,1,0:T(8,128)(2,1)S(1)} %get-tuple-element.182), channel_id=1, source_target_pairs={{0,16},{1,17},{2,18},{3,19},{4,20},{5,21},{6,22},{7,23},{8,24},{9,... | collective-permute-start | bytes 344072 | tf_op jit(solution)/shard_map/ppermute | solution.py:632
  52.1 20.8 %copy-start.1 = (f32[8,768]{1,0:T(8,128)S(1)}, f32[8,768]{1,0:T(8,128)}, u32[]{:S(2)}) copy-start(f32[8,768]{1,0:T(8,128)} %refs_2_.1) | copy-start | bytes 73732
  52.1 20.8 %copy-start.2 = (f32[8,768]{1,0:T(8,128)S(1)}, f32[8,768]{1,0:T(8,128)}, u32[]{:S(2)}) copy-start(f32[8,768]{1,0:T(8,128)} %refs_0_.1) | copy-start | bytes 73732
  52.1 20.8 %copy-start.3 = (f32[24,256]{1,0:T(8,128)S(1)}, f32[24,256]{1,0:T(8,128)}, u32[]{:S(2)}) copy-start(f32[24,256]{1,0:T(8,128)} %refs_3_.1) | copy-start | bytes 73732
  52.1 20.8 %copy-start.4 = (f32[8,256]{1,0:T(8,128)S(1)}, f32[8,256]{1,0:T(8,128)}, u32[]{:S(2)}) copy-start(f32[8,256]{1,0:T(8,128)} %refs_1_.1) | copy-start | bytes 24580
  52.1 20.8 %copy-start.5 = (f32[8,768]{1,0:T(8,128)S(1)}, f32[8,768]{1,0:T(8,128)}, u32[]{:S(2)}) copy-start(f32[8,768]{1,0:T(8,128)} %refs_10_.1) | copy-start | bytes 73732
  52.1 20.8 %copy-start.6 = (f32[8,768]{1,0:T(8,128)S(1)}, f32[8,768]{1,0:T(8,128)}, u32[]{:S(2)}) copy-start(f32[8,768]{1,0:T(8,128)} %refs_12_.1) | copy-start | bytes 73732
  52.2 20.8 %copy-start.7 = (f32[24,256]{1,0:T(8,128)S(1)}, f32[24,256]{1,0:T(8,128)}, u32[]{:S(2)}) copy-start(f32[24,256]{1,0:T(8,128)} %refs_13_.1) | copy-start | bytes 73732
  52.2 20.8 %copy-start.8 = (f32[8,768]{1,0:T(8,128)S(1)}, f32[8,768]{1,0:T(8,128)}, u32[]{:S(2)}) copy-start(f32[8,768]{1,0:T(8,128)} %refs_16_.1) | copy-start | bytes 73732
  52.2 20.8 %copy-start.9 = (f32[8,768]{1,0:T(8,128)S(1)}, f32[8,768]{1,0:T(8,128)}, u32[]{:S(2)}) copy-start(f32[8,768]{1,0:T(8,128)} %refs_18_.1) | copy-start | bytes 73732
  52.2 20.8 %copy-start.10 = (f32[24,256]{1,0:T(8,128)S(1)}, f32[24,256]{1,0:T(8,128)}, u32[]{:S(2)}) copy-start(f32[24,256]{1,0:T(8,128)} %refs_19_.1) | copy-start | bytes 73732
  52.2 20.8 %copy-start.11 = (f32[11,8]{0,1:T(8,128)S(1)}, f32[11,8]{0,1:T(8,128)}, u32[]{:S(2)}) copy-start(f32[11,8]{0,1:T(8,128)} %param.28) | copy-start | bytes 1060
  52.2 20.8 %copy-start.12 = (f32[8,256]{1,0:T(8,128)S(1)}, f32[8,256]{1,0:T(8,128)}, u32[]{:S(2)}) copy-start(f32[8,256]{1,0:T(8,128)} %refs_11_.1) | copy-start | bytes 24580
  52.2 20.8 %copy-start.13 = (f32[8,256]{1,0:T(8,128)S(1)}, f32[8,256]{1,0:T(8,128)}, u32[]{:S(2)}) copy-start(f32[8,256]{1,0:T(8,128)} %refs_17_.1) | copy-start | bytes 24580
  52.2 20.8 %copy-start.14 = (f32[11,8]{0,1:T(8,128)S(1)}, f32[11,8]{0,1:T(8,128)}, u32[]{:S(2)}) copy-start(f32[11,8]{0,1:T(8,128)} %param.38) | copy-start | bytes 1060
  52.3 20.8 %copy-start.15 = (f32[8,49]{1,0:T(8,128)S(1)}, f32[8,49]{1,0:T(8,128)}, u32[]{:S(2)}) copy-start(f32[8,49]{1,0:T(8,128)} %refs_15_.1) | copy-start | bytes 4708
  52.3 20.8 %copy-start.16 = (f32[11,8]{0,1:T(8,128)S(1)}, f32[11,8]{0,1:T(8,128)}, u32[]{:S(2)}) copy-start(f32[11,8]{0,1:T(8,128)} %param.39) | copy-start | bytes 1060
  52.3 20.7 %copy-start.17 = (f32[8,49]{1,0:T(8,128)S(1)}, f32[8,49]{1,0:T(8,128)}, u32[]{:S(2)}) copy-start(f32[8,49]{1,0:T(8,128)} %refs_21_.1) | copy-start | bytes 4708
  52.3 20.7 %copy-start.19 = (f32[8,49]{1,0:T(8,128)S(1)}, f32[8,49]{1,0:T(8,128)}, u32[]{:S(2)}) copy-start(f32[8,49]{1,0:T(8,128)} %refs_5_.3) | copy-start | bytes 4708
  52.3 4.1 %collective-permute-start.18 = (bf16[16,16,512]{2,1,0:T(8,128)(2,1)S(1)}, bf16[16,16,512]{2,1,0:T(8,128)(2,1)S(1)}, u32[]{:S(2)}, u32[]{:S(2)}) collective-permute-start(bf16[16,16,512]{2,1,0:T(8,128)(2,1)S(1)} %slice.70), channel_id=1, source_target_pairs={{0,1},{1,0},{2,3},{3,2},{4,5},{5,4},{6,7},{7,6},{8,9},{9,8},{10,11... | collective-permute-start | bytes 786440 | tf_op jit(solution)/shard_map/ppermute | solution.py:632
  56.5 4.5 %collective-permute-start.19 = (bf16[4,16,512]{2,1,0:T(8,128)(2,1)S(1)}, bf16[4,16,512]{2,1,0:T(8,128)(2,1)S(1)}, u32[]{:S(2)}, u32[]{:S(2)}) collective-permute-start(bf16[4,16,512]{2,1,0:T(8,128)(2,1)S(1)} %get-tuple-element.183), channel_id=1, source_target_pairs={{0,8},{1,9},{2,10},{3,11},{4,12},{5,13},{6,14},{7,15},{8,0},{9,1},... | collective-permute-start | bytes 196616 | tf_op jit(solution)/shard_map/ppermute | solution.py:632
  58.1 5.2 %collective-permute-start.21 = (bf16[4,16,512]{2,1,0:T(8,128)(2,1)S(1)}, bf16[4,16,512]{2,1,0:T(8,128)(2,1)S(1)}, u32[]{:S(2)}, u32[]{:S(2)}) collective-permute-start(bf16[4,16,512]{2,1,0:T(8,128)(2,1)S(1)} %get-tuple-element.184), channel_id=1, source_target_pairs={{0,24},{1,25},{2,26},{3,27},{4,28},{5,29},{6,30},{7,31},{8,16},{9,... | collective-permute-start | bytes 196616 | tf_op jit(solution)/shard_map/ppermute | solution.py:632
  59.5 5.1 %collective-permute-start.20 = (bf16[4,16,512]{2,1,0:T(8,128)(2,1)S(1)}, bf16[4,16,512]{2,1,0:T(8,128)(2,1)S(1)}, u32[]{:S(2)}, u32[]{:S(2)}) collective-permute-start(bf16[4,16,512]{2,1,0:T(8,128)(2,1)S(1)} %get-tuple-element.185), channel_id=1, source_target_pairs={{0,16},{1,17},{2,18},{3,19},{4,20},{5,21},{6,22},{7,23},{8,24},{9,... | collective-permute-start | bytes 196616 | tf_op jit(solution)/shard_map/ppermute | solution.py:632
  64.6 6.4 %collective-permute-start.24 = (bf16[16,1408]{1,0:T(8,128)(2,1)S(1)}, bf16[16,1408]{1,0:T(8,128)(2,1)S(1)}, u32[]{:S(2)}, u32[]{:S(2)}) collective-permute-start(bf16[16,1408]{1,0:T(8,128)(2,1)S(1)} %get-tuple-element.186), channel_id=1, source_target_pairs={{0,6},{1,7},{2,4},{3,5},{4,2},{5,3},{6,0},{7,1},{8,14},{9,15},{10,... | collective-permute-start | bytes 135176 | tf_op jit(solution)/shard_map/ppermute | solution.py:632
  66.1 6.6 %collective-permute-start.23 = (bf16[16,1408]{1,0:T(8,128)(2,1)S(1)}, bf16[16,1408]{1,0:T(8,128)(2,1)S(1)}, u32[]{:S(2)}, u32[]{:S(2)}) collective-permute-start(bf16[16,1408]{1,0:T(8,128)(2,1)S(1)} %get-tuple-element.187), channel_id=1, source_target_pairs={{0,4},{1,5},{2,6},{3,7},{4,0},{5,1},{6,2},{7,3},{8,12},{9,13},{10,... | collective-permute-start | bytes 135176 | tf_op jit(solution)/shard_map/ppermute | solution.py:632
  68.3 4.6 %collective-permute-start.22 = (bf16[16,1408]{1,0:T(8,128)(2,1)S(1)}, bf16[16,1408]{1,0:T(8,128)(2,1)S(1)}, u32[]{:S(2)}, u32[]{:S(2)}) collective-permute-start(bf16[16,1408]{1,0:T(8,128)(2,1)S(1)} %get-tuple-element.188), channel_id=1, source_target_pairs={{0,2},{1,3},{2,0},{3,1},{4,6},{5,7},{6,4},{7,5},{8,10},{9,11},{10,... | collective-permute-start | bytes 135176 | tf_op jit(solution)/shard_map/ppermute | solution.py:632
  73.9 1.2 %collective-permute-start.25 = (f32[8,128]{1,0:T(8,128)S(1)}, f32[8,128]{1,0:T(8,128)S(1)}, u32[]{:S(2)}, u32[]{:S(2)}) collective-permute-start(f32[8,128]{1,0:T(8,128)S(1)} %get-tuple-element.153.mine_ref), channel_id=1, source_target_pairs={{0,1},{1,0},{2,3},{3,2},{4,5},{5,4},{6,7},{7,6},{8,9},{9,8},{10,11... | collective-permute-start | bytes 12296 | tf_op jit(solution)/shard_map/ppermute | solution.py:632
  75.2 4.5 %collective-permute-start.28 = (f32[8,128]{1,0:T(8,128)S(1)}, f32[8,128]{1,0:T(8,128)S(1)}, u32[]{:S(2)}, u32[]{:S(2)}) collective-permute-start(f32[8,128]{1,0:T(8,128)S(1)} %add.82), channel_id=1, source_target_pairs={{0,24},{1,25},{2,26},{3,27},{4,28},{5,29},{6,30},{7,31},{8,16},{9,... | collective-permute-start | bytes 12296 | tf_op jit(solution)/shard_map/ppermute | solution.py:632
  76.6 3.6 %collective-permute-start.27 = (f32[8,128]{1,0:T(8,128)S(1)}, f32[8,128]{1,0:T(8,128)S(1)}, u32[]{:S(2)}, u32[]{:S(2)}) collective-permute-start(f32[8,128]{1,0:T(8,128)S(1)} %add.82), channel_id=1, source_target_pairs={{0,16},{1,17},{2,18},{3,19},{4,20},{5,21},{6,22},{7,23},{8,24},{9,... | collective-permute-start | bytes 12296 | tf_op jit(solution)/shard_map/ppermute | solution.py:632
  77.7 3.6 %collective-permute-start.26 = (f32[8,128]{1,0:T(8,128)S(1)}, f32[8,128]{1,0:T(8,128)S(1)}, u32[]{:S(2)}, u32[]{:S(2)}) collective-permute-start(f32[8,128]{1,0:T(8,128)S(1)} %add.82), channel_id=1, source_target_pairs={{0,8},{1,9},{2,10},{3,11},{4,12},{5,13},{6,14},{7,15},{8,0},{9,1},... | collective-permute-start | bytes 12296 | tf_op jit(solution)/shard_map/ppermute | solution.py:632
  81.3 6.0 %collective-permute-start.31 = (f32[8,128]{1,0:T(8,128)S(1)}, f32[8,128]{1,0:T(8,128)S(1)}, u32[]{:S(2)}, u32[]{:S(2)}) collective-permute-start(f32[8,128]{1,0:T(8,128)S(1)} %add_add_fusion.a_ref), channel_id=1, source_target_pairs={{0,6},{1,7},{2,4},{3,5},{4,2},{5,3},{6,0},{7,1},{8,14},{9,15},{10,... | collective-permute-start | bytes 12296 | tf_op jit(solution)/shard_map/ppermute | solution.py:632
  82.3 5.0 %collective-permute-start.30 = (f32[8,128]{1,0:T(8,128)S(1)}, f32[8,128]{1,0:T(8,128)S(1)}, u32[]{:S(2)}, u32[]{:S(2)}) collective-permute-start(f32[8,128]{1,0:T(8,128)S(1)} %add_add_fusion.a_ref), channel_id=1, source_target_pairs={{0,4},{1,5},{2,6},{3,7},{4,0},{5,1},{6,2},{7,3},{8,12},{9,13},{10,... | collective-permute-start | bytes 12296 | tf_op jit(solution)/shard_map/ppermute | solution.py:632
  82.8 4.5 %collective-permute-start.29 = (f32[8,128]{1,0:T(8,128)S(1)}, f32[8,128]{1,0:T(8,128)S(1)}, u32[]{:S(2)}, u32[]{:S(2)}) collective-permute-start(f32[8,128]{1,0:T(8,128)S(1)} %add_add_fusion.a_ref), channel_id=1, source_target_pairs={{0,2},{1,3},{2,0},{3,1},{4,6},{5,7},{6,4},{7,5},{8,10},{9,11},{10,... | collective-permute-start | bytes 12296 | tf_op jit(solution)/shard_map/ppermute | solution.py:632

commit v6 on v5

--- a/solution.py
+++ b/solution.py
@@ -160,14 +160,13 @@
     lax.fori_loop(0, 4, block, 0, unroll=2)
 
 
-def project_kernel(xhat_ref, xk_ref, wqkv_ref, vec_ref, a1_ref, q_ref, k_ref, v_ref):
+def project_kernel(xhat_ref, xk_ref, wqkv_ref, vec_ref, q_ref, k_ref, v_ref):
     def vrow(i):
         return vec_ref[i : i + 1, :]
 
     def block(rc, _):
         at = pl.ds(pl.multiple_of(rc * 192, 192), 192)
         a1 = (xhat_ref[at, :] * vrow(0) + vrow(1)).astype(BF)
-        a1_ref[at, :] = a1
         q_ref[at, :] = (dot(a1, wqkv_ref[:, 0:256]) + vrow(2)).astype(BF)
         at = pl.ds(pl.multiple_of(rc * 512, 512), 512)
         a1k = (xk_ref[at, :] * vrow(0) + vrow(1)).astype(BF)
@@ -284,6 +283,7 @@
     rimz_ref,
     dsl_ref,
     tacc_ref,
+    dkv_ref,
 ):
     odd = (lax.axis_index("band") & 1) == 1
     scale = 32 ** (-0.5)
@@ -304,6 +304,8 @@
         dsl = ds.astype(BF)
         dsl_ref[at_k, :] = dsl
         dk = dot(dsl, qbd) * scale
+        dkv_ref[at_k, 0:256] = dk.astype(BF)
+        dkv_ref[at_k, 256:512] = dv.astype(BF)
         own_ref[at_q, 0:256] = dk[0:QN]
         own_ref[at_q, 256:512] = dv[0:QN]
         after = jnp.concatenate([dk[QN : QN + RIM], dv[QN : QN + RIM]], axis=1)
@@ -329,40 +331,7 @@
     fo[...] = dot_tn(mixed_ref[...], da_ref[...])
 
 
-def window_kernel(
-    x1_ref,
-    act_ref,
-    dsl_ref,
-    k_ref,
-    tacc_ref,
-    a1_ref,
-    wd_ref,
-    wqkv_ref,
-    vec_ref,
-    po_ref,
-    out_ref,
-    dnq_ref,
-    fwq_ref,
-    tgrad_ref,
-    qsum_ref,
-    dq_ref,
-):
-    scale = 32 ** (-0.5)
-    lane_head = lax.broadcasted_iota(jnp.int32, (QN, 256), 1) >> 5
-
-    def query(k, _):
-        at_q = pl.ds(pl.multiple_of(k * QN, QN), QN)
-        at_k = pl.ds(pl.multiple_of(k * KN, KN), KN)
-        dq = pick_heads(dot_tn(dsl_ref[at_k, :], k_ref[at_k, :]), lane_head) * scale
-        dq_ref[at_q, :] = dq.astype(BF)
-        return 0
-
-    lax.fori_loop(0, CLS, query, 0, unroll=16)
-    dq = dq_ref[...]
-    qsum_ref[...] = jnp.sum(dq.astype(F32), axis=0, keepdims=True)
-    fwq_ref[...] = dot_tn(a1_ref[...], dq)
-    dnq_ref[...] = dot_nt(dq, wqkv_ref[:, 0:256])
-
+def output_kernel(x1_ref, act_ref, wd_ref, vec_ref, po_ref, out_ref):
     def result(rc, _):
         at = pl.ds(pl.multiple_of(rc * 192, 192), 192)
         res = x1_ref[at, :] + dot(act_ref[at, :], wd_ref[...]) + vec_ref[7:8, :]
@@ -371,7 +340,61 @@
             out_ref[4 * i + rc] = back[48 * i : 48 * i + 48]
         return 0
 
-    lax.fori_loop(0, 4, result, 0, unroll=2)
+    lax.fori_loop(0, 4, result, 0, unroll=4)
+
+
+def late_grads(
+    dsl_ref,
+    k_ref,
+    tacc_ref,
+    xhat_ref,
+    xk_ref,
+    dkv_ref,
+    wqkv_ref,
+    vt_ref,
+    sums_ref,
+    zsum_ref,
+    dq_ref,
+    fq_ref,
+    fv_ref,
+    tgrad_ref,
+):
+    scale = 32 ** (-0.5)
+    lane_head = lax.broadcasted_iota(jnp.int32, (QN, 256), 1) >> 5
+
+    def query(k, _):
+        at_q = pl.ds(pl.multiple_of(k * QN, QN), QN)
+        at_k = pl.ds(pl.multiple_of(k * KN, KN), KN)
+        dq = pick_heads(dot_tn(dsl_ref[at_k, :], k_ref[at_k, :]), lane_head) * scale
+        dq_ref[at_q, :] = dq.astype(BF)
+        return 0
+
+    lax.fori_loop(0, CLS, query, 0, unroll=16)
+    dq = dq_ref[...]
+    gain, shift = vt_ref[:, 0:1], vt_ref[:, 1:2]
+    qsum = jnp.sum(dq.astype(F32), axis=0, keepdims=True)
+    m = dot_tn(xhat_ref[...].astype(BF), dq)
+    weight = wqkv_ref[:, 0:256].astype(F32)
+    fq_ref[:, 0:256] = gain * m + shift * qsum
+    gain_grad = jnp.sum(weight * m, axis=1, keepdims=True)
+    shift_grad = jnp.sum(weight * qsum, axis=1, keepdims=True)
+    xk = xk_ref[...].astype(BF)
+    for cols in (slice(256, 512), slice(512, 768)):
+        dkv = dkv_ref[:, cols.start - 256 : cols.stop - 256]
+        kvsum = jnp.sum(dkv.astype(F32), axis=0, keepdims=True)
+        m = dot_tn(xk, dkv)
+        weight = wqkv_ref[:, cols].astype(F32)
+        fq_ref[:, cols] = gain * m + shift * kvsum
+        gain_grad = gain_grad + jnp.sum(weight * m, axis=1, keepdims=True)
+        shift_grad = shift_grad + jnp.sum(weight * kvsum, axis=1, keepdims=True)
+    lines = jnp.concatenate(
+        [jnp.zeros((2, 256), F32), qsum, kvsum, sums_ref[4:8, :]]
+        + [zsum_ref[:, 256 * i : 256 * i + 256] for i in range(3)]
+        + [jnp.zeros((117, 256), F32)],
+        axis=0,
+    )
+    lane = lax.broadcasted_iota(jnp.int32, (256, 128), 1)
+    fv_ref[...] = jnp.where(lane == 0, gain_grad, jnp.where(lane == 1, shift_grad, lines.T))
 
     flat = tacc_ref[...].T
     qi = lax.broadcasted_iota(jnp.int32, (QN, KN), 0)
@@ -385,21 +408,10 @@
     tgrad_ref[...] = jnp.concatenate(lines, axis=0)
 
 
-def finish_kernel(
-    own_ref,
-    gotc_ref,
-    gotz_ref,
-    dnq_ref,
-    xhat_ref,
-    wqkv_ref,
-    a1_ref,
-    dn_ref,
-    fkv_ref,
-    sums_ref,
-    dkv_ref,
+def input_kernel(
+    own_ref, gotc_ref, gotz_ref, dq_ref, dx1_ref, xhat_ref, rstd_ref, wqkv_ref, vec_ref, po_ref, tok_ref
 ):
     odd = (lax.axis_index("band") & 1) == 1
-    sums_ref[...] = jnp.zeros_like(sums_ref)
 
     def block(rc, _):
         at = pl.ds(pl.multiple_of(rc * 192, 192), 192)
@@ -415,22 +427,8 @@
             b = jnp.concatenate([gap, got_b[i * RIM : (i + 1) * RIM]], axis=0)
             parts.append(mine[i * QN : (i + 1) * QN] + a + b)
         dkv = jnp.concatenate(parts, axis=0).astype(BF)
-        dkv_ref[at, :] = dkv
-        dn = dnq_ref[at, :] + dot_nt(dkv, wqkv_ref[:, 256:768])
-        dn_ref[at, :] = dn
-        sums_ref[0:1, :] += jnp.sum(dn * xhat_ref[at, :], axis=0, keepdims=True)
-        sums_ref[1:2, :] += jnp.sum(dn, axis=0, keepdims=True)
-        sums_ref[3:4, :] += jnp.sum(dkv[:, 256:512].astype(F32), axis=0, keepdims=True)
-        return 0
-
-    lax.fori_loop(0, 4, block, 0, unroll=4)
-    fkv_ref[...] = dot_tn(a1_ref[...], dkv_ref[...])
-
-
-def input_kernel(dn_ref, dx1_ref, xhat_ref, rstd_ref, vec_ref, po_ref, tok_ref):
-    def block(rc, _):
-        at = pl.ds(pl.multiple_of(rc * 192, 192), 192)
-        dx = dx1_ref[at, :] + norm_back(dn_ref[at, :] * vec_ref[0:1, :], xhat_ref[at, :], rstd_ref[at, 0:1])
+        dn = dot_nt(dq_ref[at, :], wqkv_ref[:, 0:256]) + dot_nt(dkv, wqkv_ref[:, 256:768])
+        dx = dx1_ref[at, :] + norm_back(dn * vec_ref[0:1, :], xhat_ref[at, :], rstd_ref[at, 0:1])
         back = dot_tn(po_ref[...], dx.astype(BF)).astype(BF)
         for i in range(4):
             tok_ref[4 * i + rc] = back[48 * i : 48 * i + 48]
@@ -477,7 +475,7 @@
 
 
 def project_packed(xhat_ref, xk_ref, b0, b1, b2, b3, b4, b5, b6, b7, *rest):
-    outs, big_qkv, vec, fq, fv = rest[:4], *rest[4:]
+    outs, big_qkv, vec, fv, fq = rest[:3], *rest[3:]
     for o, slab in sorted_slabs((b0, b1, b2, b3, b4, b5, b6, b7)):
         at = pl.ds(pl.multiple_of(o * 8, 8), 8)
         fq[at, :] = slab[0:8, 0:768]
@@ -506,40 +504,18 @@
     return (m & 1) * 16 + (m >> 3) * 4 + ((m >> 1) & 3)
 
 
-def early_kernel(*refs):
-    out_ref, fd, fu, fo = refs[6:]
+def grads_kernel(*refs):
+    dq_ref, out_ref, fd, fu, fo, fq, fv, tgrad = refs[16:]
     early_grads(*refs[:6], fd, fu, fo)
-    me = own_index()
-    for o in range(32):
-        at = slice(8 * o, 8 * o + 8)
-        top = [fd[24 * o + 8 * b : 24 * o + 8 * b + 8, :] for b in range(3)] + [fo[at, 0:128]]
-        low = [fu[at, :], fo[at, 128:256]]
-        both = jnp.concatenate([jnp.concatenate(top, axis=1), jnp.concatenate(low, axis=1)], axis=0)
-        out_ref[frame_slot(me, o)] = both.astype(BF)
-
-
-def qrow(line):
-    return jnp.where(lax.broadcasted_iota(jnp.int32, (8, 256), 0) == 2, line, 0.0)
-
-
-def late_kernel(*refs):
-    sums, zsum, qsum, fwq, tgrad = refs[7:12]
-    dn_ref, out_ref, fkv, sums2, dkv, fv = refs[12:]
-    finish_kernel(*refs[:7], dn_ref, fkv, sums2, dkv)
-    lines = jnp.concatenate(
-        [sums[...] + sums2[...] + qrow(qsum[...])]
-        + [zsum[:, 256 * i : 256 * i + 256] for i in range(3)]
-        + [jnp.zeros((117, 256), F32)],
-        axis=0,
-    )
-    fv[...] = lines.T
+    late_grads(*refs[6:16], dq_ref, fq, fv, tgrad)
     table = tgrad[...]
     me = own_index()
     for o in range(32):
         at = slice(8 * o, 8 * o + 8)
-        top = jnp.concatenate([fwq[at, :], fkv[at, 0:256]], axis=1)
-        low = jnp.concatenate([fkv[at, 256:512], fv[at, :], table], axis=1)
-        out_ref[frame_slot(me, o)] = jnp.concatenate([top, low], axis=0).astype(BF)
+        top = [fd[24 * o + 8 * b : 24 * o + 8 * b + 8, :] for b in range(3)] + [fo[at, 0:128], fq[at, 0:512]]
+        low = [fu[at, :], fo[at, 128:256], fq[at, 512:768], fv[at, :], table]
+        both = jnp.concatenate([jnp.concatenate(top, axis=1), jnp.concatenate(low, axis=1)], axis=0)
+        out_ref[frame_slot(me, o)] = both.astype(BF)
 
 
 def adam_kernel(*refs):
@@ -690,7 +666,7 @@
 
 
 def project_outputs():
-    return (sds((768, 256)), sds((768, 256)), sds((CLS * KN, 256)), sds((CLS * KN, 256)))
+    return (sds((768, 256)), sds((CLS * KN, 256)), sds((CLS * KN, 256)))
 
 
 def attend_outputs():
@@ -718,16 +694,16 @@
         sds((CLS * RIM, 512)),
         sds((CLS * KN, 384)),
         sds((KN, 384), F32),
-    )
-
-
-def window_outputs():
+        sds((CLS * KN, 512)),
+    )
+
+
+def late_outputs():
     return (
-        sds((16, 48, 256)),
-        sds((768, 256), F32),
-        sds((256, 256), F32),
+        sds((768, 256)),
+        sds((256, 768), F32),
+        sds((256, 128), F32),
         sds((HEADS, KN), F32),
-        sds((1, 256), F32),
     )
 
 
@@ -762,10 +738,10 @@
     *far, pk = lax.optimization_barrier((*blocks[1:], pk))
     xk = call(halo_kernel, sds((CLS * KN, 256), F32), [], x, x_core, x_next, pk, flops=10**9, vmem=8)
     blocks = [blocks[0]] + far + [swap(block, 1, count) for block in [blocks[0]] + far]
-    a1, queries, keys, values, big_qkv, vec = call(
+    queries, keys, values, big_qkv, vec, vt = call(
         project_packed,
-        project_outputs() + (sds((256, 768)), sds((vrows, 256), F32)),
-        [pltpu.VMEM((256, 768), F32), pltpu.VMEM((256, 128), F32)],
+        project_outputs() + (sds((256, 768)), sds((vrows, 256), F32), sds((256, 128), F32)),
+        [pltpu.VMEM((256, 768), F32)],
         xhat, xk, *blocks,
         flops=10**9, vmem=8,
     )
@@ -780,46 +756,27 @@
         dy, dysum, mixed, xp, vec, *blocks,
         flops=4 * 10**9, vmem=8,
     )
-    early = call(
-        early_kernel,
-        sds((count, 16, EARLY)),
-        [pltpu.VMEM((768, 256), F32), pltpu.VMEM((256, 768), F32), pltpu.VMEM((256, 256), F32)],
-        act, dy, a2, dz, mixed, da,
+    own, rim_c, rim_z, dsl, tacc, dkv = call(
+        back_kernel, back_outputs(), [], queries, values, probs, dmix, flops=4 * 10**9, vmem=8
+    )
+    dq, grads = call(
+        grads_kernel,
+        (sds((768, 256)), sds((count, 16, EARLY + LATE))),
+        [pltpu.VMEM(m, F32) for m in ((768, 256), (256, 768), (256, 256))]
+        + [pltpu.VMEM(o.shape, o.dtype) for o in late_outputs()[1:]],
+        act, dy, a2, dz, mixed, da, dsl, keys, tacc, xhat, xk, dkv, big_qkv, vt, sums, zsum,
+        flops=5 * 10**9, vmem=8,
+    )
+    layer_out = call(output_kernel, sds((16, 48, 256)), [], x1, act, big_down, vec, po, flops=10**9, vmem=8)
+    got_c, got_z = beside((rim_c, rim_z), 8)
+    tokens_grad = call(
+        input_kernel, sds((16, 48, 256)), [], own, got_c, got_z, dq, dx1, xhat, rstd, big_qkv, vec, po,
         flops=10**9, vmem=8,
     )
-    early, dmix = lax.optimization_barrier((early, dmix))
-    own, rim_c, rim_z, dsl, tacc = call(
-        back_kernel, back_outputs(), [], queries, values, probs, dmix, flops=4 * 10**9, vmem=8
-    )
-    got_c, got_z = beside((rim_c, rim_z), 8)
-    early = add_stage(early, 0, 1, count)
-    early, tacc = lax.optimization_barrier((early, tacc))
-    layer_out, dnq, fwq, tgrad, qsum = call(
-        window_kernel,
-        window_outputs(),
-        [pltpu.VMEM((768, 256), BF)],
-        x1, act, dsl, keys, tacc, a1, big_down, big_qkv, vec, po,
-        flops=3 * 10**9,
-    )
-    early = add_stage(early, 3, 2, count)
-    early, own = lax.optimization_barrier((early, own))
-    dn, late = call(
-        late_kernel,
-        (sds((768, 256), F32), sds((count, 16, LATE))),
-        [
-            pltpu.VMEM((256, 512), F32),
-            pltpu.VMEM((8, 256), F32),
-            pltpu.VMEM((768, 512), BF),
-            pltpu.VMEM((256, 128), F32),
-        ],
-        own, got_c, got_z, dnq, xhat, big_qkv, a1, sums, zsum, qsum, fwq, tgrad,
-        flops=10**9, vmem=8,
-    )
-    tokens_grad = call(input_kernel, sds((16, 48, 256)), [], dn, dx1, xhat, rstd, vec, po, flops=10**9, vmem=8)
-    late = add_stage(add_stage(late, 0, 1, count), 3, 2, count)
-    grads = jnp.concatenate([early, late], axis=-1)
+    grads = add_stage(add_stage(grads, 0, 1, count), 3, 2, count)
     low = grads.astype(BF)
     parts = [grads[0]] + [swap(low[d], d << 1, count) for d in (1, 2, 3)]
+    parts[0], tokens_grad = lax.optimization_barrier((parts[0], tokens_grad))
 
     shapes = [sds(w.shape, F32) for w in weights]
     moments = call(
@@ -908,13 +865,14 @@
     big_down = (
         whole[:, 1792:2560].reshape(count, rows, 3, 256).transpose(0, 2, 1, 3).reshape(768, 256)
     )
-    vec = whole[:, 2560 : 2560 + vrows].T.astype(F32)
+    vt = whole[:, 2560:].astype(F32)
+    vec = vt[:, :vrows].T
 
     bias, limits, po, pk, xp, xhat, rstd, dy, dysum = call(
         prep_kernel, prep_outputs(), [], map_sizes, pos_table, tokens_in, cotangent, smem=1, flops=2 * 10**9
     )
     xk = call(halo_kernel, sds((CLS * KN, 256), F32), [], tokens_in, x_core, x_next, pk, flops=10**9)
-    a1, queries, keys, values = call(project_kernel, project_outputs(), [], xhat, xk, big_qkv, vec, flops=10**9)
+    queries, keys, values = call(project_kernel, project_outputs(), [], xhat, xk, big_qkv, vec, flops=10**9)
     mixed, probs = call(attend_kernel, attend_outputs(), [], limits, bias, queries, keys, values, flops=3 * 10**9)
     act, dz, a2, da, dx1, x1, dmix, sums, zsum = call(
         feed_kernel,
@@ -923,7 +881,9 @@
         dy, dysum, mixed, xp, big_out, big_up, big_down, vec,
         flops=4 * 10**9,
     )
-    own, rim_c, rim_z, dsl, tacc = call(back_kernel, back_outputs(), [], queries, values, probs, dmix, flops=4 * 10**9)
+    own, rim_c, rim_z, dsl, tacc, dkv = call(
+        back_kernel, back_outputs(), [], queries, values, probs, dmix, flops=4 * 10**9
+    )
     got_c, got_z = beside((rim_c, rim_z), band)
     grad_down, grad_up, grad_out = call(
         early_grads,
@@ -932,24 +892,17 @@
         act, dy, a2, dz, mixed, da,
         flops=10**9,
     )
-    layer_out, dnq, fwq, table_grad, qsum = call(
-        window_kernel,
-        window_outputs(),
-        [pltpu.VMEM((768, 256), BF)],
-        x1, act, dsl, keys, tacc, a1, big_down, big_qkv, vec, po,
+    dq, grad_qkv, grad_vec, table_grad = call(
+        late_grads,
+        late_outputs(),
+        [],
+        dsl, keys, tacc, xhat, xk, dkv, big_qkv, vt, sums, zsum,
         flops=3 * 10**9,
     )
-    dn, fkv, sums2 = call(
-        finish_kernel,
-        (sds((768, 256), F32), sds((256, 512), F32), sds((8, 256), F32)),
-        [pltpu.VMEM((768, 512), BF)],
-        own, got_c, got_z, dnq, xhat, big_qkv, a1,
-        flops=10**9,
-    )
-    tokens_grad = call(input_kernel, sds((16, 48, 256)), [], dn, dx1, xhat, rstd, vec, po, flops=10**9)
-    grad_qkv = jnp.concatenate([fwq, fkv], axis=1)
-    sums2 = sums2.at[2:3].add(qsum)
-    grad_vec = jnp.concatenate([sums + sums2, zsum.reshape(3, 256)], axis=0)
+    layer_out = call(output_kernel, sds((16, 48, 256)), [], x1, act, big_down, vec, po, flops=10**9)
+    tokens_grad = call(
+        input_kernel, sds((16, 48, 256)), [], own, got_c, got_z, dq, dx1, xhat, rstd, big_qkv, vec, po, flops=10**9
+    )
 
     packed = jnp.concatenate(
         [
@@ -957,7 +910,7 @@
             grad_out.reshape(count, rows, 256),
             grad_up.reshape(count, rows, 768),
             grad_down.reshape(count, 3, rows, 256).transpose(0, 2, 1, 3).reshape(count, rows, 768),
-            jnp.pad(grad_vec.T, ((0, 0), (0, 128 - vrows))).reshape(count, rows, 128),
+            grad_vec.reshape(count, rows, 128),
         ],
         axis=2,
     )

time: 88.4 us -> 84.3 us (0.954)
  starting transfers between devices: 36.2 us -> 29.5 us
  waiting for transfers between devices: 21.9 us -> 23.3 us
  Pallas kernels: 23.3 us -> 24.6 us
    ppermute x28 -> x24, starting transfers between devices: 32.8 us -> 26.3 us  [swap(): return lax.ppermute(block, AXES, [(k, k ^ mask) for k in range(count)])]
    ppermute x28 -> x24, waiting for transfers between devices: 21.9 us -> 23.3 us  [swap(): return lax.ppermute(block, AXES, [(k, k ^ mask) for k in range(count)])]
    pallas_call x13 -> x12, Pallas kernels: 23.3 us -> 24.6 us  [call(): pl.pallas_call(kernel, out_shape=out_shape, in_specs=specs, out_specs=jax...]
  transfers between devices with their start and end apart: 32 -> 28, of which waited for: 17 -> 13; matrix products, arithmetic and copies ran while one was open for 0% -> 0% of each run, Pallas kernels for 13% -> 9%
where the time goes in v6:
time: 84.3 us; the launch traced here: 84 us
  starting transfers between devices  29.5 us (35%)
  Pallas kernels  24.6 us (29%)
  waiting for transfers between devices  23.3 us (28%)
  local copies, waits for them, and re-layouts  4.29 us (5%)
  between operations  1.11 us (1%)
  other arithmetic  1.08 us (1%)
    ppermute x24, starting transfers between devices, swap(): return lax.ppermute(block, AXES, [(k, k ^ mask) for k in range(count)])  26.3 us
    pallas_call x12, Pallas kernels, call(): pl.pallas_call(kernel, out_shape=out_shape, in_specs=specs, out_specs=jax...  24.6 us
    ppermute x24, waiting for transfers between devices, swap(): return lax.ppermute(block, AXES, [(k, k ^ mask) for k in range(count)])  23.3 us
    unnamed x44, local copies, waits for them, and re-layouts  3.43 us
    ppermute x2, starting transfers between devices, beside(): lax.ppermute(block[0], 'band', [(b, b ^ 1) for b in range(band)])  1.86 us
  transfers between devices with their start and end apart: 28, of which 13 were waited for; matrix products, arithmetic and copies ran while one was open for 0% of the time, Pallas kernels for 9%

profile of v6, /device:TPU:0, one launch (start us, length us, event | category | flops | bytes accessed | tf_op | source)
XLA Modules:
  0.0 84.0 jit_solution(17480718546052150829)
XLA Ops:
  0.7 0.7 fusion.6
  1.4 0.8 add_convert_fusion.refs_0_
  2.2 5.1 %collective-permute-start.2 = (bf16[16,1408]{1,0:T(8,128)(2,1)S(1)}, bf16[16,1408]{1,0:T(8,128)(2,1)S(1)}, u32[]{:S(2)}, u32[]{:S(2)}) collective-permute-start(bf16[16,1408]{1,0:T(8,128)(2,1)S(1)} %add_convert_fusion.refs_0_), channel_id=1, source_target_pairs={{0,6},{1,7},{2,4},{3,5},{4,2},{5,3},{6,0},{7,1},{8,14},{9,15},{10,... | collective-permute-start | bytes 135176 | tf_op jit(solution)/shard_map/ppermute | solution.py:608
  7.3 0.6 collective-permute-start
  7.9 1.4 %collective-permute-done.2.refs_3_ = bf16[16,1408]{1,0:T(8,128)(2,1)S(1)} collective-permute-done((bf16[16,1408]{1,0:T(8,128)(2,1)S(1)}, bf16[16,1408]{1,0:T(8,128)(2,1)S(1)}, u32[]{:S(2)}, u32[]{:S(2)}) %collective-permute-start.2) | collective-permute-done | bytes 45088 | tf_op jit(solution)/shard_map/ppermute | solution.py:608
  9.4 2.9 %collective-permute-done.1.refs_2_ = bf16[16,1408]{1,0:T(8,128)(2,1)S(1)} collective-permute-done((bf16[16,1408]{1,0:T(8,128)(2,1)S(1)}, bf16[16,1408]{1,0:T(8,128)(2,1)S(1)}, u32[]{:S(2)}, u32[]{:S(2)}) %collective-permute-start.1) | collective-permute-done | bytes 45088 | tf_op jit(solution)/shard_map/ppermute | solution.py:608
  12.2 0.7 collective-permute-start.4
  12.9 1.8 %collective-permute-start.3 = (bf16[16,48,256]{2,1,0:T(8,128)(2,1)}, bf16[16,48,256]{2,1,0:T(8,128)(2,1)S(1)}, u32[]{:S(2)}, u32[]{:S(2)}) collective-permute-start(bf16[16,48,256]{2,1,0:T(8,128)(2,1)} %x_ref.1), channel_id=1, source_target_pairs={{0,1},{1,0},{2,3},{3,2},{4,5},{5,4},{6,7},{7,6},{8,9},{9,8},{10,11... | collective-permute-start | bytes 1179656 | tf_op jit(solution)/shard_map/ppermute | solution.py:713
  14.7 2.4 %collective-permute-start.7 = (bf16[4,16,1408]{2,1,0:T(8,128)(2,1)S(1)}, bf16[4,16,1408]{2,1,0:T(8,128)(2,1)S(1)}, u32[]{:S(2)}, u32[]{:S(2)}) collective-permute-start(bf16[4,16,1408]{2,1,0:T(8,128)(2,1)S(1)} %shard_map.372.b0), channel_id=1, source_target_pairs={{0,24},{1,25},{2,26},{3,27},{4,28},{5,29},{6,30},{7,31},{8,16},{9,... | collective-permute-start | bytes 540680 | tf_op jit(solution)/shard_map/ppermute | solution.py:608
  17.2 0.5 collective-permute-start.6
  17.7 0.5 collective-permute-start.5
  18.2 1.0 %copy-done = bf16[16,48,256]{2,1,0:T(8,128)(2,1)S(1)} copy-done((bf16[16,48,256]{2,1,0:T(8,128)(2,1)S(1)}, bf16[16,48,256]{2,1,0:T(8,128)(2,1)}, u32[]{:S(2)}) %copy-start) | copy-done | bytes 393240
  19.2 0.7 copy-done.18
  19.9 1.0 %copy-done.20 = bf16[16,48,256]{2,1,0:T(8,128)(2,1)S(1)} copy-done((bf16[16,48,256]{2,1,0:T(8,128)(2,1)S(1)}, bf16[16,48,256]{2,1,0:T(8,128)(2,1)}, u32[]{:S(2)}) %copy-start.20) | copy-done | bytes 393240
  20.9 0.7 copy-done.21
  21.5 1.5 %shard_map.373 = (f32[128,384]{1,0:T(8,128)S(1)}, s32[8,128]{1,0:T(8,128)S(1)}, bf16[192,192]{1,0:T(8,128)(2,1)S(1)}, bf16[512,480]{1,0:T(8,128)(2,1)S(1)}, f32[...) custom-call(s32[1,2]{1,0:T(1,128)S(1)} %copy-done.21, ...), custom_call_target="tpu_custom_call" | custom-call | flops 2000000000 | bytes 1000000 | tf_op jit(solution)/shard_map/pallas_call | solution.py:585
  23.1 0.1 collective-permute-start.8
  23.2 2.8 %collective-permute-done.6.b2 = bf16[4,16,1408]{2,1,0:T(8,128)(2,1)S(1)} collective-permute-done((bf16[4,16,1408]{2,1,0:T(8,128)(2,1)S(1)}, bf16[4,16,1408]{2,1,0:T(8,128)(2,1)S(1)}, u32[]{:S(2)}, u32[]{:S(2)}) %collective-permute-start.6) | collective-permute-done | bytes 180256 | tf_op jit(solution)/shard_map/ppermute | solution.py:608
  26.0 0.1 collective-permute-done.5.b1
  26.1 0.5 collective-permute-start.10
  26.6 1.4 %shard_map.374.xk_ref.refs_10_ = f32[2048,256]{1,0:T(8,128)S(1)} custom-call(bf16[16,48,256]{2,1,0:T(8,128)(2,1)S(1)} %copy-done, bf16[16,48,256]{2,1,0:T(8,128)(2,1)S(1)} %collective-permute-done.3.xc_ref, bf16[16,48,256]{2,1,0:T(8,128)(2,1)S(1)} %collective-permute-done.4.xz_ref, bf16[512,480]{1,0:T(8,128)(2,1)S(1)} %get-tuple-element.100.pk_ref), custom_call_target="tpu_custom_call" | custom-call | flops 1000000000 | bytes 1000000 | tf_op jit(solution)/shard_map/pallas_call | solution.py:585
  28.1 1.4 %shard_map.375 = (bf16[768,256]{1,0:T(8,128)(2,1)S(1)}, bf16[2048,256]{1,0:T(8,128)(2,1)S(1)}, bf16[2048,256]{1,0:T(8,128)(2,1)S(1)}, bf16[256,768]{1,0:T(8,128)...) custom-call(f32[768,256]{1,0:T(8,128)S(1)} %get-tuple-element.97.xhat_ref.refs_9_, ...), custom_call_target="tpu_custom_call" | custom-call | flops 1000000000 | bytes 1000000 | tf_op jit(solution)/shard_map/pallas_call | solution.py:585
  29.5 2.6 %shard_map.376 = (bf16[768,256]{1,0:T(8,128)(2,1)S(1)}, f32[2048,384]{1,0:T(8,128)S(1)}) custom-call(s32[8,128]{1,0:T(8,128)S(1)} %get-tuple-element.95.limits_ref, f32[128,384]{1,0:T(8,128)S(1)} %get-tuple-element.96.bias_ref, bf16[768,256]{1,0:T(8,128)(2,1)S(1)} %get-tuple-element.104.q_ref, bf16[2048,256]{1,0:T(8,128)(2,1)S(1)} %get-tuple-element.105.k_ref.refs_7_, ...), custom_call_target="tpu_custom_call" | custom-call | flops 3000000000 | bytes 1000000 | tf_op jit(solution)/shard_map/pallas_call | solution.py:585
  32.1 4.4 %shard_map.377 = (bf16[768,768]{1,0:T(8,128)(2,1)S(1)}, bf16[768,768]{1,0:T(8,128)(2,1)S(1)}, bf16[768,256]{1,0:T(8,128)(2,1)S(1)}, bf16[768,256]{1,0:T(8,128)(2...) custom-call(bf16[768,256]{1,0:T(8,128)(2,1)S(1)} %get-tuple-element., ...), custom_call_target="tpu_custom_call" | custom-call | flops 4000000000 | bytes 1000000 | tf_op jit(solution)/shard_map/pallas_call | solution.py:585
  36.5 3.5 %shard_map.379 = (f32[768,512]{1,0:T(8,128)S(1)}, bf16[640,512]{1,0:T(8,128)(2,1)S(1)}, bf16[640,512]{1,0:T(8,128)(2,1)S(1)}, bf16[2048,384]{1,0:T(8,128)(2,1)S(...) custom-call(bf16[768,256]{1,0:T(8,128)(2,1)S(1)} %get-tuple-element.104.q_ref, ...), custom_call_target="tpu_custom_call" | custom-call | flops 4000000000 | bytes 1000000 | tf_op jit(solution)/shard_map/pallas_call | solution.py:585
  40.0 3.4 %shard_map.380 = (bf16[768,256]{1,0:T(8,128)(2,1)S(1)}, bf16[32,16,1408]{2,1,0:T(8,128)(2,1)S(1)}) custom-call(bf16[768,768]{1,0:T(8,128)(2,1)S(1)} %get-tuple-element.111.act_ref.refs_0_, bf16[768,256]{1,0:T(8,128)(2,1)S(1)} %get-tuple-element.93.dy_ref.refs_1_, bf16[768,256]{1,0:T(8,128)(2,1)S(1)} %get-tuple-element.114.refs_2_, ...), custom_call_target="tpu_custom_call" | custom-call | flops 5000000000 | bytes 1000000 | tf_op jit(solution)/shard_map/pallas_call | solution.py:585
  43.5 0.1 slice.40
  43.5 0.6 collective-permute-start.12
  44.1 0.1 collective-permute-start.16
  44.2 0.7 collective-permute-start.17
  44.9 1.0 %collective-permute-done.12 = bf16[16,16,1408]{2,1,0:T(8,128)(2,1)S(1)} collective-permute-done((bf16[16,16,1408]{2,1,0:T(8,128)(2,1)S(1)}, bf16[16,16,1408]{2,1,0:T(8,128)(2,1)S(1)}, u32[]{:S(2)}, u32[]{:S(2)}) %collective-permute-start.12) | collective-permute-done | bytes 720928 | tf_op jit(solution)/shard_map/ppermute | solution.py:608
  45.9 0.2 convert_add_fusion
  46.1 1.6 %collective-permute-start.13 = (bf16[4,16,1408]{2,1,0:T(8,128)(2,1)S(1)}, bf16[4,16,1408]{2,1,0:T(8,128)(2,1)S(1)}, u32[]{:S(2)}, u32[]{:S(2)}) collective-permute-start(bf16[4,16,1408]{2,1,0:T(8,128)(2,1)S(1)} %get-tuple-element.166), channel_id=1, source_target_pairs={{0,8},{1,9},{2,10},{3,11},{4,12},{5,13},{6,14},{7,15},{8,0},{9,1},... | collective-permute-start | bytes 540680 | tf_op jit(solution)/shard_map/ppermute | solution.py:608
  47.7 1.4 %collective-permute-start.15 = (bf16[4,16,1408]{2,1,0:T(8,128)(2,1)S(1)}, bf16[4,16,1408]{2,1,0:T(8,128)(2,1)S(1)}, u32[]{:S(2)}, u32[]{:S(2)}) collective-permute-start(bf16[4,16,1408]{2,1,0:T(8,128)(2,1)S(1)} %get-tuple-element.167), channel_id=1, source_target_pairs={{0,24},{1,25},{2,26},{3,27},{4,28},{5,29},{6,30},{7,31},{8,16},{9,... | collective-permute-start | bytes 540680 | tf_op jit(solution)/shard_map/ppermute | solution.py:608
  49.1 0.6 collective-permute-start.14
  49.7 2.6 %shard_map.381 = bf16[16,48,256]{2,1,0:T(8,128)(2,1)} custom-call(f32[768,512]{1,0:T(8,128)S(1)} %get-tuple-element.127.own_ref, bf16[640,512]{1,0:T(8,128)(2,1)S(1)} %collective-permute-done.16.gotc_ref, bf16[640,512]{1,0:T(8,128)(2,1)S(1)} %collective-permute-done.17.gotz_ref, bf16[768,256]{1,0:T(8,128)(2,1)S(1)} %get-tuple-element.130.dq_ref, ...), custom_call_target="tpu_custom_call" | custom-call | flops 1000000000 | bytes 1000000 | tf_op jit(solution)/shard_map/pallas_call | solution.py:585
  52.4 0.0 copy-start.5
  52.4 0.0 copy-start.6
  52.4 0.0 copy-start.8
  52.4 0.0 copy-start.9
  52.5 0.0 copy-start.12
  52.5 0.0 copy-start.13
  52.5 4.3 %collective-permute-done.15 = bf16[4,16,1408]{2,1,0:T(8,128)(2,1)S(1)} collective-permute-done((bf16[4,16,1408]{2,1,0:T(8,128)(2,1)S(1)}, bf16[4,16,1408]{2,1,0:T(8,128)(2,1)S(1)}, u32[]{:S(2)}, u32[]{:S(2)}) %collective-permute-start.15) | collective-permute-done | bytes 180256 | tf_op jit(solution)/shard_map/ppermute | solution.py:608
  56.9 2.9 %collective-permute-done.14 = bf16[4,16,1408]{2,1,0:T(8,128)(2,1)S(1)} collective-permute-done((bf16[4,16,1408]{2,1,0:T(8,128)(2,1)S(1)}, bf16[4,16,1408]{2,1,0:T(8,128)(2,1)S(1)}, u32[]{:S(2)}, u32[]{:S(2)}) %collective-permute-start.14) | collective-permute-done | bytes 180256 | tf_op jit(solution)/shard_map/ppermute | solution.py:608
  59.8 0.1 fusion.3
  59.9 1.3 %collective-permute-start.20 = (bf16[16,1408]{1,0:T(8,128)(2,1)S(1)}, bf16[16,1408]{1,0:T(8,128)(2,1)S(1)}, u32[]{:S(2)}, u32[]{:S(2)}) collective-permute-start(bf16[16,1408]{1,0:T(8,128)(2,1)S(1)} %get-tuple-element.169), channel_id=1, source_target_pairs={{0,6},{1,7},{2,4},{3,5},{4,2},{5,3},{6,0},{7,1},{8,14},{9,15},{10,... | collective-permute-start | bytes 135176 | tf_op jit(solution)/shard_map/ppermute | solution.py:608
  61.2 2.2 %collective-permute-start.19 = (bf16[16,1408]{1,0:T(8,128)(2,1)S(1)}, bf16[16,1408]{1,0:T(8,128)(2,1)S(1)}, u32[]{:S(2)}, u32[]{:S(2)}) collective-permute-start(bf16[16,1408]{1,0:T(8,128)(2,1)S(1)} %get-tuple-element.170), channel_id=1, source_target_pairs={{0,4},{1,5},{2,6},{3,7},{4,0},{5,1},{6,2},{7,3},{8,12},{9,13},{10,... | collective-permute-start | bytes 135176 | tf_op jit(solution)/shard_map/ppermute | solution.py:608
  63.4 1.0 %collective-permute-start.18 = (bf16[16,1408]{1,0:T(8,128)(2,1)S(1)}, bf16[16,1408]{1,0:T(8,128)(2,1)S(1)}, u32[]{:S(2)}, u32[]{:S(2)}) collective-permute-start(bf16[16,1408]{1,0:T(8,128)(2,1)S(1)} %get-tuple-element.171), channel_id=1, source_target_pairs={{0,2},{1,3},{2,0},{3,1},{4,6},{5,7},{6,4},{7,5},{8,10},{9,11},{10,... | collective-permute-start | bytes 135176 | tf_op jit(solution)/shard_map/ppermute | solution.py:608
  64.4 2.0 %collective-permute-done.20.refs_3_ = bf16[16,1408]{1,0:T(8,128)(2,1)S(1)} collective-permute-done((bf16[16,1408]{1,0:T(8,128)(2,1)S(1)}, bf16[16,1408]{1,0:T(8,128)(2,1)S(1)}, u32[]{:S(2)}, u32[]{:S(2)}) %collective-permute-start.20) | collective-permute-done | bytes 45088 | tf_op jit(solution)/shard_map/ppermute | solution.py:608
  66.3 1.6 %collective-permute-done.19.refs_2_ = bf16[16,1408]{1,0:T(8,128)(2,1)S(1)} collective-permute-done((bf16[16,1408]{1,0:T(8,128)(2,1)S(1)}, bf16[16,1408]{1,0:T(8,128)(2,1)S(1)}, u32[]{:S(2)}, u32[]{:S(2)}) %collective-permute-start.19) | collective-permute-done | bytes 45088 | tf_op jit(solution)/shard_map/ppermute | solution.py:608
  68.1 0.9 %shard_map.382 = (f32[8,768]{1,0:T(8,128)}, f32[8,768]{1,0:T(8,128)}, f32[8,768]{1,0:T(8,128)S(1)}, f32[8,256]{1,0:T(8,128)}, f32[8,256]{1,0:T(8,128)}, /*index=...) custom-call(f32[16,1408]{1,0:T(8,128)S(1)} %slice_bitcast_fusion.ref, ...), custom_call_target="tpu_custom_call" | custom-call | flops 100000000 | bytes 1000000 | tf_op jit(solution)/shard_map/pallas_call | solution.py:585
  69.0 0.1 collective-permute-start.21
  69.0 1.2 %collective-permute-done.21 = f32[8,128]{1,0:T(8,128)S(1)} collective-permute-done((f32[8,128]{1,0:T(8,128)S(1)}, f32[8,128]{1,0:T(8,128)S(1)}, u32[]{:S(2)}, u32[]{:S(2)}) %collective-permute-start.21) | collective-permute-done | bytes 4128 | tf_op jit(solution)/shard_map/ppermute | solution.py:608
  70.2 1.7 %collective-permute-start.24 = (f32[8,128]{1,0:T(8,128)S(1)}, f32[8,128]{1,0:T(8,128)S(1)}, u32[]{:S(2)}, u32[]{:S(2)}) collective-permute-start(f32[8,128]{1,0:T(8,128)S(1)} %add.66), channel_id=1, source_target_pairs={{0,24},{1,25},{2,26},{3,27},{4,28},{5,29},{6,30},{7,31},{8,16},{9,... | collective-permute-start | bytes 12296 | tf_op jit(solution)/shard_map/ppermute | solution.py:608
  71.9 1.3 %collective-permute-start.23 = (f32[8,128]{1,0:T(8,128)S(1)}, f32[8,128]{1,0:T(8,128)S(1)}, u32[]{:S(2)}, u32[]{:S(2)}) collective-permute-start(f32[8,128]{1,0:T(8,128)S(1)} %add.66), channel_id=1, source_target_pairs={{0,16},{1,17},{2,18},{3,19},{4,20},{5,21},{6,22},{7,23},{8,24},{9,... | collective-permute-start | bytes 12296 | tf_op jit(solution)/shard_map/ppermute | solution.py:608
  73.2 0.5 collective-permute-start.22
  73.7 1.0 %collective-permute-done.24 = f32[8,128]{1,0:T(8,128)S(1)} collective-permute-done((f32[8,128]{1,0:T(8,128)S(1)}, f32[8,128]{1,0:T(8,128)S(1)}, u32[]{:S(2)}, u32[]{:S(2)}) %collective-permute-start.24) | collective-permute-done | bytes 4128 | tf_op jit(solution)/shard_map/ppermute | solution.py:608
  74.7 0.8 collective-permute-done.23
  75.5 1.3 %collective-permute-done.22 = f32[8,128]{1,0:T(8,128)S(1)} collective-permute-done((f32[8,128]{1,0:T(8,128)S(1)}, f32[8,128]{1,0:T(8,128)S(1)}, u32[]{:S(2)}, u32[]{:S(2)}) %collective-permute-start.22) | collective-permute-done | bytes 4128 | tf_op jit(solution)/shard_map/ppermute | solution.py:608
  76.8 1.1 %collective-permute-start.27 = (f32[8,128]{1,0:T(8,128)S(1)}, f32[8,128]{1,0:T(8,128)S(1)}, u32[]{:S(2)}, u32[]{:S(2)}) collective-permute-start(f32[8,128]{1,0:T(8,128)S(1)} %add_add_fusion.a_ref), channel_id=1, source_target_pairs={{0,6},{1,7},{2,4},{3,5},{4,2},{5,3},{6,0},{7,1},{8,14},{9,15},{10,... | collective-permute-start | bytes 12296 | tf_op jit(solution)/shard_map/ppermute | solution.py:608
  77.8 0.2 collective-permute-start.26
  78.1 3.1 %collective-permute-start.25 = (f32[8,128]{1,0:T(8,128)S(1)}, f32[8,128]{1,0:T(8,128)S(1)}, u32[]{:S(2)}, u32[]{:S(2)}) collective-permute-start(f32[8,128]{1,0:T(8,128)S(1)} %add_add_fusion.a_ref), channel_id=1, source_target_pairs={{0,2},{1,3},{2,0},{3,1},{4,6},{5,7},{6,4},{7,5},{8,10},{9,11},{10,... | collective-permute-start | bytes 12296 | tf_op jit(solution)/shard_map/ppermute | solution.py:608
  81.2 2.0 %shard_map.378 = bf16[16,48,256]{2,1,0:T(8,128)(2,1)} custom-call(f32[768,256]{1,0:T(8,128)S(1)} %get-tuple-element.110.x1_ref, bf16[768,768]{1,0:T(8,128)(2,1)S(1)} %get-tuple-element.111.act_ref.refs_0_, bf16[768,256]{1,0:T(8,128)(2,1)S(1)} %get-tuple-element.112.wd_ref, f32[11,256]{1,0:T(8,128)S(1)} %get-tuple-element.109.vec_ref, ...), custom_call_target="tpu_custom_call" | custom-call | flops 1000000000 | bytes 1000000 | tf_op jit(solution)/shard_map/pallas_call | solution.py:585
  83.2 0.8 shard_map.383
  (58 shorter events, 0.2 us)
Async XLA Ops:
  2.2 7.2 %collective-permute-start.2 = (bf16[16,1408]{1,0:T(8,128)(2,1)S(1)}, bf16[16,1408]{1,0:T(8,128)(2,1)S(1)}, u32[]{:S(2)}, u32[]{:S(2)}) collective-permute-start(bf16[16,1408]{1,0:T(8,128)(2,1)S(1)} %add_convert_fusion.refs_0_), channel_id=1, source_target_pairs={{0,6},{1,7},{2,4},{3,5},{4,2},{5,3},{6,0},{7,1},{8,14},{9,15},{10,... | collective-permute-start | bytes 135176 | tf_op jit(solution)/shard_map/ppermute | solution.py:608
  7.3 4.9 %collective-permute-start.1 = (bf16[16,1408]{1,0:T(8,128)(2,1)S(1)}, bf16[16,1408]{1,0:T(8,128)(2,1)S(1)}, u32[]{:S(2)}, u32[]{:S(2)}) collective-permute-start(bf16[16,1408]{1,0:T(8,128)(2,1)S(1)} %add_convert_fusion.refs_0_), channel_id=1, source_target_pairs={{0,4},{1,5},{2,6},{3,7},{4,0},{5,1},{6,2},{7,3},{8,12},{9,13},{10,... | collective-permute-start | bytes 135176 | tf_op jit(solution)/shard_map/ppermute | solution.py:608
  7.3 4.9 %collective-permute-start = (bf16[16,1408]{1,0:T(8,128)(2,1)S(1)}, bf16[16,1408]{1,0:T(8,128)(2,1)S(1)}, u32[]{:S(2)}, u32[]{:S(2)}) collective-permute-start(bf16[16,1408]{1,0:T(8,128)(2,1)S(1)} %add_convert_fusion.refs_0_), channel_id=1, source_target_pairs={{0,2},{1,3},{2,0},{3,1},{4,6},{5,7},{6,4},{7,5},{8,10},{9,11},{10,... | collective-permute-start | bytes 135176 | tf_op jit(solution)/shard_map/ppermute | solution.py:608
  12.2 14.4 %collective-permute-start.4 = (bf16[16,48,256]{2,1,0:T(8,128)(2,1)}, bf16[16,48,256]{2,1,0:T(8,128)(2,1)S(1)}, u32[]{:S(2)}, u32[]{:S(2)}) collective-permute-start(bf16[16,48,256]{2,1,0:T(8,128)(2,1)} %x_ref.1), channel_id=1, source_target_pairs={{1,2},{2,1},{3,4},{4,3},{5,6},{6,5},{9,10},{10,9},{11,12},{12,11},... | collective-permute-start | bytes 1179656 | tf_op jit(solution)/shard_map/ppermute | solution.py:714
  12.9 13.7 %collective-permute-start.3 = (bf16[16,48,256]{2,1,0:T(8,128)(2,1)}, bf16[16,48,256]{2,1,0:T(8,128)(2,1)S(1)}, u32[]{:S(2)}, u32[]{:S(2)}) collective-permute-start(bf16[16,48,256]{2,1,0:T(8,128)(2,1)} %x_ref.1), channel_id=1, source_target_pairs={{0,1},{1,0},{2,3},{3,2},{4,5},{5,4},{6,7},{7,6},{8,9},{9,8},{10,11... | collective-permute-start | bytes 1179656 | tf_op jit(solution)/shard_map/ppermute | solution.py:713
  14.7 8.4 %collective-permute-start.7 = (bf16[4,16,1408]{2,1,0:T(8,128)(2,1)S(1)}, bf16[4,16,1408]{2,1,0:T(8,128)(2,1)S(1)}, u32[]{:S(2)}, u32[]{:S(2)}) collective-permute-start(bf16[4,16,1408]{2,1,0:T(8,128)(2,1)S(1)} %shard_map.372.b0), channel_id=1, source_target_pairs={{0,24},{1,25},{2,26},{3,27},{4,28},{5,29},{6,30},{7,31},{8,16},{9,... | collective-permute-start | bytes 540680 | tf_op jit(solution)/shard_map/ppermute | solution.py:608
  17.2 8.8 %collective-permute-start.6 = (bf16[4,16,1408]{2,1,0:T(8,128)(2,1)S(1)}, bf16[4,16,1408]{2,1,0:T(8,128)(2,1)S(1)}, u32[]{:S(2)}, u32[]{:S(2)}) collective-permute-start(bf16[4,16,1408]{2,1,0:T(8,128)(2,1)S(1)} %shard_map.372.b0), channel_id=1, source_target_pairs={{0,16},{1,17},{2,18},{3,19},{4,20},{5,21},{6,22},{7,23},{8,24},{9,... | collective-permute-start | bytes 540680 | tf_op jit(solution)/shard_map/ppermute | solution.py:608
  17.7 8.4 %collective-permute-start.5 = (bf16[4,16,1408]{2,1,0:T(8,128)(2,1)S(1)}, bf16[4,16,1408]{2,1,0:T(8,128)(2,1)S(1)}, u32[]{:S(2)}, u32[]{:S(2)}) collective-permute-start(bf16[4,16,1408]{2,1,0:T(8,128)(2,1)S(1)} %shard_map.372.b0), channel_id=1, source_target_pairs={{0,8},{1,9},{2,10},{3,11},{4,12},{5,13},{6,14},{7,15},{8,0},{9,1},... | collective-permute-start | bytes 540680 | tf_op jit(solution)/shard_map/ppermute | solution.py:608
  18.2 1.0 %copy-start = (bf16[16,48,256]{2,1,0:T(8,128)(2,1)S(1)}, bf16[16,48,256]{2,1,0:T(8,128)(2,1)}, u32[]{:S(2)}) copy-start(bf16[16,48,256]{2,1,0:T(8,128)(2,1)} %x_ref.1) | copy-start | bytes 1179652
  19.2 0.7 copy-start.18
  19.9 1.0 %copy-start.20 = (bf16[16,48,256]{2,1,0:T(8,128)(2,1)S(1)}, bf16[16,48,256]{2,1,0:T(8,128)(2,1)}, u32[]{:S(2)}) copy-start(bf16[16,48,256]{2,1,0:T(8,128)(2,1)} %cot_ref.1) | copy-start | bytes 1179652
  20.9 0.7 copy-start.21
  23.1 5.0 %collective-permute-start.8 = (bf16[4,16,1408]{2,1,0:T(8,128)(2,1)S(1)}, bf16[4,16,1408]{2,1,0:T(8,128)(2,1)S(1)}, u32[]{:S(2)}, u32[]{:S(2)}) collective-permute-start(bf16[4,16,1408]{2,1,0:T(8,128)(2,1)S(1)} %shard_map.372.b0), channel_id=1, source_target_pairs={{0,1},{1,0},{2,3},{3,2},{4,5},{5,4},{6,7},{7,6},{8,9},{9,8},{10,11... | collective-permute-start | bytes 540680 | tf_op jit(solution)/shard_map/ppermute | solution.py:608
  26.1 2.0 %collective-permute-start.9 = (bf16[4,16,1408]{2,1,0:T(8,128)(2,1)S(1)}, bf16[4,16,1408]{2,1,0:T(8,128)(2,1)S(1)}, u32[]{:S(2)}, u32[]{:S(2)}) collective-permute-start(bf16[4,16,1408]{2,1,0:T(8,128)(2,1)S(1)} %collective-permute-done.5.b1), channel_id=1, source_target_pairs={{0,1},{1,0},{2,3},{3,2},{4,5},{5,4},{6,7},{7,6},{8,9},{9,8},{10,11... | collective-permute-start | bytes 540680 | tf_op jit(solution)/shard_map/ppermute | solution.py:608
  26.1 2.0 %collective-permute-start.10 = (bf16[4,16,1408]{2,1,0:T(8,128)(2,1)S(1)}, bf16[4,16,1408]{2,1,0:T(8,128)(2,1)S(1)}, u32[]{:S(2)}, u32[]{:S(2)}) collective-permute-start(bf16[4,16,1408]{2,1,0:T(8,128)(2,1)S(1)} %collective-permute-done.6.b2), channel_id=1, source_target_pairs={{0,1},{1,0},{2,3},{3,2},{4,5},{5,4},{6,7},{7,6},{8,9},{9,8},{10,11... | collective-permute-start | bytes 540680 | tf_op jit(solution)/shard_map/ppermute | solution.py:608
  26.6 1.5 %collective-permute-start.11 = (bf16[4,16,1408]{2,1,0:T(8,128)(2,1)S(1)}, bf16[4,16,1408]{2,1,0:T(8,128)(2,1)S(1)}, u32[]{:S(2)}, u32[]{:S(2)}) collective-permute-start(bf16[4,16,1408]{2,1,0:T(8,128)(2,1)S(1)} %collective-permute-done.7.b3), channel_id=1, source_target_pairs={{0,1},{1,0},{2,3},{3,2},{4,5},{5,4},{6,7},{7,6},{8,9},{9,8},{10,11... | collective-permute-start | bytes 540680 | tf_op jit(solution)/shard_map/ppermute | solution.py:608
  43.5 2.4 %collective-permute-start.12 = (bf16[16,16,1408]{2,1,0:T(8,128)(2,1)S(1)}, bf16[16,16,1408]{2,1,0:T(8,128)(2,1)S(1)}, u32[]{:S(2)}, u32[]{:S(2)}) collective-permute-start(bf16[16,16,1408]{2,1,0:T(8,128)(2,1)S(1)} %slice.40), channel_id=1, source_target_pairs={{0,1},{1,0},{2,3},{3,2},{4,5},{5,4},{6,7},{7,6},{8,9},{9,8},{10,11... | collective-permute-start | bytes 2162696 | tf_op jit(solution)/shard_map/ppermute | solution.py:608
  44.1 5.6 %collective-permute-start.16 = (bf16[640,512]{1,0:T(8,128)(2,1)S(1)}, bf16[640,512]{1,0:T(8,128)(2,1)S(1)}, u32[]{:S(2)}, u32[]{:S(2)}) collective-permute-start(bf16[640,512]{1,0:T(8,128)(2,1)S(1)} %get-tuple-element.128), channel_id=1, source_target_pairs={{0,1},{1,0},{2,3},{3,2},{4,5},{5,4},{6,7},{7,6},{8,9},{9,8},{10,11... | collective-permute-start | bytes 1966088 | tf_op jit(solution)/shard_map/ppermute | solution.py:713
  44.2 5.6 %collective-permute-start.17 = (bf16[640,512]{1,0:T(8,128)(2,1)S(1)}, bf16[640,512]{1,0:T(8,128)(2,1)S(1)}, u32[]{:S(2)}, u32[]{:S(2)}) collective-permute-start(bf16[640,512]{1,0:T(8,128)(2,1)S(1)} %get-tuple-element.129), channel_id=1, source_target_pairs={{1,2},{2,1},{3,4},{4,3},{5,6},{6,5},{9,10},{10,9},{11,12},{12,11},... | collective-permute-start | bytes 1966088 | tf_op jit(solution)/shard_map/ppermute | solution.py:714
  46.1 6.4 %collective-permute-start.13 = (bf16[4,16,1408]{2,1,0:T(8,128)(2,1)S(1)}, bf16[4,16,1408]{2,1,0:T(8,128)(2,1)S(1)}, u32[]{:S(2)}, u32[]{:S(2)}) collective-permute-start(bf16[4,16,1408]{2,1,0:T(8,128)(2,1)S(1)} %get-tuple-element.166), channel_id=1, source_target_pairs={{0,8},{1,9},{2,10},{3,11},{4,12},{5,13},{6,14},{7,15},{8,0},{9,1},... | collective-permute-start | bytes 540680 | tf_op jit(solution)/shard_map/ppermute | solution.py:608
  47.7 9.2 %collective-permute-start.15 = (bf16[4,16,1408]{2,1,0:T(8,128)(2,1)S(1)}, bf16[4,16,1408]{2,1,0:T(8,128)(2,1)S(1)}, u32[]{:S(2)}, u32[]{:S(2)}) collective-permute-start(bf16[4,16,1408]{2,1,0:T(8,128)(2,1)S(1)} %get-tuple-element.167), channel_id=1, source_target_pairs={{0,24},{1,25},{2,26},{3,27},{4,28},{5,29},{6,30},{7,31},{8,16},{9,... | collective-permute-start | bytes 540680 | tf_op jit(solution)/shard_map/ppermute | solution.py:608
  49.1 10.7 %collective-permute-start.14 = (bf16[4,16,1408]{2,1,0:T(8,128)(2,1)S(1)}, bf16[4,16,1408]{2,1,0:T(8,128)(2,1)S(1)}, u32[]{:S(2)}, u32[]{:S(2)}) collective-permute-start(bf16[4,16,1408]{2,1,0:T(8,128)(2,1)S(1)} %get-tuple-element.168), channel_id=1, source_target_pairs={{0,16},{1,17},{2,18},{3,19},{4,20},{5,21},{6,22},{7,23},{8,24},{9,... | collective-permute-start | bytes 540680 | tf_op jit(solution)/shard_map/ppermute | solution.py:608
  52.4 15.6 %copy-start.1 = (f32[8,768]{1,0:T(8,128)S(1)}, f32[8,768]{1,0:T(8,128)}, u32[]{:S(2)}) copy-start(f32[8,768]{1,0:T(8,128)} %refs_2_.1) | copy-start | bytes 73732
  52.4 15.6 %copy-start.2 = (f32[8,768]{1,0:T(8,128)S(1)}, f32[8,768]{1,0:T(8,128)}, u32[]{:S(2)}) copy-start(f32[8,768]{1,0:T(8,128)} %refs_0_.1) | copy-start | bytes 73732
  52.4 15.6 %copy-start.3 = (f32[24,256]{1,0:T(8,128)S(1)}, f32[24,256]{1,0:T(8,128)}, u32[]{:S(2)}) copy-start(f32[24,256]{1,0:T(8,128)} %refs_3_.1) | copy-start | bytes 73732
  52.4 15.6 %copy-start.4 = (f32[8,256]{1,0:T(8,128)S(1)}, f32[8,256]{1,0:T(8,128)}, u32[]{:S(2)}) copy-start(f32[8,256]{1,0:T(8,128)} %refs_1_.1) | copy-start | bytes 24580
  52.4 15.6 %copy-start.5 = (f32[8,768]{1,0:T(8,128)S(1)}, f32[8,768]{1,0:T(8,128)}, u32[]{:S(2)}) copy-start(f32[8,768]{1,0:T(8,128)} %refs_10_.1) | copy-start | bytes 73732
  52.4 15.6 %copy-start.6 = (f32[8,768]{1,0:T(8,128)S(1)}, f32[8,768]{1,0:T(8,128)}, u32[]{:S(2)}) copy-start(f32[8,768]{1,0:T(8,128)} %refs_12_.1) | copy-start | bytes 73732
  52.4 15.6 %copy-start.7 = (f32[24,256]{1,0:T(8,128)S(1)}, f32[24,256]{1,0:T(8,128)}, u32[]{:S(2)}) copy-start(f32[24,256]{1,0:T(8,128)} %refs_13_.1) | copy-start | bytes 73732
  52.4 15.6 %copy-start.8 = (f32[8,768]{1,0:T(8,128)S(1)}, f32[8,768]{1,0:T(8,128)}, u32[]{:S(2)}) copy-start(f32[8,768]{1,0:T(8,128)} %refs_16_.1) | copy-start | bytes 73732
  52.4 15.6 %copy-start.9 = (f32[8,768]{1,0:T(8,128)S(1)}, f32[8,768]{1,0:T(8,128)}, u32[]{:S(2)}) copy-start(f32[8,768]{1,0:T(8,128)} %refs_18_.1) | copy-start | bytes 73732
  52.4 15.6 %copy-start.10 = (f32[24,256]{1,0:T(8,128)S(1)}, f32[24,256]{1,0:T(8,128)}, u32[]{:S(2)}) copy-start(f32[24,256]{1,0:T(8,128)} %refs_19_.1) | copy-start | bytes 73732
  52.4 15.6 %copy-start.11 = (f32[11,8]{0,1:T(8,128)S(1)}, f32[11,8]{0,1:T(8,128)}, u32[]{:S(2)}) copy-start(f32[11,8]{0,1:T(8,128)} %param.28) | copy-start | bytes 1060
  52.5 15.6 %copy-start.12 = (f32[8,256]{1,0:T(8,128)S(1)}, f32[8,256]{1,0:T(8,128)}, u32[]{:S(2)}) copy-start(f32[8,256]{1,0:T(8,128)} %refs_11_.1) | copy-start | bytes 24580
  52.5 15.6 %copy-start.13 = (f32[8,256]{1,0:T(8,128)S(1)}, f32[8,256]{1,0:T(8,128)}, u32[]{:S(2)}) copy-start(f32[8,256]{1,0:T(8,128)} %refs_17_.1) | copy-start | bytes 24580
  52.5 15.6 %copy-start.14 = (f32[11,8]{0,1:T(8,128)S(1)}, f32[11,8]{0,1:T(8,128)}, u32[]{:S(2)}) copy-start(f32[11,8]{0,1:T(8,128)} %param.38) | copy-start | bytes 1060
  52.5 15.6 %copy-start.15 = (f32[8,49]{1,0:T(8,128)S(1)}, f32[8,49]{1,0:T(8,128)}, u32[]{:S(2)}) copy-start(f32[8,49]{1,0:T(8,128)} %refs_15_.1) | copy-start | bytes 4708
  52.5 15.6 %copy-start.16 = (f32[11,8]{0,1:T(8,128)S(1)}, f32[11,8]{0,1:T(8,128)}, u32[]{:S(2)}) copy-start(f32[11,8]{0,1:T(8,128)} %param.39) | copy-start | bytes 1060
  52.5 15.6 %copy-start.17 = (f32[8,49]{1,0:T(8,128)S(1)}, f32[8,49]{1,0:T(8,128)}, u32[]{:S(2)}) copy-start(f32[8,49]{1,0:T(8,128)} %refs_21_.1) | copy-start | bytes 4708
  52.5 15.6 %copy-start.19 = (f32[8,49]{1,0:T(8,128)S(1)}, f32[8,49]{1,0:T(8,128)}, u32[]{:S(2)}) copy-start(f32[8,49]{1,0:T(8,128)} %refs_5_.3) | copy-start | bytes 4708
  59.9 6.4 %collective-permute-start.20 = (bf16[16,1408]{1,0:T(8,128)(2,1)S(1)}, bf16[16,1408]{1,0:T(8,128)(2,1)S(1)}, u32[]{:S(2)}, u32[]{:S(2)}) collective-permute-start(bf16[16,1408]{1,0:T(8,128)(2,1)S(1)} %get-tuple-element.169), channel_id=1, source_target_pairs={{0,6},{1,7},{2,4},{3,5},{4,2},{5,3},{6,0},{7,1},{8,14},{9,15},{10,... | collective-permute-start | bytes 135176 | tf_op jit(solution)/shard_map/ppermute | solution.py:608
  61.2 6.7 %collective-permute-start.19 = (bf16[16,1408]{1,0:T(8,128)(2,1)S(1)}, bf16[16,1408]{1,0:T(8,128)(2,1)S(1)}, u32[]{:S(2)}, u32[]{:S(2)}) collective-permute-start(bf16[16,1408]{1,0:T(8,128)(2,1)S(1)} %get-tuple-element.170), channel_id=1, source_target_pairs={{0,4},{1,5},{2,6},{3,7},{4,0},{5,1},{6,2},{7,3},{8,12},{9,13},{10,... | collective-permute-start | bytes 135176 | tf_op jit(solution)/shard_map/ppermute | solution.py:608
  63.4 4.5 %collective-permute-start.18 = (bf16[16,1408]{1,0:T(8,128)(2,1)S(1)}, bf16[16,1408]{1,0:T(8,128)(2,1)S(1)}, u32[]{:S(2)}, u32[]{:S(2)}) collective-permute-start(bf16[16,1408]{1,0:T(8,128)(2,1)S(1)} %get-tuple-element.171), channel_id=1, source_target_pairs={{0,2},{1,3},{2,0},{3,1},{4,6},{5,7},{6,4},{7,5},{8,10},{9,11},{10,... | collective-permute-start | bytes 135176 | tf_op jit(solution)/shard_map/ppermute | solution.py:608
  69.0 1.2 %collective-permute-start.21 = (f32[8,128]{1,0:T(8,128)S(1)}, f32[8,128]{1,0:T(8,128)S(1)}, u32[]{:S(2)}, u32[]{:S(2)}) collective-permute-start(f32[8,128]{1,0:T(8,128)S(1)} %get-tuple-element.137.mine_ref), channel_id=1, source_target_pairs={{0,1},{1,0},{2,3},{3,2},{4,5},{5,4},{6,7},{7,6},{8,9},{9,8},{10,11... | collective-permute-start | bytes 12296 | tf_op jit(solution)/shard_map/ppermute | solution.py:608
  70.2 4.5 %collective-permute-start.24 = (f32[8,128]{1,0:T(8,128)S(1)}, f32[8,128]{1,0:T(8,128)S(1)}, u32[]{:S(2)}, u32[]{:S(2)}) collective-permute-start(f32[8,128]{1,0:T(8,128)S(1)} %add.66), channel_id=1, source_target_pairs={{0,24},{1,25},{2,26},{3,27},{4,28},{5,29},{6,30},{7,31},{8,16},{9,... | collective-permute-start | bytes 12296 | tf_op jit(solution)/shard_map/ppermute | solution.py:608
  71.9 3.6 %collective-permute-start.23 = (f32[8,128]{1,0:T(8,128)S(1)}, f32[8,128]{1,0:T(8,128)S(1)}, u32[]{:S(2)}, u32[]{:S(2)}) collective-permute-start(f32[8,128]{1,0:T(8,128)S(1)} %add.66), channel_id=1, source_target_pairs={{0,16},{1,17},{2,18},{3,19},{4,20},{5,21},{6,22},{7,23},{8,24},{9,... | collective-permute-start | bytes 12296 | tf_op jit(solution)/shard_map/ppermute | solution.py:608
  73.2 3.6 %collective-permute-start.22 = (f32[8,128]{1,0:T(8,128)S(1)}, f32[8,128]{1,0:T(8,128)S(1)}, u32[]{:S(2)}, u32[]{:S(2)}) collective-permute-start(f32[8,128]{1,0:T(8,128)S(1)} %add.66), channel_id=1, source_target_pairs={{0,8},{1,9},{2,10},{3,11},{4,12},{5,13},{6,14},{7,15},{8,0},{9,1},... | collective-permute-start | bytes 12296 | tf_op jit(solution)/shard_map/ppermute | solution.py:608
  76.8 6.4 %collective-permute-start.27 = (f32[8,128]{1,0:T(8,128)S(1)}, f32[8,128]{1,0:T(8,128)S(1)}, u32[]{:S(2)}, u32[]{:S(2)}) collective-permute-start(f32[8,128]{1,0:T(8,128)S(1)} %add_add_fusion.a_ref), channel_id=1, source_target_pairs={{0,6},{1,7},{2,4},{3,5},{4,2},{5,3},{6,0},{7,1},{8,14},{9,15},{10,... | collective-permute-start | bytes 12296 | tf_op jit(solution)/shard_map/ppermute | solution.py:608
  77.8 5.3 %collective-permute-start.26 = (f32[8,128]{1,0:T(8,128)S(1)}, f32[8,128]{1,0:T(8,128)S(1)}, u32[]{:S(2)}, u32[]{:S(2)}) collective-permute-start(f32[8,128]{1,0:T(8,128)S(1)} %add_add_fusion.a_ref), channel_id=1, source_target_pairs={{0,4},{1,5},{2,6},{3,7},{4,0},{5,1},{6,2},{7,3},{8,12},{9,13},{10,... | collective-permute-start | bytes 12296 | tf_op jit(solution)/shard_map/ppermute | solution.py:608
  78.1 5.1 %collective-permute-start.25 = (f32[8,128]{1,0:T(8,128)S(1)}, f32[8,128]{1,0:T(8,128)S(1)}, u32[]{:S(2)}, u32[]{:S(2)}) collective-permute-start(f32[8,128]{1,0:T(8,128)S(1)} %add_add_fusion.a_ref), channel_id=1, source_target_pairs={{0,2},{1,3},{2,0},{3,1},{4,6},{5,7},{6,4},{7,5},{8,10},{9,11},{10,... | collective-permute-start | bytes 12296 | tf_op jit(solution)/shard_map/ppermute | solution.py:608

commit v7 on v6

--- a/solution.py
+++ b/solution.py
@@ -102,9 +102,7 @@
     return (((12 * (nr - 3) + nc - 3) & (KN - 1)) == lane).astype(F32)
 
 
-def prep_kernel(
-    sizes_ref, table_ref, x_ref, cot_ref, bias_ref, limits_ref, po_ref, pk_ref, xp_ref, xhat_ref, rstd_ref, dy_ref, dysum_ref
-):
+def bias_kernel(sizes_ref, table_ref, bias_ref, limits_ref, po_ref, pk_ref):
     po_ref[...] = select((4 * QN, 4 * 48), own_source)
     pk_ref[...] = select((4 * KN, 10 * 48), key_source)
     row = lax.broadcasted_iota(jnp.int32, (8, 128), 0)
@@ -130,6 +128,13 @@
         rows.append(jnp.where(window, line, MASKED))
     bias_ref[...] = jnp.concatenate(rows, axis=0).T
 
+
+def prep_kernel(x_ref, cot_ref, po_ref, xp_ref, xhat_ref, rstd_ref, dy_ref, dysum_ref, toc_ref, toz_ref):
+    odd = (lax.axis_index("band") & 1) == 1
+    for i in range(12):
+        toc_ref[i] = jnp.where(odd, x_ref[i], x_ref[4 + i])
+        toz_ref[i] = jnp.where(odd, x_ref[4 + i], x_ref[i])
+
     def block(rc, _):
         at = pl.ds(pl.multiple_of(rc * 192, 192), 192)
         xp = dot(po_ref[...], jnp.concatenate([x_ref[4 * i + rc] for i in range(4)], axis=0))
@@ -150,7 +155,7 @@
     odd = (lax.axis_index("band") & 1) == 1
 
     def block(rc, _):
-        rows = [jnp.where(odd, xc_ref[4 + 4 * i + rc], xz_ref[4 + 4 * i + rc]) for i in range(3)]
+        rows = [jnp.where(odd, xc_ref[4 * i + rc], xz_ref[4 * i + rc]) for i in range(3)]
         rows += [x_ref[4 * i + rc] for i in range(4)]
         rows += [jnp.where(odd, xz_ref[4 * i + rc], xc_ref[4 * i + rc]) for i in range(3)]
         xk = dot(pk_ref[...], jnp.concatenate(rows, axis=0))
@@ -466,48 +471,40 @@
     return lax.axis_index("maps") * 8 + lax.axis_index("band")
 
 
-def sorted_slabs(blocks):
+def unpack(blocks, big_qkv, big_out, big_up, big_down, vec, vt, fq, fo, fu, fd):
     me = own_index()
     for index, block in enumerate(blocks):
         core, across = divmod(index, 4)
         for z in range(4):
-            yield me ^ (core | (z << 1) | (across << 3)), block[z].astype(F32)
-
-
-def project_packed(xhat_ref, xk_ref, b0, b1, b2, b3, b4, b5, b6, b7, *rest):
-    outs, big_qkv, vec, fv, fq = rest[:3], *rest[3:]
-    for o, slab in sorted_slabs((b0, b1, b2, b3, b4, b5, b6, b7)):
-        at = pl.ds(pl.multiple_of(o * 8, 8), 8)
-        fq[at, :] = slab[0:8, 0:768]
-        fv[at, :] = slab[0:8, 1280:1408]
+            slab = block[z].astype(F32)
+            o = me ^ (core | (z << 1) | (across << 3))
+            at = pl.ds(pl.multiple_of(o * 8, 8), 8)
+            fq[at, :] = slab[0:8, 0:768]
+            vt[at, :] = slab[0:8, 1280:1408]
+            for b, rows in enumerate((slab[0:8, 1024:1280], slab[8:16, 768:1024], slab[8:16, 1024:1280])):
+                fd[pl.ds(pl.multiple_of(o * 24 + 8 * b, 8), 8), :] = rows
+            fo[at, :] = slab[0:8, 768:1024]
+            fu[at, :] = slab[8:16, 0:768]
     big_qkv[...] = fq[...].astype(BF)
-    vec[...] = fv[...].T[0 : vec.shape[0]]
-    project_kernel(xhat_ref, xk_ref, big_qkv, vec, *outs)
-
-
-def feed_packed(dy_ref, dysum_ref, mixed_ref, xp_ref, vec_ref, b0, b1, b2, b3, b4, b5, b6, b7, *rest):
-    outs, big_down, (big_out, big_up, fo, fu, fd) = rest[:9], rest[9], rest[10:]
-    for o, slab in sorted_slabs((b0, b1, b2, b3, b4, b5, b6, b7)):
-        at = pl.ds(pl.multiple_of(o * 8, 8), 8)
-        for b, rows in enumerate((slab[0:8, 1024:1280], slab[8:16, 768:1024], slab[8:16, 1024:1280])):
-            fd[pl.ds(pl.multiple_of(o * 24 + 8 * b, 8), 8), :] = rows
-        fo[at, :] = slab[0:8, 768:1024]
-        fu[at, :] = slab[8:16, 0:768]
+    vec[...] = vt[...].T[0 : vec.shape[0]]
     big_out[...] = fo[...].astype(BF)
     big_up[...] = fu[...].astype(BF)
     big_down[...] = fd[...].astype(BF)
-    feed_kernel(dy_ref, dysum_ref, mixed_ref, xp_ref, big_out, big_up, big_down, vec_ref, *outs)
-
-
-def frame_slot(me, o):
-    m = me ^ o
-    return (m & 1) * 16 + (m >> 3) * 4 + ((m >> 1) & 3)
-
-
-def grads_kernel(*refs):
-    dq_ref, out_ref, fd, fu, fo, fq, fv, tgrad = refs[16:]
-    early_grads(*refs[:6], fd, fu, fo)
-    late_grads(*refs[6:16], dq_ref, fq, fv, tgrad)
+
+
+def main_kernel(*refs):
+    blocks, (xhat, x, xz, xc, pk, xp, bias, limits, dy, dysum) = refs[:8], refs[8:18]
+    act, dx1, x1, own, rimc, rimz, dq, out_ref, big_qkv, big_down, vec = refs[18:29]
+    q, k, v, mixed, p, dz, a2, da, dmix, sums, zsum, dsl, tacc, dkv = refs[29:43]
+    fq, fv, tgrad, fd, fu, fo, big_out, big_up, vt, xk = refs[43:]
+    halo_kernel(x, xc, xz, pk, xk)
+    unpack(blocks, big_qkv, big_out, big_up, big_down, vec, vt, fq, fo, fu, fd)
+    project_kernel(xhat, xk, big_qkv, vec, q, k, v)
+    attend_kernel(limits, bias, q, k, v, mixed, p)
+    feed_kernel(dy, dysum, mixed, xp, big_out, big_up, big_down, vec, act, dz, a2, da, dx1, x1, dmix, sums, zsum)
+    back_kernel(q, v, p, dmix, own, rimc, rimz, dsl, tacc, dkv)
+    early_grads(act, dy, a2, dz, mixed, da, fd, fu, fo)
+    late_grads(dsl, k, tacc, xhat, xk, dkv, big_qkv, vt, sums, zsum, dq, fq, fv, tgrad)
     table = tgrad[...]
     me = own_index()
     for o in range(32):
@@ -518,13 +515,15 @@
         out_ref[frame_slot(me, o)] = both.astype(BF)
 
 
-def adam_kernel(*refs):
-    w, first, second = refs[4:10], refs[10:16], refs[16:22]
-    outs = refs[22:]
+def frame_slot(me, o):
+    m = me ^ o
+    return (m & 1) * 16 + (m >> 3) * 4 + ((m >> 1) & 3)
+
+
+def shard_grads(refs, vrows):
     total = refs[0][...] + sum(ref[...].astype(F32) for ref in refs[1:4])
     early, late = total[:, :EARLY], total[:, EARLY:]
-    vrows = w[4].shape[1]
-    grads = [
+    return [
         jnp.concatenate([late[0:8], late[8:16, 0:256]], axis=1),
         jnp.concatenate([early[0:8, 768:896], early[8:16, 768:896]], axis=1),
         early[8:16, 0:768],
@@ -538,22 +537,36 @@
             preferred_element_type=F32,
         ),
     ]
+
+
+def update_kernel(*refs):
+    w, first, second, outs = refs[4:10], refs[10:16], refs[16:22], refs[22:]
+    vrows = w[4].shape[1]
+    grads = shard_grads(refs, vrows)
     row = lax.broadcasted_iota(jnp.int32, (8, 128), 0)
     lane = lax.broadcasted_iota(jnp.int32, (8, 128), 1)
     norms = jnp.zeros((8, 128), F32)
     for i in range(6):
-        new_first, new_second, update = adam_parts(w[i][...], grads[i], first[i][...], second[i][...])
-        outs[3 * i][...] = new_first
-        outs[3 * i + 1][...] = new_second
-        outs[3 * i + 2][...] = update
+        update = adam_parts(w[i][...], grads[i], first[i][...], second[i][...])[2]
+        outs[i][...] = update
         for line, v in ((0, w[i][...]), (1, update)):
+            sums = jnp.sum(v * v, axis=0, keepdims=True)
             if i == 4:
-                sums = pltpu.roll(widen(jnp.sum(v * v, axis=0, keepdims=True)), 4, 1)
+                sums = pltpu.roll(widen(sums), 4, 1)
                 norms = jnp.where((row == line) & (lane >= 4) & (lane < 4 + vrows), sums, norms)
             else:
                 at = i if i < 4 else 4 + vrows
-                norms = jnp.where((row == line) & (lane == at), jnp.sum(v * v), norms)
-    outs[18][...] = norms
+                norms = jnp.where((row == line) & (lane == at), jnp.sum(sums, axis=1, keepdims=True), norms)
+    outs[6][...] = norms
+
+
+def moments_kernel(*refs):
+    first, second, outs = refs[4:10], refs[10:16], refs[16:]
+    grads = shard_grads(refs, first[4].shape[1])
+    for i in range(6):
+        new_first, new_second, _ = adam_parts(0.0, grads[i], first[i][...], second[i][...])
+        outs[2 * i][...] = new_first
+        outs[2 * i + 1][...] = new_second
 
 
 def step_kernel(mine_ref, a_ref, b_ref, c_ref, d_ref, *refs):
@@ -651,17 +664,19 @@
     )
 
 
+def bias_outputs():
+    return (sds((KN, 384), F32), sds((8, 128), jnp.int32), sds((4 * QN, 4 * 48)), sds((4 * KN, 10 * 48)))
+
+
 def prep_outputs():
     return (
-        sds((KN, 384), F32),
-        sds((8, 128), jnp.int32),
-        sds((4 * QN, 4 * 48)),
-        sds((4 * KN, 10 * 48)),
         sds((768, 256), F32),
         sds((768, 256), F32),
         sds((768, 128), F32),
         sds((768, 256)),
         sds((1, 256), F32),
+        sds((12, 48, 256)),
+        sds((12, 48, 256)),
     )
 
 
@@ -721,82 +736,67 @@
     turn = lambda arrays: tuple(a.T if i == 4 else a for i, a in enumerate(arrays))
     weights, firsts, seconds = turn(weights), turn(firsts), turn(seconds)
     slab = pack(*weights[:5])
-    column = call(
-        stack_kernel,
-        sds((4, 16, EARLY + LATE)),
-        [],
-        slab,
-        *[swap(slab, d << 1, count) for d in (1, 2, 3)],
-        vmem=4,
-    )
+    slab, sizes = lax.optimization_barrier((slab, map_sizes))
+    slabs = [slab] + [swap(slab, d << 1, count) for d in (1, 2, 3)]
+    bias, limits, po, pk = call(bias_kernel, bias_outputs(), [], sizes, weights[5], smem=1, flops=10**9, vmem=4)
+    *slabs, bias = lax.optimization_barrier((*slabs, bias))
+    column = call(stack_kernel, sds((4, 16, EARLY + LATE)), [], *slabs, vmem=4)
     column, x = lax.optimization_barrier((column, tokens_in))
     blocks = [column] + [swap(column, d << 3, count) for d in (1, 2, 3)]
-    x_core, x_next = beside((x, x), 8)
-    bias, limits, po, pk, xp, xhat, rstd, dy, dysum = call(
-        prep_kernel, prep_outputs(), [], map_sizes, weights[5], x, cotangent, smem=1, flops=2 * 10**9, vmem=8
-    )
-    *far, pk = lax.optimization_barrier((*blocks[1:], pk))
-    xk = call(halo_kernel, sds((CLS * KN, 256), F32), [], x, x_core, x_next, pk, flops=10**9, vmem=8)
+    xp, xhat, rstd, dy, dysum, *edges = call(prep_kernel, prep_outputs(), [], x, cotangent, po, flops=2 * 10**9, vmem=8)
+    x_core, x_next = beside(edges, 8)
+    *far, xp = lax.optimization_barrier((*blocks[1:], xp))
     blocks = [blocks[0]] + far + [swap(block, 1, count) for block in [blocks[0]] + far]
-    queries, keys, values, big_qkv, vec, vt = call(
-        project_packed,
-        project_outputs() + (sds((256, 768)), sds((vrows, 256), F32), sds((256, 128), F32)),
-        [pltpu.VMEM((256, 768), F32)],
-        xhat, xk, *blocks,
-        flops=10**9, vmem=8,
-    )
-    mixed, probs = call(
-        attend_kernel, attend_outputs(), [], limits, bias, queries, keys, values, flops=3 * 10**9, vmem=8
-    )
-    act, dz, a2, da, dx1, x1, dmix, sums, zsum, big_down = call(
-        feed_packed,
-        feed_outputs() + (sds((768, 256)),),
-        [pltpu.VMEM((256, 256), BF), pltpu.VMEM((256, 768), BF)]
-        + [pltpu.VMEM(m, F32) for m in ((256, 256), (256, 768), (768, 256))],
-        dy, dysum, mixed, xp, vec, *blocks,
-        flops=4 * 10**9, vmem=8,
-    )
-    own, rim_c, rim_z, dsl, tacc, dkv = call(
-        back_kernel, back_outputs(), [], queries, values, probs, dmix, flops=4 * 10**9, vmem=8
-    )
-    dq, grads = call(
-        grads_kernel,
-        (sds((768, 256)), sds((count, 16, EARLY + LATE))),
-        [pltpu.VMEM(m, F32) for m in ((768, 256), (256, 768), (256, 256))]
-        + [pltpu.VMEM(o.shape, o.dtype) for o in late_outputs()[1:]],
-        act, dy, a2, dz, mixed, da, dsl, keys, tacc, xhat, xk, dkv, big_qkv, vt, sums, zsum,
-        flops=5 * 10**9, vmem=8,
+    act_s, dz_s, a2_s, da_s, dx1_s, x1_s, dmix_s, sums_s, zsum_s = feed_outputs()
+    own_s, rimc_s, rimz_s, dsl_s, tacc_s, dkv_s = back_outputs()
+    dq_s, fq_s, fv_s, tgrad_s = late_outputs()
+    act, dx1, x1, own, rim_c, rim_z, dq, grads, big_qkv, big_down, vec = call(
+        main_kernel,
+        (act_s, dx1_s, x1_s, own_s, rimc_s, rimz_s, dq_s)
+        + (sds((count, 16, EARLY + LATE)), sds((256, 768)), sds((768, 256)), sds((vrows, 256), F32)),
+        [
+            pltpu.VMEM(o.shape, o.dtype)
+            for o in project_outputs()
+            + attend_outputs()
+            + (dz_s, a2_s, da_s, dmix_s, sums_s, zsum_s, dsl_s, tacc_s, dkv_s, fq_s, fv_s, tgrad_s)
+            + (sds((768, 256), F32), sds((256, 768), F32), sds((256, 256), F32))
+            + (sds((256, 256)), sds((256, 768)), sds((256, 128), F32), sds((CLS * KN, 256), F32))
+        ],
+        *blocks, xhat, x, x_next, x_core, pk, xp, bias, limits, dy, dysum,
+        flops=15 * 10**9, vmem=24,
     )
     layer_out = call(output_kernel, sds((16, 48, 256)), [], x1, act, big_down, vec, po, flops=10**9, vmem=8)
     got_c, got_z = beside((rim_c, rim_z), 8)
+    grads = add_stage(add_stage(grads, 0, 1, count), 3, 2, count)
+    grads, own = lax.optimization_barrier((grads, own))
     tokens_grad = call(
         input_kernel, sds((16, 48, 256)), [], own, got_c, got_z, dq, dx1, xhat, rstd, big_qkv, vec, po,
         flops=10**9, vmem=8,
     )
-    grads = add_stage(add_stage(grads, 0, 1, count), 3, 2, count)
     low = grads.astype(BF)
     parts = [grads[0]] + [swap(low[d], d << 1, count) for d in (1, 2, 3)]
-    parts[0], tokens_grad = lax.optimization_barrier((parts[0], tokens_grad))
+    parts[0], tokens_grad, layer_out = lax.optimization_barrier((parts[0], tokens_grad, layer_out))
 
     shapes = [sds(w.shape, F32) for w in weights]
+    *updates, mine = call(
+        update_kernel, tuple(shapes) + (sds((8, 128), F32),), [], *parts, *weights, *firsts, *seconds, vmem=4
+    )
     moments = call(
-        adam_kernel,
-        tuple(shape for shape in shapes for _ in range(3)) + (sds((8, 128), F32),),
-        [],
-        *parts, *weights, *firsts, *seconds,
-    )
-    mine = moments[18]
+        moments_kernel, tuple(shape for shape in shapes for _ in range(2)), [], *parts, *firsts, *seconds, vmem=4
+    )
     squares = mine + swap(mine, 1, count)
     squares = squares + swap(squares, 8, count) + swap(squares, 16, count) + swap(squares, 24, count)
+    last = [swap(squares, d << 1, count) for d in (1, 2, 3)]
+    squares, *moments = lax.optimization_barrier((squares, *moments))
     news = call(
         step_kernel,
         tuple(shapes) + (sds((1, 16), F32),) * 2,
         [],
-        mine, squares, *[swap(squares, d << 1, count) for d in (1, 2, 3)], *weights, *moments[2:18:3],
+        mine, squares, *last, *weights, *updates, vmem=4,
     )
     results = [layer_out, tokens_grad]
     for i in range(6):
-        three = (moments[3 * i], moments[3 * i + 1], news[i])
+        three = (moments[2 * i], moments[2 * i + 1], news[i])
         results += [a.T for a in three] if i == 4 else three
     return tuple(results) + (news[6].reshape(16), news[7].reshape(16))
 
@@ -848,8 +848,6 @@
     masks = np.array(frame_masks(groups))
     inverse = np.argsort(masks)
     me = lax.axis_index(AXES)
-    x_core, x_next = beside((tokens_in, tokens_in), band)
-
     def pack(qkv, out, upw, dnw, vec):
         dn = dnw.reshape(3, rows, 256).transpose(1, 0, 2).reshape(rows, 768)
         vt = jnp.pad(vec.T, ((0, 0), (0, 128 - vrows)))
@@ -868,9 +866,9 @@
     vt = whole[:, 2560:].astype(F32)
     vec = vt[:, :vrows].T
 
-    bias, limits, po, pk, xp, xhat, rstd, dy, dysum = call(
-        prep_kernel, prep_outputs(), [], map_sizes, pos_table, tokens_in, cotangent, smem=1, flops=2 * 10**9
-    )
+    bias, limits, po, pk = call(bias_kernel, bias_outputs(), [], map_sizes, pos_table, smem=1, flops=10**9)
+    xp, xhat, rstd, dy, dysum, *edges = call(prep_kernel, prep_outputs(), [], tokens_in, cotangent, po, flops=2 * 10**9)
+    x_core, x_next = beside(edges, band)
     xk = call(halo_kernel, sds((CLS * KN, 256), F32), [], tokens_in, x_core, x_next, pk, flops=10**9)
     queries, keys, values = call(project_kernel, project_outputs(), [], xhat, xk, big_qkv, vec, flops=10**9)
     mixed, probs = call(attend_kernel, attend_outputs(), [], limits, bias, queries, keys, values, flops=3 * 10**9)

time: 84.3 us -> 80.2 us (0.951)
  starting transfers between devices: 29.5 us -> 27.5 us
  local copies, waits for them, and re-layouts: 4.29 us -> 2.32 us
  Pallas kernels: 24.6 us -> 23.7 us
  waiting for transfers between devices: 23.3 us -> 24.2 us
    unnamed x44, local copies, waits for them, and re-layouts: 3.43 us -> 1.46 us
    ppermute x2, starting transfers between devices: 1.86 us -> 0.01 us  [beside(): lax.ppermute(block[0], 'band', [(b, b ^ 1) for b in range(band)])]
    ppermute x24, waiting for transfers between devices: 23.3 us -> 24.2 us  [swap(): return lax.ppermute(block, AXES, [(k, k ^ mask) for k in range(count)])]
    pallas_call x12 -> x9, Pallas kernels: 24.6 us -> 23.7 us  [call(): pl.pallas_call(kernel, out_shape=out_shape, in_specs=specs, out_specs=jax...]
  transfers between devices with their start and end apart: 28 -> 28, of which waited for: 13 -> 18; matrix products, arithmetic and copies ran while one was open for 0% -> 0% of each run, Pallas kernels for 9% -> 9%
where the time goes in v7:
time: 80.2 us; the launch traced here: 79.9 us
  starting transfers between devices  27.5 us (34%)
  waiting for transfers between devices  24.2 us (30%)
  Pallas kernels  23.7 us (30%)
  local copies, waits for them, and re-layouts  2.32 us (3%)
  other arithmetic  1.12 us (1%)
  between operations  1.09 us (1%)
    ppermute x24, starting transfers between devices, swap(): return lax.ppermute(block, AXES, [(k, k ^ mask) for k in range(count)])  26.1 us
    ppermute x24, waiting for transfers between devices, swap(): return lax.ppermute(block, AXES, [(k, k ^ mask) for k in range(count)])  24.2 us
    pallas_call x9, Pallas kernels, call(): pl.pallas_call(kernel, out_shape=out_shape, in_specs=specs, out_specs=jax...  23.7 us
  transfers between devices with their start and end apart: 28, of which 18 were waited for; matrix products, arithmetic and copies ran while one was open for 0% of the time, Pallas kernels for 9%

profile of v7, /device:TPU:0, one launch (start us, length us, event | category | flops | bytes accessed | tf_op | source)
XLA Modules:
  0.0 79.9 jit_solution(10836284375076165189)
XLA Ops:
  0.7 0.7 fusion.4
  1.4 0.8 add_convert_fusion.refs_0_
  2.2 5.1 %collective-permute-start.2 = (bf16[16,1408]{1,0:T(8,128)(2,1)S(1)}, bf16[16,1408]{1,0:T(8,128)(2,1)S(1)}, u32[]{:S(2)}, u32[]{:S(2)}) collective-permute-start(bf16[16,1408]{1,0:T(8,128)(2,1)S(1)} %add_convert_fusion.refs_0_), channel_id=1, source_target_pairs={{0,6},{1,7},{2,4},{3,5},{4,2},{5,3},{6,0},{7,1},{8,14},{9,15},{10,... | collective-permute-start | bytes 135176 | tf_op jit(solution)/shard_map/ppermute | solution.py:621
  7.3 0.6 collective-permute-start
  7.9 0.7 copy-done.17
  8.6 0.7 copy-done.21
  9.3 1.3 %shard_map.372 = (f32[128,384]{1,0:T(8,128)S(1)}, s32[8,128]{1,0:T(8,128)S(1)}, bf16[192,192]{1,0:T(8,128)(2,1)S(1)}, bf16[512,480]{1,0:T(8,128)(2,1)S(1)}) custom-call(s32[1,2]{1,0:T(1,128)S(1)} %copy-done.21, f32[8,49]{1,0:T(8,128)S(1)} %copy-done.17), custom_call_target="tpu_custom_call" | custom-call | flops 1000000000 | bytes 1000000 | tf_op jit(solution)/shard_map/pallas_call | solution.py:598
  10.6 1.6 %collective-permute-done.1.refs_2_ = bf16[16,1408]{1,0:T(8,128)(2,1)S(1)} collective-permute-done((bf16[16,1408]{1,0:T(8,128)(2,1)S(1)}, bf16[16,1408]{1,0:T(8,128)(2,1)S(1)}, u32[]{:S(2)}, u32[]{:S(2)}) %collective-permute-start.1) | collective-permute-done | bytes 45088 | tf_op jit(solution)/shard_map/ppermute | solution.py:621
  12.2 0.1 collective-permute-start.6
  12.3 2.5 %collective-permute-start.5 = (bf16[4,16,1408]{2,1,0:T(8,128)(2,1)S(1)}, bf16[4,16,1408]{2,1,0:T(8,128)(2,1)S(1)}, u32[]{:S(2)}, u32[]{:S(2)}) collective-permute-start(bf16[4,16,1408]{2,1,0:T(8,128)(2,1)S(1)} %shard_map.373.refs_0_), channel_id=1, source_target_pairs={{0,24},{1,25},{2,26},{3,27},{4,28},{5,29},{6,30},{7,31},{8,16},{9,... | collective-permute-start | bytes 540680 | tf_op jit(solution)/shard_map/ppermute | solution.py:621
  14.8 0.5 collective-permute-start.4
  15.3 0.5 collective-permute-start.3
  15.9 0.6 shard_map.374
  16.4 0.7 collective-permute-start.10
  17.1 3.5 %collective-permute-done.5.refs_3_ = bf16[4,16,1408]{2,1,0:T(8,128)(2,1)S(1)} collective-permute-done((bf16[4,16,1408]{2,1,0:T(8,128)(2,1)S(1)}, bf16[4,16,1408]{2,1,0:T(8,128)(2,1)S(1)}, u32[]{:S(2)}, u32[]{:S(2)}) %collective-permute-start.5) | collective-permute-done | bytes 180256 | tf_op jit(solution)/shard_map/ppermute | solution.py:621
  20.7 3.4 %collective-permute-done.4.refs_2_ = bf16[4,16,1408]{2,1,0:T(8,128)(2,1)S(1)} collective-permute-done((bf16[4,16,1408]{2,1,0:T(8,128)(2,1)S(1)}, bf16[4,16,1408]{2,1,0:T(8,128)(2,1)S(1)}, u32[]{:S(2)}, u32[]{:S(2)}) %collective-permute-start.4) | collective-permute-done | bytes 180256 | tf_op jit(solution)/shard_map/ppermute | solution.py:621
  24.1 0.1 collective-permute-done.3.refs_1_
  24.2 0.5 collective-permute-start.8
  24.7 0.9 %collective-permute-done.7.refs_5_ = bf16[4,16,1408]{2,1,0:T(8,128)(2,1)S(1)} collective-permute-done((bf16[4,16,1408]{2,1,0:T(8,128)(2,1)S(1)}, bf16[4,16,1408]{2,1,0:T(8,128)(2,1)S(1)}, u32[]{:S(2)}, u32[]{:S(2)}) %collective-permute-start.7) | collective-permute-done | bytes 180256 | tf_op jit(solution)/shard_map/ppermute | solution.py:621
  25.6 0.3 collective-permute-done.8.refs_6_
  25.8 0.3 collective-permute-done.9.refs_7_
  26.1 15.4 %shard_map.375 = (bf16[768,768]{1,0:T(8,128)(2,1)S(1)}, f32[768,256]{1,0:T(8,128)S(1)}, f32[768,256]{1,0:T(8,128)S(1)}, f32[768,512]{1,0:T(8,128)S(1)}, bf16[640...) custom-call(bf16[4,16,1408]{2,1,0:T(8,128)(2,1)S(1)} %shard_map.373., ...), custom_call_target="tpu_custom_call" | custom-call | flops 15000000512 | bytes 1000000 | tf_op jit(solution)/shard_map/pallas_call | solution.py:598
  41.5 0.1 slice.40
  41.5 0.3 collective-permute-start.12
  41.8 2.0 %collective-permute-done.12 = bf16[16,16,1408]{2,1,0:T(8,128)(2,1)S(1)} collective-permute-done((bf16[16,16,1408]{2,1,0:T(8,128)(2,1)S(1)}, bf16[16,16,1408]{2,1,0:T(8,128)(2,1)S(1)}, u32[]{:S(2)}, u32[]{:S(2)}) %collective-permute-start.12) | collective-permute-done | bytes 720928 | tf_op jit(solution)/shard_map/ppermute | solution.py:621
  43.8 0.2 fusion.2
  44.0 1.6 %collective-permute-start.13 = (bf16[4,16,1408]{2,1,0:T(8,128)(2,1)S(1)}, bf16[4,16,1408]{2,1,0:T(8,128)(2,1)S(1)}, u32[]{:S(2)}, u32[]{:S(2)}) collective-permute-start(bf16[4,16,1408]{2,1,0:T(8,128)(2,1)S(1)} %get-tuple-element.184), channel_id=1, source_target_pairs={{0,8},{1,9},{2,10},{3,11},{4,12},{5,13},{6,14},{7,15},{8,0},{9,1},... | collective-permute-start | bytes 540680 | tf_op jit(solution)/shard_map/ppermute | solution.py:621
  45.6 1.4 %collective-permute-start.15 = (bf16[4,16,1408]{2,1,0:T(8,128)(2,1)S(1)}, bf16[4,16,1408]{2,1,0:T(8,128)(2,1)S(1)}, u32[]{:S(2)}, u32[]{:S(2)}) collective-permute-start(bf16[4,16,1408]{2,1,0:T(8,128)(2,1)S(1)} %get-tuple-element.185), channel_id=1, source_target_pairs={{0,24},{1,25},{2,26},{3,27},{4,28},{5,29},{6,30},{7,31},{8,16},{9,... | collective-permute-start | bytes 540680 | tf_op jit(solution)/shard_map/ppermute | solution.py:621
  47.0 0.6 collective-permute-start.14
  47.6 0.7 collective-permute-start.17
  48.3 2.0 %shard_map.377 = bf16[16,48,256]{2,1,0:T(8,128)(2,1)} custom-call(f32[768,256]{1,0:T(8,128)S(1)} %get-tuple-element.136.x1_ref, bf16[768,768]{1,0:T(8,128)(2,1)S(1)} %get-tuple-element.137.act_ref, bf16[768,256]{1,0:T(8,128)(2,1)S(1)} %get-tuple-element.138.wd_ref, f32[11,256]{1,0:T(8,128)S(1)} %get-tuple-element.135.vec_ref, ...), custom_call_target="tpu_custom_call" | custom-call | flops 1000000000 | bytes 1000000 | tf_op jit(solution)/shard_map/pallas_call | solution.py:598
  50.3 1.2 %collective-permute-done.13 = bf16[4,16,1408]{2,1,0:T(8,128)(2,1)S(1)} collective-permute-done((bf16[4,16,1408]{2,1,0:T(8,128)(2,1)S(1)}, bf16[4,16,1408]{2,1,0:T(8,128)(2,1)S(1)}, u32[]{:S(2)}, u32[]{:S(2)}) %collective-permute-start.13) | collective-permute-done | bytes 180256 | tf_op jit(solution)/shard_map/ppermute | solution.py:621
  51.5 4.1 %collective-permute-done.15 = bf16[4,16,1408]{2,1,0:T(8,128)(2,1)S(1)} collective-permute-done((bf16[4,16,1408]{2,1,0:T(8,128)(2,1)S(1)}, bf16[4,16,1408]{2,1,0:T(8,128)(2,1)S(1)}, u32[]{:S(2)}, u32[]{:S(2)}) %collective-permute-start.15) | collective-permute-done | bytes 180256 | tf_op jit(solution)/shard_map/ppermute | solution.py:621
  55.6 1.4 %collective-permute-done.14 = bf16[4,16,1408]{2,1,0:T(8,128)(2,1)S(1)} collective-permute-done((bf16[4,16,1408]{2,1,0:T(8,128)(2,1)S(1)}, bf16[4,16,1408]{2,1,0:T(8,128)(2,1)S(1)}, u32[]{:S(2)}, u32[]{:S(2)}) %collective-permute-start.14) | collective-permute-done | bytes 180256 | tf_op jit(solution)/shard_map/ppermute | solution.py:621
  57.0 0.1 fusion.1
  57.1 2.2 %collective-permute-start.20 = (bf16[16,1408]{1,0:T(8,128)(2,1)S(1)}, bf16[16,1408]{1,0:T(8,128)(2,1)S(1)}, u32[]{:S(2)}, u32[]{:S(2)}) collective-permute-start(bf16[16,1408]{1,0:T(8,128)(2,1)S(1)} %get-tuple-element.187), channel_id=1, source_target_pairs={{0,6},{1,7},{2,4},{3,5},{4,2},{5,3},{6,0},{7,1},{8,14},{9,15},{10,... | collective-permute-start | bytes 135176 | tf_op jit(solution)/shard_map/ppermute | solution.py:621
  59.3 2.2 %collective-permute-start.18 = (bf16[16,1408]{1,0:T(8,128)(2,1)S(1)}, bf16[16,1408]{1,0:T(8,128)(2,1)S(1)}, u32[]{:S(2)}, u32[]{:S(2)}) collective-permute-start(bf16[16,1408]{1,0:T(8,128)(2,1)S(1)} %get-tuple-element.189), channel_id=1, source_target_pairs={{0,2},{1,3},{2,0},{3,1},{4,6},{5,7},{6,4},{7,5},{8,10},{9,11},{10,... | collective-permute-start | bytes 135176 | tf_op jit(solution)/shard_map/ppermute | solution.py:621
  61.6 0.0 copy-start
  61.6 0.0 copy-start.1
  61.6 0.0 copy-start.3
  61.7 0.0 copy-start.4
  61.7 0.0 copy-start.7
  61.7 0.0 copy-start.8
  61.7 0.0 copy-start.10
  61.7 0.0 copy-start.11
  61.8 0.0 copy-start.14
  61.8 0.0 copy-start.15
  61.8 2.7 %shard_map.376 = bf16[16,48,256]{2,1,0:T(8,128)(2,1)} custom-call(f32[768,512]{1,0:T(8,128)S(1)} %get-tuple-element.128.own_ref, bf16[640,512]{1,0:T(8,128)(2,1)S(1)} %collective-permute-done.16.gotc_ref, bf16[640,512]{1,0:T(8,128)(2,1)S(1)} %collective-permute-done.17.gotz_ref, bf16[768,256]{1,0:T(8,128)(2,1)S(1)} %get-tuple-element.131.dq_ref, ...), custom_call_target="tpu_custom_call" | custom-call | flops 1000000000 | bytes 1000000 | tf_op jit(solution)/shard_map/pallas_call | solution.py:598
  64.5 0.2 collective-permute-done.19.refs_2_
  64.8 0.3 shard_map.378
  65.1 0.0 collective-permute-start.21
  65.2 1.2 %collective-permute-done.21 = f32[8,128]{1,0:T(8,128)S(1)} collective-permute-done((f32[8,128]{1,0:T(8,128)S(1)}, f32[8,128]{1,0:T(8,128)S(1)}, u32[]{:S(2)}, u32[]{:S(2)}) %collective-permute-start.21) | collective-permute-done | bytes 4128 | tf_op jit(solution)/shard_map/ppermute | solution.py:621
  66.3 1.5 %collective-permute-start.24 = (f32[8,128]{1,0:T(8,128)S(1)}, f32[8,128]{1,0:T(8,128)S(1)}, u32[]{:S(2)}, u32[]{:S(2)}) collective-permute-start(f32[8,128]{1,0:T(8,128)S(1)} %add.66), channel_id=1, source_target_pairs={{0,24},{1,25},{2,26},{3,27},{4,28},{5,29},{6,30},{7,31},{8,16},{9,... | collective-permute-start | bytes 12296 | tf_op jit(solution)/shard_map/ppermute | solution.py:621
  67.8 1.3 %collective-permute-start.23 = (f32[8,128]{1,0:T(8,128)S(1)}, f32[8,128]{1,0:T(8,128)S(1)}, u32[]{:S(2)}, u32[]{:S(2)}) collective-permute-start(f32[8,128]{1,0:T(8,128)S(1)} %add.66), channel_id=1, source_target_pairs={{0,16},{1,17},{2,18},{3,19},{4,20},{5,21},{6,22},{7,23},{8,24},{9,... | collective-permute-start | bytes 12296 | tf_op jit(solution)/shard_map/ppermute | solution.py:621
  69.1 0.7 collective-permute-start.22
  69.8 1.0 %collective-permute-done.24 = f32[8,128]{1,0:T(8,128)S(1)} collective-permute-done((f32[8,128]{1,0:T(8,128)S(1)}, f32[8,128]{1,0:T(8,128)S(1)}, u32[]{:S(2)}, u32[]{:S(2)}) %collective-permute-start.24) | collective-permute-done | bytes 4128 | tf_op jit(solution)/shard_map/ppermute | solution.py:621
  70.8 0.6 collective-permute-done.23
  71.5 1.3 %collective-permute-done.22 = f32[8,128]{1,0:T(8,128)S(1)} collective-permute-done((f32[8,128]{1,0:T(8,128)S(1)}, f32[8,128]{1,0:T(8,128)S(1)}, u32[]{:S(2)}, u32[]{:S(2)}) %collective-permute-start.22) | collective-permute-done | bytes 4128 | tf_op jit(solution)/shard_map/ppermute | solution.py:621
  72.8 1.9 %collective-permute-start.27 = (f32[8,128]{1,0:T(8,128)S(1)}, f32[8,128]{1,0:T(8,128)S(1)}, u32[]{:S(2)}, u32[]{:S(2)}) collective-permute-start(f32[8,128]{1,0:T(8,128)S(1)} %add_add_fusion.a_ref), channel_id=1, source_target_pairs={{0,6},{1,7},{2,4},{3,5},{4,2},{5,3},{6,0},{7,1},{8,14},{9,15},{10,... | collective-permute-start | bytes 12296 | tf_op jit(solution)/shard_map/ppermute | solution.py:621
  74.7 2.5 %collective-permute-start.25 = (f32[8,128]{1,0:T(8,128)S(1)}, f32[8,128]{1,0:T(8,128)S(1)}, u32[]{:S(2)}, u32[]{:S(2)}) collective-permute-start(f32[8,128]{1,0:T(8,128)S(1)} %add_add_fusion.a_ref), channel_id=1, source_target_pairs={{0,2},{1,3},{2,0},{3,1},{4,6},{5,7},{6,4},{7,5},{8,10},{9,11},{10,... | collective-permute-start | bytes 12296 | tf_op jit(solution)/shard_map/ppermute | solution.py:621
  77.1 0.8 shard_map.379
  77.9 0.2 collective-permute-done.27.d_ref
  78.2 1.0 %collective-permute-done.26.c_ref = f32[8,128]{1,0:T(8,128)S(1)} collective-permute-done((f32[8,128]{1,0:T(8,128)S(1)}, f32[8,128]{1,0:T(8,128)S(1)}, u32[]{:S(2)}, u32[]{:S(2)}) %collective-permute-start.26) | collective-permute-done | bytes 4128 | tf_op jit(solution)/shard_map/ppermute | solution.py:621
  79.2 0.8 shard_map.380
  (56 shorter events, 0.2 us)
Async XLA Ops:
  2.2 8.4 %collective-permute-start.2 = (bf16[16,1408]{1,0:T(8,128)(2,1)S(1)}, bf16[16,1408]{1,0:T(8,128)(2,1)S(1)}, u32[]{:S(2)}, u32[]{:S(2)}) collective-permute-start(bf16[16,1408]{1,0:T(8,128)(2,1)S(1)} %add_convert_fusion.refs_0_), channel_id=1, source_target_pairs={{0,6},{1,7},{2,4},{3,5},{4,2},{5,3},{6,0},{7,1},{8,14},{9,15},{10,... | collective-permute-start | bytes 135176 | tf_op jit(solution)/shard_map/ppermute | solution.py:621
  7.3 4.9 %collective-permute-start.1 = (bf16[16,1408]{1,0:T(8,128)(2,1)S(1)}, bf16[16,1408]{1,0:T(8,128)(2,1)S(1)}, u32[]{:S(2)}, u32[]{:S(2)}) collective-permute-start(bf16[16,1408]{1,0:T(8,128)(2,1)S(1)} %add_convert_fusion.refs_0_), channel_id=1, source_target_pairs={{0,4},{1,5},{2,6},{3,7},{4,0},{5,1},{6,2},{7,3},{8,12},{9,13},{10,... | collective-permute-start | bytes 135176 | tf_op jit(solution)/shard_map/ppermute | solution.py:621
  7.3 4.9 %collective-permute-start = (bf16[16,1408]{1,0:T(8,128)(2,1)S(1)}, bf16[16,1408]{1,0:T(8,128)(2,1)S(1)}, u32[]{:S(2)}, u32[]{:S(2)}) collective-permute-start(bf16[16,1408]{1,0:T(8,128)(2,1)S(1)} %add_convert_fusion.refs_0_), channel_id=1, source_target_pairs={{0,2},{1,3},{2,0},{3,1},{4,6},{5,7},{6,4},{7,5},{8,10},{9,11},{10,... | collective-permute-start | bytes 135176 | tf_op jit(solution)/shard_map/ppermute | solution.py:621
  7.9 0.7 copy-start.17
  8.6 0.7 copy-start.21
  9.3 6.6 %copy-start.19 = (bf16[16,48,256]{2,1,0:T(8,128)(2,1)S(1)}, bf16[16,48,256]{2,1,0:T(8,128)(2,1)}, u32[]{:S(2)}) copy-start(bf16[16,48,256]{2,1,0:T(8,128)(2,1)} %cot_ref.1) | copy-start | bytes 1179652
  9.3 6.6 %copy-start.20 = (bf16[16,48,256]{2,1,0:T(8,128)(2,1)S(1)}, bf16[16,48,256]{2,1,0:T(8,128)(2,1)}, u32[]{:S(2)}) copy-start(bf16[16,48,256]{2,1,0:T(8,128)(2,1)} %refs_9_.2) | copy-start | bytes 1179652
  12.2 12.4 %collective-permute-start.6 = (bf16[4,16,1408]{2,1,0:T(8,128)(2,1)S(1)}, bf16[4,16,1408]{2,1,0:T(8,128)(2,1)S(1)}, u32[]{:S(2)}, u32[]{:S(2)}) collective-permute-start(bf16[4,16,1408]{2,1,0:T(8,128)(2,1)S(1)} %shard_map.373.refs_0_), channel_id=1, source_target_pairs={{0,1},{1,0},{2,3},{3,2},{4,5},{5,4},{6,7},{7,6},{8,9},{9,8},{10,11... | collective-permute-start | bytes 540680 | tf_op jit(solution)/shard_map/ppermute | solution.py:621
  12.3 8.4 %collective-permute-start.5 = (bf16[4,16,1408]{2,1,0:T(8,128)(2,1)S(1)}, bf16[4,16,1408]{2,1,0:T(8,128)(2,1)S(1)}, u32[]{:S(2)}, u32[]{:S(2)}) collective-permute-start(bf16[4,16,1408]{2,1,0:T(8,128)(2,1)S(1)} %shard_map.373.refs_0_), channel_id=1, source_target_pairs={{0,24},{1,25},{2,26},{3,27},{4,28},{5,29},{6,30},{7,31},{8,16},{9,... | collective-permute-start | bytes 540680 | tf_op jit(solution)/shard_map/ppermute | solution.py:621
  14.8 9.2 %collective-permute-start.4 = (bf16[4,16,1408]{2,1,0:T(8,128)(2,1)S(1)}, bf16[4,16,1408]{2,1,0:T(8,128)(2,1)S(1)}, u32[]{:S(2)}, u32[]{:S(2)}) collective-permute-start(bf16[4,16,1408]{2,1,0:T(8,128)(2,1)S(1)} %shard_map.373.refs_0_), channel_id=1, source_target_pairs={{0,16},{1,17},{2,18},{3,19},{4,20},{5,21},{6,22},{7,23},{8,24},{9,... | collective-permute-start | bytes 540680 | tf_op jit(solution)/shard_map/ppermute | solution.py:621
  15.3 8.8 %collective-permute-start.3 = (bf16[4,16,1408]{2,1,0:T(8,128)(2,1)S(1)}, bf16[4,16,1408]{2,1,0:T(8,128)(2,1)S(1)}, u32[]{:S(2)}, u32[]{:S(2)}) collective-permute-start(bf16[4,16,1408]{2,1,0:T(8,128)(2,1)S(1)} %shard_map.373.refs_0_), channel_id=1, source_target_pairs={{0,8},{1,9},{2,10},{3,11},{4,12},{5,13},{6,14},{7,15},{8,0},{9,1},... | collective-permute-start | bytes 540680 | tf_op jit(solution)/shard_map/ppermute | solution.py:621
  16.4 8.2 %collective-permute-start.10 = (bf16[12,48,256]{2,1,0:T(8,128)(2,1)S(1)}, bf16[12,48,256]{2,1,0:T(8,128)(2,1)S(1)}, u32[]{:S(2)}, u32[]{:S(2)}) collective-permute-start(bf16[12,48,256]{2,1,0:T(8,128)(2,1)S(1)} %get-tuple-element.117), channel_id=1, source_target_pairs={{1,2},{2,1},{3,4},{4,3},{5,6},{6,5},{9,10},{10,9},{11,12},{12,11},... | collective-permute-start | bytes 884744 | tf_op jit(solution)/shard_map/ppermute | solution.py:729
  20.7 4.0 %collective-permute-start.11 = (bf16[12,48,256]{2,1,0:T(8,128)(2,1)S(1)}, bf16[12,48,256]{2,1,0:T(8,128)(2,1)S(1)}, u32[]{:S(2)}, u32[]{:S(2)}) collective-permute-start(bf16[12,48,256]{2,1,0:T(8,128)(2,1)S(1)} %get-tuple-element.118), channel_id=1, source_target_pairs={{0,1},{1,0},{2,3},{3,2},{4,5},{5,4},{6,7},{7,6},{8,9},{9,8},{10,11... | collective-permute-start | bytes 884744 | tf_op jit(solution)/shard_map/ppermute | solution.py:728
  24.2 1.4 %collective-permute-start.7 = (bf16[4,16,1408]{2,1,0:T(8,128)(2,1)S(1)}, bf16[4,16,1408]{2,1,0:T(8,128)(2,1)S(1)}, u32[]{:S(2)}, u32[]{:S(2)}) collective-permute-start(bf16[4,16,1408]{2,1,0:T(8,128)(2,1)S(1)} %collective-permute-done.3.refs_1_), channel_id=1, source_target_pairs={{0,1},{1,0},{2,3},{3,2},{4,5},{5,4},{6,7},{7,6},{8,9},{9,8},{10,11... | collective-permute-start | bytes 540680 | tf_op jit(solution)/shard_map/ppermute | solution.py:621
  24.2 1.7 %collective-permute-start.8 = (bf16[4,16,1408]{2,1,0:T(8,128)(2,1)S(1)}, bf16[4,16,1408]{2,1,0:T(8,128)(2,1)S(1)}, u32[]{:S(2)}, u32[]{:S(2)}) collective-permute-start(bf16[4,16,1408]{2,1,0:T(8,128)(2,1)S(1)} %collective-permute-done.4.refs_2_), channel_id=1, source_target_pairs={{0,1},{1,0},{2,3},{3,2},{4,5},{5,4},{6,7},{7,6},{8,9},{9,8},{10,11... | collective-permute-start | bytes 540680 | tf_op jit(solution)/shard_map/ppermute | solution.py:621
  24.7 1.4 %collective-permute-start.9 = (bf16[4,16,1408]{2,1,0:T(8,128)(2,1)S(1)}, bf16[4,16,1408]{2,1,0:T(8,128)(2,1)S(1)}, u32[]{:S(2)}, u32[]{:S(2)}) collective-permute-start(bf16[4,16,1408]{2,1,0:T(8,128)(2,1)S(1)} %collective-permute-done.5.refs_3_), channel_id=1, source_target_pairs={{0,1},{1,0},{2,3},{3,2},{4,5},{5,4},{6,7},{7,6},{8,9},{9,8},{10,11... | collective-permute-start | bytes 540680 | tf_op jit(solution)/shard_map/ppermute | solution.py:621
  41.5 2.3 %collective-permute-start.12 = (bf16[16,16,1408]{2,1,0:T(8,128)(2,1)S(1)}, bf16[16,16,1408]{2,1,0:T(8,128)(2,1)S(1)}, u32[]{:S(2)}, u32[]{:S(2)}) collective-permute-start(bf16[16,16,1408]{2,1,0:T(8,128)(2,1)S(1)} %slice.40), channel_id=1, source_target_pairs={{0,1},{1,0},{2,3},{3,2},{4,5},{5,4},{6,7},{7,6},{8,9},{9,8},{10,11... | collective-permute-start | bytes 2162696 | tf_op jit(solution)/shard_map/ppermute | solution.py:621
  44.0 7.4 %collective-permute-start.13 = (bf16[4,16,1408]{2,1,0:T(8,128)(2,1)S(1)}, bf16[4,16,1408]{2,1,0:T(8,128)(2,1)S(1)}, u32[]{:S(2)}, u32[]{:S(2)}) collective-permute-start(bf16[4,16,1408]{2,1,0:T(8,128)(2,1)S(1)} %get-tuple-element.184), channel_id=1, source_target_pairs={{0,8},{1,9},{2,10},{3,11},{4,12},{5,13},{6,14},{7,15},{8,0},{9,1},... | collective-permute-start | bytes 540680 | tf_op jit(solution)/shard_map/ppermute | solution.py:621
  45.6 10.0 %collective-permute-start.15 = (bf16[4,16,1408]{2,1,0:T(8,128)(2,1)S(1)}, bf16[4,16,1408]{2,1,0:T(8,128)(2,1)S(1)}, u32[]{:S(2)}, u32[]{:S(2)}) collective-permute-start(bf16[4,16,1408]{2,1,0:T(8,128)(2,1)S(1)} %get-tuple-element.185), channel_id=1, source_target_pairs={{0,24},{1,25},{2,26},{3,27},{4,28},{5,29},{6,30},{7,31},{8,16},{9,... | collective-permute-start | bytes 540680 | tf_op jit(solution)/shard_map/ppermute | solution.py:621
  47.0 10.0 %collective-permute-start.14 = (bf16[4,16,1408]{2,1,0:T(8,128)(2,1)S(1)}, bf16[4,16,1408]{2,1,0:T(8,128)(2,1)S(1)}, u32[]{:S(2)}, u32[]{:S(2)}) collective-permute-start(bf16[4,16,1408]{2,1,0:T(8,128)(2,1)S(1)} %get-tuple-element.186), channel_id=1, source_target_pairs={{0,16},{1,17},{2,18},{3,19},{4,20},{5,21},{6,22},{7,23},{8,24},{9,... | collective-permute-start | bytes 540680 | tf_op jit(solution)/shard_map/ppermute | solution.py:621
  47.6 14.0 %collective-permute-start.16 = (bf16[640,512]{1,0:T(8,128)(2,1)S(1)}, bf16[640,512]{1,0:T(8,128)(2,1)S(1)}, u32[]{:S(2)}, u32[]{:S(2)}) collective-permute-start(bf16[640,512]{1,0:T(8,128)(2,1)S(1)} %get-tuple-element.129), channel_id=1, source_target_pairs={{0,1},{1,0},{2,3},{3,2},{4,5},{5,4},{6,7},{7,6},{8,9},{9,8},{10,11... | collective-permute-start | bytes 1966088 | tf_op jit(solution)/shard_map/ppermute | solution.py:728
  47.6 14.0 %collective-permute-start.17 = (bf16[640,512]{1,0:T(8,128)(2,1)S(1)}, bf16[640,512]{1,0:T(8,128)(2,1)S(1)}, u32[]{:S(2)}, u32[]{:S(2)}) collective-permute-start(bf16[640,512]{1,0:T(8,128)(2,1)S(1)} %get-tuple-element.130), channel_id=1, source_target_pairs={{1,2},{2,1},{3,4},{4,3},{5,6},{6,5},{9,10},{10,9},{11,12},{12,11},... | collective-permute-start | bytes 1966088 | tf_op jit(solution)/shard_map/ppermute | solution.py:729
  57.1 7.4 %collective-permute-start.20 = (bf16[16,1408]{1,0:T(8,128)(2,1)S(1)}, bf16[16,1408]{1,0:T(8,128)(2,1)S(1)}, u32[]{:S(2)}, u32[]{:S(2)}) collective-permute-start(bf16[16,1408]{1,0:T(8,128)(2,1)S(1)} %get-tuple-element.187), channel_id=1, source_target_pairs={{0,6},{1,7},{2,4},{3,5},{4,2},{5,3},{6,0},{7,1},{8,14},{9,15},{10,... | collective-permute-start | bytes 135176 | tf_op jit(solution)/shard_map/ppermute | solution.py:621
  59.3 5.3 %collective-permute-start.19 = (bf16[16,1408]{1,0:T(8,128)(2,1)S(1)}, bf16[16,1408]{1,0:T(8,128)(2,1)S(1)}, u32[]{:S(2)}, u32[]{:S(2)}) collective-permute-start(bf16[16,1408]{1,0:T(8,128)(2,1)S(1)} %get-tuple-element.188), channel_id=1, source_target_pairs={{0,4},{1,5},{2,6},{3,7},{4,0},{5,1},{6,2},{7,3},{8,12},{9,13},{10,... | collective-permute-start | bytes 135176 | tf_op jit(solution)/shard_map/ppermute | solution.py:621
  59.3 5.3 %collective-permute-start.18 = (bf16[16,1408]{1,0:T(8,128)(2,1)S(1)}, bf16[16,1408]{1,0:T(8,128)(2,1)S(1)}, u32[]{:S(2)}, u32[]{:S(2)}) collective-permute-start(bf16[16,1408]{1,0:T(8,128)(2,1)S(1)} %get-tuple-element.189), channel_id=1, source_target_pairs={{0,2},{1,3},{2,0},{3,1},{4,6},{5,7},{6,4},{7,5},{8,10},{9,11},{10,... | collective-permute-start | bytes 135176 | tf_op jit(solution)/shard_map/ppermute | solution.py:621
  61.6 3.1 %copy-start = (f32[8,768]{1,0:T(8,128)S(1)}, f32[8,768]{1,0:T(8,128)}, u32[]{:S(2)}) copy-start(f32[8,768]{1,0:T(8,128)} %refs_4_.3) | copy-start | bytes 73732
  61.6 3.1 %copy-start.1 = (f32[8,768]{1,0:T(8,128)S(1)}, f32[8,768]{1,0:T(8,128)}, u32[]{:S(2)}) copy-start(f32[8,768]{1,0:T(8,128)} %refs_6_.3) | copy-start | bytes 73732
  61.6 3.0 %copy-start.2 = (f32[24,256]{1,0:T(8,128)S(1)}, f32[24,256]{1,0:T(8,128)}, u32[]{:S(2)}) copy-start(f32[24,256]{1,0:T(8,128)} %refs_7_.3) | copy-start | bytes 73732
  61.6 3.0 %copy-start.3 = (f32[8,768]{1,0:T(8,128)S(1)}, f32[8,768]{1,0:T(8,128)}, u32[]{:S(2)}) copy-start(f32[8,768]{1,0:T(8,128)} %refs_10_.3) | copy-start | bytes 73732
  61.7 3.0 %copy-start.4 = (f32[8,768]{1,0:T(8,128)S(1)}, f32[8,768]{1,0:T(8,128)}, u32[]{:S(2)}) copy-start(f32[8,768]{1,0:T(8,128)} %refs_12_.3) | copy-start | bytes 73732
  61.7 3.0 %copy-start.5 = (f32[24,256]{1,0:T(8,128)S(1)}, f32[24,256]{1,0:T(8,128)}, u32[]{:S(2)}) copy-start(f32[24,256]{1,0:T(8,128)} %refs_13_.3) | copy-start | bytes 73732
  61.7 3.0 %copy-start.6 = (f32[8,768]{1,0:T(8,128)S(1)}, f32[8,768]{1,0:T(8,128)}, u32[]{:S(2)}) copy-start(f32[8,768]{1,0:T(8,128)} %refs_2_.1) | copy-start | bytes 73732
  61.7 3.0 %copy-start.7 = (f32[8,768]{1,0:T(8,128)S(1)}, f32[8,768]{1,0:T(8,128)}, u32[]{:S(2)}) copy-start(f32[8,768]{1,0:T(8,128)} %refs_0_.1) | copy-start | bytes 73732
  61.7 3.0 %copy-start.8 = (f32[24,256]{1,0:T(8,128)S(1)}, f32[24,256]{1,0:T(8,128)}, u32[]{:S(2)}) copy-start(f32[24,256]{1,0:T(8,128)} %refs_3_.1) | copy-start | bytes 73732
  61.7 3.0 %copy-start.9 = (f32[8,256]{1,0:T(8,128)S(1)}, f32[8,256]{1,0:T(8,128)}, u32[]{:S(2)}) copy-start(f32[8,256]{1,0:T(8,128)} %refs_5_.4) | copy-start | bytes 24580
  61.7 3.0 %copy-start.10 = (f32[8,256]{1,0:T(8,128)S(1)}, f32[8,256]{1,0:T(8,128)}, u32[]{:S(2)}) copy-start(f32[8,256]{1,0:T(8,128)} %refs_11_.3) | copy-start | bytes 24580
  61.7 3.0 %copy-start.11 = (f32[8,256]{1,0:T(8,128)S(1)}, f32[8,256]{1,0:T(8,128)}, u32[]{:S(2)}) copy-start(f32[8,256]{1,0:T(8,128)} %refs_1_.1) | copy-start | bytes 24580
  61.8 3.0 %copy-start.12 = (f32[11,8]{0,1:T(8,128)S(1)}, f32[11,8]{0,1:T(8,128)}, u32[]{:S(2)}) copy-start(f32[11,8]{0,1:T(8,128)} %param.38) | copy-start | bytes 1060
  61.8 3.0 %copy-start.13 = (f32[8,49]{1,0:T(8,128)S(1)}, f32[8,49]{1,0:T(8,128)}, u32[]{:S(2)}) copy-start(f32[8,49]{1,0:T(8,128)} %refs_9_.4) | copy-start | bytes 4708
  61.8 3.0 %copy-start.14 = (f32[11,8]{0,1:T(8,128)S(1)}, f32[11,8]{0,1:T(8,128)}, u32[]{:S(2)}) copy-start(f32[11,8]{0,1:T(8,128)} %param.39) | copy-start | bytes 1060
  61.8 3.0 %copy-start.15 = (f32[8,49]{1,0:T(8,128)S(1)}, f32[8,49]{1,0:T(8,128)}, u32[]{:S(2)}) copy-start(f32[8,49]{1,0:T(8,128)} %refs_15_.3) | copy-start | bytes 4708
  61.8 3.0 %copy-start.16 = (f32[11,8]{0,1:T(8,128)S(1)}, f32[11,8]{0,1:T(8,128)}, u32[]{:S(2)}) copy-start(f32[11,8]{0,1:T(8,128)} %param.28) | copy-start | bytes 1060
  61.8 3.0 %copy-start.18 = (f32[8,49]{1,0:T(8,128)S(1)}, f32[8,49]{1,0:T(8,128)}, u32[]{:S(2)}) copy-start(f32[8,49]{1,0:T(8,128)} %refs_5_.5) | copy-start | bytes 4708
  65.1 1.2 %collective-permute-start.21 = (f32[8,128]{1,0:T(8,128)S(1)}, f32[8,128]{1,0:T(8,128)S(1)}, u32[]{:S(2)}, u32[]{:S(2)}) collective-permute-start(f32[8,128]{1,0:T(8,128)S(1)} %get-tuple-element.142.mine_ref), channel_id=1, source_target_pairs={{0,1},{1,0},{2,3},{3,2},{4,5},{5,4},{6,7},{7,6},{8,9},{9,8},{10,11... | collective-permute-start | bytes 12296 | tf_op jit(solution)/shard_map/ppermute | solution.py:621
  66.3 4.5 %collective-permute-start.24 = (f32[8,128]{1,0:T(8,128)S(1)}, f32[8,128]{1,0:T(8,128)S(1)}, u32[]{:S(2)}, u32[]{:S(2)}) collective-permute-start(f32[8,128]{1,0:T(8,128)S(1)} %add.66), channel_id=1, source_target_pairs={{0,24},{1,25},{2,26},{3,27},{4,28},{5,29},{6,30},{7,31},{8,16},{9,... | collective-permute-start | bytes 12296 | tf_op jit(solution)/shard_map/ppermute | solution.py:621
  67.8 3.6 %collective-permute-start.23 = (f32[8,128]{1,0:T(8,128)S(1)}, f32[8,128]{1,0:T(8,128)S(1)}, u32[]{:S(2)}, u32[]{:S(2)}) collective-permute-start(f32[8,128]{1,0:T(8,128)S(1)} %add.66), channel_id=1, source_target_pairs={{0,16},{1,17},{2,18},{3,19},{4,20},{5,21},{6,22},{7,23},{8,24},{9,... | collective-permute-start | bytes 12296 | tf_op jit(solution)/shard_map/ppermute | solution.py:621
  69.1 3.6 %collective-permute-start.22 = (f32[8,128]{1,0:T(8,128)S(1)}, f32[8,128]{1,0:T(8,128)S(1)}, u32[]{:S(2)}, u32[]{:S(2)}) collective-permute-start(f32[8,128]{1,0:T(8,128)S(1)} %add.66), channel_id=1, source_target_pairs={{0,8},{1,9},{2,10},{3,11},{4,12},{5,13},{6,14},{7,15},{8,0},{9,1},... | collective-permute-start | bytes 12296 | tf_op jit(solution)/shard_map/ppermute | solution.py:621
  72.8 5.4 %collective-permute-start.27 = (f32[8,128]{1,0:T(8,128)S(1)}, f32[8,128]{1,0:T(8,128)S(1)}, u32[]{:S(2)}, u32[]{:S(2)}) collective-permute-start(f32[8,128]{1,0:T(8,128)S(1)} %add_add_fusion.a_ref), channel_id=1, source_target_pairs={{0,6},{1,7},{2,4},{3,5},{4,2},{5,3},{6,0},{7,1},{8,14},{9,15},{10,... | collective-permute-start | bytes 12296 | tf_op jit(solution)/shard_map/ppermute | solution.py:621
  74.7 4.5 %collective-permute-start.26 = (f32[8,128]{1,0:T(8,128)S(1)}, f32[8,128]{1,0:T(8,128)S(1)}, u32[]{:S(2)}, u32[]{:S(2)}) collective-permute-start(f32[8,128]{1,0:T(8,128)S(1)} %add_add_fusion.a_ref), channel_id=1, source_target_pairs={{0,4},{1,5},{2,6},{3,7},{4,0},{5,1},{6,2},{7,3},{8,12},{9,13},{10,... | collective-permute-start | bytes 12296 | tf_op jit(solution)/shard_map/ppermute | solution.py:621
  74.7 4.5 %collective-permute-start.25 = (f32[8,128]{1,0:T(8,128)S(1)}, f32[8,128]{1,0:T(8,128)S(1)}, u32[]{:S(2)}, u32[]{:S(2)}) collective-permute-start(f32[8,128]{1,0:T(8,128)S(1)} %add_add_fusion.a_ref), channel_id=1, source_target_pairs={{0,2},{1,3},{2,0},{3,1},{4,6},{5,7},{6,4},{7,5},{8,10},{9,11},{10,... | collective-permute-start | bytes 12296 | tf_op jit(solution)/shard_map/ppermute | solution.py:621

commit v8 on v7

--- a/solution.py
+++ b/solution.py
@@ -78,15 +78,23 @@
 
 
 def spread_heads(v, lane_head):
-    zero = jnp.zeros_like(v)
-    return jnp.concatenate([jnp.where(lane_head == h, v, zero) for h in range(HEADS)], axis=0)
+    zero = jnp.zeros((QN, 128), v.dtype)
+    rows = []
+    for h in range(HEADS):
+        half = [zero, zero]
+        half[h // 4] = jnp.where(lane_head == h % 4, v[:, 128 * (h // 4) : 128 * (h // 4) + 128], zero)
+        rows.append(jnp.concatenate(half, axis=1))
+    return jnp.concatenate(rows, axis=0)
 
 
 def pick_heads(full, lane_head):
-    out = jnp.where(lane_head == 0, full[0:QN], 0.0)
-    for h in range(1, HEADS):
-        out = out + jnp.where(lane_head == h, full[h * QN : (h + 1) * QN], 0.0)
-    return out
+    halves = []
+    for side in range(2):
+        parts = [full[h * QN : (h + 1) * QN, 128 * side : 128 * side + 128] for h in range(4 * side, 4 * side + 4)]
+        low = jnp.where(lane_head == 0, parts[0], parts[1])
+        high = jnp.where(lane_head == 2, parts[2], parts[3])
+        halves.append(jnp.where(lane_head < 2, low, high))
+    return jnp.concatenate(halves, axis=1)
 
 
 def split12(v):
@@ -182,18 +190,16 @@
     lax.fori_loop(0, 4, block, 0, unroll=2)
 
 
-def attend_kernel(limits_ref, bias_ref, q_ref, k_ref, v_ref, mixed_ref, p_ref):
+def attend_kernel(limits_ref, bias_ref, q_ref, k_ref, v_ref, mixed_ref, p_ref, other_ref):
     scale = 32 ** (-0.5)
-    lane_head = lax.broadcasted_iota(jnp.int32, (QN, 256), 1) >> 5
+    lane_head = lax.broadcasted_iota(jnp.int32, (QN, 128), 1) >> 5
     row0 = lax.axis_index("band") * 16
     height = limits_ref[0:1, 0:1]
     wide = limits_ref[1:2, 0:1]
     ks = lax.broadcasted_iota(jnp.int32, (KN, 384), 0)
     ql = lax.broadcasted_iota(jnp.int32, (KN, 384), 1)
-    kj = (ks + 36) & (KN - 1)
-    krow, kcol = split12(kj)
-    qin = ql - 48 * ((ql * 171) >> 13)
-    same = ks == qin
+    other_ref[...] = jnp.where(ks == ql - 48 * ((ql * 171) >> 13), 0.0, 1.0)
+    krow, kcol = split12((lax.broadcasted_iota(jnp.int32, (KN, 128), 0) + 36) & (KN - 1))
 
     def attend(k, _):
         rc = k >> 2
@@ -201,11 +207,11 @@
         at_q = pl.ds(pl.multiple_of(k * QN, QN), QN)
         at_k = pl.ds(pl.multiple_of(k * KN, KN), KN)
         qbd = spread_heads(q_ref[at_q, :], lane_head)
-        s = dot_nt(k_ref[at_k, :], qbd) * (scale * LOG2E) + bias_ref[...]
         r = krow * 4 + (rc - 12)
         c = kcol * 4 + cc
-        okay = ((r >= -row0) & (r < height) & (c < wide)) | same
-        s = jnp.where(okay, s, MASKED)
+        off = jnp.where((r >= -row0) & (r < height) & (c < wide), 0.0, MASKED)
+        off = bias_ref[...] + jnp.concatenate([off] * 3, axis=1) * other_ref[...]
+        s = dot_nt(k_ref[at_k, :], qbd) * (scale * LOG2E) + off
         top = jnp.max(s, axis=0, keepdims=True)
         e = jnp.exp2(s - top)
         p = e * (1.0 / jnp.sum(e, axis=0, keepdims=True))
@@ -235,6 +241,8 @@
     dmix_ref,
     sums_ref,
     zsum_ref,
+    xhat_ref,
+    rstd_ref,
 ):
     def vrow(i):
         return vec_ref[i : i + 1, :]
@@ -243,39 +251,49 @@
     sums_ref[7:8, :] = dysum_ref[...]
     zsum_ref[...] = jnp.zeros_like(zsum_ref)
 
-    def feed(rc, _):
+    def inner(rc, _):
         at = pl.ds(pl.multiple_of(rc * 192, 192), 192)
         x1 = xp_ref[at, :] + (dot(mixed_ref[at, :], wo_ref[...]) + vrow(4))
         x1_ref[at, :] = x1
         xhat, rstd = normed(x1)
-        a2 = (xhat * vrow(5) + vrow(6)).astype(BF)
-        a2_ref[at, :] = a2
-        dy = dy_ref[at, :]
-        dn = jnp.zeros((192, 256), F32)
+        xhat_ref[at, :] = xhat
+        rstd_ref[at, :] = jnp.broadcast_to(rstd, (192, 128))
+        a2_ref[at, :] = (xhat * vrow(5) + vrow(6)).astype(BF)
+        return 0
+
+    lax.fori_loop(0, 4, inner, 0, unroll=4)
+
+    def hidden(rc, _):
+        at = pl.ds(pl.multiple_of(rc * 192, 192), 192)
         for part in range(3):
             cols = slice(256 * part, 256 * part + 256)
-            z = dot(a2, wu_ref[:, cols]) + vrow(8 + part)
+            z = dot(a2_ref[at, :], wu_ref[:, cols]) + vrow(8 + part)
             cube = (GELU0 * GELU1) * (z * z)
-            up = 1.0 + jnp.tanh(z * (GELU0 + cube))
-            hz = 0.5 * z
-            act_ref[at, cols] = (hz * up).astype(BF)
-            slope = up * (0.5 + hz * (2.0 - up) * (GELU0 + 3.0 * cube))
-            dz = (dot_nt(dy, wd_ref[cols, :]) * slope).astype(BF)
-            dz_ref[at, cols] = dz
-            zsum_ref[:, cols] += jnp.sum(dz.astype(F32), axis=0, keepdims=True)
-            dn = dn + dot_nt(dz, wu_ref[:, cols])
-        dyf = dy.astype(F32)
-        dx1 = dyf + norm_back(dn * vrow(5), xhat, rstd)
+            up = 0.5 + 0.5 * jnp.tanh(z * (GELU0 + cube))
+            act = z * up
+            act_ref[at, cols] = act.astype(BF)
+            slope = up * (1.0 + (z - act) * (2.0 * GELU0 + 6.0 * cube))
+            dz = dot_nt(dy_ref[at, :], wd_ref[cols, :]) * slope
+            zsum_ref[:, cols] += jnp.sum(dz, axis=0, keepdims=True)
+            dz_ref[at, cols] = dz.astype(BF)
+        return 0
+
+    lax.fori_loop(0, 4, hidden, 0, unroll=4)
+
+    def outer(rc, _):
+        at = pl.ds(pl.multiple_of(rc * 192, 192), 192)
+        dn = dot_nt(dz_ref[at, :], wu_ref[...])
+        xhat = xhat_ref[at, :]
+        dx1 = dy_ref[at, :].astype(F32) + norm_back(dn * vrow(5), xhat, rstd_ref[at, 0:1])
         dx1_ref[at, :] = dx1
-        da = dx1.astype(BF)
-        da_ref[at, :] = da
-        dmix_ref[at, :] = dot_nt(da, wo_ref[...]).astype(BF)
-        sums_ref[4:5, :] += jnp.sum(da.astype(F32), axis=0, keepdims=True)
+        da_ref[at, :] = dx1.astype(BF)
+        sums_ref[4:5, :] += jnp.sum(dx1, axis=0, keepdims=True)
         sums_ref[5:6, :] += jnp.sum(dn * xhat, axis=0, keepdims=True)
         sums_ref[6:7, :] += jnp.sum(dn, axis=0, keepdims=True)
         return 0
 
-    lax.fori_loop(0, 4, feed, 0, unroll=4)
+    lax.fori_loop(0, 4, outer, 0, unroll=4)
+    dmix_ref[...] = dot_nt(da_ref[...], wo_ref[...]).astype(BF)
 
 
 def back_kernel(
@@ -292,23 +310,27 @@
 ):
     odd = (lax.axis_index("band") & 1) == 1
     scale = 32 ** (-0.5)
-    lane_head = lax.broadcasted_iota(jnp.int32, (QN, 256), 1) >> 5
+    lane_head = lax.broadcasted_iota(jnp.int32, (QN, 128), 1) >> 5
     tacc_ref[...] = jnp.zeros_like(tacc_ref)
+
+    def scores_back(k, _):
+        at_q = pl.ds(pl.multiple_of(k * QN, QN), QN)
+        at_k = pl.ds(pl.multiple_of(k * KN, KN), KN)
+        dp = dot_nt(v_ref[at_k, :], spread_heads(dmix_ref[at_q, :], lane_head))
+        p = p_ref[at_k, :]
+        pdp = p * dp
+        ds = pdp - p * jnp.sum(pdp, axis=0, keepdims=True)
+        tacc_ref[...] += ds
+        dsl_ref[at_k, :] = ds.astype(BF)
+        return 0
+
+    lax.fori_loop(0, CLS, scores_back, 0, unroll=CLS)
 
     def back_class(k):
         at_q = pl.ds(pl.multiple_of(k * QN, QN), QN)
         at_k = pl.ds(pl.multiple_of(k * KN, KN), KN)
-        qbd = spread_heads(q_ref[at_q, :], lane_head)
-        dobd = spread_heads(dmix_ref[at_q, :], lane_head)
-        p = p_ref[at_k, :]
-        dp = dot_nt(v_ref[at_k, :], dobd)
-        dv = dot(p.astype(BF), dobd)
-        pdp = p * dp
-        ds = pdp - p * jnp.sum(pdp, axis=0, keepdims=True)
-        tacc_ref[...] += ds
-        dsl = ds.astype(BF)
-        dsl_ref[at_k, :] = dsl
-        dk = dot(dsl, qbd) * scale
+        dv = dot(p_ref[at_k, :].astype(BF), spread_heads(dmix_ref[at_q, :], lane_head))
+        dk = dot(dsl_ref[at_k, :], spread_heads(q_ref[at_q, :], lane_head)) * scale
         dkv_ref[at_k, 0:256] = dk.astype(BF)
         dkv_ref[at_k, 256:512] = dv.astype(BF)
         own_ref[at_q, 0:256] = dk[0:QN]
@@ -365,7 +387,7 @@
     tgrad_ref,
 ):
     scale = 32 ** (-0.5)
-    lane_head = lax.broadcasted_iota(jnp.int32, (QN, 256), 1) >> 5
+    lane_head = lax.broadcasted_iota(jnp.int32, (QN, 128), 1) >> 5
 
     def query(k, _):
         at_q = pl.ds(pl.multiple_of(k * QN, QN), QN)
@@ -496,12 +518,12 @@
     blocks, (xhat, x, xz, xc, pk, xp, bias, limits, dy, dysum) = refs[:8], refs[8:18]
     act, dx1, x1, own, rimc, rimz, dq, out_ref, big_qkv, big_down, vec = refs[18:29]
     q, k, v, mixed, p, dz, a2, da, dmix, sums, zsum, dsl, tacc, dkv = refs[29:43]
-    fq, fv, tgrad, fd, fu, fo, big_out, big_up, vt, xk = refs[43:]
+    fq, fv, tgrad, fd, fu, fo, big_out, big_up, vt, xk, other, xhat1, rstd1 = refs[43:]
     halo_kernel(x, xc, xz, pk, xk)
     unpack(blocks, big_qkv, big_out, big_up, big_down, vec, vt, fq, fo, fu, fd)
     project_kernel(xhat, xk, big_qkv, vec, q, k, v)
-    attend_kernel(limits, bias, q, k, v, mixed, p)
-    feed_kernel(dy, dysum, mixed, xp, big_out, big_up, big_down, vec, act, dz, a2, da, dx1, x1, dmix, sums, zsum)
+    attend_kernel(limits, bias, q, k, v, mixed, p, other)
+    feed_kernel(dy, dysum, mixed, xp, big_out, big_up, big_down, vec, act, dz, a2, da, dx1, x1, dmix, sums, zsum, xhat1, rstd1)
     back_kernel(q, v, p, dmix, own, rimc, rimz, dsl, tacc, dkv)
     early_grads(act, dy, a2, dz, mixed, da, fd, fu, fo)
     late_grads(dsl, k, tacc, xhat, xk, dkv, big_qkv, vt, sums, zsum, dq, fq, fv, tgrad)
@@ -760,7 +782,8 @@
             + attend_outputs()
             + (dz_s, a2_s, da_s, dmix_s, sums_s, zsum_s, dsl_s, tacc_s, dkv_s, fq_s, fv_s, tgrad_s)
             + (sds((768, 256), F32), sds((256, 768), F32), sds((256, 256), F32))
-            + (sds((256, 256)), sds((256, 768)), sds((256, 128), F32), sds((CLS * KN, 256), F32))
+            + (sds((256, 256)), sds((256, 768)), sds((256, 128), F32), sds((CLS * KN, 256), F32), sds((KN, 384), F32))
+            + (sds((768, 256), F32), sds((768, 128), F32))
         ],
         *blocks, xhat, x, x_next, x_core, pk, xp, bias, limits, dy, dysum,
         flops=15 * 10**9, vmem=24,
@@ -871,11 +894,11 @@
     x_core, x_next = beside(edges, band)
     xk = call(halo_kernel, sds((CLS * KN, 256), F32), [], tokens_in, x_core, x_next, pk, flops=10**9)
     queries, keys, values = call(project_kernel, project_outputs(), [], xhat, xk, big_qkv, vec, flops=10**9)
-    mixed, probs = call(attend_kernel, attend_outputs(), [], limits, bias, queries, keys, values, flops=3 * 10**9)
+    mixed, probs = call(attend_kernel, attend_outputs(), [pltpu.VMEM((KN, 384), F32)], limits, bias, queries, keys, values, flops=3 * 10**9)
     act, dz, a2, da, dx1, x1, dmix, sums, zsum = call(
         feed_kernel,
         feed_outputs(),
-        [],
+        [pltpu.VMEM((768, 256), F32), pltpu.VMEM((768, 128), F32)],
         dy, dysum, mixed, xp, big_out, big_up, big_down, vec,
         flops=4 * 10**9,
     )

time: 80.2 us -> 77.6 us (0.968)
  Pallas kernels: 23.7 us -> 21.1 us
    pallas_call x9, Pallas kernels: 23.7 us -> 21.1 us  [call(): pl.pallas_call(kernel, out_shape=out_shape, in_specs=specs, out_specs=jax...]
where the time goes in v8:
time: 77.6 us; the launch traced here: 77.3 us
  starting transfers between devices  27.7 us (36%)
  waiting for transfers between devices  24 us (31%)
  Pallas kernels  21.1 us (27%)
  local copies, waits for them, and re-layouts  2.32 us (3%)
  other arithmetic  1.12 us (1%)
  between operations  1.09 us (1%)
    ppermute x24, starting transfers between devices, swap(): return lax.ppermute(block, AXES, [(k, k ^ mask) for k in range(count)])  26.1 us
    ppermute x24, waiting for transfers between devices, swap(): return lax.ppermute(block, AXES, [(k, k ^ mask) for k in range(count)])  24 us
    pallas_call x9, Pallas kernels, call(): pl.pallas_call(kernel, out_shape=out_shape, in_specs=specs, out_specs=jax...  21.1 us
  transfers between devices with their start and end apart: 28, of which 18 were waited for; matrix products, arithmetic and copies ran while one was open for 0% of the time, Pallas kernels for 9%

profile of v8, /device:TPU:0, one launch (start us, length us, event | category | flops | bytes accessed | tf_op | source)
XLA Modules:
  0.0 77.3 jit_solution(7562239721139898721)
XLA Ops:
  0.7 0.7 fusion.4
  1.4 0.8 %add_convert_fusion.refs_0_ = bf16[16,1408]{1,0:T(8,128)(2,1)S(1)} fusion(f32[8,256]{1,0:T(8,128)S(1)} %get-tuple-element.191, f32[8,256]{1,0:T(8,128)S(1)} %get-tuple-element.192, f32[8,768]{1,0:T(8,128)} %refs_2_.1, f32[8,11]{1,0:T(8,128)} %bitcast.20, f32[8,256]{1,0:T(8,128)S(1)} %get-tuple-element.190, f32[8,256]{1,0:T(8,128)} %refs_1_.1, f32[8,768]{1,0:T(8,128)} %refs_0_.1), kind=kLoop, calls=%fused_computation.5 | loop fusion | flops 157696 | bytes 127328 | tf_op jit(solution)/shard_map/convert_element_type | solution.py:489
  2.2 5.1 %collective-permute-start.2 = (bf16[16,1408]{1,0:T(8,128)(2,1)S(1)}, bf16[16,1408]{1,0:T(8,128)(2,1)S(1)}, u32[]{:S(2)}, u32[]{:S(2)}) collective-permute-start(bf16[16,1408]{1,0:T(8,128)(2,1)S(1)} %add_convert_fusion.refs_0_), channel_id=1, source_target_pairs={{0,6},{1,7},{2,4},{3,5},{4,2},{5,3},{6,0},{7,1},{8,14},{9,15},{10,... | collective-permute-start | bytes 135176 | tf_op jit(solution)/shard_map/ppermute | solution.py:643
  7.3 0.6 collective-permute-start
  7.9 0.7 copy-done.17
  8.6 0.7 copy-done.21
  9.3 1.3 %shard_map.372 = (f32[128,384]{1,0:T(8,128)S(1)}, s32[8,128]{1,0:T(8,128)S(1)}, bf16[192,192]{1,0:T(8,128)(2,1)S(1)}, bf16[512,480]{1,0:T(8,128)(2,1)S(1)}) custom-call(s32[1,2]{1,0:T(1,128)S(1)} %copy-done.21, f32[8,49]{1,0:T(8,128)S(1)} %copy-done.17), custom_call_target="tpu_custom_call" | custom-call | flops 1000000000 | bytes 1000000 | tf_op jit(solution)/shard_map/pallas_call | solution.py:620
  10.6 1.6 %collective-permute-done.1.refs_2_ = bf16[16,1408]{1,0:T(8,128)(2,1)S(1)} collective-permute-done((bf16[16,1408]{1,0:T(8,128)(2,1)S(1)}, bf16[16,1408]{1,0:T(8,128)(2,1)S(1)}, u32[]{:S(2)}, u32[]{:S(2)}) %collective-permute-start.1) | collective-permute-done | bytes 45088 | tf_op jit(solution)/shard_map/ppermute | solution.py:643
  12.2 0.1 collective-permute-start.6
  12.3 2.5 %collective-permute-start.5 = (bf16[4,16,1408]{2,1,0:T(8,128)(2,1)S(1)}, bf16[4,16,1408]{2,1,0:T(8,128)(2,1)S(1)}, u32[]{:S(2)}, u32[]{:S(2)}) collective-permute-start(bf16[4,16,1408]{2,1,0:T(8,128)(2,1)S(1)} %shard_map.373.refs_0_), channel_id=1, source_target_pairs={{0,24},{1,25},{2,26},{3,27},{4,28},{5,29},{6,30},{7,31},{8,16},{9,... | collective-permute-start | bytes 540680 | tf_op jit(solution)/shard_map/ppermute | solution.py:643
  14.8 0.5 collective-permute-start.4
  15.3 0.5 collective-permute-start.3
  15.9 0.6 shard_map.374
  16.4 0.7 collective-permute-start.10
  17.1 3.5 %collective-permute-done.5.refs_3_ = bf16[4,16,1408]{2,1,0:T(8,128)(2,1)S(1)} collective-permute-done((bf16[4,16,1408]{2,1,0:T(8,128)(2,1)S(1)}, bf16[4,16,1408]{2,1,0:T(8,128)(2,1)S(1)}, u32[]{:S(2)}, u32[]{:S(2)}) %collective-permute-start.5) | collective-permute-done | bytes 180256 | tf_op jit(solution)/shard_map/ppermute | solution.py:643
  20.7 3.4 %collective-permute-done.4.refs_2_ = bf16[4,16,1408]{2,1,0:T(8,128)(2,1)S(1)} collective-permute-done((bf16[4,16,1408]{2,1,0:T(8,128)(2,1)S(1)}, bf16[4,16,1408]{2,1,0:T(8,128)(2,1)S(1)}, u32[]{:S(2)}, u32[]{:S(2)}) %collective-permute-start.4) | collective-permute-done | bytes 180256 | tf_op jit(solution)/shard_map/ppermute | solution.py:643
  24.1 0.1 collective-permute-done.3.refs_1_
  24.2 0.5 collective-permute-start.8
  24.7 0.9 %collective-permute-done.7.refs_5_ = bf16[4,16,1408]{2,1,0:T(8,128)(2,1)S(1)} collective-permute-done((bf16[4,16,1408]{2,1,0:T(8,128)(2,1)S(1)}, bf16[4,16,1408]{2,1,0:T(8,128)(2,1)S(1)}, u32[]{:S(2)}, u32[]{:S(2)}) %collective-permute-start.7) | collective-permute-done | bytes 180256 | tf_op jit(solution)/shard_map/ppermute | solution.py:643
  25.6 0.3 collective-permute-done.8.refs_6_
  25.8 0.3 collective-permute-done.9.refs_7_
  26.1 12.7 %shard_map.375 = (bf16[768,768]{1,0:T(8,128)(2,1)S(1)}, f32[768,256]{1,0:T(8,128)S(1)}, f32[768,256]{1,0:T(8,128)S(1)}, f32[768,512]{1,0:T(8,128)S(1)}, bf16[640...) custom-call(bf16[4,16,1408]{2,1,0:T(8,128)(2,1)S(1)} %shard_map.373., ...), custom_call_target="tpu_custom_call" | custom-call | flops 15000000512 | bytes 1000000 | tf_op jit(solution)/shard_map/pallas_call | solution.py:620
  38.8 0.1 slice.40
  38.9 0.3 collective-permute-start.12
  39.2 1.9 %collective-permute-done.12 = bf16[16,16,1408]{2,1,0:T(8,128)(2,1)S(1)} collective-permute-done((bf16[16,16,1408]{2,1,0:T(8,128)(2,1)S(1)}, bf16[16,16,1408]{2,1,0:T(8,128)(2,1)S(1)}, u32[]{:S(2)}, u32[]{:S(2)}) %collective-permute-start.12) | collective-permute-done | bytes 720928 | tf_op jit(solution)/shard_map/ppermute | solution.py:643
  41.1 0.2 fusion.2
  41.4 1.5 %collective-permute-start.13 = (bf16[4,16,1408]{2,1,0:T(8,128)(2,1)S(1)}, bf16[4,16,1408]{2,1,0:T(8,128)(2,1)S(1)}, u32[]{:S(2)}, u32[]{:S(2)}) collective-permute-start(bf16[4,16,1408]{2,1,0:T(8,128)(2,1)S(1)} %get-tuple-element.184), channel_id=1, source_target_pairs={{0,8},{1,9},{2,10},{3,11},{4,12},{5,13},{6,14},{7,15},{8,0},{9,1},... | collective-permute-start | bytes 540680 | tf_op jit(solution)/shard_map/ppermute | solution.py:643
  42.9 1.4 %collective-permute-start.15 = (bf16[4,16,1408]{2,1,0:T(8,128)(2,1)S(1)}, bf16[4,16,1408]{2,1,0:T(8,128)(2,1)S(1)}, u32[]{:S(2)}, u32[]{:S(2)}) collective-permute-start(bf16[4,16,1408]{2,1,0:T(8,128)(2,1)S(1)} %get-tuple-element.185), channel_id=1, source_target_pairs={{0,24},{1,25},{2,26},{3,27},{4,28},{5,29},{6,30},{7,31},{8,16},{9,... | collective-permute-start | bytes 540680 | tf_op jit(solution)/shard_map/ppermute | solution.py:643
  44.3 0.6 collective-permute-start.14
  44.9 0.9 %collective-permute-start.17 = (bf16[640,512]{1,0:T(8,128)(2,1)S(1)}, bf16[640,512]{1,0:T(8,128)(2,1)S(1)}, u32[]{:S(2)}, u32[]{:S(2)}) collective-permute-start(bf16[640,512]{1,0:T(8,128)(2,1)S(1)} %get-tuple-element.130), channel_id=1, source_target_pairs={{1,2},{2,1},{3,4},{4,3},{5,6},{6,5},{9,10},{10,9},{11,12},{12,11},... | collective-permute-start | bytes 1966088 | tf_op jit(solution)/shard_map/ppermute | solution.py:751
  45.8 2.0 %shard_map.377 = bf16[16,48,256]{2,1,0:T(8,128)(2,1)} custom-call(f32[768,256]{1,0:T(8,128)S(1)} %get-tuple-element.136.x1_ref, bf16[768,768]{1,0:T(8,128)(2,1)S(1)} %get-tuple-element.137.act_ref, bf16[768,256]{1,0:T(8,128)(2,1)S(1)} %get-tuple-element.138.wd_ref, f32[11,256]{1,0:T(8,128)S(1)} %get-tuple-element.135.vec_ref, ...), custom_call_target="tpu_custom_call" | custom-call | flops 1000000000 | bytes 1000000 | tf_op jit(solution)/shard_map/pallas_call | solution.py:620
  47.9 1.0 %collective-permute-done.13 = bf16[4,16,1408]{2,1,0:T(8,128)(2,1)S(1)} collective-permute-done((bf16[4,16,1408]{2,1,0:T(8,128)(2,1)S(1)}, bf16[4,16,1408]{2,1,0:T(8,128)(2,1)S(1)}, u32[]{:S(2)}, u32[]{:S(2)}) %collective-permute-start.13) | collective-permute-done | bytes 180256 | tf_op jit(solution)/shard_map/ppermute | solution.py:643
  48.8 4.2 %collective-permute-done.15 = bf16[4,16,1408]{2,1,0:T(8,128)(2,1)S(1)} collective-permute-done((bf16[4,16,1408]{2,1,0:T(8,128)(2,1)S(1)}, bf16[4,16,1408]{2,1,0:T(8,128)(2,1)S(1)}, u32[]{:S(2)}, u32[]{:S(2)}) %collective-permute-start.15) | collective-permute-done | bytes 180256 | tf_op jit(solution)/shard_map/ppermute | solution.py:643
  53.0 1.4 %collective-permute-done.14 = bf16[4,16,1408]{2,1,0:T(8,128)(2,1)S(1)} collective-permute-done((bf16[4,16,1408]{2,1,0:T(8,128)(2,1)S(1)}, bf16[4,16,1408]{2,1,0:T(8,128)(2,1)S(1)}, u32[]{:S(2)}, u32[]{:S(2)}) %collective-permute-start.14) | collective-permute-done | bytes 180256 | tf_op jit(solution)/shard_map/ppermute | solution.py:643
  54.4 0.1 fusion.1
  54.5 2.2 %collective-permute-start.20 = (bf16[16,1408]{1,0:T(8,128)(2,1)S(1)}, bf16[16,1408]{1,0:T(8,128)(2,1)S(1)}, u32[]{:S(2)}, u32[]{:S(2)}) collective-permute-start(bf16[16,1408]{1,0:T(8,128)(2,1)S(1)} %get-tuple-element.187), channel_id=1, source_target_pairs={{0,6},{1,7},{2,4},{3,5},{4,2},{5,3},{6,0},{7,1},{8,14},{9,15},{10,... | collective-permute-start | bytes 135176 | tf_op jit(solution)/shard_map/ppermute | solution.py:643
  56.7 2.3 %collective-permute-start.18 = (bf16[16,1408]{1,0:T(8,128)(2,1)S(1)}, bf16[16,1408]{1,0:T(8,128)(2,1)S(1)}, u32[]{:S(2)}, u32[]{:S(2)}) collective-permute-start(bf16[16,1408]{1,0:T(8,128)(2,1)S(1)} %get-tuple-element.189), channel_id=1, source_target_pairs={{0,2},{1,3},{2,0},{3,1},{4,6},{5,7},{6,4},{7,5},{8,10},{9,11},{10,... | collective-permute-start | bytes 135176 | tf_op jit(solution)/shard_map/ppermute | solution.py:643
  59.0 0.0 copy-start
  59.0 0.0 copy-start.1
  59.0 0.0 copy-start.3
  59.0 0.0 copy-start.4
  59.1 0.0 copy-start.7
  59.1 0.0 copy-start.8
  59.1 0.0 copy-start.11
  59.1 0.0 copy-start.12
  59.1 0.0 copy-start.14
  59.2 0.0 copy-start.15
  59.2 2.7 %shard_map.376 = bf16[16,48,256]{2,1,0:T(8,128)(2,1)} custom-call(f32[768,512]{1,0:T(8,128)S(1)} %get-tuple-element.128.own_ref, bf16[640,512]{1,0:T(8,128)(2,1)S(1)} %collective-permute-done.16.gotc_ref, bf16[640,512]{1,0:T(8,128)(2,1)S(1)} %collective-permute-done.17.gotz_ref, bf16[768,256]{1,0:T(8,128)(2,1)S(1)} %get-tuple-element.131.dq_ref, ...), custom_call_target="tpu_custom_call" | custom-call | flops 1000000000 | bytes 1000000 | tf_op jit(solution)/shard_map/pallas_call | solution.py:620
  61.9 0.1 collective-permute-done.19.refs_2_
  62.2 0.3 shard_map.378
  62.5 0.0 collective-permute-start.21
  62.5 1.2 %collective-permute-done.21 = f32[8,128]{1,0:T(8,128)S(1)} collective-permute-done((f32[8,128]{1,0:T(8,128)S(1)}, f32[8,128]{1,0:T(8,128)S(1)}, u32[]{:S(2)}, u32[]{:S(2)}) %collective-permute-start.21) | collective-permute-done | bytes 4128 | tf_op jit(solution)/shard_map/ppermute | solution.py:643
  63.6 1.5 %collective-permute-start.24 = (f32[8,128]{1,0:T(8,128)S(1)}, f32[8,128]{1,0:T(8,128)S(1)}, u32[]{:S(2)}, u32[]{:S(2)}) collective-permute-start(f32[8,128]{1,0:T(8,128)S(1)} %add.66), channel_id=1, source_target_pairs={{0,24},{1,25},{2,26},{3,27},{4,28},{5,29},{6,30},{7,31},{8,16},{9,... | collective-permute-start | bytes 12296 | tf_op jit(solution)/shard_map/ppermute | solution.py:643
  65.2 1.3 %collective-permute-start.23 = (f32[8,128]{1,0:T(8,128)S(1)}, f32[8,128]{1,0:T(8,128)S(1)}, u32[]{:S(2)}, u32[]{:S(2)}) collective-permute-start(f32[8,128]{1,0:T(8,128)S(1)} %add.66), channel_id=1, source_target_pairs={{0,16},{1,17},{2,18},{3,19},{4,20},{5,21},{6,22},{7,23},{8,24},{9,... | collective-permute-start | bytes 12296 | tf_op jit(solution)/shard_map/ppermute | solution.py:643
  66.5 0.6 collective-permute-start.22
  67.1 1.0 %collective-permute-done.24 = f32[8,128]{1,0:T(8,128)S(1)} collective-permute-done((f32[8,128]{1,0:T(8,128)S(1)}, f32[8,128]{1,0:T(8,128)S(1)}, u32[]{:S(2)}, u32[]{:S(2)}) %collective-permute-start.24) | collective-permute-done | bytes 4128 | tf_op jit(solution)/shard_map/ppermute | solution.py:643
  68.2 0.6 collective-permute-done.23
  68.8 1.3 %collective-permute-done.22 = f32[8,128]{1,0:T(8,128)S(1)} collective-permute-done((f32[8,128]{1,0:T(8,128)S(1)}, f32[8,128]{1,0:T(8,128)S(1)}, u32[]{:S(2)}, u32[]{:S(2)}) %collective-permute-start.22) | collective-permute-done | bytes 4128 | tf_op jit(solution)/shard_map/ppermute | solution.py:643
  70.1 1.9 %collective-permute-start.27 = (f32[8,128]{1,0:T(8,128)S(1)}, f32[8,128]{1,0:T(8,128)S(1)}, u32[]{:S(2)}, u32[]{:S(2)}) collective-permute-start(f32[8,128]{1,0:T(8,128)S(1)} %add_add_fusion.a_ref), channel_id=1, source_target_pairs={{0,6},{1,7},{2,4},{3,5},{4,2},{5,3},{6,0},{7,1},{8,14},{9,15},{10,... | collective-permute-start | bytes 12296 | tf_op jit(solution)/shard_map/ppermute | solution.py:643
  72.0 2.5 %collective-permute-start.25 = (f32[8,128]{1,0:T(8,128)S(1)}, f32[8,128]{1,0:T(8,128)S(1)}, u32[]{:S(2)}, u32[]{:S(2)}) collective-permute-start(f32[8,128]{1,0:T(8,128)S(1)} %add_add_fusion.a_ref), channel_id=1, source_target_pairs={{0,2},{1,3},{2,0},{3,1},{4,6},{5,7},{6,4},{7,5},{8,10},{9,11},{10,... | collective-permute-start | bytes 12296 | tf_op jit(solution)/shard_map/ppermute | solution.py:643
  74.5 0.8 shard_map.379
  75.3 0.2 collective-permute-done.27.d_ref
  75.5 1.0 %collective-permute-done.26.c_ref = f32[8,128]{1,0:T(8,128)S(1)} collective-permute-done((f32[8,128]{1,0:T(8,128)S(1)}, f32[8,128]{1,0:T(8,128)S(1)}, u32[]{:S(2)}, u32[]{:S(2)}) %collective-permute-start.26) | collective-permute-done | bytes 4128 | tf_op jit(solution)/shard_map/ppermute | solution.py:643
  76.5 0.8 shard_map.380
  (56 shorter events, 0.2 us)
Async XLA Ops:
  2.2 8.4 %collective-permute-start.2 = (bf16[16,1408]{1,0:T(8,128)(2,1)S(1)}, bf16[16,1408]{1,0:T(8,128)(2,1)S(1)}, u32[]{:S(2)}, u32[]{:S(2)}) collective-permute-start(bf16[16,1408]{1,0:T(8,128)(2,1)S(1)} %add_convert_fusion.refs_0_), channel_id=1, source_target_pairs={{0,6},{1,7},{2,4},{3,5},{4,2},{5,3},{6,0},{7,1},{8,14},{9,15},{10,... | collective-permute-start | bytes 135176 | tf_op jit(solution)/shard_map/ppermute | solution.py:643
  7.3 4.9 %collective-permute-start.1 = (bf16[16,1408]{1,0:T(8,128)(2,1)S(1)}, bf16[16,1408]{1,0:T(8,128)(2,1)S(1)}, u32[]{:S(2)}, u32[]{:S(2)}) collective-permute-start(bf16[16,1408]{1,0:T(8,128)(2,1)S(1)} %add_convert_fusion.refs_0_), channel_id=1, source_target_pairs={{0,4},{1,5},{2,6},{3,7},{4,0},{5,1},{6,2},{7,3},{8,12},{9,13},{10,... | collective-permute-start | bytes 135176 | tf_op jit(solution)/shard_map/ppermute | solution.py:643
  7.3 4.9 %collective-permute-start = (bf16[16,1408]{1,0:T(8,128)(2,1)S(1)}, bf16[16,1408]{1,0:T(8,128)(2,1)S(1)}, u32[]{:S(2)}, u32[]{:S(2)}) collective-permute-start(bf16[16,1408]{1,0:T(8,128)(2,1)S(1)} %add_convert_fusion.refs_0_), channel_id=1, source_target_pairs={{0,2},{1,3},{2,0},{3,1},{4,6},{5,7},{6,4},{7,5},{8,10},{9,11},{10,... | collective-permute-start | bytes 135176 | tf_op jit(solution)/shard_map/ppermute | solution.py:643
  7.9 0.7 copy-start.17
  8.6 0.7 copy-start.21
  9.3 6.6 %copy-start.19 = (bf16[16,48,256]{2,1,0:T(8,128)(2,1)S(1)}, bf16[16,48,256]{2,1,0:T(8,128)(2,1)}, u32[]{:S(2)}) copy-start(bf16[16,48,256]{2,1,0:T(8,128)(2,1)} %cot_ref.1) | copy-start | bytes 1179652
  9.3 6.6 %copy-start.20 = (bf16[16,48,256]{2,1,0:T(8,128)(2,1)S(1)}, bf16[16,48,256]{2,1,0:T(8,128)(2,1)}, u32[]{:S(2)}) copy-start(bf16[16,48,256]{2,1,0:T(8,128)(2,1)} %refs_9_.2) | copy-start | bytes 1179652
  12.2 12.4 %collective-permute-start.6 = (bf16[4,16,1408]{2,1,0:T(8,128)(2,1)S(1)}, bf16[4,16,1408]{2,1,0:T(8,128)(2,1)S(1)}, u32[]{:S(2)}, u32[]{:S(2)}) collective-permute-start(bf16[4,16,1408]{2,1,0:T(8,128)(2,1)S(1)} %shard_map.373.refs_0_), channel_id=1, source_target_pairs={{0,1},{1,0},{2,3},{3,2},{4,5},{5,4},{6,7},{7,6},{8,9},{9,8},{10,11... | collective-permute-start | bytes 540680 | tf_op jit(solution)/shard_map/ppermute | solution.py:643
  12.3 8.4 %collective-permute-start.5 = (bf16[4,16,1408]{2,1,0:T(8,128)(2,1)S(1)}, bf16[4,16,1408]{2,1,0:T(8,128)(2,1)S(1)}, u32[]{:S(2)}, u32[]{:S(2)}) collective-permute-start(bf16[4,16,1408]{2,1,0:T(8,128)(2,1)S(1)} %shard_map.373.refs_0_), channel_id=1, source_target_pairs={{0,24},{1,25},{2,26},{3,27},{4,28},{5,29},{6,30},{7,31},{8,16},{9,... | collective-permute-start | bytes 540680 | tf_op jit(solution)/shard_map/ppermute | solution.py:643
  14.8 9.2 %collective-permute-start.4 = (bf16[4,16,1408]{2,1,0:T(8,128)(2,1)S(1)}, bf16[4,16,1408]{2,1,0:T(8,128)(2,1)S(1)}, u32[]{:S(2)}, u32[]{:S(2)}) collective-permute-start(bf16[4,16,1408]{2,1,0:T(8,128)(2,1)S(1)} %shard_map.373.refs_0_), channel_id=1, source_target_pairs={{0,16},{1,17},{2,18},{3,19},{4,20},{5,21},{6,22},{7,23},{8,24},{9,... | collective-permute-start | bytes 540680 | tf_op jit(solution)/shard_map/ppermute | solution.py:643
  15.3 8.8 %collective-permute-start.3 = (bf16[4,16,1408]{2,1,0:T(8,128)(2,1)S(1)}, bf16[4,16,1408]{2,1,0:T(8,128)(2,1)S(1)}, u32[]{:S(2)}, u32[]{:S(2)}) collective-permute-start(bf16[4,16,1408]{2,1,0:T(8,128)(2,1)S(1)} %shard_map.373.refs_0_), channel_id=1, source_target_pairs={{0,8},{1,9},{2,10},{3,11},{4,12},{5,13},{6,14},{7,15},{8,0},{9,1},... | collective-permute-start | bytes 540680 | tf_op jit(solution)/shard_map/ppermute | solution.py:643
  16.4 8.2 %collective-permute-start.10 = (bf16[12,48,256]{2,1,0:T(8,128)(2,1)S(1)}, bf16[12,48,256]{2,1,0:T(8,128)(2,1)S(1)}, u32[]{:S(2)}, u32[]{:S(2)}) collective-permute-start(bf16[12,48,256]{2,1,0:T(8,128)(2,1)S(1)} %get-tuple-element.117), channel_id=1, source_target_pairs={{1,2},{2,1},{3,4},{4,3},{5,6},{6,5},{9,10},{10,9},{11,12},{12,11},... | collective-permute-start | bytes 884744 | tf_op jit(solution)/shard_map/ppermute | solution.py:751
  20.7 4.0 %collective-permute-start.11 = (bf16[12,48,256]{2,1,0:T(8,128)(2,1)S(1)}, bf16[12,48,256]{2,1,0:T(8,128)(2,1)S(1)}, u32[]{:S(2)}, u32[]{:S(2)}) collective-permute-start(bf16[12,48,256]{2,1,0:T(8,128)(2,1)S(1)} %get-tuple-element.118), channel_id=1, source_target_pairs={{0,1},{1,0},{2,3},{3,2},{4,5},{5,4},{6,7},{7,6},{8,9},{9,8},{10,11... | collective-permute-start | bytes 884744 | tf_op jit(solution)/shard_map/ppermute | solution.py:750
  24.2 1.4 %collective-permute-start.7 = (bf16[4,16,1408]{2,1,0:T(8,128)(2,1)S(1)}, bf16[4,16,1408]{2,1,0:T(8,128)(2,1)S(1)}, u32[]{:S(2)}, u32[]{:S(2)}) collective-permute-start(bf16[4,16,1408]{2,1,0:T(8,128)(2,1)S(1)} %collective-permute-done.3.refs_1_), channel_id=1, source_target_pairs={{0,1},{1,0},{2,3},{3,2},{4,5},{5,4},{6,7},{7,6},{8,9},{9,8},{10,11... | collective-permute-start | bytes 540680 | tf_op jit(solution)/shard_map/ppermute | solution.py:643
  24.2 1.7 %collective-permute-start.8 = (bf16[4,16,1408]{2,1,0:T(8,128)(2,1)S(1)}, bf16[4,16,1408]{2,1,0:T(8,128)(2,1)S(1)}, u32[]{:S(2)}, u32[]{:S(2)}) collective-permute-start(bf16[4,16,1408]{2,1,0:T(8,128)(2,1)S(1)} %collective-permute-done.4.refs_2_), channel_id=1, source_target_pairs={{0,1},{1,0},{2,3},{3,2},{4,5},{5,4},{6,7},{7,6},{8,9},{9,8},{10,11... | collective-permute-start | bytes 540680 | tf_op jit(solution)/shard_map/ppermute | solution.py:643
  24.7 1.4 %collective-permute-start.9 = (bf16[4,16,1408]{2,1,0:T(8,128)(2,1)S(1)}, bf16[4,16,1408]{2,1,0:T(8,128)(2,1)S(1)}, u32[]{:S(2)}, u32[]{:S(2)}) collective-permute-start(bf16[4,16,1408]{2,1,0:T(8,128)(2,1)S(1)} %collective-permute-done.5.refs_3_), channel_id=1, source_target_pairs={{0,1},{1,0},{2,3},{3,2},{4,5},{5,4},{6,7},{7,6},{8,9},{9,8},{10,11... | collective-permute-start | bytes 540680 | tf_op jit(solution)/shard_map/ppermute | solution.py:643
  38.9 2.3 %collective-permute-start.12 = (bf16[16,16,1408]{2,1,0:T(8,128)(2,1)S(1)}, bf16[16,16,1408]{2,1,0:T(8,128)(2,1)S(1)}, u32[]{:S(2)}, u32[]{:S(2)}) collective-permute-start(bf16[16,16,1408]{2,1,0:T(8,128)(2,1)S(1)} %slice.40), channel_id=1, source_target_pairs={{0,1},{1,0},{2,3},{3,2},{4,5},{5,4},{6,7},{7,6},{8,9},{9,8},{10,11... | collective-permute-start | bytes 2162696 | tf_op jit(solution)/shard_map/ppermute | solution.py:643
  41.4 7.4 %collective-permute-start.13 = (bf16[4,16,1408]{2,1,0:T(8,128)(2,1)S(1)}, bf16[4,16,1408]{2,1,0:T(8,128)(2,1)S(1)}, u32[]{:S(2)}, u32[]{:S(2)}) collective-permute-start(bf16[4,16,1408]{2,1,0:T(8,128)(2,1)S(1)} %get-tuple-element.184), channel_id=1, source_target_pairs={{0,8},{1,9},{2,10},{3,11},{4,12},{5,13},{6,14},{7,15},{8,0},{9,1},... | collective-permute-start | bytes 540680 | tf_op jit(solution)/shard_map/ppermute | solution.py:643
  42.9 10.1 %collective-permute-start.15 = (bf16[4,16,1408]{2,1,0:T(8,128)(2,1)S(1)}, bf16[4,16,1408]{2,1,0:T(8,128)(2,1)S(1)}, u32[]{:S(2)}, u32[]{:S(2)}) collective-permute-start(bf16[4,16,1408]{2,1,0:T(8,128)(2,1)S(1)} %get-tuple-element.185), channel_id=1, source_target_pairs={{0,24},{1,25},{2,26},{3,27},{4,28},{5,29},{6,30},{7,31},{8,16},{9,... | collective-permute-start | bytes 540680 | tf_op jit(solution)/shard_map/ppermute | solution.py:643
  44.3 10.0 %collective-permute-start.14 = (bf16[4,16,1408]{2,1,0:T(8,128)(2,1)S(1)}, bf16[4,16,1408]{2,1,0:T(8,128)(2,1)S(1)}, u32[]{:S(2)}, u32[]{:S(2)}) collective-permute-start(bf16[4,16,1408]{2,1,0:T(8,128)(2,1)S(1)} %get-tuple-element.186), channel_id=1, source_target_pairs={{0,16},{1,17},{2,18},{3,19},{4,20},{5,21},{6,22},{7,23},{8,24},{9,... | collective-permute-start | bytes 540680 | tf_op jit(solution)/shard_map/ppermute | solution.py:643
  44.9 14.0 %collective-permute-start.16 = (bf16[640,512]{1,0:T(8,128)(2,1)S(1)}, bf16[640,512]{1,0:T(8,128)(2,1)S(1)}, u32[]{:S(2)}, u32[]{:S(2)}) collective-permute-start(bf16[640,512]{1,0:T(8,128)(2,1)S(1)} %get-tuple-element.129), channel_id=1, source_target_pairs={{0,1},{1,0},{2,3},{3,2},{4,5},{5,4},{6,7},{7,6},{8,9},{9,8},{10,11... | collective-permute-start | bytes 1966088 | tf_op jit(solution)/shard_map/ppermute | solution.py:750
  44.9 14.0 %collective-permute-start.17 = (bf16[640,512]{1,0:T(8,128)(2,1)S(1)}, bf16[640,512]{1,0:T(8,128)(2,1)S(1)}, u32[]{:S(2)}, u32[]{:S(2)}) collective-permute-start(bf16[640,512]{1,0:T(8,128)(2,1)S(1)} %get-tuple-element.130), channel_id=1, source_target_pairs={{1,2},{2,1},{3,4},{4,3},{5,6},{6,5},{9,10},{10,9},{11,12},{12,11},... | collective-permute-start | bytes 1966088 | tf_op jit(solution)/shard_map/ppermute | solution.py:751
  54.5 7.4 %collective-permute-start.20 = (bf16[16,1408]{1,0:T(8,128)(2,1)S(1)}, bf16[16,1408]{1,0:T(8,128)(2,1)S(1)}, u32[]{:S(2)}, u32[]{:S(2)}) collective-permute-start(bf16[16,1408]{1,0:T(8,128)(2,1)S(1)} %get-tuple-element.187), channel_id=1, source_target_pairs={{0,6},{1,7},{2,4},{3,5},{4,2},{5,3},{6,0},{7,1},{8,14},{9,15},{10,... | collective-permute-start | bytes 135176 | tf_op jit(solution)/shard_map/ppermute | solution.py:643
  56.7 5.3 %collective-permute-start.19 = (bf16[16,1408]{1,0:T(8,128)(2,1)S(1)}, bf16[16,1408]{1,0:T(8,128)(2,1)S(1)}, u32[]{:S(2)}, u32[]{:S(2)}) collective-permute-start(bf16[16,1408]{1,0:T(8,128)(2,1)S(1)} %get-tuple-element.188), channel_id=1, source_target_pairs={{0,4},{1,5},{2,6},{3,7},{4,0},{5,1},{6,2},{7,3},{8,12},{9,13},{10,... | collective-permute-start | bytes 135176 | tf_op jit(solution)/shard_map/ppermute | solution.py:643
  56.7 5.3 %collective-permute-start.18 = (bf16[16,1408]{1,0:T(8,128)(2,1)S(1)}, bf16[16,1408]{1,0:T(8,128)(2,1)S(1)}, u32[]{:S(2)}, u32[]{:S(2)}) collective-permute-start(bf16[16,1408]{1,0:T(8,128)(2,1)S(1)} %get-tuple-element.189), channel_id=1, source_target_pairs={{0,2},{1,3},{2,0},{3,1},{4,6},{5,7},{6,4},{7,5},{8,10},{9,11},{10,... | collective-permute-start | bytes 135176 | tf_op jit(solution)/shard_map/ppermute | solution.py:643
  59.0 3.0 %copy-start = (f32[8,768]{1,0:T(8,128)S(1)}, f32[8,768]{1,0:T(8,128)}, u32[]{:S(2)}) copy-start(f32[8,768]{1,0:T(8,128)} %refs_4_.3) | copy-start | bytes 73732
  59.0 3.0 %copy-start.1 = (f32[8,768]{1,0:T(8,128)S(1)}, f32[8,768]{1,0:T(8,128)}, u32[]{:S(2)}) copy-start(f32[8,768]{1,0:T(8,128)} %refs_6_.3) | copy-start | bytes 73732
  59.0 3.0 %copy-start.2 = (f32[24,256]{1,0:T(8,128)S(1)}, f32[24,256]{1,0:T(8,128)}, u32[]{:S(2)}) copy-start(f32[24,256]{1,0:T(8,128)} %refs_7_.3) | copy-start | bytes 73732
  59.0 3.0 %copy-start.3 = (f32[8,768]{1,0:T(8,128)S(1)}, f32[8,768]{1,0:T(8,128)}, u32[]{:S(2)}) copy-start(f32[8,768]{1,0:T(8,128)} %refs_10_.3) | copy-start | bytes 73732
  59.0 3.0 %copy-start.4 = (f32[8,768]{1,0:T(8,128)S(1)}, f32[8,768]{1,0:T(8,128)}, u32[]{:S(2)}) copy-start(f32[8,768]{1,0:T(8,128)} %refs_12_.3) | copy-start | bytes 73732
  59.0 3.0 %copy-start.5 = (f32[24,256]{1,0:T(8,128)S(1)}, f32[24,256]{1,0:T(8,128)}, u32[]{:S(2)}) copy-start(f32[24,256]{1,0:T(8,128)} %refs_13_.3) | copy-start | bytes 73732
  59.0 3.0 %copy-start.6 = (f32[8,768]{1,0:T(8,128)S(1)}, f32[8,768]{1,0:T(8,128)}, u32[]{:S(2)}) copy-start(f32[8,768]{1,0:T(8,128)} %refs_2_.1) | copy-start | bytes 73732
  59.1 3.0 %copy-start.7 = (f32[8,768]{1,0:T(8,128)S(1)}, f32[8,768]{1,0:T(8,128)}, u32[]{:S(2)}) copy-start(f32[8,768]{1,0:T(8,128)} %refs_0_.1) | copy-start | bytes 73732
  59.1 3.0 %copy-start.8 = (f32[24,256]{1,0:T(8,128)S(1)}, f32[24,256]{1,0:T(8,128)}, u32[]{:S(2)}) copy-start(f32[24,256]{1,0:T(8,128)} %refs_3_.1) | copy-start | bytes 73732
  59.1 3.0 %copy-start.9 = (f32[8,256]{1,0:T(8,128)S(1)}, f32[8,256]{1,0:T(8,128)}, u32[]{:S(2)}) copy-start(f32[8,256]{1,0:T(8,128)} %refs_5_.4) | copy-start | bytes 24580
  59.1 3.0 %copy-start.10 = (f32[8,256]{1,0:T(8,128)S(1)}, f32[8,256]{1,0:T(8,128)}, u32[]{:S(2)}) copy-start(f32[8,256]{1,0:T(8,128)} %refs_11_.3) | copy-start | bytes 24580
  59.1 3.0 %copy-start.11 = (f32[8,256]{1,0:T(8,128)S(1)}, f32[8,256]{1,0:T(8,128)}, u32[]{:S(2)}) copy-start(f32[8,256]{1,0:T(8,128)} %refs_1_.1) | copy-start | bytes 24580
  59.1 3.0 %copy-start.12 = (f32[11,8]{0,1:T(8,128)S(1)}, f32[11,8]{0,1:T(8,128)}, u32[]{:S(2)}) copy-start(f32[11,8]{0,1:T(8,128)} %param.38) | copy-start | bytes 1060
  59.1 3.0 %copy-start.13 = (f32[8,49]{1,0:T(8,128)S(1)}, f32[8,49]{1,0:T(8,128)}, u32[]{:S(2)}) copy-start(f32[8,49]{1,0:T(8,128)} %refs_9_.4) | copy-start | bytes 4708
  59.1 3.0 %copy-start.14 = (f32[11,8]{0,1:T(8,128)S(1)}, f32[11,8]{0,1:T(8,128)}, u32[]{:S(2)}) copy-start(f32[11,8]{0,1:T(8,128)} %param.39) | copy-start | bytes 1060
  59.2 3.0 %copy-start.15 = (f32[8,49]{1,0:T(8,128)S(1)}, f32[8,49]{1,0:T(8,128)}, u32[]{:S(2)}) copy-start(f32[8,49]{1,0:T(8,128)} %refs_15_.3) | copy-start | bytes 4708
  59.2 3.0 %copy-start.16 = (f32[11,8]{0,1:T(8,128)S(1)}, f32[11,8]{0,1:T(8,128)}, u32[]{:S(2)}) copy-start(f32[11,8]{0,1:T(8,128)} %param.28) | copy-start | bytes 1060
  59.2 3.0 %copy-start.18 = (f32[8,49]{1,0:T(8,128)S(1)}, f32[8,49]{1,0:T(8,128)}, u32[]{:S(2)}) copy-start(f32[8,49]{1,0:T(8,128)} %refs_5_.5) | copy-start | bytes 4708
  62.5 1.2 %collective-permute-start.21 = (f32[8,128]{1,0:T(8,128)S(1)}, f32[8,128]{1,0:T(8,128)S(1)}, u32[]{:S(2)}, u32[]{:S(2)}) collective-permute-start(f32[8,128]{1,0:T(8,128)S(1)} %get-tuple-element.142.mine_ref), channel_id=1, source_target_pairs={{0,1},{1,0},{2,3},{3,2},{4,5},{5,4},{6,7},{7,6},{8,9},{9,8},{10,11... | collective-permute-start | bytes 12296 | tf_op jit(solution)/shard_map/ppermute | solution.py:643
  63.6 4.5 %collective-permute-start.24 = (f32[8,128]{1,0:T(8,128)S(1)}, f32[8,128]{1,0:T(8,128)S(1)}, u32[]{:S(2)}, u32[]{:S(2)}) collective-permute-start(f32[8,128]{1,0:T(8,128)S(1)} %add.66), channel_id=1, source_target_pairs={{0,24},{1,25},{2,26},{3,27},{4,28},{5,29},{6,30},{7,31},{8,16},{9,... | collective-permute-start | bytes 12296 | tf_op jit(solution)/shard_map/ppermute | solution.py:643
  65.2 3.6 %collective-permute-start.23 = (f32[8,128]{1,0:T(8,128)S(1)}, f32[8,128]{1,0:T(8,128)S(1)}, u32[]{:S(2)}, u32[]{:S(2)}) collective-permute-start(f32[8,128]{1,0:T(8,128)S(1)} %add.66), channel_id=1, source_target_pairs={{0,16},{1,17},{2,18},{3,19},{4,20},{5,21},{6,22},{7,23},{8,24},{9,... | collective-permute-start | bytes 12296 | tf_op jit(solution)/shard_map/ppermute | solution.py:643
  66.5 3.6 %collective-permute-start.22 = (f32[8,128]{1,0:T(8,128)S(1)}, f32[8,128]{1,0:T(8,128)S(1)}, u32[]{:S(2)}, u32[]{:S(2)}) collective-permute-start(f32[8,128]{1,0:T(8,128)S(1)} %add.66), channel_id=1, source_target_pairs={{0,8},{1,9},{2,10},{3,11},{4,12},{5,13},{6,14},{7,15},{8,0},{9,1},... | collective-permute-start | bytes 12296 | tf_op jit(solution)/shard_map/ppermute | solution.py:643
  70.1 5.4 %collective-permute-start.27 = (f32[8,128]{1,0:T(8,128)S(1)}, f32[8,128]{1,0:T(8,128)S(1)}, u32[]{:S(2)}, u32[]{:S(2)}) collective-permute-start(f32[8,128]{1,0:T(8,128)S(1)} %add_add_fusion.a_ref), channel_id=1, source_target_pairs={{0,6},{1,7},{2,4},{3,5},{4,2},{5,3},{6,0},{7,1},{8,14},{9,15},{10,... | collective-permute-start | bytes 12296 | tf_op jit(solution)/shard_map/ppermute | solution.py:643
  72.0 4.5 %collective-permute-start.26 = (f32[8,128]{1,0:T(8,128)S(1)}, f32[8,128]{1,0:T(8,128)S(1)}, u32[]{:S(2)}, u32[]{:S(2)}) collective-permute-start(f32[8,128]{1,0:T(8,128)S(1)} %add_add_fusion.a_ref), channel_id=1, source_target_pairs={{0,4},{1,5},{2,6},{3,7},{4,0},{5,1},{6,2},{7,3},{8,12},{9,13},{10,... | collective-permute-start | bytes 12296 | tf_op jit(solution)/shard_map/ppermute | solution.py:643
  72.0 4.5 %collective-permute-start.25 = (f32[8,128]{1,0:T(8,128)S(1)}, f32[8,128]{1,0:T(8,128)S(1)}, u32[]{:S(2)}, u32[]{:S(2)}) collective-permute-start(f32[8,128]{1,0:T(8,128)S(1)} %add_add_fusion.a_ref), channel_id=1, source_target_pairs={{0,2},{1,3},{2,0},{3,1},{4,6},{5,7},{6,4},{7,5},{8,10},{9,11},{10,... | collective-permute-start | bytes 12296 | tf_op jit(solution)/shard_map/ppermute | solution.py:643

commit v9 on v8

--- a/solution.py
+++ b/solution.py
@@ -170,7 +170,7 @@
         xk_ref[pl.ds(pl.multiple_of(rc * 512, 512), 512), :] = normed(xk)[0]
         return 0
 
-    lax.fori_loop(0, 4, block, 0, unroll=2)
+    lax.fori_loop(0, 4, block, 0, unroll=4)
 
 
 def project_kernel(xhat_ref, xk_ref, wqkv_ref, vec_ref, q_ref, k_ref, v_ref):
@@ -187,7 +187,7 @@
         v_ref[at, :] = (dot(a1k, wqkv_ref[:, 512:768]) + vrow(3)).astype(BF)
         return 0
 
-    lax.fori_loop(0, 4, block, 0, unroll=2)
+    lax.fori_loop(0, 4, block, 0, unroll=4)
 
 
 def attend_kernel(limits_ref, bias_ref, q_ref, k_ref, v_ref, mixed_ref, p_ref, other_ref):
@@ -525,8 +525,8 @@
     attend_kernel(limits, bias, q, k, v, mixed, p, other)
     feed_kernel(dy, dysum, mixed, xp, big_out, big_up, big_down, vec, act, dz, a2, da, dx1, x1, dmix, sums, zsum, xhat1, rstd1)
     back_kernel(q, v, p, dmix, own, rimc, rimz, dsl, tacc, dkv)
+    late_grads(dsl, k, tacc, xhat, xk, dkv, big_qkv, vt, sums, zsum, dq, fq, fv, tgrad)
     early_grads(act, dy, a2, dz, mixed, da, fd, fu, fo)
-    late_grads(dsl, k, tacc, xhat, xk, dkv, big_qkv, vt, sums, zsum, dq, fq, fv, tgrad)
     table = tgrad[...]
     me = own_index()
     for o in range(32):

time: 77.6 us -> 76.5 us (0.986)
  Pallas kernels: 21.1 us -> 19.9 us
    pallas_call x9, Pallas kernels: 21.1 us -> 19.9 us  [call(): pl.pallas_call(kernel, out_shape=out_shape, in_specs=specs, out_specs=jax...]
  transfers between devices with their start and end apart: 28 -> 28, of which waited for: 18 -> 18; matrix products, arithmetic and copies ran while one was open for 0% -> 0% of each run, Pallas kernels for 9% -> 10%
where the time goes in v9:
time: 76.5 us; the launch traced here: 76.2 us
  starting transfers between devices  27.7 us (36%)
  waiting for transfers between devices  24 us (31%)
  Pallas kernels  19.9 us (26%)
  local copies, waits for them, and re-layouts  2.32 us (3%)
  other arithmetic  1.12 us (1%)
  between operations  1.09 us (1%)
    ppermute x24, starting transfers between devices, swap(): return lax.ppermute(block, AXES, [(k, k ^ mask) for k in range(count)])  26.1 us
    ppermute x24, waiting for transfers between devices, swap(): return lax.ppermute(block, AXES, [(k, k ^ mask) for k in range(count)])  24 us
    pallas_call x9, Pallas kernels, call(): pl.pallas_call(kernel, out_shape=out_shape, in_specs=specs, out_specs=jax...  19.9 us
    ppermute x2, starting transfers between devices, beside(): lax.ppermute(block[1], 'band', [(b, to) for b, to in touching if 0 <= to...  1.55 us
  transfers between devices with their start and end apart: 28, of which 18 were waited for; matrix products, arithmetic and copies ran while one was open for 0% of the time, Pallas kernels for 10%

profile of v9, /device:TPU:0, one launch (start us, length us, event | category | flops | bytes accessed | tf_op | source)
XLA Modules:
  0.0 76.2 jit_solution(6287419260414702072)
XLA Ops:
  0.7 0.7 fusion.4
  1.4 0.8 %add_convert_fusion.refs_0_ = bf16[16,1408]{1,0:T(8,128)(2,1)S(1)} fusion(f32[8,256]{1,0:T(8,128)S(1)} %get-tuple-element.191, f32[8,256]{1,0:T(8,128)S(1)} %get-tuple-element.192, f32[8,768]{1,0:T(8,128)} %refs_2_.1, f32[8,11]{1,0:T(8,128)} %bitcast.20, f32[8,256]{1,0:T(8,128)S(1)} %get-tuple-element.190, f32[8,256]{1,0:T(8,128)} %refs_1_.1, f32[8,768]{1,0:T(8,128)} %refs_0_.1), kind=kLoop, calls=%fused_computation.5 | loop fusion | flops 157696 | bytes 127328 | tf_op jit(solution)/shard_map/convert_element_type | solution.py:489
  2.2 5.1 %collective-permute-start.2 = (bf16[16,1408]{1,0:T(8,128)(2,1)S(1)}, bf16[16,1408]{1,0:T(8,128)(2,1)S(1)}, u32[]{:S(2)}, u32[]{:S(2)}) collective-permute-start(bf16[16,1408]{1,0:T(8,128)(2,1)S(1)} %add_convert_fusion.refs_0_), channel_id=1, source_target_pairs={{0,6},{1,7},{2,4},{3,5},{4,2},{5,3},{6,0},{7,1},{8,14},{9,15},{10,... | collective-permute-start | bytes 135176 | tf_op jit(solution)/shard_map/ppermute | solution.py:643
  7.3 0.6 collective-permute-start
  7.9 0.7 copy-done.17
  8.6 0.7 copy-done.21
  9.3 1.3 %shard_map.372 = (f32[128,384]{1,0:T(8,128)S(1)}, s32[8,128]{1,0:T(8,128)S(1)}, bf16[192,192]{1,0:T(8,128)(2,1)S(1)}, bf16[512,480]{1,0:T(8,128)(2,1)S(1)}) custom-call(s32[1,2]{1,0:T(1,128)S(1)} %copy-done.21, f32[8,49]{1,0:T(8,128)S(1)} %copy-done.17), custom_call_target="tpu_custom_call" | custom-call | flops 1000000000 | bytes 1000000 | tf_op jit(solution)/shard_map/pallas_call | solution.py:620
  10.6 1.6 %collective-permute-done.1.refs_2_ = bf16[16,1408]{1,0:T(8,128)(2,1)S(1)} collective-permute-done((bf16[16,1408]{1,0:T(8,128)(2,1)S(1)}, bf16[16,1408]{1,0:T(8,128)(2,1)S(1)}, u32[]{:S(2)}, u32[]{:S(2)}) %collective-permute-start.1) | collective-permute-done | bytes 45088 | tf_op jit(solution)/shard_map/ppermute | solution.py:643
  12.2 0.1 collective-permute-start.6
  12.3 2.5 %collective-permute-start.5 = (bf16[4,16,1408]{2,1,0:T(8,128)(2,1)S(1)}, bf16[4,16,1408]{2,1,0:T(8,128)(2,1)S(1)}, u32[]{:S(2)}, u32[]{:S(2)}) collective-permute-start(bf16[4,16,1408]{2,1,0:T(8,128)(2,1)S(1)} %shard_map.373.refs_0_), channel_id=1, source_target_pairs={{0,24},{1,25},{2,26},{3,27},{4,28},{5,29},{6,30},{7,31},{8,16},{9,... | collective-permute-start | bytes 540680 | tf_op jit(solution)/shard_map/ppermute | solution.py:643
  14.8 0.5 collective-permute-start.4
  15.3 0.5 collective-permute-start.3
  15.9 0.6 shard_map.374
  16.4 0.7 collective-permute-start.10
  17.1 3.5 %collective-permute-done.5.refs_3_ = bf16[4,16,1408]{2,1,0:T(8,128)(2,1)S(1)} collective-permute-done((bf16[4,16,1408]{2,1,0:T(8,128)(2,1)S(1)}, bf16[4,16,1408]{2,1,0:T(8,128)(2,1)S(1)}, u32[]{:S(2)}, u32[]{:S(2)}) %collective-permute-start.5) | collective-permute-done | bytes 180256 | tf_op jit(solution)/shard_map/ppermute | solution.py:643
  20.7 3.4 %collective-permute-done.4.refs_2_ = bf16[4,16,1408]{2,1,0:T(8,128)(2,1)S(1)} collective-permute-done((bf16[4,16,1408]{2,1,0:T(8,128)(2,1)S(1)}, bf16[4,16,1408]{2,1,0:T(8,128)(2,1)S(1)}, u32[]{:S(2)}, u32[]{:S(2)}) %collective-permute-start.4) | collective-permute-done | bytes 180256 | tf_op jit(solution)/shard_map/ppermute | solution.py:643
  24.1 0.1 collective-permute-done.3.refs_1_
  24.2 0.5 collective-permute-start.8
  24.7 0.9 %collective-permute-done.7.refs_5_ = bf16[4,16,1408]{2,1,0:T(8,128)(2,1)S(1)} collective-permute-done((bf16[4,16,1408]{2,1,0:T(8,128)(2,1)S(1)}, bf16[4,16,1408]{2,1,0:T(8,128)(2,1)S(1)}, u32[]{:S(2)}, u32[]{:S(2)}) %collective-permute-start.7) | collective-permute-done | bytes 180256 | tf_op jit(solution)/shard_map/ppermute | solution.py:643
  25.6 0.3 collective-permute-done.8.refs_6_
  25.8 0.3 collective-permute-done.9.refs_7_
  26.1 11.6 %shard_map.375 = (bf16[768,768]{1,0:T(8,128)(2,1)S(1)}, f32[768,256]{1,0:T(8,128)S(1)}, f32[768,256]{1,0:T(8,128)S(1)}, f32[768,512]{1,0:T(8,128)S(1)}, bf16[640...) custom-call(bf16[4,16,1408]{2,1,0:T(8,128)(2,1)S(1)} %shard_map.373., ...), custom_call_target="tpu_custom_call" | custom-call | flops 15000000512 | bytes 1000000 | tf_op jit(solution)/shard_map/pallas_call | solution.py:620
  37.7 0.1 slice.40
  37.7 0.3 collective-permute-start.12
  38.1 1.9 %collective-permute-done.12 = bf16[16,16,1408]{2,1,0:T(8,128)(2,1)S(1)} collective-permute-done((bf16[16,16,1408]{2,1,0:T(8,128)(2,1)S(1)}, bf16[16,16,1408]{2,1,0:T(8,128)(2,1)S(1)}, u32[]{:S(2)}, u32[]{:S(2)}) %collective-permute-start.12) | collective-permute-done | bytes 720928 | tf_op jit(solution)/shard_map/ppermute | solution.py:643
  40.0 0.2 fusion.2
  40.3 1.6 %collective-permute-start.13 = (bf16[4,16,1408]{2,1,0:T(8,128)(2,1)S(1)}, bf16[4,16,1408]{2,1,0:T(8,128)(2,1)S(1)}, u32[]{:S(2)}, u32[]{:S(2)}) collective-permute-start(bf16[4,16,1408]{2,1,0:T(8,128)(2,1)S(1)} %get-tuple-element.184), channel_id=1, source_target_pairs={{0,8},{1,9},{2,10},{3,11},{4,12},{5,13},{6,14},{7,15},{8,0},{9,1},... | collective-permute-start | bytes 540680 | tf_op jit(solution)/shard_map/ppermute | solution.py:643
  41.8 1.4 %collective-permute-start.15 = (bf16[4,16,1408]{2,1,0:T(8,128)(2,1)S(1)}, bf16[4,16,1408]{2,1,0:T(8,128)(2,1)S(1)}, u32[]{:S(2)}, u32[]{:S(2)}) collective-permute-start(bf16[4,16,1408]{2,1,0:T(8,128)(2,1)S(1)} %get-tuple-element.185), channel_id=1, source_target_pairs={{0,24},{1,25},{2,26},{3,27},{4,28},{5,29},{6,30},{7,31},{8,16},{9,... | collective-permute-start | bytes 540680 | tf_op jit(solution)/shard_map/ppermute | solution.py:643
  43.2 0.6 collective-permute-start.14
  43.8 0.9 %collective-permute-start.17 = (bf16[640,512]{1,0:T(8,128)(2,1)S(1)}, bf16[640,512]{1,0:T(8,128)(2,1)S(1)}, u32[]{:S(2)}, u32[]{:S(2)}) collective-permute-start(bf16[640,512]{1,0:T(8,128)(2,1)S(1)} %get-tuple-element.130), channel_id=1, source_target_pairs={{1,2},{2,1},{3,4},{4,3},{5,6},{6,5},{9,10},{10,9},{11,12},{12,11},... | collective-permute-start | bytes 1966088 | tf_op jit(solution)/shard_map/ppermute | solution.py:751
  44.7 2.0 %shard_map.377 = bf16[16,48,256]{2,1,0:T(8,128)(2,1)} custom-call(f32[768,256]{1,0:T(8,128)S(1)} %get-tuple-element.136.x1_ref, bf16[768,768]{1,0:T(8,128)(2,1)S(1)} %get-tuple-element.137.act_ref, bf16[768,256]{1,0:T(8,128)(2,1)S(1)} %get-tuple-element.138.wd_ref, f32[11,256]{1,0:T(8,128)S(1)} %get-tuple-element.135.vec_ref, ...), custom_call_target="tpu_custom_call" | custom-call | flops 1000000000 | bytes 1000000 | tf_op jit(solution)/shard_map/pallas_call | solution.py:620
  46.7 1.0 %collective-permute-done.13 = bf16[4,16,1408]{2,1,0:T(8,128)(2,1)S(1)} collective-permute-done((bf16[4,16,1408]{2,1,0:T(8,128)(2,1)S(1)}, bf16[4,16,1408]{2,1,0:T(8,128)(2,1)S(1)}, u32[]{:S(2)}, u32[]{:S(2)}) %collective-permute-start.13) | collective-permute-done | bytes 180256 | tf_op jit(solution)/shard_map/ppermute | solution.py:643
  47.7 4.2 %collective-permute-done.15 = bf16[4,16,1408]{2,1,0:T(8,128)(2,1)S(1)} collective-permute-done((bf16[4,16,1408]{2,1,0:T(8,128)(2,1)S(1)}, bf16[4,16,1408]{2,1,0:T(8,128)(2,1)S(1)}, u32[]{:S(2)}, u32[]{:S(2)}) %collective-permute-start.15) | collective-permute-done | bytes 180256 | tf_op jit(solution)/shard_map/ppermute | solution.py:643
  51.9 1.4 %collective-permute-done.14 = bf16[4,16,1408]{2,1,0:T(8,128)(2,1)S(1)} collective-permute-done((bf16[4,16,1408]{2,1,0:T(8,128)(2,1)S(1)}, bf16[4,16,1408]{2,1,0:T(8,128)(2,1)S(1)}, u32[]{:S(2)}, u32[]{:S(2)}) %collective-permute-start.14) | collective-permute-done | bytes 180256 | tf_op jit(solution)/shard_map/ppermute | solution.py:643
  53.2 0.1 fusion.1
  53.4 2.2 %collective-permute-start.20 = (bf16[16,1408]{1,0:T(8,128)(2,1)S(1)}, bf16[16,1408]{1,0:T(8,128)(2,1)S(1)}, u32[]{:S(2)}, u32[]{:S(2)}) collective-permute-start(bf16[16,1408]{1,0:T(8,128)(2,1)S(1)} %get-tuple-element.187), channel_id=1, source_target_pairs={{0,6},{1,7},{2,4},{3,5},{4,2},{5,3},{6,0},{7,1},{8,14},{9,15},{10,... | collective-permute-start | bytes 135176 | tf_op jit(solution)/shard_map/ppermute | solution.py:643
  55.5 2.3 %collective-permute-start.18 = (bf16[16,1408]{1,0:T(8,128)(2,1)S(1)}, bf16[16,1408]{1,0:T(8,128)(2,1)S(1)}, u32[]{:S(2)}, u32[]{:S(2)}) collective-permute-start(bf16[16,1408]{1,0:T(8,128)(2,1)S(1)} %get-tuple-element.189), channel_id=1, source_target_pairs={{0,2},{1,3},{2,0},{3,1},{4,6},{5,7},{6,4},{7,5},{8,10},{9,11},{10,... | collective-permute-start | bytes 135176 | tf_op jit(solution)/shard_map/ppermute | solution.py:643
  57.8 0.0 copy-start
  57.9 0.0 copy-start.1
  57.9 0.0 copy-start.4
  57.9 0.0 copy-start.5
  57.9 0.0 copy-start.8
  58.0 0.0 copy-start.9
  58.0 0.0 copy-start.12
  58.0 0.0 copy-start.13
  58.0 0.0 copy-start.16
  58.0 0.0 copy-start.18
  58.1 2.7 %shard_map.376 = bf16[16,48,256]{2,1,0:T(8,128)(2,1)} custom-call(f32[768,512]{1,0:T(8,128)S(1)} %get-tuple-element.128.own_ref, bf16[640,512]{1,0:T(8,128)(2,1)S(1)} %collective-permute-done.16.gotc_ref, bf16[640,512]{1,0:T(8,128)(2,1)S(1)} %collective-permute-done.17.gotz_ref, bf16[768,256]{1,0:T(8,128)(2,1)S(1)} %get-tuple-element.131.dq_ref, ...), custom_call_target="tpu_custom_call" | custom-call | flops 1000000000 | bytes 1000000 | tf_op jit(solution)/shard_map/pallas_call | solution.py:620
  60.7 0.1 collective-permute-done.19.refs_2_
  61.0 0.3 shard_map.378
  61.3 0.0 collective-permute-start.21
  61.4 1.2 %collective-permute-done.21 = f32[8,128]{1,0:T(8,128)S(1)} collective-permute-done((f32[8,128]{1,0:T(8,128)S(1)}, f32[8,128]{1,0:T(8,128)S(1)}, u32[]{:S(2)}, u32[]{:S(2)}) %collective-permute-start.21) | collective-permute-done | bytes 4128 | tf_op jit(solution)/shard_map/ppermute | solution.py:643
  62.5 1.5 %collective-permute-start.24 = (f32[8,128]{1,0:T(8,128)S(1)}, f32[8,128]{1,0:T(8,128)S(1)}, u32[]{:S(2)}, u32[]{:S(2)}) collective-permute-start(f32[8,128]{1,0:T(8,128)S(1)} %add.66), channel_id=1, source_target_pairs={{0,24},{1,25},{2,26},{3,27},{4,28},{5,29},{6,30},{7,31},{8,16},{9,... | collective-permute-start | bytes 12296 | tf_op jit(solution)/shard_map/ppermute | solution.py:643
  64.1 1.3 %collective-permute-start.23 = (f32[8,128]{1,0:T(8,128)S(1)}, f32[8,128]{1,0:T(8,128)S(1)}, u32[]{:S(2)}, u32[]{:S(2)}) collective-permute-start(f32[8,128]{1,0:T(8,128)S(1)} %add.66), channel_id=1, source_target_pairs={{0,16},{1,17},{2,18},{3,19},{4,20},{5,21},{6,22},{7,23},{8,24},{9,... | collective-permute-start | bytes 12296 | tf_op jit(solution)/shard_map/ppermute | solution.py:643
  65.3 0.7 collective-permute-start.22
  66.0 1.0 %collective-permute-done.24 = f32[8,128]{1,0:T(8,128)S(1)} collective-permute-done((f32[8,128]{1,0:T(8,128)S(1)}, f32[8,128]{1,0:T(8,128)S(1)}, u32[]{:S(2)}, u32[]{:S(2)}) %collective-permute-start.24) | collective-permute-done | bytes 4128 | tf_op jit(solution)/shard_map/ppermute | solution.py:643
  67.0 0.6 collective-permute-done.23
  67.7 1.3 %collective-permute-done.22 = f32[8,128]{1,0:T(8,128)S(1)} collective-permute-done((f32[8,128]{1,0:T(8,128)S(1)}, f32[8,128]{1,0:T(8,128)S(1)}, u32[]{:S(2)}, u32[]{:S(2)}) %collective-permute-start.22) | collective-permute-done | bytes 4128 | tf_op jit(solution)/shard_map/ppermute | solution.py:643
  69.0 1.9 %collective-permute-start.27 = (f32[8,128]{1,0:T(8,128)S(1)}, f32[8,128]{1,0:T(8,128)S(1)}, u32[]{:S(2)}, u32[]{:S(2)}) collective-permute-start(f32[8,128]{1,0:T(8,128)S(1)} %add_add_fusion.a_ref), channel_id=1, source_target_pairs={{0,6},{1,7},{2,4},{3,5},{4,2},{5,3},{6,0},{7,1},{8,14},{9,15},{10,... | collective-permute-start | bytes 12296 | tf_op jit(solution)/shard_map/ppermute | solution.py:643
  70.9 2.5 %collective-permute-start.25 = (f32[8,128]{1,0:T(8,128)S(1)}, f32[8,128]{1,0:T(8,128)S(1)}, u32[]{:S(2)}, u32[]{:S(2)}) collective-permute-start(f32[8,128]{1,0:T(8,128)S(1)} %add_add_fusion.a_ref), channel_id=1, source_target_pairs={{0,2},{1,3},{2,0},{3,1},{4,6},{5,7},{6,4},{7,5},{8,10},{9,11},{10,... | collective-permute-start | bytes 12296 | tf_op jit(solution)/shard_map/ppermute | solution.py:643
  73.4 0.8 %shard_map.379 = (f32[8,768]{1,0:T(8,128)}, f32[8,768]{1,0:T(8,128)}, f32[8,256]{1,0:T(8,128)}, f32[8,256]{1,0:T(8,128)}, f32[8,768]{1,0:T(8,128)}, /*index=5*/f...) custom-call(f32[16,1408]{1,0:T(8,128)S(1)} %slice_bitcast_fusion.ref, ...), custom_call_target="tpu_custom_call" | custom-call | flops 100000000 | bytes 1000000 | tf_op jit(solution)/shard_map/pallas_call | solution.py:620
  74.1 0.2 collective-permute-done.27.d_ref
  74.4 1.0 %collective-permute-done.26.c_ref = f32[8,128]{1,0:T(8,128)S(1)} collective-permute-done((f32[8,128]{1,0:T(8,128)S(1)}, f32[8,128]{1,0:T(8,128)S(1)}, u32[]{:S(2)}, u32[]{:S(2)}) %collective-permute-start.26) | collective-permute-done | bytes 4128 | tf_op jit(solution)/shard_map/ppermute | solution.py:643
  75.4 0.8 shard_map.380
  (56 shorter events, 0.2 us)
Async XLA Ops:
  2.2 8.4 %collective-permute-start.2 = (bf16[16,1408]{1,0:T(8,128)(2,1)S(1)}, bf16[16,1408]{1,0:T(8,128)(2,1)S(1)}, u32[]{:S(2)}, u32[]{:S(2)}) collective-permute-start(bf16[16,1408]{1,0:T(8,128)(2,1)S(1)} %add_convert_fusion.refs_0_), channel_id=1, source_target_pairs={{0,6},{1,7},{2,4},{3,5},{4,2},{5,3},{6,0},{7,1},{8,14},{9,15},{10,... | collective-permute-start | bytes 135176 | tf_op jit(solution)/shard_map/ppermute | solution.py:643
  7.3 4.9 %collective-permute-start.1 = (bf16[16,1408]{1,0:T(8,128)(2,1)S(1)}, bf16[16,1408]{1,0:T(8,128)(2,1)S(1)}, u32[]{:S(2)}, u32[]{:S(2)}) collective-permute-start(bf16[16,1408]{1,0:T(8,128)(2,1)S(1)} %add_convert_fusion.refs_0_), channel_id=1, source_target_pairs={{0,4},{1,5},{2,6},{3,7},{4,0},{5,1},{6,2},{7,3},{8,12},{9,13},{10,... | collective-permute-start | bytes 135176 | tf_op jit(solution)/shard_map/ppermute | solution.py:643
  7.3 4.9 %collective-permute-start = (bf16[16,1408]{1,0:T(8,128)(2,1)S(1)}, bf16[16,1408]{1,0:T(8,128)(2,1)S(1)}, u32[]{:S(2)}, u32[]{:S(2)}) collective-permute-start(bf16[16,1408]{1,0:T(8,128)(2,1)S(1)} %add_convert_fusion.refs_0_), channel_id=1, source_target_pairs={{0,2},{1,3},{2,0},{3,1},{4,6},{5,7},{6,4},{7,5},{8,10},{9,11},{10,... | collective-permute-start | bytes 135176 | tf_op jit(solution)/shard_map/ppermute | solution.py:643
  7.9 0.7 copy-start.17
  8.6 0.7 copy-start.21
  9.3 6.6 %copy-start.19 = (bf16[16,48,256]{2,1,0:T(8,128)(2,1)S(1)}, bf16[16,48,256]{2,1,0:T(8,128)(2,1)}, u32[]{:S(2)}) copy-start(bf16[16,48,256]{2,1,0:T(8,128)(2,1)} %cot_ref.1) | copy-start | bytes 1179652
  9.3 6.6 %copy-start.20 = (bf16[16,48,256]{2,1,0:T(8,128)(2,1)S(1)}, bf16[16,48,256]{2,1,0:T(8,128)(2,1)}, u32[]{:S(2)}) copy-start(bf16[16,48,256]{2,1,0:T(8,128)(2,1)} %refs_9_.2) | copy-start | bytes 1179652
  12.2 12.4 %collective-permute-start.6 = (bf16[4,16,1408]{2,1,0:T(8,128)(2,1)S(1)}, bf16[4,16,1408]{2,1,0:T(8,128)(2,1)S(1)}, u32[]{:S(2)}, u32[]{:S(2)}) collective-permute-start(bf16[4,16,1408]{2,1,0:T(8,128)(2,1)S(1)} %shard_map.373.refs_0_), channel_id=1, source_target_pairs={{0,1},{1,0},{2,3},{3,2},{4,5},{5,4},{6,7},{7,6},{8,9},{9,8},{10,11... | collective-permute-start | bytes 540680 | tf_op jit(solution)/shard_map/ppermute | solution.py:643
  12.3 8.4 %collective-permute-start.5 = (bf16[4,16,1408]{2,1,0:T(8,128)(2,1)S(1)}, bf16[4,16,1408]{2,1,0:T(8,128)(2,1)S(1)}, u32[]{:S(2)}, u32[]{:S(2)}) collective-permute-start(bf16[4,16,1408]{2,1,0:T(8,128)(2,1)S(1)} %shard_map.373.refs_0_), channel_id=1, source_target_pairs={{0,24},{1,25},{2,26},{3,27},{4,28},{5,29},{6,30},{7,31},{8,16},{9,... | collective-permute-start | bytes 540680 | tf_op jit(solution)/shard_map/ppermute | solution.py:643
  14.8 9.2 %collective-permute-start.4 = (bf16[4,16,1408]{2,1,0:T(8,128)(2,1)S(1)}, bf16[4,16,1408]{2,1,0:T(8,128)(2,1)S(1)}, u32[]{:S(2)}, u32[]{:S(2)}) collective-permute-start(bf16[4,16,1408]{2,1,0:T(8,128)(2,1)S(1)} %shard_map.373.refs_0_), channel_id=1, source_target_pairs={{0,16},{1,17},{2,18},{3,19},{4,20},{5,21},{6,22},{7,23},{8,24},{9,... | collective-permute-start | bytes 540680 | tf_op jit(solution)/shard_map/ppermute | solution.py:643
  15.3 8.8 %collective-permute-start.3 = (bf16[4,16,1408]{2,1,0:T(8,128)(2,1)S(1)}, bf16[4,16,1408]{2,1,0:T(8,128)(2,1)S(1)}, u32[]{:S(2)}, u32[]{:S(2)}) collective-permute-start(bf16[4,16,1408]{2,1,0:T(8,128)(2,1)S(1)} %shard_map.373.refs_0_), channel_id=1, source_target_pairs={{0,8},{1,9},{2,10},{3,11},{4,12},{5,13},{6,14},{7,15},{8,0},{9,1},... | collective-permute-start | bytes 540680 | tf_op jit(solution)/shard_map/ppermute | solution.py:643
  16.4 8.2 %collective-permute-start.10 = (bf16[12,48,256]{2,1,0:T(8,128)(2,1)S(1)}, bf16[12,48,256]{2,1,0:T(8,128)(2,1)S(1)}, u32[]{:S(2)}, u32[]{:S(2)}) collective-permute-start(bf16[12,48,256]{2,1,0:T(8,128)(2,1)S(1)} %get-tuple-element.117), channel_id=1, source_target_pairs={{1,2},{2,1},{3,4},{4,3},{5,6},{6,5},{9,10},{10,9},{11,12},{12,11},... | collective-permute-start | bytes 884744 | tf_op jit(solution)/shard_map/ppermute | solution.py:751
  20.7 4.0 %collective-permute-start.11 = (bf16[12,48,256]{2,1,0:T(8,128)(2,1)S(1)}, bf16[12,48,256]{2,1,0:T(8,128)(2,1)S(1)}, u32[]{:S(2)}, u32[]{:S(2)}) collective-permute-start(bf16[12,48,256]{2,1,0:T(8,128)(2,1)S(1)} %get-tuple-element.118), channel_id=1, source_target_pairs={{0,1},{1,0},{2,3},{3,2},{4,5},{5,4},{6,7},{7,6},{8,9},{9,8},{10,11... | collective-permute-start | bytes 884744 | tf_op jit(solution)/shard_map/ppermute | solution.py:750
  24.2 1.4 %collective-permute-start.7 = (bf16[4,16,1408]{2,1,0:T(8,128)(2,1)S(1)}, bf16[4,16,1408]{2,1,0:T(8,128)(2,1)S(1)}, u32[]{:S(2)}, u32[]{:S(2)}) collective-permute-start(bf16[4,16,1408]{2,1,0:T(8,128)(2,1)S(1)} %collective-permute-done.3.refs_1_), channel_id=1, source_target_pairs={{0,1},{1,0},{2,3},{3,2},{4,5},{5,4},{6,7},{7,6},{8,9},{9,8},{10,11... | collective-permute-start | bytes 540680 | tf_op jit(solution)/shard_map/ppermute | solution.py:643
  24.2 1.7 %collective-permute-start.8 = (bf16[4,16,1408]{2,1,0:T(8,128)(2,1)S(1)}, bf16[4,16,1408]{2,1,0:T(8,128)(2,1)S(1)}, u32[]{:S(2)}, u32[]{:S(2)}) collective-permute-start(bf16[4,16,1408]{2,1,0:T(8,128)(2,1)S(1)} %collective-permute-done.4.refs_2_), channel_id=1, source_target_pairs={{0,1},{1,0},{2,3},{3,2},{4,5},{5,4},{6,7},{7,6},{8,9},{9,8},{10,11... | collective-permute-start | bytes 540680 | tf_op jit(solution)/shard_map/ppermute | solution.py:643
  24.7 1.4 %collective-permute-start.9 = (bf16[4,16,1408]{2,1,0:T(8,128)(2,1)S(1)}, bf16[4,16,1408]{2,1,0:T(8,128)(2,1)S(1)}, u32[]{:S(2)}, u32[]{:S(2)}) collective-permute-start(bf16[4,16,1408]{2,1,0:T(8,128)(2,1)S(1)} %collective-permute-done.5.refs_3_), channel_id=1, source_target_pairs={{0,1},{1,0},{2,3},{3,2},{4,5},{5,4},{6,7},{7,6},{8,9},{9,8},{10,11... | collective-permute-start | bytes 540680 | tf_op jit(solution)/shard_map/ppermute | solution.py:643
  37.7 2.3 %collective-permute-start.12 = (bf16[16,16,1408]{2,1,0:T(8,128)(2,1)S(1)}, bf16[16,16,1408]{2,1,0:T(8,128)(2,1)S(1)}, u32[]{:S(2)}, u32[]{:S(2)}) collective-permute-start(bf16[16,16,1408]{2,1,0:T(8,128)(2,1)S(1)} %slice.40), channel_id=1, source_target_pairs={{0,1},{1,0},{2,3},{3,2},{4,5},{5,4},{6,7},{7,6},{8,9},{9,8},{10,11... | collective-permute-start | bytes 2162696 | tf_op jit(solution)/shard_map/ppermute | solution.py:643
  40.3 7.4 %collective-permute-start.13 = (bf16[4,16,1408]{2,1,0:T(8,128)(2,1)S(1)}, bf16[4,16,1408]{2,1,0:T(8,128)(2,1)S(1)}, u32[]{:S(2)}, u32[]{:S(2)}) collective-permute-start(bf16[4,16,1408]{2,1,0:T(8,128)(2,1)S(1)} %get-tuple-element.184), channel_id=1, source_target_pairs={{0,8},{1,9},{2,10},{3,11},{4,12},{5,13},{6,14},{7,15},{8,0},{9,1},... | collective-permute-start | bytes 540680 | tf_op jit(solution)/shard_map/ppermute | solution.py:643
  41.8 10.0 %collective-permute-start.15 = (bf16[4,16,1408]{2,1,0:T(8,128)(2,1)S(1)}, bf16[4,16,1408]{2,1,0:T(8,128)(2,1)S(1)}, u32[]{:S(2)}, u32[]{:S(2)}) collective-permute-start(bf16[4,16,1408]{2,1,0:T(8,128)(2,1)S(1)} %get-tuple-element.185), channel_id=1, source_target_pairs={{0,24},{1,25},{2,26},{3,27},{4,28},{5,29},{6,30},{7,31},{8,16},{9,... | collective-permute-start | bytes 540680 | tf_op jit(solution)/shard_map/ppermute | solution.py:643
  43.2 10.0 %collective-permute-start.14 = (bf16[4,16,1408]{2,1,0:T(8,128)(2,1)S(1)}, bf16[4,16,1408]{2,1,0:T(8,128)(2,1)S(1)}, u32[]{:S(2)}, u32[]{:S(2)}) collective-permute-start(bf16[4,16,1408]{2,1,0:T(8,128)(2,1)S(1)} %get-tuple-element.186), channel_id=1, source_target_pairs={{0,16},{1,17},{2,18},{3,19},{4,20},{5,21},{6,22},{7,23},{8,24},{9,... | collective-permute-start | bytes 540680 | tf_op jit(solution)/shard_map/ppermute | solution.py:643
  43.8 14.0 %collective-permute-start.16 = (bf16[640,512]{1,0:T(8,128)(2,1)S(1)}, bf16[640,512]{1,0:T(8,128)(2,1)S(1)}, u32[]{:S(2)}, u32[]{:S(2)}) collective-permute-start(bf16[640,512]{1,0:T(8,128)(2,1)S(1)} %get-tuple-element.129), channel_id=1, source_target_pairs={{0,1},{1,0},{2,3},{3,2},{4,5},{5,4},{6,7},{7,6},{8,9},{9,8},{10,11... | collective-permute-start | bytes 1966088 | tf_op jit(solution)/shard_map/ppermute | solution.py:750
  43.8 14.0 %collective-permute-start.17 = (bf16[640,512]{1,0:T(8,128)(2,1)S(1)}, bf16[640,512]{1,0:T(8,128)(2,1)S(1)}, u32[]{:S(2)}, u32[]{:S(2)}) collective-permute-start(bf16[640,512]{1,0:T(8,128)(2,1)S(1)} %get-tuple-element.130), channel_id=1, source_target_pairs={{1,2},{2,1},{3,4},{4,3},{5,6},{6,5},{9,10},{10,9},{11,12},{12,11},... | collective-permute-start | bytes 1966088 | tf_op jit(solution)/shard_map/ppermute | solution.py:751
  53.4 7.4 %collective-permute-start.20 = (bf16[16,1408]{1,0:T(8,128)(2,1)S(1)}, bf16[16,1408]{1,0:T(8,128)(2,1)S(1)}, u32[]{:S(2)}, u32[]{:S(2)}) collective-permute-start(bf16[16,1408]{1,0:T(8,128)(2,1)S(1)} %get-tuple-element.187), channel_id=1, source_target_pairs={{0,6},{1,7},{2,4},{3,5},{4,2},{5,3},{6,0},{7,1},{8,14},{9,15},{10,... | collective-permute-start | bytes 135176 | tf_op jit(solution)/shard_map/ppermute | solution.py:643
  55.5 5.3 %collective-permute-start.19 = (bf16[16,1408]{1,0:T(8,128)(2,1)S(1)}, bf16[16,1408]{1,0:T(8,128)(2,1)S(1)}, u32[]{:S(2)}, u32[]{:S(2)}) collective-permute-start(bf16[16,1408]{1,0:T(8,128)(2,1)S(1)} %get-tuple-element.188), channel_id=1, source_target_pairs={{0,4},{1,5},{2,6},{3,7},{4,0},{5,1},{6,2},{7,3},{8,12},{9,13},{10,... | collective-permute-start | bytes 135176 | tf_op jit(solution)/shard_map/ppermute | solution.py:643
  55.5 5.3 %collective-permute-start.18 = (bf16[16,1408]{1,0:T(8,128)(2,1)S(1)}, bf16[16,1408]{1,0:T(8,128)(2,1)S(1)}, u32[]{:S(2)}, u32[]{:S(2)}) collective-permute-start(bf16[16,1408]{1,0:T(8,128)(2,1)S(1)} %get-tuple-element.189), channel_id=1, source_target_pairs={{0,2},{1,3},{2,0},{3,1},{4,6},{5,7},{6,4},{7,5},{8,10},{9,11},{10,... | collective-permute-start | bytes 135176 | tf_op jit(solution)/shard_map/ppermute | solution.py:643
  57.8 3.0 %copy-start = (f32[8,768]{1,0:T(8,128)S(1)}, f32[8,768]{1,0:T(8,128)}, u32[]{:S(2)}) copy-start(f32[8,768]{1,0:T(8,128)} %refs_4_.3) | copy-start | bytes 73732
  57.9 3.0 %copy-start.1 = (f32[8,768]{1,0:T(8,128)S(1)}, f32[8,768]{1,0:T(8,128)}, u32[]{:S(2)}) copy-start(f32[8,768]{1,0:T(8,128)} %refs_6_.3) | copy-start | bytes 73732
  57.9 3.0 %copy-start.2 = (f32[24,256]{1,0:T(8,128)S(1)}, f32[24,256]{1,0:T(8,128)}, u32[]{:S(2)}) copy-start(f32[24,256]{1,0:T(8,128)} %refs_7_.3) | copy-start | bytes 73732
  57.9 3.0 %copy-start.3 = (f32[8,768]{1,0:T(8,128)S(1)}, f32[8,768]{1,0:T(8,128)}, u32[]{:S(2)}) copy-start(f32[8,768]{1,0:T(8,128)} %refs_10_.3) | copy-start | bytes 73732
  57.9 3.0 %copy-start.4 = (f32[8,768]{1,0:T(8,128)S(1)}, f32[8,768]{1,0:T(8,128)}, u32[]{:S(2)}) copy-start(f32[8,768]{1,0:T(8,128)} %refs_12_.3) | copy-start | bytes 73732
  57.9 3.0 %copy-start.5 = (f32[24,256]{1,0:T(8,128)S(1)}, f32[24,256]{1,0:T(8,128)}, u32[]{:S(2)}) copy-start(f32[24,256]{1,0:T(8,128)} %refs_13_.3) | copy-start | bytes 73732
  57.9 3.0 %copy-start.6 = (f32[8,768]{1,0:T(8,128)S(1)}, f32[8,768]{1,0:T(8,128)}, u32[]{:S(2)}) copy-start(f32[8,768]{1,0:T(8,128)} %refs_2_.1) | copy-start | bytes 73732
  57.9 3.0 %copy-start.7 = (f32[8,768]{1,0:T(8,128)S(1)}, f32[8,768]{1,0:T(8,128)}, u32[]{:S(2)}) copy-start(f32[8,768]{1,0:T(8,128)} %refs_0_.1) | copy-start | bytes 73732
  57.9 3.0 %copy-start.8 = (f32[24,256]{1,0:T(8,128)S(1)}, f32[24,256]{1,0:T(8,128)}, u32[]{:S(2)}) copy-start(f32[24,256]{1,0:T(8,128)} %refs_3_.1) | copy-start | bytes 73732
  58.0 3.0 %copy-start.9 = (f32[8,256]{1,0:T(8,128)S(1)}, f32[8,256]{1,0:T(8,128)}, u32[]{:S(2)}) copy-start(f32[8,256]{1,0:T(8,128)} %refs_5_.4) | copy-start | bytes 24580
  58.0 3.0 %copy-start.10 = (f32[8,256]{1,0:T(8,128)S(1)}, f32[8,256]{1,0:T(8,128)}, u32[]{:S(2)}) copy-start(f32[8,256]{1,0:T(8,128)} %refs_11_.3) | copy-start | bytes 24580
  58.0 3.0 %copy-start.11 = (f32[8,256]{1,0:T(8,128)S(1)}, f32[8,256]{1,0:T(8,128)}, u32[]{:S(2)}) copy-start(f32[8,256]{1,0:T(8,128)} %refs_1_.1) | copy-start | bytes 24580
  58.0 3.0 %copy-start.12 = (f32[11,8]{0,1:T(8,128)S(1)}, f32[11,8]{0,1:T(8,128)}, u32[]{:S(2)}) copy-start(f32[11,8]{0,1:T(8,128)} %param.38) | copy-start | bytes 1060
  58.0 3.0 %copy-start.13 = (f32[8,49]{1,0:T(8,128)S(1)}, f32[8,49]{1,0:T(8,128)}, u32[]{:S(2)}) copy-start(f32[8,49]{1,0:T(8,128)} %refs_9_.4) | copy-start | bytes 4708
  58.0 3.0 %copy-start.14 = (f32[11,8]{0,1:T(8,128)S(1)}, f32[11,8]{0,1:T(8,128)}, u32[]{:S(2)}) copy-start(f32[11,8]{0,1:T(8,128)} %param.39) | copy-start | bytes 1060
  58.0 3.0 %copy-start.15 = (f32[8,49]{1,0:T(8,128)S(1)}, f32[8,49]{1,0:T(8,128)}, u32[]{:S(2)}) copy-start(f32[8,49]{1,0:T(8,128)} %refs_15_.3) | copy-start | bytes 4708
  58.0 3.0 %copy-start.16 = (f32[11,8]{0,1:T(8,128)S(1)}, f32[11,8]{0,1:T(8,128)}, u32[]{:S(2)}) copy-start(f32[11,8]{0,1:T(8,128)} %param.28) | copy-start | bytes 1060
  58.0 3.0 %copy-start.18 = (f32[8,49]{1,0:T(8,128)S(1)}, f32[8,49]{1,0:T(8,128)}, u32[]{:S(2)}) copy-start(f32[8,49]{1,0:T(8,128)} %refs_5_.5) | copy-start | bytes 4708
  61.3 1.2 %collective-permute-start.21 = (f32[8,128]{1,0:T(8,128)S(1)}, f32[8,128]{1,0:T(8,128)S(1)}, u32[]{:S(2)}, u32[]{:S(2)}) collective-permute-start(f32[8,128]{1,0:T(8,128)S(1)} %get-tuple-element.142.mine_ref), channel_id=1, source_target_pairs={{0,1},{1,0},{2,3},{3,2},{4,5},{5,4},{6,7},{7,6},{8,9},{9,8},{10,11... | collective-permute-start | bytes 12296 | tf_op jit(solution)/shard_map/ppermute | solution.py:643
  62.5 4.5 %collective-permute-start.24 = (f32[8,128]{1,0:T(8,128)S(1)}, f32[8,128]{1,0:T(8,128)S(1)}, u32[]{:S(2)}, u32[]{:S(2)}) collective-permute-start(f32[8,128]{1,0:T(8,128)S(1)} %add.66), channel_id=1, source_target_pairs={{0,24},{1,25},{2,26},{3,27},{4,28},{5,29},{6,30},{7,31},{8,16},{9,... | collective-permute-start | bytes 12296 | tf_op jit(solution)/shard_map/ppermute | solution.py:643
  64.1 3.6 %collective-permute-start.23 = (f32[8,128]{1,0:T(8,128)S(1)}, f32[8,128]{1,0:T(8,128)S(1)}, u32[]{:S(2)}, u32[]{:S(2)}) collective-permute-start(f32[8,128]{1,0:T(8,128)S(1)} %add.66), channel_id=1, source_target_pairs={{0,16},{1,17},{2,18},{3,19},{4,20},{5,21},{6,22},{7,23},{8,24},{9,... | collective-permute-start | bytes 12296 | tf_op jit(solution)/shard_map/ppermute | solution.py:643
  65.3 3.6 %collective-permute-start.22 = (f32[8,128]{1,0:T(8,128)S(1)}, f32[8,128]{1,0:T(8,128)S(1)}, u32[]{:S(2)}, u32[]{:S(2)}) collective-permute-start(f32[8,128]{1,0:T(8,128)S(1)} %add.66), channel_id=1, source_target_pairs={{0,8},{1,9},{2,10},{3,11},{4,12},{5,13},{6,14},{7,15},{8,0},{9,1},... | collective-permute-start | bytes 12296 | tf_op jit(solution)/shard_map/ppermute | solution.py:643
  69.0 5.4 %collective-permute-start.27 = (f32[8,128]{1,0:T(8,128)S(1)}, f32[8,128]{1,0:T(8,128)S(1)}, u32[]{:S(2)}, u32[]{:S(2)}) collective-permute-start(f32[8,128]{1,0:T(8,128)S(1)} %add_add_fusion.a_ref), channel_id=1, source_target_pairs={{0,6},{1,7},{2,4},{3,5},{4,2},{5,3},{6,0},{7,1},{8,14},{9,15},{10,... | collective-permute-start | bytes 12296 | tf_op jit(solution)/shard_map/ppermute | solution.py:643
  70.9 4.5 %collective-permute-start.26 = (f32[8,128]{1,0:T(8,128)S(1)}, f32[8,128]{1,0:T(8,128)S(1)}, u32[]{:S(2)}, u32[]{:S(2)}) collective-permute-start(f32[8,128]{1,0:T(8,128)S(1)} %add_add_fusion.a_ref), channel_id=1, source_target_pairs={{0,4},{1,5},{2,6},{3,7},{4,0},{5,1},{6,2},{7,3},{8,12},{9,13},{10,... | collective-permute-start | bytes 12296 | tf_op jit(solution)/shard_map/ppermute | solution.py:643
  70.9 4.5 %collective-permute-start.25 = (f32[8,128]{1,0:T(8,128)S(1)}, f32[8,128]{1,0:T(8,128)S(1)}, u32[]{:S(2)}, u32[]{:S(2)}) collective-permute-start(f32[8,128]{1,0:T(8,128)S(1)} %add_add_fusion.a_ref), channel_id=1, source_target_pairs={{0,2},{1,3},{2,0},{3,1},{4,6},{5,7},{6,4},{7,5},{8,10},{9,11},{10,... | collective-permute-start | bytes 12296 | tf_op jit(solution)/shard_map/ppermute | solution.py:643

commit v10 on v9

--- a/solution.py
+++ b/solution.py
@@ -808,8 +808,8 @@
         moments_kernel, tuple(shape for shape in shapes for _ in range(2)), [], *parts, *firsts, *seconds, vmem=4
     )
     squares = mine + swap(mine, 1, count)
-    squares = squares + swap(squares, 8, count) + swap(squares, 16, count) + swap(squares, 24, count)
-    last = [swap(squares, d << 1, count) for d in (1, 2, 3)]
+    squares = squares + swap(squares, 2, count) + swap(squares, 4, count) + swap(squares, 6, count)
+    last = [swap(squares, d << 3, count) for d in (1, 2, 3)]
     squares, *moments = lax.optimization_barrier((squares, *moments))
     news = call(
         step_kernel,

time: 76.5 us -> 76.5 us (level)
  no operation moved by 1% of the time
where the time goes in v10:
time: 76.5 us; the launch traced here: 76.2 us
  starting transfers between devices  27.7 us (36%)
  waiting for transfers between devices  24 us (31%)
  Pallas kernels  19.9 us (26%)
  local copies, waits for them, and re-layouts  2.32 us (3%)
  other arithmetic  1.12 us (1%)
  between operations  1.09 us (1%)
    ppermute x24, starting transfers between devices, swap(): return lax.ppermute(block, AXES, [(k, k ^ mask) for k in range(count)])  26.2 us
    ppermute x24, waiting for transfers between devices, swap(): return lax.ppermute(block, AXES, [(k, k ^ mask) for k in range(count)])  24 us
    pallas_call x9, Pallas kernels, call(): pl.pallas_call(kernel, out_shape=out_shape, in_specs=specs, out_specs=jax...  19.9 us
    ppermute x2, starting transfers between devices, beside(): lax.ppermute(block[1], 'band', [(b, to) for b, to in touching if 0 <= to...  1.55 us
  transfers between devices with their start and end apart: 28, of which 18 were waited for; matrix products, arithmetic and copies ran while one was open for 0% of the time, Pallas kernels for 10%

profile of v10, /device:TPU:0, one launch (start us, length us, event | category | flops | bytes accessed | tf_op | source)
XLA Modules:
  0.0 76.2 jit_solution(3460702545978060269)
XLA Ops:
  0.7 0.7 fusion.4
  1.4 0.8 %add_convert_fusion.refs_0_ = bf16[16,1408]{1,0:T(8,128)(2,1)S(1)} fusion(f32[8,256]{1,0:T(8,128)S(1)} %get-tuple-element.191, f32[8,256]{1,0:T(8,128)S(1)} %get-tuple-element.192, f32[8,768]{1,0:T(8,128)} %refs_2_.1, f32[8,11]{1,0:T(8,128)} %bitcast.20, f32[8,256]{1,0:T(8,128)S(1)} %get-tuple-element.190, f32[8,256]{1,0:T(8,128)} %refs_1_.1, f32[8,768]{1,0:T(8,128)} %refs_0_.1), kind=kLoop, calls=%fused_computation.5 | loop fusion | flops 157696 | bytes 127328 | tf_op jit(solution)/shard_map/convert_element_type | solution.py:489
  2.2 5.1 %collective-permute-start.2 = (bf16[16,1408]{1,0:T(8,128)(2,1)S(1)}, bf16[16,1408]{1,0:T(8,128)(2,1)S(1)}, u32[]{:S(2)}, u32[]{:S(2)}) collective-permute-start(bf16[16,1408]{1,0:T(8,128)(2,1)S(1)} %add_convert_fusion.refs_0_), channel_id=1, source_target_pairs={{0,6},{1,7},{2,4},{3,5},{4,2},{5,3},{6,0},{7,1},{8,14},{9,15},{10,... | collective-permute-start | bytes 135176 | tf_op jit(solution)/shard_map/ppermute | solution.py:643
  7.3 0.6 collective-permute-start
  7.9 0.7 copy-done.17
  8.6 0.7 copy-done.21
  9.3 1.3 %shard_map.372 = (f32[128,384]{1,0:T(8,128)S(1)}, s32[8,128]{1,0:T(8,128)S(1)}, bf16[192,192]{1,0:T(8,128)(2,1)S(1)}, bf16[512,480]{1,0:T(8,128)(2,1)S(1)}) custom-call(s32[1,2]{1,0:T(1,128)S(1)} %copy-done.21, f32[8,49]{1,0:T(8,128)S(1)} %copy-done.17), custom_call_target="tpu_custom_call" | custom-call | flops 1000000000 | bytes 1000000 | tf_op jit(solution)/shard_map/pallas_call | solution.py:620
  10.6 1.6 %collective-permute-done.1.refs_2_ = bf16[16,1408]{1,0:T(8,128)(2,1)S(1)} collective-permute-done((bf16[16,1408]{1,0:T(8,128)(2,1)S(1)}, bf16[16,1408]{1,0:T(8,128)(2,1)S(1)}, u32[]{:S(2)}, u32[]{:S(2)}) %collective-permute-start.1) | collective-permute-done | bytes 45088 | tf_op jit(solution)/shard_map/ppermute | solution.py:643
  12.2 0.1 collective-permute-start.6
  12.3 2.5 %collective-permute-start.5 = (bf16[4,16,1408]{2,1,0:T(8,128)(2,1)S(1)}, bf16[4,16,1408]{2,1,0:T(8,128)(2,1)S(1)}, u32[]{:S(2)}, u32[]{:S(2)}) collective-permute-start(bf16[4,16,1408]{2,1,0:T(8,128)(2,1)S(1)} %shard_map.373.refs_0_), channel_id=1, source_target_pairs={{0,24},{1,25},{2,26},{3,27},{4,28},{5,29},{6,30},{7,31},{8,16},{9,... | collective-permute-start | bytes 540680 | tf_op jit(solution)/shard_map/ppermute | solution.py:643
  14.8 0.5 collective-permute-start.4
  15.3 0.5 collective-permute-start.3
  15.9 0.6 shard_map.374
  16.4 0.7 collective-permute-start.10
  17.1 3.5 %collective-permute-done.5.refs_3_ = bf16[4,16,1408]{2,1,0:T(8,128)(2,1)S(1)} collective-permute-done((bf16[4,16,1408]{2,1,0:T(8,128)(2,1)S(1)}, bf16[4,16,1408]{2,1,0:T(8,128)(2,1)S(1)}, u32[]{:S(2)}, u32[]{:S(2)}) %collective-permute-start.5) | collective-permute-done | bytes 180256 | tf_op jit(solution)/shard_map/ppermute | solution.py:643
  20.7 3.4 %collective-permute-done.4.refs_2_ = bf16[4,16,1408]{2,1,0:T(8,128)(2,1)S(1)} collective-permute-done((bf16[4,16,1408]{2,1,0:T(8,128)(2,1)S(1)}, bf16[4,16,1408]{2,1,0:T(8,128)(2,1)S(1)}, u32[]{:S(2)}, u32[]{:S(2)}) %collective-permute-start.4) | collective-permute-done | bytes 180256 | tf_op jit(solution)/shard_map/ppermute | solution.py:643
  24.1 0.1 collective-permute-done.3.refs_1_
  24.2 0.5 collective-permute-start.8
  24.7 0.9 %collective-permute-done.7.refs_5_ = bf16[4,16,1408]{2,1,0:T(8,128)(2,1)S(1)} collective-permute-done((bf16[4,16,1408]{2,1,0:T(8,128)(2,1)S(1)}, bf16[4,16,1408]{2,1,0:T(8,128)(2,1)S(1)}, u32[]{:S(2)}, u32[]{:S(2)}) %collective-permute-start.7) | collective-permute-done | bytes 180256 | tf_op jit(solution)/shard_map/ppermute | solution.py:643
  25.6 0.3 collective-permute-done.8.refs_6_
  25.8 0.3 collective-permute-done.9.refs_7_
  26.1 11.6 %shard_map.375 = (bf16[768,768]{1,0:T(8,128)(2,1)S(1)}, f32[768,256]{1,0:T(8,128)S(1)}, f32[768,256]{1,0:T(8,128)S(1)}, f32[768,512]{1,0:T(8,128)S(1)}, bf16[640...) custom-call(bf16[4,16,1408]{2,1,0:T(8,128)(2,1)S(1)} %shard_map.373., ...), custom_call_target="tpu_custom_call" | custom-call | flops 15000000512 | bytes 1000000 | tf_op jit(solution)/shard_map/pallas_call | solution.py:620
  37.7 0.1 slice.40
  37.7 0.3 collective-permute-start.12
  38.1 1.9 %collective-permute-done.12 = bf16[16,16,1408]{2,1,0:T(8,128)(2,1)S(1)} collective-permute-done((bf16[16,16,1408]{2,1,0:T(8,128)(2,1)S(1)}, bf16[16,16,1408]{2,1,0:T(8,128)(2,1)S(1)}, u32[]{:S(2)}, u32[]{:S(2)}) %collective-permute-start.12) | collective-permute-done | bytes 720928 | tf_op jit(solution)/shard_map/ppermute | solution.py:643
  40.0 0.2 fusion.2
  40.3 1.6 %collective-permute-start.13 = (bf16[4,16,1408]{2,1,0:T(8,128)(2,1)S(1)}, bf16[4,16,1408]{2,1,0:T(8,128)(2,1)S(1)}, u32[]{:S(2)}, u32[]{:S(2)}) collective-permute-start(bf16[4,16,1408]{2,1,0:T(8,128)(2,1)S(1)} %get-tuple-element.184), channel_id=1, source_target_pairs={{0,8},{1,9},{2,10},{3,11},{4,12},{5,13},{6,14},{7,15},{8,0},{9,1},... | collective-permute-start | bytes 540680 | tf_op jit(solution)/shard_map/ppermute | solution.py:643
  41.8 1.4 %collective-permute-start.15 = (bf16[4,16,1408]{2,1,0:T(8,128)(2,1)S(1)}, bf16[4,16,1408]{2,1,0:T(8,128)(2,1)S(1)}, u32[]{:S(2)}, u32[]{:S(2)}) collective-permute-start(bf16[4,16,1408]{2,1,0:T(8,128)(2,1)S(1)} %get-tuple-element.185), channel_id=1, source_target_pairs={{0,24},{1,25},{2,26},{3,27},{4,28},{5,29},{6,30},{7,31},{8,16},{9,... | collective-permute-start | bytes 540680 | tf_op jit(solution)/shard_map/ppermute | solution.py:643
  43.2 0.6 collective-permute-start.14
  43.8 0.9 %collective-permute-start.17 = (bf16[640,512]{1,0:T(8,128)(2,1)S(1)}, bf16[640,512]{1,0:T(8,128)(2,1)S(1)}, u32[]{:S(2)}, u32[]{:S(2)}) collective-permute-start(bf16[640,512]{1,0:T(8,128)(2,1)S(1)} %get-tuple-element.130), channel_id=1, source_target_pairs={{1,2},{2,1},{3,4},{4,3},{5,6},{6,5},{9,10},{10,9},{11,12},{12,11},... | collective-permute-start | bytes 1966088 | tf_op jit(solution)/shard_map/ppermute | solution.py:751
  44.7 2.0 %shard_map.377 = bf16[16,48,256]{2,1,0:T(8,128)(2,1)} custom-call(f32[768,256]{1,0:T(8,128)S(1)} %get-tuple-element.136.x1_ref, bf16[768,768]{1,0:T(8,128)(2,1)S(1)} %get-tuple-element.137.act_ref, bf16[768,256]{1,0:T(8,128)(2,1)S(1)} %get-tuple-element.138.wd_ref, f32[11,256]{1,0:T(8,128)S(1)} %get-tuple-element.135.vec_ref, ...), custom_call_target="tpu_custom_call" | custom-call | flops 1000000000 | bytes 1000000 | tf_op jit(solution)/shard_map/pallas_call | solution.py:620
  46.7 1.0 %collective-permute-done.13 = bf16[4,16,1408]{2,1,0:T(8,128)(2,1)S(1)} collective-permute-done((bf16[4,16,1408]{2,1,0:T(8,128)(2,1)S(1)}, bf16[4,16,1408]{2,1,0:T(8,128)(2,1)S(1)}, u32[]{:S(2)}, u32[]{:S(2)}) %collective-permute-start.13) | collective-permute-done | bytes 180256 | tf_op jit(solution)/shard_map/ppermute | solution.py:643
  47.7 4.2 %collective-permute-done.15 = bf16[4,16,1408]{2,1,0:T(8,128)(2,1)S(1)} collective-permute-done((bf16[4,16,1408]{2,1,0:T(8,128)(2,1)S(1)}, bf16[4,16,1408]{2,1,0:T(8,128)(2,1)S(1)}, u32[]{:S(2)}, u32[]{:S(2)}) %collective-permute-start.15) | collective-permute-done | bytes 180256 | tf_op jit(solution)/shard_map/ppermute | solution.py:643
  51.9 1.4 %collective-permute-done.14 = bf16[4,16,1408]{2,1,0:T(8,128)(2,1)S(1)} collective-permute-done((bf16[4,16,1408]{2,1,0:T(8,128)(2,1)S(1)}, bf16[4,16,1408]{2,1,0:T(8,128)(2,1)S(1)}, u32[]{:S(2)}, u32[]{:S(2)}) %collective-permute-start.14) | collective-permute-done | bytes 180256 | tf_op jit(solution)/shard_map/ppermute | solution.py:643
  53.2 0.1 fusion.1
  53.4 2.2 %collective-permute-start.20 = (bf16[16,1408]{1,0:T(8,128)(2,1)S(1)}, bf16[16,1408]{1,0:T(8,128)(2,1)S(1)}, u32[]{:S(2)}, u32[]{:S(2)}) collective-permute-start(bf16[16,1408]{1,0:T(8,128)(2,1)S(1)} %get-tuple-element.187), channel_id=1, source_target_pairs={{0,6},{1,7},{2,4},{3,5},{4,2},{5,3},{6,0},{7,1},{8,14},{9,15},{10,... | collective-permute-start | bytes 135176 | tf_op jit(solution)/shard_map/ppermute | solution.py:643
  55.5 2.3 %collective-permute-start.18 = (bf16[16,1408]{1,0:T(8,128)(2,1)S(1)}, bf16[16,1408]{1,0:T(8,128)(2,1)S(1)}, u32[]{:S(2)}, u32[]{:S(2)}) collective-permute-start(bf16[16,1408]{1,0:T(8,128)(2,1)S(1)} %get-tuple-element.189), channel_id=1, source_target_pairs={{0,2},{1,3},{2,0},{3,1},{4,6},{5,7},{6,4},{7,5},{8,10},{9,11},{10,... | collective-permute-start | bytes 135176 | tf_op jit(solution)/shard_map/ppermute | solution.py:643
  57.9 0.0 copy-start.2
  57.9 0.0 copy-start.3
  57.9 0.0 copy-start.6
  57.9 0.0 copy-start.7
  58.0 0.0 copy-start.10
  58.0 0.0 copy-start.11
  58.0 0.0 copy-start.14
  58.0 0.0 copy-start.15
  58.0 0.0 copy-start.18
  58.1 2.7 %shard_map.376 = bf16[16,48,256]{2,1,0:T(8,128)(2,1)} custom-call(f32[768,512]{1,0:T(8,128)S(1)} %get-tuple-element.128.own_ref, bf16[640,512]{1,0:T(8,128)(2,1)S(1)} %collective-permute-done.16.gotc_ref, bf16[640,512]{1,0:T(8,128)(2,1)S(1)} %collective-permute-done.17.gotz_ref, bf16[768,256]{1,0:T(8,128)(2,1)S(1)} %get-tuple-element.131.dq_ref, ...), custom_call_target="tpu_custom_call" | custom-call | flops 1000000000 | bytes 1000000 | tf_op jit(solution)/shard_map/pallas_call | solution.py:620
  60.7 0.1 collective-permute-done.19.refs_2_
  61.0 0.3 shard_map.378
  61.3 0.0 collective-permute-start.21
  61.4 1.2 %collective-permute-done.21 = f32[8,128]{1,0:T(8,128)S(1)} collective-permute-done((f32[8,128]{1,0:T(8,128)S(1)}, f32[8,128]{1,0:T(8,128)S(1)}, u32[]{:S(2)}, u32[]{:S(2)}) %collective-permute-start.21) | collective-permute-done | bytes 4128 | tf_op jit(solution)/shard_map/ppermute | solution.py:643
  62.5 2.0 %collective-permute-start.24 = (f32[8,128]{1,0:T(8,128)S(1)}, f32[8,128]{1,0:T(8,128)S(1)}, u32[]{:S(2)}, u32[]{:S(2)}) collective-permute-start(f32[8,128]{1,0:T(8,128)S(1)} %add.66), channel_id=1, source_target_pairs={{0,6},{1,7},{2,4},{3,5},{4,2},{5,3},{6,0},{7,1},{8,14},{9,15},{10,... | collective-permute-start | bytes 12296 | tf_op jit(solution)/shard_map/ppermute | solution.py:643
  64.6 0.4 collective-permute-start.23
  65.0 1.9 %collective-permute-start.22 = (f32[8,128]{1,0:T(8,128)S(1)}, f32[8,128]{1,0:T(8,128)S(1)}, u32[]{:S(2)}, u32[]{:S(2)}) collective-permute-start(f32[8,128]{1,0:T(8,128)S(1)} %add.66), channel_id=1, source_target_pairs={{0,2},{1,3},{2,0},{3,1},{4,6},{5,7},{6,4},{7,5},{8,10},{9,11},{10,... | collective-permute-start | bytes 12296 | tf_op jit(solution)/shard_map/ppermute | solution.py:643
  66.9 1.0 %collective-permute-done.24 = f32[8,128]{1,0:T(8,128)S(1)} collective-permute-done((f32[8,128]{1,0:T(8,128)S(1)}, f32[8,128]{1,0:T(8,128)S(1)}, u32[]{:S(2)}, u32[]{:S(2)}) %collective-permute-start.24) | collective-permute-done | bytes 4128 | tf_op jit(solution)/shard_map/ppermute | solution.py:643
  67.9 1.1 %collective-permute-done.23 = f32[8,128]{1,0:T(8,128)S(1)} collective-permute-done((f32[8,128]{1,0:T(8,128)S(1)}, f32[8,128]{1,0:T(8,128)S(1)}, u32[]{:S(2)}, u32[]{:S(2)}) %collective-permute-start.23) | collective-permute-done | bytes 4128 | tf_op jit(solution)/shard_map/ppermute | solution.py:643
  69.1 1.7 %collective-permute-start.27 = (f32[8,128]{1,0:T(8,128)S(1)}, f32[8,128]{1,0:T(8,128)S(1)}, u32[]{:S(2)}, u32[]{:S(2)}) collective-permute-start(f32[8,128]{1,0:T(8,128)S(1)} %add_add_fusion.a_ref), channel_id=1, source_target_pairs={{0,24},{1,25},{2,26},{3,27},{4,28},{5,29},{6,30},{7,31},{8,16},{9,... | collective-permute-start | bytes 12296 | tf_op jit(solution)/shard_map/ppermute | solution.py:643
  70.8 1.0 %collective-permute-start.26 = (f32[8,128]{1,0:T(8,128)S(1)}, f32[8,128]{1,0:T(8,128)S(1)}, u32[]{:S(2)}, u32[]{:S(2)}) collective-permute-start(f32[8,128]{1,0:T(8,128)S(1)} %add_add_fusion.a_ref), channel_id=1, source_target_pairs={{0,16},{1,17},{2,18},{3,19},{4,20},{5,21},{6,22},{7,23},{8,24},{9,... | collective-permute-start | bytes 12296 | tf_op jit(solution)/shard_map/ppermute | solution.py:643
  71.9 0.8 %collective-permute-start.25 = (f32[8,128]{1,0:T(8,128)S(1)}, f32[8,128]{1,0:T(8,128)S(1)}, u32[]{:S(2)}, u32[]{:S(2)}) collective-permute-start(f32[8,128]{1,0:T(8,128)S(1)} %add_add_fusion.a_ref), channel_id=1, source_target_pairs={{0,8},{1,9},{2,10},{3,11},{4,12},{5,13},{6,14},{7,15},{8,0},{9,1},... | collective-permute-start | bytes 12296 | tf_op jit(solution)/shard_map/ppermute | solution.py:643
  72.6 0.8 %shard_map.379 = (f32[8,768]{1,0:T(8,128)}, f32[8,768]{1,0:T(8,128)}, f32[8,256]{1,0:T(8,128)}, f32[8,256]{1,0:T(8,128)}, f32[8,768]{1,0:T(8,128)}, /*index=5*/f...) custom-call(f32[16,1408]{1,0:T(8,128)S(1)} %slice_bitcast_fusion.ref, ...), custom_call_target="tpu_custom_call" | custom-call | flops 100000000 | bytes 1000000 | tf_op jit(solution)/shard_map/pallas_call | solution.py:620
  73.4 0.2 collective-permute-done.27.d_ref
  73.7 0.8 collective-permute-done.26.c_ref
  74.4 1.0 %collective-permute-done.25.b_ref = f32[8,128]{1,0:T(8,128)S(1)} collective-permute-done((f32[8,128]{1,0:T(8,128)S(1)}, f32[8,128]{1,0:T(8,128)S(1)}, u32[]{:S(2)}, u32[]{:S(2)}) %collective-permute-start.25) | collective-permute-done | bytes 4128 | tf_op jit(solution)/shard_map/ppermute | solution.py:643
  75.5 0.8 shard_map.380
  (56 shorter events, 0.2 us)
Async XLA Ops:
  2.2 8.4 %collective-permute-start.2 = (bf16[16,1408]{1,0:T(8,128)(2,1)S(1)}, bf16[16,1408]{1,0:T(8,128)(2,1)S(1)}, u32[]{:S(2)}, u32[]{:S(2)}) collective-permute-start(bf16[16,1408]{1,0:T(8,128)(2,1)S(1)} %add_convert_fusion.refs_0_), channel_id=1, source_target_pairs={{0,6},{1,7},{2,4},{3,5},{4,2},{5,3},{6,0},{7,1},{8,14},{9,15},{10,... | collective-permute-start | bytes 135176 | tf_op jit(solution)/shard_map/ppermute | solution.py:643
  7.3 4.9 %collective-permute-start.1 = (bf16[16,1408]{1,0:T(8,128)(2,1)S(1)}, bf16[16,1408]{1,0:T(8,128)(2,1)S(1)}, u32[]{:S(2)}, u32[]{:S(2)}) collective-permute-start(bf16[16,1408]{1,0:T(8,128)(2,1)S(1)} %add_convert_fusion.refs_0_), channel_id=1, source_target_pairs={{0,4},{1,5},{2,6},{3,7},{4,0},{5,1},{6,2},{7,3},{8,12},{9,13},{10,... | collective-permute-start | bytes 135176 | tf_op jit(solution)/shard_map/ppermute | solution.py:643
  7.3 4.9 %collective-permute-start = (bf16[16,1408]{1,0:T(8,128)(2,1)S(1)}, bf16[16,1408]{1,0:T(8,128)(2,1)S(1)}, u32[]{:S(2)}, u32[]{:S(2)}) collective-permute-start(bf16[16,1408]{1,0:T(8,128)(2,1)S(1)} %add_convert_fusion.refs_0_), channel_id=1, source_target_pairs={{0,2},{1,3},{2,0},{3,1},{4,6},{5,7},{6,4},{7,5},{8,10},{9,11},{10,... | collective-permute-start | bytes 135176 | tf_op jit(solution)/shard_map/ppermute | solution.py:643
  7.9 0.7 copy-start.17
  8.6 0.7 copy-start.21
  9.3 6.6 %copy-start.19 = (bf16[16,48,256]{2,1,0:T(8,128)(2,1)S(1)}, bf16[16,48,256]{2,1,0:T(8,128)(2,1)}, u32[]{:S(2)}) copy-start(bf16[16,48,256]{2,1,0:T(8,128)(2,1)} %cot_ref.1) | copy-start | bytes 1179652
  9.3 6.6 %copy-start.20 = (bf16[16,48,256]{2,1,0:T(8,128)(2,1)S(1)}, bf16[16,48,256]{2,1,0:T(8,128)(2,1)}, u32[]{:S(2)}) copy-start(bf16[16,48,256]{2,1,0:T(8,128)(2,1)} %refs_9_.2) | copy-start | bytes 1179652
  12.2 12.4 %collective-permute-start.6 = (bf16[4,16,1408]{2,1,0:T(8,128)(2,1)S(1)}, bf16[4,16,1408]{2,1,0:T(8,128)(2,1)S(1)}, u32[]{:S(2)}, u32[]{:S(2)}) collective-permute-start(bf16[4,16,1408]{2,1,0:T(8,128)(2,1)S(1)} %shard_map.373.refs_0_), channel_id=1, source_target_pairs={{0,1},{1,0},{2,3},{3,2},{4,5},{5,4},{6,7},{7,6},{8,9},{9,8},{10,11... | collective-permute-start | bytes 540680 | tf_op jit(solution)/shard_map/ppermute | solution.py:643
  12.3 8.4 %collective-permute-start.5 = (bf16[4,16,1408]{2,1,0:T(8,128)(2,1)S(1)}, bf16[4,16,1408]{2,1,0:T(8,128)(2,1)S(1)}, u32[]{:S(2)}, u32[]{:S(2)}) collective-permute-start(bf16[4,16,1408]{2,1,0:T(8,128)(2,1)S(1)} %shard_map.373.refs_0_), channel_id=1, source_target_pairs={{0,24},{1,25},{2,26},{3,27},{4,28},{5,29},{6,30},{7,31},{8,16},{9,... | collective-permute-start | bytes 540680 | tf_op jit(solution)/shard_map/ppermute | solution.py:643
  14.8 9.2 %collective-permute-start.4 = (bf16[4,16,1408]{2,1,0:T(8,128)(2,1)S(1)}, bf16[4,16,1408]{2,1,0:T(8,128)(2,1)S(1)}, u32[]{:S(2)}, u32[]{:S(2)}) collective-permute-start(bf16[4,16,1408]{2,1,0:T(8,128)(2,1)S(1)} %shard_map.373.refs_0_), channel_id=1, source_target_pairs={{0,16},{1,17},{2,18},{3,19},{4,20},{5,21},{6,22},{7,23},{8,24},{9,... | collective-permute-start | bytes 540680 | tf_op jit(solution)/shard_map/ppermute | solution.py:643
  15.3 8.8 %collective-permute-start.3 = (bf16[4,16,1408]{2,1,0:T(8,128)(2,1)S(1)}, bf16[4,16,1408]{2,1,0:T(8,128)(2,1)S(1)}, u32[]{:S(2)}, u32[]{:S(2)}) collective-permute-start(bf16[4,16,1408]{2,1,0:T(8,128)(2,1)S(1)} %shard_map.373.refs_0_), channel_id=1, source_target_pairs={{0,8},{1,9},{2,10},{3,11},{4,12},{5,13},{6,14},{7,15},{8,0},{9,1},... | collective-permute-start | bytes 540680 | tf_op jit(solution)/shard_map/ppermute | solution.py:643
  16.4 8.2 %collective-permute-start.10 = (bf16[12,48,256]{2,1,0:T(8,128)(2,1)S(1)}, bf16[12,48,256]{2,1,0:T(8,128)(2,1)S(1)}, u32[]{:S(2)}, u32[]{:S(2)}) collective-permute-start(bf16[12,48,256]{2,1,0:T(8,128)(2,1)S(1)} %get-tuple-element.117), channel_id=1, source_target_pairs={{1,2},{2,1},{3,4},{4,3},{5,6},{6,5},{9,10},{10,9},{11,12},{12,11},... | collective-permute-start | bytes 884744 | tf_op jit(solution)/shard_map/ppermute | solution.py:751
  20.7 4.0 %collective-permute-start.11 = (bf16[12,48,256]{2,1,0:T(8,128)(2,1)S(1)}, bf16[12,48,256]{2,1,0:T(8,128)(2,1)S(1)}, u32[]{:S(2)}, u32[]{:S(2)}) collective-permute-start(bf16[12,48,256]{2,1,0:T(8,128)(2,1)S(1)} %get-tuple-element.118), channel_id=1, source_target_pairs={{0,1},{1,0},{2,3},{3,2},{4,5},{5,4},{6,7},{7,6},{8,9},{9,8},{10,11... | collective-permute-start | bytes 884744 | tf_op jit(solution)/shard_map/ppermute | solution.py:750
  24.2 1.4 %collective-permute-start.7 = (bf16[4,16,1408]{2,1,0:T(8,128)(2,1)S(1)}, bf16[4,16,1408]{2,1,0:T(8,128)(2,1)S(1)}, u32[]{:S(2)}, u32[]{:S(2)}) collective-permute-start(bf16[4,16,1408]{2,1,0:T(8,128)(2,1)S(1)} %collective-permute-done.3.refs_1_), channel_id=1, source_target_pairs={{0,1},{1,0},{2,3},{3,2},{4,5},{5,4},{6,7},{7,6},{8,9},{9,8},{10,11... | collective-permute-start | bytes 540680 | tf_op jit(solution)/shard_map/ppermute | solution.py:643
  24.2 1.7 %collective-permute-start.8 = (bf16[4,16,1408]{2,1,0:T(8,128)(2,1)S(1)}, bf16[4,16,1408]{2,1,0:T(8,128)(2,1)S(1)}, u32[]{:S(2)}, u32[]{:S(2)}) collective-permute-start(bf16[4,16,1408]{2,1,0:T(8,128)(2,1)S(1)} %collective-permute-done.4.refs_2_), channel_id=1, source_target_pairs={{0,1},{1,0},{2,3},{3,2},{4,5},{5,4},{6,7},{7,6},{8,9},{9,8},{10,11... | collective-permute-start | bytes 540680 | tf_op jit(solution)/shard_map/ppermute | solution.py:643
  24.7 1.4 %collective-permute-start.9 = (bf16[4,16,1408]{2,1,0:T(8,128)(2,1)S(1)}, bf16[4,16,1408]{2,1,0:T(8,128)(2,1)S(1)}, u32[]{:S(2)}, u32[]{:S(2)}) collective-permute-start(bf16[4,16,1408]{2,1,0:T(8,128)(2,1)S(1)} %collective-permute-done.5.refs_3_), channel_id=1, source_target_pairs={{0,1},{1,0},{2,3},{3,2},{4,5},{5,4},{6,7},{7,6},{8,9},{9,8},{10,11... | collective-permute-start | bytes 540680 | tf_op jit(solution)/shard_map/ppermute | solution.py:643
  37.7 2.3 %collective-permute-start.12 = (bf16[16,16,1408]{2,1,0:T(8,128)(2,1)S(1)}, bf16[16,16,1408]{2,1,0:T(8,128)(2,1)S(1)}, u32[]{:S(2)}, u32[]{:S(2)}) collective-permute-start(bf16[16,16,1408]{2,1,0:T(8,128)(2,1)S(1)} %slice.40), channel_id=1, source_target_pairs={{0,1},{1,0},{2,3},{3,2},{4,5},{5,4},{6,7},{7,6},{8,9},{9,8},{10,11... | collective-permute-start | bytes 2162696 | tf_op jit(solution)/shard_map/ppermute | solution.py:643
  40.3 7.4 %collective-permute-start.13 = (bf16[4,16,1408]{2,1,0:T(8,128)(2,1)S(1)}, bf16[4,16,1408]{2,1,0:T(8,128)(2,1)S(1)}, u32[]{:S(2)}, u32[]{:S(2)}) collective-permute-start(bf16[4,16,1408]{2,1,0:T(8,128)(2,1)S(1)} %get-tuple-element.184), channel_id=1, source_target_pairs={{0,8},{1,9},{2,10},{3,11},{4,12},{5,13},{6,14},{7,15},{8,0},{9,1},... | collective-permute-start | bytes 540680 | tf_op jit(solution)/shard_map/ppermute | solution.py:643
  41.8 10.0 %collective-permute-start.15 = (bf16[4,16,1408]{2,1,0:T(8,128)(2,1)S(1)}, bf16[4,16,1408]{2,1,0:T(8,128)(2,1)S(1)}, u32[]{:S(2)}, u32[]{:S(2)}) collective-permute-start(bf16[4,16,1408]{2,1,0:T(8,128)(2,1)S(1)} %get-tuple-element.185), channel_id=1, source_target_pairs={{0,24},{1,25},{2,26},{3,27},{4,28},{5,29},{6,30},{7,31},{8,16},{9,... | collective-permute-start | bytes 540680 | tf_op jit(solution)/shard_map/ppermute | solution.py:643
  43.2 10.0 %collective-permute-start.14 = (bf16[4,16,1408]{2,1,0:T(8,128)(2,1)S(1)}, bf16[4,16,1408]{2,1,0:T(8,128)(2,1)S(1)}, u32[]{:S(2)}, u32[]{:S(2)}) collective-permute-start(bf16[4,16,1408]{2,1,0:T(8,128)(2,1)S(1)} %get-tuple-element.186), channel_id=1, source_target_pairs={{0,16},{1,17},{2,18},{3,19},{4,20},{5,21},{6,22},{7,23},{8,24},{9,... | collective-permute-start | bytes 540680 | tf_op jit(solution)/shard_map/ppermute | solution.py:643
  43.8 14.0 %collective-permute-start.16 = (bf16[640,512]{1,0:T(8,128)(2,1)S(1)}, bf16[640,512]{1,0:T(8,128)(2,1)S(1)}, u32[]{:S(2)}, u32[]{:S(2)}) collective-permute-start(bf16[640,512]{1,0:T(8,128)(2,1)S(1)} %get-tuple-element.129), channel_id=1, source_target_pairs={{0,1},{1,0},{2,3},{3,2},{4,5},{5,4},{6,7},{7,6},{8,9},{9,8},{10,11... | collective-permute-start | bytes 1966088 | tf_op jit(solution)/shard_map/ppermute | solution.py:750
  43.8 14.0 %collective-permute-start.17 = (bf16[640,512]{1,0:T(8,128)(2,1)S(1)}, bf16[640,512]{1,0:T(8,128)(2,1)S(1)}, u32[]{:S(2)}, u32[]{:S(2)}) collective-permute-start(bf16[640,512]{1,0:T(8,128)(2,1)S(1)} %get-tuple-element.130), channel_id=1, source_target_pairs={{1,2},{2,1},{3,4},{4,3},{5,6},{6,5},{9,10},{10,9},{11,12},{12,11},... | collective-permute-start | bytes 1966088 | tf_op jit(solution)/shard_map/ppermute | solution.py:751
  53.4 7.4 %collective-permute-start.20 = (bf16[16,1408]{1,0:T(8,128)(2,1)S(1)}, bf16[16,1408]{1,0:T(8,128)(2,1)S(1)}, u32[]{:S(2)}, u32[]{:S(2)}) collective-permute-start(bf16[16,1408]{1,0:T(8,128)(2,1)S(1)} %get-tuple-element.187), channel_id=1, source_target_pairs={{0,6},{1,7},{2,4},{3,5},{4,2},{5,3},{6,0},{7,1},{8,14},{9,15},{10,... | collective-permute-start | bytes 135176 | tf_op jit(solution)/shard_map/ppermute | solution.py:643
  55.5 5.3 %collective-permute-start.19 = (bf16[16,1408]{1,0:T(8,128)(2,1)S(1)}, bf16[16,1408]{1,0:T(8,128)(2,1)S(1)}, u32[]{:S(2)}, u32[]{:S(2)}) collective-permute-start(bf16[16,1408]{1,0:T(8,128)(2,1)S(1)} %get-tuple-element.188), channel_id=1, source_target_pairs={{0,4},{1,5},{2,6},{3,7},{4,0},{5,1},{6,2},{7,3},{8,12},{9,13},{10,... | collective-permute-start | bytes 135176 | tf_op jit(solution)/shard_map/ppermute | solution.py:643
  55.5 5.3 %collective-permute-start.18 = (bf16[16,1408]{1,0:T(8,128)(2,1)S(1)}, bf16[16,1408]{1,0:T(8,128)(2,1)S(1)}, u32[]{:S(2)}, u32[]{:S(2)}) collective-permute-start(bf16[16,1408]{1,0:T(8,128)(2,1)S(1)} %get-tuple-element.189), channel_id=1, source_target_pairs={{0,2},{1,3},{2,0},{3,1},{4,6},{5,7},{6,4},{7,5},{8,10},{9,11},{10,... | collective-permute-start | bytes 135176 | tf_op jit(solution)/shard_map/ppermute | solution.py:643
  57.8 3.0 %copy-start = (f32[8,768]{1,0:T(8,128)S(1)}, f32[8,768]{1,0:T(8,128)}, u32[]{:S(2)}) copy-start(f32[8,768]{1,0:T(8,128)} %refs_4_.3) | copy-start | bytes 73732
  57.9 3.0 %copy-start.1 = (f32[8,768]{1,0:T(8,128)S(1)}, f32[8,768]{1,0:T(8,128)}, u32[]{:S(2)}) copy-start(f32[8,768]{1,0:T(8,128)} %refs_6_.3) | copy-start | bytes 73732
  57.9 3.0 %copy-start.2 = (f32[24,256]{1,0:T(8,128)S(1)}, f32[24,256]{1,0:T(8,128)}, u32[]{:S(2)}) copy-start(f32[24,256]{1,0:T(8,128)} %refs_7_.3) | copy-start | bytes 73732
  57.9 3.0 %copy-start.3 = (f32[8,768]{1,0:T(8,128)S(1)}, f32[8,768]{1,0:T(8,128)}, u32[]{:S(2)}) copy-start(f32[8,768]{1,0:T(8,128)} %refs_10_.3) | copy-start | bytes 73732
  57.9 3.0 %copy-start.4 = (f32[8,768]{1,0:T(8,128)S(1)}, f32[8,768]{1,0:T(8,128)}, u32[]{:S(2)}) copy-start(f32[8,768]{1,0:T(8,128)} %refs_12_.3) | copy-start | bytes 73732
  57.9 3.0 %copy-start.5 = (f32[24,256]{1,0:T(8,128)S(1)}, f32[24,256]{1,0:T(8,128)}, u32[]{:S(2)}) copy-start(f32[24,256]{1,0:T(8,128)} %refs_13_.3) | copy-start | bytes 73732
  57.9 3.0 %copy-start.6 = (f32[8,768]{1,0:T(8,128)S(1)}, f32[8,768]{1,0:T(8,128)}, u32[]{:S(2)}) copy-start(f32[8,768]{1,0:T(8,128)} %refs_2_.1) | copy-start | bytes 73732
  57.9 3.0 %copy-start.7 = (f32[8,768]{1,0:T(8,128)S(1)}, f32[8,768]{1,0:T(8,128)}, u32[]{:S(2)}) copy-start(f32[8,768]{1,0:T(8,128)} %refs_0_.1) | copy-start | bytes 73732
  57.9 3.0 %copy-start.8 = (f32[24,256]{1,0:T(8,128)S(1)}, f32[24,256]{1,0:T(8,128)}, u32[]{:S(2)}) copy-start(f32[24,256]{1,0:T(8,128)} %refs_3_.1) | copy-start | bytes 73732
  58.0 3.0 %copy-start.9 = (f32[8,256]{1,0:T(8,128)S(1)}, f32[8,256]{1,0:T(8,128)}, u32[]{:S(2)}) copy-start(f32[8,256]{1,0:T(8,128)} %refs_5_.4) | copy-start | bytes 24580
  58.0 3.0 %copy-start.10 = (f32[8,256]{1,0:T(8,128)S(1)}, f32[8,256]{1,0:T(8,128)}, u32[]{:S(2)}) copy-start(f32[8,256]{1,0:T(8,128)} %refs_11_.3) | copy-start | bytes 24580
  58.0 3.0 %copy-start.11 = (f32[8,256]{1,0:T(8,128)S(1)}, f32[8,256]{1,0:T(8,128)}, u32[]{:S(2)}) copy-start(f32[8,256]{1,0:T(8,128)} %refs_1_.1) | copy-start | bytes 24580
  58.0 3.0 %copy-start.12 = (f32[11,8]{0,1:T(8,128)S(1)}, f32[11,8]{0,1:T(8,128)}, u32[]{:S(2)}) copy-start(f32[11,8]{0,1:T(8,128)} %param.38) | copy-start | bytes 1060
  58.0 3.0 %copy-start.13 = (f32[8,49]{1,0:T(8,128)S(1)}, f32[8,49]{1,0:T(8,128)}, u32[]{:S(2)}) copy-start(f32[8,49]{1,0:T(8,128)} %refs_9_.4) | copy-start | bytes 4708
  58.0 3.0 %copy-start.14 = (f32[11,8]{0,1:T(8,128)S(1)}, f32[11,8]{0,1:T(8,128)}, u32[]{:S(2)}) copy-start(f32[11,8]{0,1:T(8,128)} %param.39) | copy-start | bytes 1060
  58.0 3.0 %copy-start.15 = (f32[8,49]{1,0:T(8,128)S(1)}, f32[8,49]{1,0:T(8,128)}, u32[]{:S(2)}) copy-start(f32[8,49]{1,0:T(8,128)} %refs_15_.3) | copy-start | bytes 4708
  58.0 3.0 %copy-start.16 = (f32[11,8]{0,1:T(8,128)S(1)}, f32[11,8]{0,1:T(8,128)}, u32[]{:S(2)}) copy-start(f32[11,8]{0,1:T(8,128)} %param.28) | copy-start | bytes 1060
  58.0 3.0 %copy-start.18 = (f32[8,49]{1,0:T(8,128)S(1)}, f32[8,49]{1,0:T(8,128)}, u32[]{:S(2)}) copy-start(f32[8,49]{1,0:T(8,128)} %refs_5_.5) | copy-start | bytes 4708
  61.3 1.2 %collective-permute-start.21 = (f32[8,128]{1,0:T(8,128)S(1)}, f32[8,128]{1,0:T(8,128)S(1)}, u32[]{:S(2)}, u32[]{:S(2)}) collective-permute-start(f32[8,128]{1,0:T(8,128)S(1)} %get-tuple-element.142.mine_ref), channel_id=1, source_target_pairs={{0,1},{1,0},{2,3},{3,2},{4,5},{5,4},{6,7},{7,6},{8,9},{9,8},{10,11... | collective-permute-start | bytes 12296 | tf_op jit(solution)/shard_map/ppermute | solution.py:643
  62.5 5.4 %collective-permute-start.24 = (f32[8,128]{1,0:T(8,128)S(1)}, f32[8,128]{1,0:T(8,128)S(1)}, u32[]{:S(2)}, u32[]{:S(2)}) collective-permute-start(f32[8,128]{1,0:T(8,128)S(1)} %add.66), channel_id=1, source_target_pairs={{0,6},{1,7},{2,4},{3,5},{4,2},{5,3},{6,0},{7,1},{8,14},{9,15},{10,... | collective-permute-start | bytes 12296 | tf_op jit(solution)/shard_map/ppermute | solution.py:643
  64.6 4.5 %collective-permute-start.23 = (f32[8,128]{1,0:T(8,128)S(1)}, f32[8,128]{1,0:T(8,128)S(1)}, u32[]{:S(2)}, u32[]{:S(2)}) collective-permute-start(f32[8,128]{1,0:T(8,128)S(1)} %add.66), channel_id=1, source_target_pairs={{0,4},{1,5},{2,6},{3,7},{4,0},{5,1},{6,2},{7,3},{8,12},{9,13},{10,... | collective-permute-start | bytes 12296 | tf_op jit(solution)/shard_map/ppermute | solution.py:643
  65.0 4.1 %collective-permute-start.22 = (f32[8,128]{1,0:T(8,128)S(1)}, f32[8,128]{1,0:T(8,128)S(1)}, u32[]{:S(2)}, u32[]{:S(2)}) collective-permute-start(f32[8,128]{1,0:T(8,128)S(1)} %add.66), channel_id=1, source_target_pairs={{0,2},{1,3},{2,0},{3,1},{4,6},{5,7},{6,4},{7,5},{8,10},{9,11},{10,... | collective-permute-start | bytes 12296 | tf_op jit(solution)/shard_map/ppermute | solution.py:643
  69.1 4.6 %collective-permute-start.27 = (f32[8,128]{1,0:T(8,128)S(1)}, f32[8,128]{1,0:T(8,128)S(1)}, u32[]{:S(2)}, u32[]{:S(2)}) collective-permute-start(f32[8,128]{1,0:T(8,128)S(1)} %add_add_fusion.a_ref), channel_id=1, source_target_pairs={{0,24},{1,25},{2,26},{3,27},{4,28},{5,29},{6,30},{7,31},{8,16},{9,... | collective-permute-start | bytes 12296 | tf_op jit(solution)/shard_map/ppermute | solution.py:643
  70.8 3.6 %collective-permute-start.26 = (f32[8,128]{1,0:T(8,128)S(1)}, f32[8,128]{1,0:T(8,128)S(1)}, u32[]{:S(2)}, u32[]{:S(2)}) collective-permute-start(f32[8,128]{1,0:T(8,128)S(1)} %add_add_fusion.a_ref), channel_id=1, source_target_pairs={{0,16},{1,17},{2,18},{3,19},{4,20},{5,21},{6,22},{7,23},{8,24},{9,... | collective-permute-start | bytes 12296 | tf_op jit(solution)/shard_map/ppermute | solution.py:643
  71.9 3.6 %collective-permute-start.25 = (f32[8,128]{1,0:T(8,128)S(1)}, f32[8,128]{1,0:T(8,128)S(1)}, u32[]{:S(2)}, u32[]{:S(2)}) collective-permute-start(f32[8,128]{1,0:T(8,128)S(1)} %add_add_fusion.a_ref), channel_id=1, source_target_pairs={{0,8},{1,9},{2,10},{3,11},{4,12},{5,13},{6,14},{7,15},{8,0},{9,1},... | collective-permute-start | bytes 12296 | tf_op jit(solution)/shard_map/ppermute | solution.py:643

commit v11 on v10

--- a/solution.py
+++ b/solution.py
@@ -307,11 +307,13 @@
     dsl_ref,
     tacc_ref,
     dkv_ref,
+    kvsum_ref,
 ):
     odd = (lax.axis_index("band") & 1) == 1
     scale = 32 ** (-0.5)
     lane_head = lax.broadcasted_iota(jnp.int32, (QN, 128), 1) >> 5
     tacc_ref[...] = jnp.zeros_like(tacc_ref)
+    kvsum_ref[...] = jnp.zeros_like(kvsum_ref)
 
     def scores_back(k, _):
         at_q = pl.ds(pl.multiple_of(k * QN, QN), QN)
@@ -333,6 +335,8 @@
         dk = dot(dsl_ref[at_k, :], spread_heads(q_ref[at_q, :], lane_head)) * scale
         dkv_ref[at_k, 0:256] = dk.astype(BF)
         dkv_ref[at_k, 256:512] = dv.astype(BF)
+        kvsum_ref[:, 0:256] += jnp.sum(dk, axis=0, keepdims=True)
+        kvsum_ref[:, 256:512] += jnp.sum(dv, axis=0, keepdims=True)
         own_ref[at_q, 0:256] = dk[0:QN]
         own_ref[at_q, 256:512] = dv[0:QN]
         after = jnp.concatenate([dk[QN : QN + RIM], dv[QN : QN + RIM]], axis=1)
@@ -377,6 +381,7 @@
     xhat_ref,
     xk_ref,
     dkv_ref,
+    kvsum_ref,
     wqkv_ref,
     vt_ref,
     sums_ref,
@@ -408,7 +413,7 @@
     xk = xk_ref[...].astype(BF)
     for cols in (slice(256, 512), slice(512, 768)):
         dkv = dkv_ref[:, cols.start - 256 : cols.stop - 256]
-        kvsum = jnp.sum(dkv.astype(F32), axis=0, keepdims=True)
+        kvsum = kvsum_ref[:, cols.start - 256 : cols.stop - 256]
         m = dot_tn(xk, dkv)
         weight = wqkv_ref[:, cols].astype(F32)
         fq_ref[:, cols] = gain * m + shift * kvsum
@@ -493,39 +498,38 @@
     return lax.axis_index("maps") * 8 + lax.axis_index("band")
 
 
-def unpack(blocks, big_qkv, big_out, big_up, big_down, vec, vt, fq, fo, fu, fd):
+def unpack(blocks, big_qkv, big_out, big_up, big_down, vec, vt):
     me = own_index()
-    for index, block in enumerate(blocks):
-        core, across = divmod(index, 4)
+    odd = (me & 1) == 1
+    for across in range(4):
         for z in range(4):
-            slab = block[z].astype(F32)
-            o = me ^ (core | (z << 1) | (across << 3))
-            at = pl.ds(pl.multiple_of(o * 8, 8), 8)
-            fq[at, :] = slab[0:8, 0:768]
-            vt[at, :] = slab[0:8, 1280:1408]
-            for b, rows in enumerate((slab[0:8, 1024:1280], slab[8:16, 768:1024], slab[8:16, 1024:1280])):
-                fd[pl.ds(pl.multiple_of(o * 24 + 8 * b, 8), 8), :] = rows
-            fo[at, :] = slab[0:8, 768:1024]
-            fu[at, :] = slab[8:16, 0:768]
-    big_qkv[...] = fq[...].astype(BF)
+            mine, other = blocks[across][z].astype(F32), blocks[across + 4][z].astype(F32)
+            pair = (jnp.where(odd, other, mine), jnp.where(odd, mine, other))
+            o = (me ^ ((z << 1) | (across << 3))) >> 1
+            at = pl.ds(pl.multiple_of(o * 16, 16), 16)
+            both = lambda rows, lanes: [slab[rows, lanes] for slab in pair]
+            top, low = slice(0, 8), slice(8, 16)
+            big_qkv[at, :] = jnp.concatenate(both(top, slice(0, 768)), axis=0).astype(BF)
+            big_out[at, :] = jnp.concatenate(both(top, slice(768, 1024)), axis=0).astype(BF)
+            big_up[at, :] = jnp.concatenate(both(low, slice(0, 768)), axis=0).astype(BF)
+            vt[at, :] = jnp.concatenate(both(top, slice(1280, 1408)), axis=0)
+            tall = [[s[0:8, 1024:1280], s[8:16, 768:1024], s[8:16, 1024:1280]] for s in pair]
+            big_down[pl.ds(pl.multiple_of(o * 48, 16), 48), :] = jnp.concatenate(tall[0] + tall[1], axis=0).astype(BF)
     vec[...] = vt[...].T[0 : vec.shape[0]]
-    big_out[...] = fo[...].astype(BF)
-    big_up[...] = fu[...].astype(BF)
-    big_down[...] = fd[...].astype(BF)
 
 
 def main_kernel(*refs):
     blocks, (xhat, x, xz, xc, pk, xp, bias, limits, dy, dysum) = refs[:8], refs[8:18]
     act, dx1, x1, own, rimc, rimz, dq, out_ref, big_qkv, big_down, vec = refs[18:29]
-    q, k, v, mixed, p, dz, a2, da, dmix, sums, zsum, dsl, tacc, dkv = refs[29:43]
-    fq, fv, tgrad, fd, fu, fo, big_out, big_up, vt, xk, other, xhat1, rstd1 = refs[43:]
+    q, k, v, mixed, p, dz, a2, da, dmix, sums, zsum, dsl, tacc, dkv, kvsum = refs[29:44]
+    fq, fv, tgrad, fd, fu, fo, big_out, big_up, vt, xk, other, xhat1, rstd1 = refs[44:]
     halo_kernel(x, xc, xz, pk, xk)
-    unpack(blocks, big_qkv, big_out, big_up, big_down, vec, vt, fq, fo, fu, fd)
+    unpack(blocks, big_qkv, big_out, big_up, big_down, vec, vt)
     project_kernel(xhat, xk, big_qkv, vec, q, k, v)
     attend_kernel(limits, bias, q, k, v, mixed, p, other)
     feed_kernel(dy, dysum, mixed, xp, big_out, big_up, big_down, vec, act, dz, a2, da, dx1, x1, dmix, sums, zsum, xhat1, rstd1)
-    back_kernel(q, v, p, dmix, own, rimc, rimz, dsl, tacc, dkv)
-    late_grads(dsl, k, tacc, xhat, xk, dkv, big_qkv, vt, sums, zsum, dq, fq, fv, tgrad)
+    back_kernel(q, v, p, dmix, own, rimc, rimz, dsl, tacc, dkv, kvsum)
+    late_grads(dsl, k, tacc, xhat, xk, dkv, kvsum, big_qkv, vt, sums, zsum, dq, fq, fv, tgrad)
     early_grads(act, dy, a2, dz, mixed, da, fd, fu, fo)
     table = tgrad[...]
     me = own_index()
@@ -732,6 +736,7 @@
         sds((CLS * KN, 384)),
         sds((KN, 384), F32),
         sds((CLS * KN, 512)),
+        sds((1, 512), F32),
     )
 
 
@@ -770,7 +775,7 @@
     *far, xp = lax.optimization_barrier((*blocks[1:], xp))
     blocks = [blocks[0]] + far + [swap(block, 1, count) for block in [blocks[0]] + far]
     act_s, dz_s, a2_s, da_s, dx1_s, x1_s, dmix_s, sums_s, zsum_s = feed_outputs()
-    own_s, rimc_s, rimz_s, dsl_s, tacc_s, dkv_s = back_outputs()
+    own_s, rimc_s, rimz_s, dsl_s, tacc_s, dkv_s, kvsum_s = back_outputs()
     dq_s, fq_s, fv_s, tgrad_s = late_outputs()
     act, dx1, x1, own, rim_c, rim_z, dq, grads, big_qkv, big_down, vec = call(
         main_kernel,
@@ -780,7 +785,7 @@
             pltpu.VMEM(o.shape, o.dtype)
             for o in project_outputs()
             + attend_outputs()
-            + (dz_s, a2_s, da_s, dmix_s, sums_s, zsum_s, dsl_s, tacc_s, dkv_s, fq_s, fv_s, tgrad_s)
+            + (dz_s, a2_s, da_s, dmix_s, sums_s, zsum_s, dsl_s, tacc_s, dkv_s, kvsum_s, fq_s, fv_s, tgrad_s)
             + (sds((768, 256), F32), sds((256, 768), F32), sds((256, 256), F32))
             + (sds((256, 256)), sds((256, 768)), sds((256, 128), F32), sds((CLS * KN, 256), F32), sds((KN, 384), F32))
             + (sds((768, 256), F32), sds((768, 128), F32))
@@ -902,7 +907,7 @@
         dy, dysum, mixed, xp, big_out, big_up, big_down, vec,
         flops=4 * 10**9,
     )
-    own, rim_c, rim_z, dsl, tacc, dkv = call(
+    own, rim_c, rim_z, dsl, tacc, dkv, kvsum = call(
         back_kernel, back_outputs(), [], queries, values, probs, dmix, flops=4 * 10**9
     )
     got_c, got_z = beside((rim_c, rim_z), band)
@@ -917,7 +922,7 @@
         late_grads,
         late_outputs(),
         [],
-        dsl, keys, tacc, xhat, xk, dkv, big_qkv, vt, sums, zsum,
+        dsl, keys, tacc, xhat, xk, dkv, kvsum, big_qkv, vt, sums, zsum,
         flops=3 * 10**9,
     )
     layer_out = call(output_kernel, sds((16, 48, 256)), [], x1, act, big_down, vec, po, flops=10**9)

time: 76.5 us -> 76.5 us (level)
  no operation moved by 1% of the time
where the time goes in v11:
time: 76.5 us; the launch traced here: 76.2 us
  starting transfers between devices  27.7 us (36%)
  waiting for transfers between devices  24 us (31%)
  Pallas kernels  19.9 us (26%)
  local copies, waits for them, and re-layouts  2.32 us (3%)
  other arithmetic  1.12 us (1%)
  between operations  1.09 us (1%)
    ppermute x24, starting transfers between devices, swap(): return lax.ppermute(block, AXES, [(k, k ^ mask) for k in range(count)])  26.2 us
    ppermute x24, waiting for transfers between devices, swap(): return lax.ppermute(block, AXES, [(k, k ^ mask) for k in range(count)])  24 us
    pallas_call x9, Pallas kernels, call(): pl.pallas_call(kernel, out_shape=out_shape, in_specs=specs, out_specs=jax...  19.9 us
    ppermute x2, starting transfers between devices, beside(): lax.ppermute(block[1], 'band', [(b, to) for b, to in touching if 0 <= to...  1.55 us
  transfers between devices with their start and end apart: 28, of which 18 were waited for; matrix products, arithmetic and copies ran while one was open for 0% of the time, Pallas kernels for 10%

profile of v11, /device:TPU:0, one launch (start us, length us, event | category | flops | bytes accessed | tf_op | source)
XLA Modules:
  0.0 76.2 jit_solution(7512047586138215995)
XLA Ops:
  0.7 0.7 fusion.4
  1.4 0.8 %add_convert_fusion.refs_0_ = bf16[16,1408]{1,0:T(8,128)(2,1)S(1)} fusion(f32[8,256]{1,0:T(8,128)S(1)} %get-tuple-element.191, f32[8,256]{1,0:T(8,128)S(1)} %get-tuple-element.192, f32[8,768]{1,0:T(8,128)} %refs_2_.1, f32[8,11]{1,0:T(8,128)} %bitcast.20, f32[8,256]{1,0:T(8,128)S(1)} %get-tuple-element.190, f32[8,256]{1,0:T(8,128)} %refs_1_.1, f32[8,768]{1,0:T(8,128)} %refs_0_.1), kind=kLoop, calls=%fused_computation.5 | loop fusion | flops 157696 | bytes 127328 | tf_op jit(solution)/shard_map/convert_element_type | solution.py:494
  2.2 5.1 %collective-permute-start.2 = (bf16[16,1408]{1,0:T(8,128)(2,1)S(1)}, bf16[16,1408]{1,0:T(8,128)(2,1)S(1)}, u32[]{:S(2)}, u32[]{:S(2)}) collective-permute-start(bf16[16,1408]{1,0:T(8,128)(2,1)S(1)} %add_convert_fusion.refs_0_), channel_id=1, source_target_pairs={{0,6},{1,7},{2,4},{3,5},{4,2},{5,3},{6,0},{7,1},{8,14},{9,15},{10,... | collective-permute-start | bytes 135176 | tf_op jit(solution)/shard_map/ppermute | solution.py:647
  7.3 0.6 collective-permute-start
  7.9 0.7 copy-done.17
  8.6 0.7 copy-done.21
  9.3 1.3 %shard_map.372 = (f32[128,384]{1,0:T(8,128)S(1)}, s32[8,128]{1,0:T(8,128)S(1)}, bf16[192,192]{1,0:T(8,128)(2,1)S(1)}, bf16[512,480]{1,0:T(8,128)(2,1)S(1)}) custom-call(s32[1,2]{1,0:T(1,128)S(1)} %copy-done.21, f32[8,49]{1,0:T(8,128)S(1)} %copy-done.17), custom_call_target="tpu_custom_call" | custom-call | flops 1000000000 | bytes 1000000 | tf_op jit(solution)/shard_map/pallas_call | solution.py:624
  10.6 1.6 %collective-permute-done.1.refs_2_ = bf16[16,1408]{1,0:T(8,128)(2,1)S(1)} collective-permute-done((bf16[16,1408]{1,0:T(8,128)(2,1)S(1)}, bf16[16,1408]{1,0:T(8,128)(2,1)S(1)}, u32[]{:S(2)}, u32[]{:S(2)}) %collective-permute-start.1) | collective-permute-done | bytes 45088 | tf_op jit(solution)/shard_map/ppermute | solution.py:647
  12.2 0.1 collective-permute-start.6
  12.3 2.5 %collective-permute-start.5 = (bf16[4,16,1408]{2,1,0:T(8,128)(2,1)S(1)}, bf16[4,16,1408]{2,1,0:T(8,128)(2,1)S(1)}, u32[]{:S(2)}, u32[]{:S(2)}) collective-permute-start(bf16[4,16,1408]{2,1,0:T(8,128)(2,1)S(1)} %shard_map.373.refs_0_), channel_id=1, source_target_pairs={{0,24},{1,25},{2,26},{3,27},{4,28},{5,29},{6,30},{7,31},{8,16},{9,... | collective-permute-start | bytes 540680 | tf_op jit(solution)/shard_map/ppermute | solution.py:647
  14.8 0.5 collective-permute-start.4
  15.3 0.5 collective-permute-start.3
  15.9 0.6 shard_map.374
  16.4 0.7 collective-permute-start.10
  17.1 3.5 %collective-permute-done.5.refs_3_ = bf16[4,16,1408]{2,1,0:T(8,128)(2,1)S(1)} collective-permute-done((bf16[4,16,1408]{2,1,0:T(8,128)(2,1)S(1)}, bf16[4,16,1408]{2,1,0:T(8,128)(2,1)S(1)}, u32[]{:S(2)}, u32[]{:S(2)}) %collective-permute-start.5) | collective-permute-done | bytes 180256 | tf_op jit(solution)/shard_map/ppermute | solution.py:647
  20.7 3.4 %collective-permute-done.4.refs_2_ = bf16[4,16,1408]{2,1,0:T(8,128)(2,1)S(1)} collective-permute-done((bf16[4,16,1408]{2,1,0:T(8,128)(2,1)S(1)}, bf16[4,16,1408]{2,1,0:T(8,128)(2,1)S(1)}, u32[]{:S(2)}, u32[]{:S(2)}) %collective-permute-start.4) | collective-permute-done | bytes 180256 | tf_op jit(solution)/shard_map/ppermute | solution.py:647
  24.1 0.1 collective-permute-done.3.refs_1_
  24.2 0.5 collective-permute-start.8
  24.7 0.9 %collective-permute-done.7.refs_5_ = bf16[4,16,1408]{2,1,0:T(8,128)(2,1)S(1)} collective-permute-done((bf16[4,16,1408]{2,1,0:T(8,128)(2,1)S(1)}, bf16[4,16,1408]{2,1,0:T(8,128)(2,1)S(1)}, u32[]{:S(2)}, u32[]{:S(2)}) %collective-permute-start.7) | collective-permute-done | bytes 180256 | tf_op jit(solution)/shard_map/ppermute | solution.py:647
  25.6 0.3 collective-permute-done.8.refs_6_
  25.8 0.3 collective-permute-done.9.refs_7_
  26.1 11.6 %shard_map.375 = (bf16[768,768]{1,0:T(8,128)(2,1)S(1)}, f32[768,256]{1,0:T(8,128)S(1)}, f32[768,256]{1,0:T(8,128)S(1)}, f32[768,512]{1,0:T(8,128)S(1)}, bf16[640...) custom-call(bf16[4,16,1408]{2,1,0:T(8,128)(2,1)S(1)} %shard_map.373., ...), custom_call_target="tpu_custom_call" | custom-call | flops 15000000512 | bytes 1000000 | tf_op jit(solution)/shard_map/pallas_call | solution.py:624
  37.7 0.1 slice.40
  37.7 0.3 collective-permute-start.12
  38.0 1.9 %collective-permute-done.12 = bf16[16,16,1408]{2,1,0:T(8,128)(2,1)S(1)} collective-permute-done((bf16[16,16,1408]{2,1,0:T(8,128)(2,1)S(1)}, bf16[16,16,1408]{2,1,0:T(8,128)(2,1)S(1)}, u32[]{:S(2)}, u32[]{:S(2)}) %collective-permute-start.12) | collective-permute-done | bytes 720928 | tf_op jit(solution)/shard_map/ppermute | solution.py:647
  40.0 0.2 fusion.2
  40.2 1.6 %collective-permute-start.13 = (bf16[4,16,1408]{2,1,0:T(8,128)(2,1)S(1)}, bf16[4,16,1408]{2,1,0:T(8,128)(2,1)S(1)}, u32[]{:S(2)}, u32[]{:S(2)}) collective-permute-start(bf16[4,16,1408]{2,1,0:T(8,128)(2,1)S(1)} %get-tuple-element.184), channel_id=1, source_target_pairs={{0,8},{1,9},{2,10},{3,11},{4,12},{5,13},{6,14},{7,15},{8,0},{9,1},... | collective-permute-start | bytes 540680 | tf_op jit(solution)/shard_map/ppermute | solution.py:647
  41.8 1.4 %collective-permute-start.15 = (bf16[4,16,1408]{2,1,0:T(8,128)(2,1)S(1)}, bf16[4,16,1408]{2,1,0:T(8,128)(2,1)S(1)}, u32[]{:S(2)}, u32[]{:S(2)}) collective-permute-start(bf16[4,16,1408]{2,1,0:T(8,128)(2,1)S(1)} %get-tuple-element.185), channel_id=1, source_target_pairs={{0,24},{1,25},{2,26},{3,27},{4,28},{5,29},{6,30},{7,31},{8,16},{9,... | collective-permute-start | bytes 540680 | tf_op jit(solution)/shard_map/ppermute | solution.py:647
  43.2 0.6 collective-permute-start.14
  43.8 0.9 %collective-permute-start.17 = (bf16[640,512]{1,0:T(8,128)(2,1)S(1)}, bf16[640,512]{1,0:T(8,128)(2,1)S(1)}, u32[]{:S(2)}, u32[]{:S(2)}) collective-permute-start(bf16[640,512]{1,0:T(8,128)(2,1)S(1)} %get-tuple-element.130), channel_id=1, source_target_pairs={{1,2},{2,1},{3,4},{4,3},{5,6},{6,5},{9,10},{10,9},{11,12},{12,11},... | collective-permute-start | bytes 1966088 | tf_op jit(solution)/shard_map/ppermute | solution.py:756
  44.7 2.0 %shard_map.377 = bf16[16,48,256]{2,1,0:T(8,128)(2,1)} custom-call(f32[768,256]{1,0:T(8,128)S(1)} %get-tuple-element.136.x1_ref, bf16[768,768]{1,0:T(8,128)(2,1)S(1)} %get-tuple-element.137.act_ref, bf16[768,256]{1,0:T(8,128)(2,1)S(1)} %get-tuple-element.138.wd_ref, f32[11,256]{1,0:T(8,128)S(1)} %get-tuple-element.135.vec_ref, ...), custom_call_target="tpu_custom_call" | custom-call | flops 1000000000 | bytes 1000000 | tf_op jit(solution)/shard_map/pallas_call | solution.py:624
  46.7 1.0 %collective-permute-done.13 = bf16[4,16,1408]{2,1,0:T(8,128)(2,1)S(1)} collective-permute-done((bf16[4,16,1408]{2,1,0:T(8,128)(2,1)S(1)}, bf16[4,16,1408]{2,1,0:T(8,128)(2,1)S(1)}, u32[]{:S(2)}, u32[]{:S(2)}) %collective-permute-start.13) | collective-permute-done | bytes 180256 | tf_op jit(solution)/shard_map/ppermute | solution.py:647
  47.7 4.2 %collective-permute-done.15 = bf16[4,16,1408]{2,1,0:T(8,128)(2,1)S(1)} collective-permute-done((bf16[4,16,1408]{2,1,0:T(8,128)(2,1)S(1)}, bf16[4,16,1408]{2,1,0:T(8,128)(2,1)S(1)}, u32[]{:S(2)}, u32[]{:S(2)}) %collective-permute-start.15) | collective-permute-done | bytes 180256 | tf_op jit(solution)/shard_map/ppermute | solution.py:647
  51.9 1.4 %collective-permute-done.14 = bf16[4,16,1408]{2,1,0:T(8,128)(2,1)S(1)} collective-permute-done((bf16[4,16,1408]{2,1,0:T(8,128)(2,1)S(1)}, bf16[4,16,1408]{2,1,0:T(8,128)(2,1)S(1)}, u32[]{:S(2)}, u32[]{:S(2)}) %collective-permute-start.14) | collective-permute-done | bytes 180256 | tf_op jit(solution)/shard_map/ppermute | solution.py:647
  53.2 0.1 fusion.1
  53.4 2.2 %collective-permute-start.20 = (bf16[16,1408]{1,0:T(8,128)(2,1)S(1)}, bf16[16,1408]{1,0:T(8,128)(2,1)S(1)}, u32[]{:S(2)}, u32[]{:S(2)}) collective-permute-start(bf16[16,1408]{1,0:T(8,128)(2,1)S(1)} %get-tuple-element.187), channel_id=1, source_target_pairs={{0,6},{1,7},{2,4},{3,5},{4,2},{5,3},{6,0},{7,1},{8,14},{9,15},{10,... | collective-permute-start | bytes 135176 | tf_op jit(solution)/shard_map/ppermute | solution.py:647
  55.6 2.3 %collective-permute-start.18 = (bf16[16,1408]{1,0:T(8,128)(2,1)S(1)}, bf16[16,1408]{1,0:T(8,128)(2,1)S(1)}, u32[]{:S(2)}, u32[]{:S(2)}) collective-permute-start(bf16[16,1408]{1,0:T(8,128)(2,1)S(1)} %get-tuple-element.189), channel_id=1, source_target_pairs={{0,2},{1,3},{2,0},{3,1},{4,6},{5,7},{6,4},{7,5},{8,10},{9,11},{10,... | collective-permute-start | bytes 135176 | tf_op jit(solution)/shard_map/ppermute | solution.py:647
  57.8 0.0 copy-start
  57.9 0.0 copy-start.1
  57.9 0.0 copy-start.4
  57.9 0.0 copy-start.5
  57.9 0.0 copy-start.8
  57.9 0.0 copy-start.9
  58.0 0.0 copy-start.12
  58.0 0.0 copy-start.13
  58.0 0.0 copy-start.16
  58.1 2.7 %shard_map.376 = bf16[16,48,256]{2,1,0:T(8,128)(2,1)} custom-call(f32[768,512]{1,0:T(8,128)S(1)} %get-tuple-element.128.own_ref, bf16[640,512]{1,0:T(8,128)(2,1)S(1)} %collective-permute-done.16.gotc_ref, bf16[640,512]{1,0:T(8,128)(2,1)S(1)} %collective-permute-done.17.gotz_ref, bf16[768,256]{1,0:T(8,128)(2,1)S(1)} %get-tuple-element.131.dq_ref, ...), custom_call_target="tpu_custom_call" | custom-call | flops 1000000000 | bytes 1000000 | tf_op jit(solution)/shard_map/pallas_call | solution.py:624
  60.7 0.1 collective-permute-done.19.refs_2_
  61.0 0.3 shard_map.378
  61.3 0.0 collective-permute-start.21
  61.4 1.2 %collective-permute-done.21 = f32[8,128]{1,0:T(8,128)S(1)} collective-permute-done((f32[8,128]{1,0:T(8,128)S(1)}, f32[8,128]{1,0:T(8,128)S(1)}, u32[]{:S(2)}, u32[]{:S(2)}) %collective-permute-start.21) | collective-permute-done | bytes 4128 | tf_op jit(solution)/shard_map/ppermute | solution.py:647
  62.5 2.0 %collective-permute-start.24 = (f32[8,128]{1,0:T(8,128)S(1)}, f32[8,128]{1,0:T(8,128)S(1)}, u32[]{:S(2)}, u32[]{:S(2)}) collective-permute-start(f32[8,128]{1,0:T(8,128)S(1)} %add.66), channel_id=1, source_target_pairs={{0,6},{1,7},{2,4},{3,5},{4,2},{5,3},{6,0},{7,1},{8,14},{9,15},{10,... | collective-permute-start | bytes 12296 | tf_op jit(solution)/shard_map/ppermute | solution.py:647
  64.6 0.4 collective-permute-start.23
  65.0 1.9 %collective-permute-start.22 = (f32[8,128]{1,0:T(8,128)S(1)}, f32[8,128]{1,0:T(8,128)S(1)}, u32[]{:S(2)}, u32[]{:S(2)}) collective-permute-start(f32[8,128]{1,0:T(8,128)S(1)} %add.66), channel_id=1, source_target_pairs={{0,2},{1,3},{2,0},{3,1},{4,6},{5,7},{6,4},{7,5},{8,10},{9,11},{10,... | collective-permute-start | bytes 12296 | tf_op jit(solution)/shard_map/ppermute | solution.py:647
  66.9 1.0 %collective-permute-done.24 = f32[8,128]{1,0:T(8,128)S(1)} collective-permute-done((f32[8,128]{1,0:T(8,128)S(1)}, f32[8,128]{1,0:T(8,128)S(1)}, u32[]{:S(2)}, u32[]{:S(2)}) %collective-permute-start.24) | collective-permute-done | bytes 4128 | tf_op jit(solution)/shard_map/ppermute | solution.py:647
  67.9 1.1 %collective-permute-done.23 = f32[8,128]{1,0:T(8,128)S(1)} collective-permute-done((f32[8,128]{1,0:T(8,128)S(1)}, f32[8,128]{1,0:T(8,128)S(1)}, u32[]{:S(2)}, u32[]{:S(2)}) %collective-permute-start.23) | collective-permute-done | bytes 4128 | tf_op jit(solution)/shard_map/ppermute | solution.py:647
  69.1 1.7 %collective-permute-start.27 = (f32[8,128]{1,0:T(8,128)S(1)}, f32[8,128]{1,0:T(8,128)S(1)}, u32[]{:S(2)}, u32[]{:S(2)}) collective-permute-start(f32[8,128]{1,0:T(8,128)S(1)} %add_add_fusion.a_ref), channel_id=1, source_target_pairs={{0,24},{1,25},{2,26},{3,27},{4,28},{5,29},{6,30},{7,31},{8,16},{9,... | collective-permute-start | bytes 12296 | tf_op jit(solution)/shard_map/ppermute | solution.py:647
  70.8 1.1 %collective-permute-start.26 = (f32[8,128]{1,0:T(8,128)S(1)}, f32[8,128]{1,0:T(8,128)S(1)}, u32[]{:S(2)}, u32[]{:S(2)}) collective-permute-start(f32[8,128]{1,0:T(8,128)S(1)} %add_add_fusion.a_ref), channel_id=1, source_target_pairs={{0,16},{1,17},{2,18},{3,19},{4,20},{5,21},{6,22},{7,23},{8,24},{9,... | collective-permute-start | bytes 12296 | tf_op jit(solution)/shard_map/ppermute | solution.py:647
  71.9 0.8 %collective-permute-start.25 = (f32[8,128]{1,0:T(8,128)S(1)}, f32[8,128]{1,0:T(8,128)S(1)}, u32[]{:S(2)}, u32[]{:S(2)}) collective-permute-start(f32[8,128]{1,0:T(8,128)S(1)} %add_add_fusion.a_ref), channel_id=1, source_target_pairs={{0,8},{1,9},{2,10},{3,11},{4,12},{5,13},{6,14},{7,15},{8,0},{9,1},... | collective-permute-start | bytes 12296 | tf_op jit(solution)/shard_map/ppermute | solution.py:647
  72.6 0.8 %shard_map.379 = (f32[8,768]{1,0:T(8,128)}, f32[8,768]{1,0:T(8,128)}, f32[8,256]{1,0:T(8,128)}, f32[8,256]{1,0:T(8,128)}, f32[8,768]{1,0:T(8,128)}, /*index=5*/f...) custom-call(f32[16,1408]{1,0:T(8,128)S(1)} %slice_bitcast_fusion.ref, ...), custom_call_target="tpu_custom_call" | custom-call | flops 100000000 | bytes 1000000 | tf_op jit(solution)/shard_map/pallas_call | solution.py:624
  73.4 0.2 collective-permute-done.27.d_ref
  73.7 0.8 collective-permute-done.26.c_ref
  74.4 1.1 %collective-permute-done.25.b_ref = f32[8,128]{1,0:T(8,128)S(1)} collective-permute-done((f32[8,128]{1,0:T(8,128)S(1)}, f32[8,128]{1,0:T(8,128)S(1)}, u32[]{:S(2)}, u32[]{:S(2)}) %collective-permute-start.25) | collective-permute-done | bytes 4128 | tf_op jit(solution)/shard_map/ppermute | solution.py:647
  75.5 0.8 shard_map.380
  (56 shorter events, 0.2 us)
Async XLA Ops:
  2.2 8.4 %collective-permute-start.2 = (bf16[16,1408]{1,0:T(8,128)(2,1)S(1)}, bf16[16,1408]{1,0:T(8,128)(2,1)S(1)}, u32[]{:S(2)}, u32[]{:S(2)}) collective-permute-start(bf16[16,1408]{1,0:T(8,128)(2,1)S(1)} %add_convert_fusion.refs_0_), channel_id=1, source_target_pairs={{0,6},{1,7},{2,4},{3,5},{4,2},{5,3},{6,0},{7,1},{8,14},{9,15},{10,... | collective-permute-start | bytes 135176 | tf_op jit(solution)/shard_map/ppermute | solution.py:647
  7.3 4.9 %collective-permute-start.1 = (bf16[16,1408]{1,0:T(8,128)(2,1)S(1)}, bf16[16,1408]{1,0:T(8,128)(2,1)S(1)}, u32[]{:S(2)}, u32[]{:S(2)}) collective-permute-start(bf16[16,1408]{1,0:T(8,128)(2,1)S(1)} %add_convert_fusion.refs_0_), channel_id=1, source_target_pairs={{0,4},{1,5},{2,6},{3,7},{4,0},{5,1},{6,2},{7,3},{8,12},{9,13},{10,... | collective-permute-start | bytes 135176 | tf_op jit(solution)/shard_map/ppermute | solution.py:647
  7.3 4.9 %collective-permute-start = (bf16[16,1408]{1,0:T(8,128)(2,1)S(1)}, bf16[16,1408]{1,0:T(8,128)(2,1)S(1)}, u32[]{:S(2)}, u32[]{:S(2)}) collective-permute-start(bf16[16,1408]{1,0:T(8,128)(2,1)S(1)} %add_convert_fusion.refs_0_), channel_id=1, source_target_pairs={{0,2},{1,3},{2,0},{3,1},{4,6},{5,7},{6,4},{7,5},{8,10},{9,11},{10,... | collective-permute-start | bytes 135176 | tf_op jit(solution)/shard_map/ppermute | solution.py:647
  7.9 0.7 copy-start.17
  8.6 0.7 copy-start.21
  9.3 6.6 %copy-start.19 = (bf16[16,48,256]{2,1,0:T(8,128)(2,1)S(1)}, bf16[16,48,256]{2,1,0:T(8,128)(2,1)}, u32[]{:S(2)}) copy-start(bf16[16,48,256]{2,1,0:T(8,128)(2,1)} %cot_ref.1) | copy-start | bytes 1179652
  9.3 6.6 %copy-start.20 = (bf16[16,48,256]{2,1,0:T(8,128)(2,1)S(1)}, bf16[16,48,256]{2,1,0:T(8,128)(2,1)}, u32[]{:S(2)}) copy-start(bf16[16,48,256]{2,1,0:T(8,128)(2,1)} %refs_9_.2) | copy-start | bytes 1179652
  12.2 12.4 %collective-permute-start.6 = (bf16[4,16,1408]{2,1,0:T(8,128)(2,1)S(1)}, bf16[4,16,1408]{2,1,0:T(8,128)(2,1)S(1)}, u32[]{:S(2)}, u32[]{:S(2)}) collective-permute-start(bf16[4,16,1408]{2,1,0:T(8,128)(2,1)S(1)} %shard_map.373.refs_0_), channel_id=1, source_target_pairs={{0,1},{1,0},{2,3},{3,2},{4,5},{5,4},{6,7},{7,6},{8,9},{9,8},{10,11... | collective-permute-start | bytes 540680 | tf_op jit(solution)/shard_map/ppermute | solution.py:647
  12.3 8.4 %collective-permute-start.5 = (bf16[4,16,1408]{2,1,0:T(8,128)(2,1)S(1)}, bf16[4,16,1408]{2,1,0:T(8,128)(2,1)S(1)}, u32[]{:S(2)}, u32[]{:S(2)}) collective-permute-start(bf16[4,16,1408]{2,1,0:T(8,128)(2,1)S(1)} %shard_map.373.refs_0_), channel_id=1, source_target_pairs={{0,24},{1,25},{2,26},{3,27},{4,28},{5,29},{6,30},{7,31},{8,16},{9,... | collective-permute-start | bytes 540680 | tf_op jit(solution)/shard_map/ppermute | solution.py:647
  14.8 9.2 %collective-permute-start.4 = (bf16[4,16,1408]{2,1,0:T(8,128)(2,1)S(1)}, bf16[4,16,1408]{2,1,0:T(8,128)(2,1)S(1)}, u32[]{:S(2)}, u32[]{:S(2)}) collective-permute-start(bf16[4,16,1408]{2,1,0:T(8,128)(2,1)S(1)} %shard_map.373.refs_0_), channel_id=1, source_target_pairs={{0,16},{1,17},{2,18},{3,19},{4,20},{5,21},{6,22},{7,23},{8,24},{9,... | collective-permute-start | bytes 540680 | tf_op jit(solution)/shard_map/ppermute | solution.py:647
  15.3 8.8 %collective-permute-start.3 = (bf16[4,16,1408]{2,1,0:T(8,128)(2,1)S(1)}, bf16[4,16,1408]{2,1,0:T(8,128)(2,1)S(1)}, u32[]{:S(2)}, u32[]{:S(2)}) collective-permute-start(bf16[4,16,1408]{2,1,0:T(8,128)(2,1)S(1)} %shard_map.373.refs_0_), channel_id=1, source_target_pairs={{0,8},{1,9},{2,10},{3,11},{4,12},{5,13},{6,14},{7,15},{8,0},{9,1},... | collective-permute-start | bytes 540680 | tf_op jit(solution)/shard_map/ppermute | solution.py:647
  16.4 8.2 %collective-permute-start.10 = (bf16[12,48,256]{2,1,0:T(8,128)(2,1)S(1)}, bf16[12,48,256]{2,1,0:T(8,128)(2,1)S(1)}, u32[]{:S(2)}, u32[]{:S(2)}) collective-permute-start(bf16[12,48,256]{2,1,0:T(8,128)(2,1)S(1)} %get-tuple-element.117), channel_id=1, source_target_pairs={{1,2},{2,1},{3,4},{4,3},{5,6},{6,5},{9,10},{10,9},{11,12},{12,11},... | collective-permute-start | bytes 884744 | tf_op jit(solution)/shard_map/ppermute | solution.py:756
  20.7 4.0 %collective-permute-start.11 = (bf16[12,48,256]{2,1,0:T(8,128)(2,1)S(1)}, bf16[12,48,256]{2,1,0:T(8,128)(2,1)S(1)}, u32[]{:S(2)}, u32[]{:S(2)}) collective-permute-start(bf16[12,48,256]{2,1,0:T(8,128)(2,1)S(1)} %get-tuple-element.118), channel_id=1, source_target_pairs={{0,1},{1,0},{2,3},{3,2},{4,5},{5,4},{6,7},{7,6},{8,9},{9,8},{10,11... | collective-permute-start | bytes 884744 | tf_op jit(solution)/shard_map/ppermute | solution.py:755
  24.2 1.4 %collective-permute-start.7 = (bf16[4,16,1408]{2,1,0:T(8,128)(2,1)S(1)}, bf16[4,16,1408]{2,1,0:T(8,128)(2,1)S(1)}, u32[]{:S(2)}, u32[]{:S(2)}) collective-permute-start(bf16[4,16,1408]{2,1,0:T(8,128)(2,1)S(1)} %collective-permute-done.3.refs_1_), channel_id=1, source_target_pairs={{0,1},{1,0},{2,3},{3,2},{4,5},{5,4},{6,7},{7,6},{8,9},{9,8},{10,11... | collective-permute-start | bytes 540680 | tf_op jit(solution)/shard_map/ppermute | solution.py:647
  24.2 1.7 %collective-permute-start.8 = (bf16[4,16,1408]{2,1,0:T(8,128)(2,1)S(1)}, bf16[4,16,1408]{2,1,0:T(8,128)(2,1)S(1)}, u32[]{:S(2)}, u32[]{:S(2)}) collective-permute-start(bf16[4,16,1408]{2,1,0:T(8,128)(2,1)S(1)} %collective-permute-done.4.refs_2_), channel_id=1, source_target_pairs={{0,1},{1,0},{2,3},{3,2},{4,5},{5,4},{6,7},{7,6},{8,9},{9,8},{10,11... | collective-permute-start | bytes 540680 | tf_op jit(solution)/shard_map/ppermute | solution.py:647
  24.7 1.4 %collective-permute-start.9 = (bf16[4,16,1408]{2,1,0:T(8,128)(2,1)S(1)}, bf16[4,16,1408]{2,1,0:T(8,128)(2,1)S(1)}, u32[]{:S(2)}, u32[]{:S(2)}) collective-permute-start(bf16[4,16,1408]{2,1,0:T(8,128)(2,1)S(1)} %collective-permute-done.5.refs_3_), channel_id=1, source_target_pairs={{0,1},{1,0},{2,3},{3,2},{4,5},{5,4},{6,7},{7,6},{8,9},{9,8},{10,11... | collective-permute-start | bytes 540680 | tf_op jit(solution)/shard_map/ppermute | solution.py:647
  37.7 2.3 %collective-permute-start.12 = (bf16[16,16,1408]{2,1,0:T(8,128)(2,1)S(1)}, bf16[16,16,1408]{2,1,0:T(8,128)(2,1)S(1)}, u32[]{:S(2)}, u32[]{:S(2)}) collective-permute-start(bf16[16,16,1408]{2,1,0:T(8,128)(2,1)S(1)} %slice.40), channel_id=1, source_target_pairs={{0,1},{1,0},{2,3},{3,2},{4,5},{5,4},{6,7},{7,6},{8,9},{9,8},{10,11... | collective-permute-start | bytes 2162696 | tf_op jit(solution)/shard_map/ppermute | solution.py:647
  40.2 7.4 %collective-permute-start.13 = (bf16[4,16,1408]{2,1,0:T(8,128)(2,1)S(1)}, bf16[4,16,1408]{2,1,0:T(8,128)(2,1)S(1)}, u32[]{:S(2)}, u32[]{:S(2)}) collective-permute-start(bf16[4,16,1408]{2,1,0:T(8,128)(2,1)S(1)} %get-tuple-element.184), channel_id=1, source_target_pairs={{0,8},{1,9},{2,10},{3,11},{4,12},{5,13},{6,14},{7,15},{8,0},{9,1},... | collective-permute-start | bytes 540680 | tf_op jit(solution)/shard_map/ppermute | solution.py:647
  41.8 10.0 %collective-permute-start.15 = (bf16[4,16,1408]{2,1,0:T(8,128)(2,1)S(1)}, bf16[4,16,1408]{2,1,0:T(8,128)(2,1)S(1)}, u32[]{:S(2)}, u32[]{:S(2)}) collective-permute-start(bf16[4,16,1408]{2,1,0:T(8,128)(2,1)S(1)} %get-tuple-element.185), channel_id=1, source_target_pairs={{0,24},{1,25},{2,26},{3,27},{4,28},{5,29},{6,30},{7,31},{8,16},{9,... | collective-permute-start | bytes 540680 | tf_op jit(solution)/shard_map/ppermute | solution.py:647
  43.2 10.0 %collective-permute-start.14 = (bf16[4,16,1408]{2,1,0:T(8,128)(2,1)S(1)}, bf16[4,16,1408]{2,1,0:T(8,128)(2,1)S(1)}, u32[]{:S(2)}, u32[]{:S(2)}) collective-permute-start(bf16[4,16,1408]{2,1,0:T(8,128)(2,1)S(1)} %get-tuple-element.186), channel_id=1, source_target_pairs={{0,16},{1,17},{2,18},{3,19},{4,20},{5,21},{6,22},{7,23},{8,24},{9,... | collective-permute-start | bytes 540680 | tf_op jit(solution)/shard_map/ppermute | solution.py:647
  43.8 14.0 %collective-permute-start.16 = (bf16[640,512]{1,0:T(8,128)(2,1)S(1)}, bf16[640,512]{1,0:T(8,128)(2,1)S(1)}, u32[]{:S(2)}, u32[]{:S(2)}) collective-permute-start(bf16[640,512]{1,0:T(8,128)(2,1)S(1)} %get-tuple-element.129), channel_id=1, source_target_pairs={{0,1},{1,0},{2,3},{3,2},{4,5},{5,4},{6,7},{7,6},{8,9},{9,8},{10,11... | collective-permute-start | bytes 1966088 | tf_op jit(solution)/shard_map/ppermute | solution.py:755
  43.8 14.0 %collective-permute-start.17 = (bf16[640,512]{1,0:T(8,128)(2,1)S(1)}, bf16[640,512]{1,0:T(8,128)(2,1)S(1)}, u32[]{:S(2)}, u32[]{:S(2)}) collective-permute-start(bf16[640,512]{1,0:T(8,128)(2,1)S(1)} %get-tuple-element.130), channel_id=1, source_target_pairs={{1,2},{2,1},{3,4},{4,3},{5,6},{6,5},{9,10},{10,9},{11,12},{12,11},... | collective-permute-start | bytes 1966088 | tf_op jit(solution)/shard_map/ppermute | solution.py:756
  53.4 7.4 %collective-permute-start.20 = (bf16[16,1408]{1,0:T(8,128)(2,1)S(1)}, bf16[16,1408]{1,0:T(8,128)(2,1)S(1)}, u32[]{:S(2)}, u32[]{:S(2)}) collective-permute-start(bf16[16,1408]{1,0:T(8,128)(2,1)S(1)} %get-tuple-element.187), channel_id=1, source_target_pairs={{0,6},{1,7},{2,4},{3,5},{4,2},{5,3},{6,0},{7,1},{8,14},{9,15},{10,... | collective-permute-start | bytes 135176 | tf_op jit(solution)/shard_map/ppermute | solution.py:647
  55.5 5.3 %collective-permute-start.19 = (bf16[16,1408]{1,0:T(8,128)(2,1)S(1)}, bf16[16,1408]{1,0:T(8,128)(2,1)S(1)}, u32[]{:S(2)}, u32[]{:S(2)}) collective-permute-start(bf16[16,1408]{1,0:T(8,128)(2,1)S(1)} %get-tuple-element.188), channel_id=1, source_target_pairs={{0,4},{1,5},{2,6},{3,7},{4,0},{5,1},{6,2},{7,3},{8,12},{9,13},{10,... | collective-permute-start | bytes 135176 | tf_op jit(solution)/shard_map/ppermute | solution.py:647
  55.6 5.3 %collective-permute-start.18 = (bf16[16,1408]{1,0:T(8,128)(2,1)S(1)}, bf16[16,1408]{1,0:T(8,128)(2,1)S(1)}, u32[]{:S(2)}, u32[]{:S(2)}) collective-permute-start(bf16[16,1408]{1,0:T(8,128)(2,1)S(1)} %get-tuple-element.189), channel_id=1, source_target_pairs={{0,2},{1,3},{2,0},{3,1},{4,6},{5,7},{6,4},{7,5},{8,10},{9,11},{10,... | collective-permute-start | bytes 135176 | tf_op jit(solution)/shard_map/ppermute | solution.py:647
  57.8 3.0 %copy-start = (f32[8,768]{1,0:T(8,128)S(1)}, f32[8,768]{1,0:T(8,128)}, u32[]{:S(2)}) copy-start(f32[8,768]{1,0:T(8,128)} %refs_4_.3) | copy-start | bytes 73732
  57.9 3.0 %copy-start.1 = (f32[8,768]{1,0:T(8,128)S(1)}, f32[8,768]{1,0:T(8,128)}, u32[]{:S(2)}) copy-start(f32[8,768]{1,0:T(8,128)} %refs_6_.3) | copy-start | bytes 73732
  57.9 3.0 %copy-start.2 = (f32[24,256]{1,0:T(8,128)S(1)}, f32[24,256]{1,0:T(8,128)}, u32[]{:S(2)}) copy-start(f32[24,256]{1,0:T(8,128)} %refs_7_.3) | copy-start | bytes 73732
  57.9 3.0 %copy-start.3 = (f32[8,768]{1,0:T(8,128)S(1)}, f32[8,768]{1,0:T(8,128)}, u32[]{:S(2)}) copy-start(f32[8,768]{1,0:T(8,128)} %refs_10_.3) | copy-start | bytes 73732
  57.9 3.0 %copy-start.4 = (f32[8,768]{1,0:T(8,128)S(1)}, f32[8,768]{1,0:T(8,128)}, u32[]{:S(2)}) copy-start(f32[8,768]{1,0:T(8,128)} %refs_12_.3) | copy-start | bytes 73732
  57.9 3.0 %copy-start.5 = (f32[24,256]{1,0:T(8,128)S(1)}, f32[24,256]{1,0:T(8,128)}, u32[]{:S(2)}) copy-start(f32[24,256]{1,0:T(8,128)} %refs_13_.3) | copy-start | bytes 73732
  57.9 3.0 %copy-start.6 = (f32[8,768]{1,0:T(8,128)S(1)}, f32[8,768]{1,0:T(8,128)}, u32[]{:S(2)}) copy-start(f32[8,768]{1,0:T(8,128)} %refs_2_.1) | copy-start | bytes 73732
  57.9 3.0 %copy-start.7 = (f32[8,768]{1,0:T(8,128)S(1)}, f32[8,768]{1,0:T(8,128)}, u32[]{:S(2)}) copy-start(f32[8,768]{1,0:T(8,128)} %refs_0_.1) | copy-start | bytes 73732
  57.9 3.0 %copy-start.8 = (f32[24,256]{1,0:T(8,128)S(1)}, f32[24,256]{1,0:T(8,128)}, u32[]{:S(2)}) copy-start(f32[24,256]{1,0:T(8,128)} %refs_3_.1) | copy-start | bytes 73732
  57.9 3.0 %copy-start.9 = (f32[8,256]{1,0:T(8,128)S(1)}, f32[8,256]{1,0:T(8,128)}, u32[]{:S(2)}) copy-start(f32[8,256]{1,0:T(8,128)} %refs_5_.4) | copy-start | bytes 24580
  58.0 3.0 %copy-start.10 = (f32[8,256]{1,0:T(8,128)S(1)}, f32[8,256]{1,0:T(8,128)}, u32[]{:S(2)}) copy-start(f32[8,256]{1,0:T(8,128)} %refs_11_.3) | copy-start | bytes 24580
  58.0 3.0 %copy-start.11 = (f32[8,256]{1,0:T(8,128)S(1)}, f32[8,256]{1,0:T(8,128)}, u32[]{:S(2)}) copy-start(f32[8,256]{1,0:T(8,128)} %refs_1_.1) | copy-start | bytes 24580
  58.0 3.0 %copy-start.12 = (f32[11,8]{0,1:T(8,128)S(1)}, f32[11,8]{0,1:T(8,128)}, u32[]{:S(2)}) copy-start(f32[11,8]{0,1:T(8,128)} %param.38) | copy-start | bytes 1060
  58.0 3.0 %copy-start.13 = (f32[8,49]{1,0:T(8,128)S(1)}, f32[8,49]{1,0:T(8,128)}, u32[]{:S(2)}) copy-start(f32[8,49]{1,0:T(8,128)} %refs_9_.4) | copy-start | bytes 4708
  58.0 3.0 %copy-start.14 = (f32[11,8]{0,1:T(8,128)S(1)}, f32[11,8]{0,1:T(8,128)}, u32[]{:S(2)}) copy-start(f32[11,8]{0,1:T(8,128)} %param.39) | copy-start | bytes 1060
  58.0 3.0 %copy-start.15 = (f32[8,49]{1,0:T(8,128)S(1)}, f32[8,49]{1,0:T(8,128)}, u32[]{:S(2)}) copy-start(f32[8,49]{1,0:T(8,128)} %refs_15_.3) | copy-start | bytes 4708
  58.0 3.0 %copy-start.16 = (f32[11,8]{0,1:T(8,128)S(1)}, f32[11,8]{0,1:T(8,128)}, u32[]{:S(2)}) copy-start(f32[11,8]{0,1:T(8,128)} %param.28) | copy-start | bytes 1060
  58.0 3.0 %copy-start.18 = (f32[8,49]{1,0:T(8,128)S(1)}, f32[8,49]{1,0:T(8,128)}, u32[]{:S(2)}) copy-start(f32[8,49]{1,0:T(8,128)} %refs_5_.5) | copy-start | bytes 4708
  61.3 1.2 %collective-permute-start.21 = (f32[8,128]{1,0:T(8,128)S(1)}, f32[8,128]{1,0:T(8,128)S(1)}, u32[]{:S(2)}, u32[]{:S(2)}) collective-permute-start(f32[8,128]{1,0:T(8,128)S(1)} %get-tuple-element.142.mine_ref), channel_id=1, source_target_pairs={{0,1},{1,0},{2,3},{3,2},{4,5},{5,4},{6,7},{7,6},{8,9},{9,8},{10,11... | collective-permute-start | bytes 12296 | tf_op jit(solution)/shard_map/ppermute | solution.py:647
  62.5 5.4 %collective-permute-start.24 = (f32[8,128]{1,0:T(8,128)S(1)}, f32[8,128]{1,0:T(8,128)S(1)}, u32[]{:S(2)}, u32[]{:S(2)}) collective-permute-start(f32[8,128]{1,0:T(8,128)S(1)} %add.66), channel_id=1, source_target_pairs={{0,6},{1,7},{2,4},{3,5},{4,2},{5,3},{6,0},{7,1},{8,14},{9,15},{10,... | collective-permute-start | bytes 12296 | tf_op jit(solution)/shard_map/ppermute | solution.py:647
  64.6 4.5 %collective-permute-start.23 = (f32[8,128]{1,0:T(8,128)S(1)}, f32[8,128]{1,0:T(8,128)S(1)}, u32[]{:S(2)}, u32[]{:S(2)}) collective-permute-start(f32[8,128]{1,0:T(8,128)S(1)} %add.66), channel_id=1, source_target_pairs={{0,4},{1,5},{2,6},{3,7},{4,0},{5,1},{6,2},{7,3},{8,12},{9,13},{10,... | collective-permute-start | bytes 12296 | tf_op jit(solution)/shard_map/ppermute | solution.py:647
  65.0 4.1 %collective-permute-start.22 = (f32[8,128]{1,0:T(8,128)S(1)}, f32[8,128]{1,0:T(8,128)S(1)}, u32[]{:S(2)}, u32[]{:S(2)}) collective-permute-start(f32[8,128]{1,0:T(8,128)S(1)} %add.66), channel_id=1, source_target_pairs={{0,2},{1,3},{2,0},{3,1},{4,6},{5,7},{6,4},{7,5},{8,10},{9,11},{10,... | collective-permute-start | bytes 12296 | tf_op jit(solution)/shard_map/ppermute | solution.py:647
  69.1 4.6 %collective-permute-start.27 = (f32[8,128]{1,0:T(8,128)S(1)}, f32[8,128]{1,0:T(8,128)S(1)}, u32[]{:S(2)}, u32[]{:S(2)}) collective-permute-start(f32[8,128]{1,0:T(8,128)S(1)} %add_add_fusion.a_ref), channel_id=1, source_target_pairs={{0,24},{1,25},{2,26},{3,27},{4,28},{5,29},{6,30},{7,31},{8,16},{9,... | collective-permute-start | bytes 12296 | tf_op jit(solution)/shard_map/ppermute | solution.py:647
  70.8 3.6 %collective-permute-start.26 = (f32[8,128]{1,0:T(8,128)S(1)}, f32[8,128]{1,0:T(8,128)S(1)}, u32[]{:S(2)}, u32[]{:S(2)}) collective-permute-start(f32[8,128]{1,0:T(8,128)S(1)} %add_add_fusion.a_ref), channel_id=1, source_target_pairs={{0,16},{1,17},{2,18},{3,19},{4,20},{5,21},{6,22},{7,23},{8,24},{9,... | collective-permute-start | bytes 12296 | tf_op jit(solution)/shard_map/ppermute | solution.py:647
  71.9 3.6 %collective-permute-start.25 = (f32[8,128]{1,0:T(8,128)S(1)}, f32[8,128]{1,0:T(8,128)S(1)}, u32[]{:S(2)}, u32[]{:S(2)}) collective-permute-start(f32[8,128]{1,0:T(8,128)S(1)} %add_add_fusion.a_ref), channel_id=1, source_target_pairs={{0,8},{1,9},{2,10},{3,11},{4,12},{5,13},{6,14},{7,15},{8,0},{9,1},... | collective-permute-start | bytes 12296 | tf_op jit(solution)/shard_map/ppermute | solution.py:647
